TPU v7x, 512 devices: a whole 4x8x8 slice. The times are simulated.
512 devices in a mesh: ctx: 128 (over y_hi, z, x), kv: 4 (over y_lo, core).
Axes of the slice: x: 4, y: 8 (y_hi: 4, y_lo: 2; y = y_hi * 2 + y_lo), z: 8, core: 2. Of those that a mesh axis runs over, the one named last changes fastest.
Arguments:
- queries: bfloat16 [16384, 64, 128], P('ctx', 'kv'), may hold values from -64 to 64
- keys: bfloat16 [16384, 8, 128], P('ctx', 'kv'), may hold values from -6.5 to 6.5
- values: bfloat16 [16384, 8, 128], P('ctx', 'kv'), may hold values from -6 to 6
- block_start: int32 [128], replicated, may hold values from 0 to 16256, as said below
- depth_k: float32 [32, 128], replicated, may hold values from -1 to 1
- point_k: float32 [128, 128], replicated, may hold values from -0.5 to 0.5
- depth_v: float32 [32, 128], replicated, may hold values from -1 to 1
- point_v: float32 [128, 128], replicated, may hold values from -0.5 to 0.5
Outputs:
- attended: bfloat16 [16384, 8192], P(('ctx', 'kv'))
Inputs may be any that keep to these rules, and one draw needn't show every extreme that they name: `block_start`: every entry is a multiple of 128; consecutive blocks of the array hold consecutive blocks of the document, the last block of the array followed by the first, starting at a drawn block, so the entries are 0 to 16256 each once.
All inputs are finite; a program needn't handle non-finite values.
Results may differ from a plain program's by a relative error of at most 0.014.
The roundings to bfloat16 on the way count: a program that leaves them out, or rounds other values in their place, can miss the bound.
Values may be sent and summed in bfloat16 or wider, within the bound.
No kernel may reach another device: no remote copies, remote signals or barrier semaphores. Data moves between devices by JAX's collectives and lax.ppermute only.
A program may use at most 64 MiB of HBM per device.

v0:
```python
import math

import jax
import jax.numpy as jnp
from jax import lax
from jax.sharding import PartitionSpec as P

rope_base = 500000.0
orig_context = 8192.0
yarn_factor = 16.0
beta_fast = 32.0
beta_slow = 1.0
neg_large = -1e30


def from_behind(block, axis, distance):
    devices = range(lax.axis_size(axis))
    route = [((i - distance) % len(devices), i) for i in devices]
    return lax.ppermute(block, axis, route)


def yarn_table(width):
    index = jnp.arange(width // 2, dtype=jnp.float32)
    inverse = jnp.exp(-(2.0 * index / width) * math.log(rope_base))
    ratio = orig_context * inverse / (2.0 * math.pi)
    ramp = jnp.clip((ratio - beta_slow) / (beta_fast - beta_slow), 0.0, 1.0)
    return inverse * (ramp + (1.0 - ramp) / yarn_factor)


def rotary(field, places, freqs):
    angle = places.astype(jnp.float32)[:, None] * freqs[None, :]
    cosine = jnp.cos(angle)[:, None, :]
    sine = jnp.sin(angle)[:, None, :]
    half = field.shape[-1] // 2
    data = field.astype(jnp.float32)
    first = data[..., :half]
    second = data[..., half:]
    mscale = 1.0 + 0.1 * math.log(yarn_factor)
    turned = (
        jnp.concatenate([first * cosine - second * sine, second * cosine + first * sine], axis=-1)
        * mscale
    )
    return turned.astype(jnp.bfloat16)


def compress(field, depth, point):
    rows, heads, width = field.shape
    stride = depth.shape[0]
    grouped = field.astype(jnp.float32).reshape(rows // stride, stride, heads, width)
    pooled = jnp.sum(grouped * depth[None, :, None, :], axis=1)
    mixed = jnp.dot(
        pooled.reshape(-1, width),
        point,
        precision=lax.Precision.HIGHEST,
        preferred_element_type=jnp.float32,
    )
    return mixed.reshape(rows // stride, heads, width).astype(jnp.bfloat16)


def lookup(table, which):
    hits = which[..., None] == jnp.arange(table.shape[0], dtype=jnp.int32)
    return jnp.sum(jnp.where(hits, table, 0), axis=-1)


def take_tile(state, grouped, tile_keys, tile_values, valid):
    highest, total, mixed = state
    scale = 1.0 / math.sqrt(grouped.shape[-1])
    scores = (
        jnp.einsum("tgqd,sgd->tgqs", grouped, tile_keys, preferred_element_type=jnp.float32) * scale
    )
    masked = jnp.where(valid, scores, neg_large)
    new_high = jnp.maximum(highest, jnp.max(masked, axis=-1))
    weight = jnp.where(valid, jnp.exp(masked - new_high[..., None]), 0.0)
    factor = jnp.exp(highest - new_high)
    total = total * factor + jnp.sum(weight, axis=-1)
    update = jnp.einsum(
        "tgqs,sgd->tgqd",
        weight.astype(jnp.bfloat16),
        tile_values,
        preferred_element_type=jnp.float32,
    )
    mixed = mixed * factor[..., None] + update
    return (new_high, total, mixed)


def maybe_tile(state, grouped, tile_keys, tile_values, valid):
    return take_tile(state, grouped, tile_keys, tile_values, valid)


def shards(queries, keys, values, block_start, depth_k, point_k, depth_v, point_v):
    rows_here, heads_here, width = queries.shape
    kv_here = keys.shape[1]
    ctx_size = lax.axis_size("ctx")
    own_index = lax.axis_index("ctx")
    offsets = jnp.arange(rows_here, dtype=jnp.int32)
    own_places = lookup(block_start, own_index) + offsets
    freqs = yarn_table(width)
    rot_q = rotary(queries, own_places, freqs)
    rot_k = rotary(keys, own_places, freqs)
    mem_k = compress(rot_k, depth_k, point_k)
    mem_v = compress(values, depth_v, point_v)
    grouped = rot_q.reshape(rows_here, kv_here, heads_here // kv_here, width)
    win_blocks = min(8, ctx_size - 1)
    window = win_blocks * rows_here
    stat_shape = (rows_here, kv_here, heads_here // kv_here)
    state = (
        jnp.full(stat_shape, neg_large, jnp.float32),
        jnp.zeros(stat_shape, jnp.float32),
        jnp.zeros(stat_shape + (width,), jnp.float32),
    )

    def raw_valid(key_places):
        inside = (key_places[None, :] <= own_places[:, None]) & (
            key_places[None, :] > own_places[:, None] - window
        )
        return inside[:, None, None, :]

    state = maybe_tile(state, grouped, rot_k, values, raw_valid(own_places))
    moving_k = rot_k
    moving_v = values
    for back in range(1, win_blocks + 1):
        moving_k, moving_v = from_behind((moving_k, moving_v), "ctx", 1)
        source = (own_index - back) % ctx_size
        state = maybe_tile(
            state, grouped, moving_k, moving_v, raw_valid(lookup(block_start, source) + offsets)
        )
    slots_here = mem_k.shape[0]
    stride = depth_k.shape[0]
    carry = state
    piece = (
        lax.all_gather(mem_k, "ctx", axis=0, tiled=True),
        lax.all_gather(mem_v, "ctx", axis=0, tiled=True),
    )
    count = piece[0].shape[0]
    span = 512

    def one_span(inner, offset):
        span_k = piece[0]
        span_v = piece[1]
        index = offset + jnp.arange(span, dtype=jnp.int32)
        ends = lookup(block_start, index // slots_here) + index % slots_here * stride + stride
        valid = (ends[None, :] <= own_places[:, None] + 1)[:, None, None, :]
        return (maybe_tile(inner, grouped, span_k, span_v, valid), None)

    carry, unused = lax.scan(one_span, carry, jnp.arange(count // span, dtype=jnp.int32) * span)
    state = carry
    highest, total, mixed = state
    attended = (
        (mixed / total[..., None]).astype(jnp.bfloat16).reshape(rows_here, heads_here * width)
    )
    return lax.all_to_all(attended, "kv", split_axis=0, concat_axis=1, tiled=True)


def solution(mesh):
    placed = (
        P("ctx", "kv", None),
        P("ctx", "kv", None),
        P("ctx", "kv", None),
        P(),
        P(),
        P(),
        P(),
        P(),
    )
    return jax.shard_map(
        shards, mesh=mesh, in_specs=placed, out_specs=P(("ctx", "kv"), None), check_vma=False
    )
```

profile of v0, /device:TPU:1, one launch (start us, length us, event | category | flops | bytes accessed | tf_op | source)
XLA Modules:
  0.0 881.3 jit_solution(9896192601183455299)
XLA Ops:
  0.1 1.5 fusion.148
  1.6 0.7 fusion.161
  2.3 0.9 copy_convert_fusion
  3.7 3.9 collective-permute-start
  7.7 0.9 copy.88
  8.5 3.1 collective-permute-start.1
  11.6 0.7 broadcast_add_fusion
  12.4 0.7 iota_add_fusion.8
  13.1 1.1 convert_element_type.72
  14.2 0.3 multiply_subtract_fusion
  14.6 0.3 copy.84
  14.9 0.3 copy.85
  15.6 324.6 %all_gather.6 = bf16[512,2,128]{2,1,0:T(2,128)(2,1)S(1)} all-gather(bf16[4,2,128]{2,1,0:T(2,128)(2,1)S(1)} %copy.97), channel_id=1, replica_groups=mesh['ctx'=128,'kv'=4] {'ctx'}, dimensions={0}, use_global_device_ids=true | all-gather | bytes 264192 | tf_op jit(solution)/shard_map/all_gather | solution.py:131
  340.8 0.4 fusion.48
  341.3 1.2 iota_add_fusion.2
  342.5 1.2 iota_add_fusion.4
  343.7 1.2 iota_add_fusion.6
  344.9 1.3 iota_add_fusion
  346.5 0.3 fusion.173
  346.8 0.8 fusion
  347.6 312.9 %all_gather.7 = bf16[512,2,128]{2,1,0:T(2,128)(2,1)S(1)} all-gather(bf16[4,2,128]{2,1,0:T(2,128)(2,1)S(1)} %copy.100), channel_id=1, replica_groups=mesh['ctx'=128,'kv'=4] {'ctx'}, dimensions={0}, use_global_device_ids=true | all-gather | bytes 264192 | tf_op jit(solution)/shard_map/all_gather | solution.py:132
  660.5 3.5 collective-permute-start.2
  664.4 1.9 collective-permute-start.3
  666.3 5.7 collective-permute-done.2
  672.0 1.9 collective-permute-start.4
  674.2 1.5 collective-permute-done.3
  675.7 1.9 collective-permute-start.5
  677.6 5.7 collective-permute-done.4
  683.3 1.9 collective-permute-start.6
  685.5 1.5 collective-permute-done.5
  687.0 1.9 collective-permute-start.7
  688.9 5.7 collective-permute-done.6
  694.6 1.9 collective-permute-start.8
  696.6 0.3 fusion.169
  696.9 1.5 collective-permute-done.7
  698.3 1.9 collective-permute-start.9
  700.3 6.2 collective-permute-done.8
  706.5 1.9 collective-permute-start.10
  708.7 1.6 collective-permute-done.9
  710.4 1.9 collective-permute-start.11
  712.3 5.5 collective-permute-done.10
  717.8 1.9 collective-permute-start.12
  720.1 1.9 collective-permute-done.11
  722.0 1.9 collective-permute-start.13
  723.9 5.2 collective-permute-done.12
  729.1 1.9 collective-permute-start.14
  731.1 0.3 fusion.166
  731.4 1.9 collective-permute-done.13
  733.3 2.1 collective-permute-start.15
  735.4 5.0 collective-permute-done.14
  740.8 1.0 fusion.1
  741.8 1.4 fusion.6
  745.2 0.8 fusion.10
  746.0 0.5 fusion.12
  746.5 0.5 fusion.14
  747.1 0.5 fusion.16
  747.6 0.5 fusion.18
  748.2 0.5 fusion.20
  748.7 0.5 fusion.22
  749.3 0.5 fusion.24
  749.8 0.9 fusion.47
  750.8 0.3 copy.104
  751.4 129.1 %all_to_all.19 = bf16[4,32,2048]{2,1,0:T(8,128)(2,1)S(1)} all-to-all(bf16[4,32,2048]{2,1,0:T(8,128)(2,1)S(1)} %all_to_all.14), channel_id=1, replica_groups=mesh['ctx'=128,'kv'=4] {'kv'}, dimensions={0} | all-to-all | bytes 1048576 | tf_op jit(solution)/shard_map/all_to_all | solution.py:151
  880.5 0.8 copy.143
  (48 shorter events, 5.7 us)
Async XLA Ops:
  0.0 15.4 %copy-start = (f32[128,128]{1,0:T(8,128)S(1)}, f32[128,128]{1,0:T(8,128)}, u32[]{:S(2)}) copy-start(f32[128,128]{1,0:T(8,128)} %param.13) | copy-start | bytes 196612
  3.7 656.8 %collective-permute-start = (bf16[128,2,128]{2,0,1:T(8,128)(2,1)S(1)}, bf16[128,2,128]{2,0,1:T(8,128)(2,1)S(1)}, u32[]{:S(2)}, u32[]{:S(2)}) collective-permute-start(bf16[128,2,128]{2,0,1:T(8,128)(2,1)S(1)} %fusion.106), channel_id=1, source_target_pairs={{508,0},{0,4},{4,8},{8,12},{12,16},{16,20},{20,24},{24,28},{28,32}... | collective-permute-start | bytes 196616 | tf_op jit(solution)/shard_map/ppermute | solution.py:19
  8.5 655.8 %collective-permute-start.1 = (bf16[128,2,128]{2,0,1:T(8,128)(2,1)S(1)}, bf16[128,2,128]{2,0,1:T(8,128)(2,1)S(1)}, u32[]{:S(2)}, u32[]{:S(2)}) collective-permute-start(bf16[128,2,128]{2,0,1:T(8,128)(2,1)S(1)} %copy.88), channel_id=1, source_target_pairs={{508,0},{0,4},{4,8},{8,12},{12,16},{16,20},{20,24},{24,28},{28,32}... | collective-permute-start | bytes 196616 | tf_op jit(solution)/shard_map/ppermute | solution.py:19
  14.2 1.1 copy-start.3
  14.2 326.1 %copy-start.5 = (s32[128]{0:T(128)S(1)}, s32[128]{0:T(128)}, u32[]{:S(2)}) copy-start(s32[128]{0:T(128)} %param.11) | copy-start | bytes 1540
  14.2 326.3 %copy-start.1 = (bf16[128,2,128]{2,1,0:T(2,128)(2,1)S(1)}, bf16[128,2,128]{2,1,0:T(2,128)(2,1)}, u32[]{:S(2)}) copy-start(bf16[128,2,128]{2,1,0:T(2,128)(2,1)} %param.10) | copy-start | bytes 196612
  14.2 326.3 %copy-start.4 = (f32[32,128]{1,0:T(8,128)S(1)}, f32[32,128]{1,0:T(8,128)}, u32[]{:S(2)}) copy-start(f32[32,128]{1,0:T(8,128)} %param.14) | copy-start | bytes 49156
  14.2 326.4 %copy-start.2 = (f32[128,128]{1,0:T(8,128)S(1)}, f32[128,128]{1,0:T(8,128)}, u32[]{:S(2)}) copy-start(f32[128,128]{1,0:T(8,128)} %param.15) | copy-start | bytes 196612
  660.5 11.4 %collective-permute-start.2 = (bf16[128,2,128]{2,0,1:T(8,128)(2,1)S(1)}, bf16[128,2,128]{2,0,1:T(8,128)(2,1)S(1)}, u32[]{:S(2)}, u32[]{:S(2)}) collective-permute-start(bf16[128,2,128]{2,0,1:T(8,128)(2,1)S(1)} %collective-permute-done), channel_id=1, source_target_pairs={{508,0},{0,4},{4,8},{8,12},{12,16},{16,20},{20,24},{24,28},{28,32}... | collective-permute-start | bytes 196616 | tf_op jit(solution)/shard_map/ppermute | solution.py:19
  664.4 11.3 %collective-permute-start.3 = (bf16[128,2,128]{2,0,1:T(8,128)(2,1)S(1)}, bf16[128,2,128]{2,0,1:T(8,128)(2,1)S(1)}, u32[]{:S(2)}, u32[]{:S(2)}) collective-permute-start(bf16[128,2,128]{2,0,1:T(8,128)(2,1)S(1)} %collective-permute-done.1), channel_id=1, source_target_pairs={{508,0},{0,4},{4,8},{8,12},{12,16},{16,20},{20,24},{24,28},{28,32}... | collective-permute-start | bytes 196616 | tf_op jit(solution)/shard_map/ppermute | solution.py:19
  672.0 11.3 %collective-permute-start.4 = (bf16[128,2,128]{2,0,1:T(8,128)(2,1)S(1)}, bf16[128,2,128]{2,0,1:T(8,128)(2,1)S(1)}, u32[]{:S(2)}, u32[]{:S(2)}) collective-permute-start(bf16[128,2,128]{2,0,1:T(8,128)(2,1)S(1)} %collective-permute-done.2), channel_id=1, source_target_pairs={{508,0},{0,4},{4,8},{8,12},{12,16},{16,20},{20,24},{24,28},{28,32}... | collective-permute-start | bytes 196616 | tf_op jit(solution)/shard_map/ppermute | solution.py:19
  675.7 11.3 %collective-permute-start.5 = (bf16[128,2,128]{2,0,1:T(8,128)(2,1)S(1)}, bf16[128,2,128]{2,0,1:T(8,128)(2,1)S(1)}, u32[]{:S(2)}, u32[]{:S(2)}) collective-permute-start(bf16[128,2,128]{2,0,1:T(8,128)(2,1)S(1)} %collective-permute-done.3), channel_id=1, source_target_pairs={{508,0},{0,4},{4,8},{8,12},{12,16},{16,20},{20,24},{24,28},{28,32}... | collective-permute-start | bytes 196616 | tf_op jit(solution)/shard_map/ppermute | solution.py:19
  683.3 11.3 %collective-permute-start.6 = (bf16[128,2,128]{2,0,1:T(8,128)(2,1)S(1)}, bf16[128,2,128]{2,0,1:T(8,128)(2,1)S(1)}, u32[]{:S(2)}, u32[]{:S(2)}) collective-permute-start(bf16[128,2,128]{2,0,1:T(8,128)(2,1)S(1)} %collective-permute-done.4), channel_id=1, source_target_pairs={{508,0},{0,4},{4,8},{8,12},{12,16},{16,20},{20,24},{24,28},{28,32}... | collective-permute-start | bytes 196616 | tf_op jit(solution)/shard_map/ppermute | solution.py:19
  687.0 11.3 %collective-permute-start.7 = (bf16[128,2,128]{2,0,1:T(8,128)(2,1)S(1)}, bf16[128,2,128]{2,0,1:T(8,128)(2,1)S(1)}, u32[]{:S(2)}, u32[]{:S(2)}) collective-permute-start(bf16[128,2,128]{2,0,1:T(8,128)(2,1)S(1)} %collective-permute-done.5), channel_id=1, source_target_pairs={{508,0},{0,4},{4,8},{8,12},{12,16},{16,20},{20,24},{24,28},{28,32}... | collective-permute-start | bytes 196616 | tf_op jit(solution)/shard_map/ppermute | solution.py:19
  694.6 11.8 %collective-permute-start.8 = (bf16[128,2,128]{2,0,1:T(8,128)(2,1)S(1)}, bf16[128,2,128]{2,0,1:T(8,128)(2,1)S(1)}, u32[]{:S(2)}, u32[]{:S(2)}) collective-permute-start(bf16[128,2,128]{2,0,1:T(8,128)(2,1)S(1)} %collective-permute-done.6), channel_id=1, source_target_pairs={{508,0},{0,4},{4,8},{8,12},{12,16},{16,20},{20,24},{24,28},{28,32}... | collective-permute-start | bytes 196616 | tf_op jit(solution)/shard_map/ppermute | solution.py:19
  698.3 12.0 %collective-permute-start.9 = (bf16[128,2,128]{2,0,1:T(8,128)(2,1)S(1)}, bf16[128,2,128]{2,0,1:T(8,128)(2,1)S(1)}, u32[]{:S(2)}, u32[]{:S(2)}) collective-permute-start(bf16[128,2,128]{2,0,1:T(8,128)(2,1)S(1)} %collective-permute-done.7), channel_id=1, source_target_pairs={{508,0},{0,4},{4,8},{8,12},{12,16},{16,20},{20,24},{24,28},{28,32}... | collective-permute-start | bytes 196616 | tf_op jit(solution)/shard_map/ppermute | solution.py:19
  706.5 11.3 %collective-permute-start.10 = (bf16[128,2,128]{2,0,1:T(8,128)(2,1)S(1)}, bf16[128,2,128]{2,0,1:T(8,128)(2,1)S(1)}, u32[]{:S(2)}, u32[]{:S(2)}) collective-permute-start(bf16[128,2,128]{2,0,1:T(8,128)(2,1)S(1)} %collective-permute-done.8), channel_id=1, source_target_pairs={{508,0},{0,4},{4,8},{8,12},{12,16},{16,20},{20,24},{24,28},{28,32}... | collective-permute-start | bytes 196616 | tf_op jit(solution)/shard_map/ppermute | solution.py:19
  710.4 11.6 %collective-permute-start.11 = (bf16[128,2,128]{2,0,1:T(8,128)(2,1)S(1)}, bf16[128,2,128]{2,0,1:T(8,128)(2,1)S(1)}, u32[]{:S(2)}, u32[]{:S(2)}) collective-permute-start(bf16[128,2,128]{2,0,1:T(8,128)(2,1)S(1)} %collective-permute-done.9), channel_id=1, source_target_pairs={{508,0},{0,4},{4,8},{8,12},{12,16},{16,20},{20,24},{24,28},{28,32}... | collective-permute-start | bytes 196616 | tf_op jit(solution)/shard_map/ppermute | solution.py:19
  717.8 11.3 %collective-permute-start.12 = (bf16[128,2,128]{2,0,1:T(8,128)(2,1)S(1)}, bf16[128,2,128]{2,0,1:T(8,128)(2,1)S(1)}, u32[]{:S(2)}, u32[]{:S(2)}) collective-permute-start(bf16[128,2,128]{2,0,1:T(8,128)(2,1)S(1)} %collective-permute-done.10), channel_id=1, source_target_pairs={{508,0},{0,4},{4,8},{8,12},{12,16},{16,20},{20,24},{24,28},{28,32}... | collective-permute-start | bytes 196616 | tf_op jit(solution)/shard_map/ppermute | solution.py:19
  722.0 11.3 %collective-permute-start.13 = (bf16[128,2,128]{2,0,1:T(8,128)(2,1)S(1)}, bf16[128,2,128]{2,0,1:T(8,128)(2,1)S(1)}, u32[]{:S(2)}, u32[]{:S(2)}) collective-permute-start(bf16[128,2,128]{2,0,1:T(8,128)(2,1)S(1)} %collective-permute-done.11), channel_id=1, source_target_pairs={{508,0},{0,4},{4,8},{8,12},{12,16},{16,20},{20,24},{24,28},{28,32}... | collective-permute-start | bytes 196616 | tf_op jit(solution)/shard_map/ppermute | solution.py:19
  729.1 11.3 %collective-permute-start.14 = (bf16[128,2,128]{2,0,1:T(8,128)(2,1)S(1)}, bf16[128,2,128]{2,0,1:T(8,128)(2,1)S(1)}, u32[]{:S(2)}, u32[]{:S(2)}) collective-permute-start(bf16[128,2,128]{2,0,1:T(8,128)(2,1)S(1)} %collective-permute-done.12), channel_id=1, source_target_pairs={{508,0},{0,4},{4,8},{8,12},{12,16},{16,20},{20,24},{24,28},{28,32}... | collective-permute-start | bytes 196616 | tf_op jit(solution)/shard_map/ppermute | solution.py:19
  733.3 16.5 %collective-permute-start.15 = (bf16[128,2,128]{2,0,1:T(8,128)(2,1)S(1)}, bf16[128,2,128]{2,0,1:T(8,128)(2,1)S(1)}, u32[]{:S(2)}, u32[]{:S(2)}) collective-permute-start(bf16[128,2,128]{2,0,1:T(8,128)(2,1)S(1)} %collective-permute-done.13), channel_id=1, source_target_pairs={{508,0},{0,4},{4,8},{8,12},{12,16},{16,20},{20,24},{24,28},{28,32}... | collective-permute-start | bytes 196616 | tf_op jit(solution)/shard_map/ppermute | solution.py:19
where the time goes:
time: 882 us; the launch traced here: 881 us
  blocking collectives  767 us (87%)
  waiting for transfers between devices  49.1 us (6%)
  starting transfers between devices  35.5 us (4%)
  other arithmetic  15.4 us (2%)
  matrix products  10.9 us (1%)
    all_gather x1, blocking collectives, shards(): lax.all_gather(mem_k, 'ctx', axis=0, tiled=True)  325 us
    all_gather x1, blocking collectives, shards(): lax.all_gather(mem_v, 'ctx', axis=0, tiled=True)  313 us
    all_to_all x1, blocking collectives, shards(): lax.all_to_all(attended, 'kv', split_axis=0, concat_axis=1, tiled=True)  129 us
    ppermute x16, waiting for transfers between devices, from_behind(): return lax.ppermute(block, axis, route)  49.1 us
    ppermute x16, starting transfers between devices, from_behind(): return lax.ppermute(block, axis, route)  35.5 us
  transfers between devices with their start and end apart: 16, of which 13 were waited for; matrix products, arithmetic and copies ran while one was open for 3% of the time, Pallas kernels for 0%

commit v1 on v0

v1 whole, which is shorter than its diff:
```python
import math

import jax
import jax.numpy as jnp
import numpy as np
from jax import lax
from jax.experimental import pallas as pl
from jax.experimental.pallas import tpu as pltpu
from jax.sharding import PartitionSpec as P

HD = 128
TOK = 128
STRIDE = 32
SLOTS = TOK // STRIDE
WIN = 8
WINDOW = WIN * TOK
BLOCKS = 128
SEQ = BLOCKS * TOK
HEADS = 16
GROUPS = 2
KV = 4
MSCALE = 1.0 + 0.1 * math.log(16.0)
SCALE2 = math.log2(math.e) / math.sqrt(HD)
NEG = -1e30
BF = jnp.bfloat16
F32 = jnp.float32


def yarn_freqs():
    index = np.arange(HD // 2, dtype=np.float32)
    inverse = np.exp(np.float32(-(2.0 / HD) * math.log(500000.0)) * index).astype(np.float32)
    ratio = np.float32(8192.0) * inverse / np.float32(2.0 * math.pi)
    ramp = np.clip((ratio - 1.0) / 31.0, 0.0, 1.0).astype(np.float32)
    freqs = inverse * (ramp + (1.0 - ramp) / np.float32(16.0))
    return np.tile(np.concatenate([freqs, freqs])[None, :], (8, 1)).astype(np.float32)


def turn_tables(place0, freqs):
    places = (place0 + lax.broadcasted_iota(jnp.int32, (TOK, HD), 0)).astype(F32)
    angle = places * freqs
    first = lax.broadcasted_iota(jnp.int32, (TOK, HD), 1) < HD // 2
    sine = jnp.sin(angle)
    return jnp.cos(angle), jnp.where(first, -sine, sine)


def turn(x, cosine, sine):
    return ((x * cosine + pltpu.roll(x, HD // 2, 1) * sine) * MSCALE).astype(BF)


def prep_kernel(bs, freqs, k, v, dk, pk, dv, pv, own, mem, scr, pool):
    me = lax.axis_index("ctx")
    cosine, sine = turn_tables(bs[me], freqs[0:1, :])
    scr[...] = k[...].astype(F32)
    for g in range(GROUPS):
        rot = turn(scr[:, g, :], cosine, sine)
        own[g * TOK : (g + 1) * TOK, :] = rot
        grouped = rot.astype(F32).reshape(SLOTS, STRIDE, HD)
        pool[g * SLOTS : (g + 1) * SLOTS, :] = jnp.sum(grouped * dk[...][None], axis=1)
    scr[...] = v[...].astype(F32)
    for g in range(GROUPS):
        val = scr[:, g, :]
        own[(GROUPS + g) * TOK : (GROUPS + g + 1) * TOK, :] = val.astype(BF)
        grouped = val.reshape(SLOTS, STRIDE, HD)
        at = (GROUPS + g) * SLOTS
        pool[at : at + SLOTS, :] = jnp.sum(grouped * dv[...][None], axis=1)
    half = GROUPS * SLOTS
    mk = jnp.dot(pool[:half, :], pk[...], precision=lax.Precision.HIGHEST, preferred_element_type=F32)
    mv = jnp.dot(pool[half:, :], pv[...], precision=lax.Precision.HIGHEST, preferred_element_type=F32)
    both = jnp.concatenate([mk, mv], axis=0).astype(BF)
    mem[...] = jnp.broadcast_to(both[None], mem.shape)


def query_kernel(bs, freqs, q, rotq, scr):
    me = lax.axis_index("ctx")
    cosine, sine = turn_tables(bs[me], freqs[0:1, :])
    scr[...] = q[...].astype(F32)
    for h in range(HEADS):
        rotq[h * TOK : (h + 1) * TOK, :] = turn(scr[:, h, :], cosine, sine)


def octet_kernel(own, prev, out):
    me = lax.rem(lax.axis_index("ctx"), 8)
    for d in range(8):

        @pl.when(me <= d)
        def _():
            out[d] = own[...]

        @pl.when(me > d)
        def _():
            out[d] = prev[...]


def unit_rows(rows):
    r = lax.broadcasted_iota(jnp.int32, (rows, TOK), 0) & (TOK - 1)
    c = lax.broadcasted_iota(jnp.int32, (rows, TOK), 1)
    return jnp.where(r == c, 1.0, 0.0).astype(BF)


def attend(qa, keys, high):
    s = lax.dot_general(qa, keys, (((1,), (1,)), ((), ())), preferred_element_type=F32)
    top = jnp.max(s, axis=1, keepdims=True)
    if high is not None:
        top = jnp.maximum(top, high)
    return jnp.exp2((s - top) * SCALE2).astype(BF), top


ROWS = 256


def window_kernel(bs, rotq, recv, prev, acc, high, kaug, vaug):
    me = lax.axis_index("ctx")
    pos = lax.rem(me, 8)
    place = bs[me] + lax.broadcasted_iota(jnp.int32, (TOK, TOK), 1)
    row = lax.broadcasted_iota(jnp.int32, (TOK, TOK), 0)
    ones = jnp.ones((TOK, HD), BF)
    for b in range(WIN + 1):
        back = WIN if b == WIN else lax.rem(pos - b + 8, 8)
        there = bs[lax.rem(me - back + BLOCKS, BLOCKS)] + row
        ok = (there <= place) & (there > place - WINDOW)
        bias = jnp.where(ok, 0.0, NEG).astype(BF)
        span = slice(b * TOK, (b + 1) * TOK)
        for g in range(GROUPS):
            ks = slice(g * TOK, (g + 1) * TOK)
            vs = slice((GROUPS + g) * TOK, (GROUPS + g + 1) * TOK)
            kaug[g, span, :HD] = prev[ks, :] if b == WIN else recv[b, ks, :]
            kaug[g, span, HD:] = bias
            vaug[g, span, :HD] = prev[vs, :] if b == WIN else recv[b, vs, :]
            vaug[g, span, HD:] = ones
    unit = unit_rows(ROWS)
    for c in range(HEADS * TOK // ROWS):
        at = slice(c * ROWS, (c + 1) * ROWS)
        g = c * ROWS // (HEADS // GROUPS * TOK)
        qa = jnp.concatenate([rotq[at, :], unit], axis=1)
        w, top = attend(qa, kaug[g], None)
        acc[at, :] = jnp.dot(w, vaug[g], preferred_element_type=F32)
        high[at, :] = jnp.broadcast_to(top, (ROWS, HD))


def memory_kernel(bs, rotq, mem, acc, high, out, scr, kaug, vaug):
    me = lax.axis_index("ctx")
    place = bs[me] + lax.broadcasted_iota(jnp.int32, (BLOCKS, TOK), 1)
    start = (bs[0] + TOK * lax.broadcasted_iota(jnp.int32, (BLOCKS, TOK), 0)) & (SEQ - 1)
    scr[...] = mem[...].astype(F32)
    ones = jnp.ones((BLOCKS, HD), BF)
    for j in range(SLOTS):
        ok = start + (j + 1) * STRIDE <= place + 1
        bias = jnp.where(ok, 0.0, NEG).astype(BF)
        span = slice(j * BLOCKS, (j + 1) * BLOCKS)
        for g in range(GROUPS):
            kaug[g, span, :HD] = scr[:, g * SLOTS + j, :].astype(BF)
            kaug[g, span, HD:] = bias
            vaug[g, span, :HD] = scr[:, (GROUPS + g) * SLOTS + j, :].astype(BF)
            vaug[g, span, HD:] = ones
    unit = unit_rows(ROWS)
    rows = TOK // KV
    for c in range(HEADS * TOK // ROWS):
        at = slice(c * ROWS, (c + 1) * ROWS)
        g = c * ROWS // (HEADS // GROUPS * TOK)
        qa = jnp.concatenate([rotq[at, :], unit], axis=1)
        before = high[at, :]
        w, top = attend(qa, kaug[g], before[:, :1])
        keep = jnp.exp2((before - top) * SCALE2)
        new = jnp.dot(w, vaug[g], preferred_element_type=F32)
        old = acc[at, :]
        mixed = old[:, :HD] * keep + new[:, :HD]
        total = old[:, HD:] * keep + new[:, HD:]
        res = (mixed / total).astype(BF)
        for i in range(ROWS // TOK):
            h = c * (ROWS // TOK) + i
            for d in range(KV):
                lo = i * TOK + d * rows
                out[d, :, h * HD : (h + 1) * HD] = res[lo : lo + rows, :]


def call(kernel, out_shape, scratch, flops, *args):
    specs = [
        pl.BlockSpec(memory_space=pltpu.SMEM if i == 0 else pltpu.VMEM) for i in range(len(args))
    ]
    if kernel is octet_kernel:
        specs[0] = pl.BlockSpec(memory_space=pltpu.VMEM)
    multi = isinstance(out_shape, tuple)
    vm = pl.BlockSpec(memory_space=pltpu.VMEM)
    return pl.pallas_call(
        kernel,
        out_shape=out_shape,
        in_specs=specs,
        out_specs=(vm,) * len(out_shape) if multi else vm,
        scratch_shapes=scratch,
        compiler_params=pltpu.CompilerParams(vmem_limit_bytes=32 * 2**20),
        cost_estimate=pl.CostEstimate(flops=flops, bytes_accessed=2**20, transcendentals=0),
    )(*args)


def shape(*dims, dtype=BF):
    return jax.ShapeDtypeStruct(dims, dtype)


octets = [[8 * o + p for p in range(8)] for o in range(BLOCKS // 8)]


def shards(queries, keys, values, block_start, depth_k, point_k, depth_v, point_v):
    freqs = jnp.asarray(yarn_freqs())
    pack = 2 * GROUPS
    own, mem = call(
        prep_kernel,
        (shape(pack * TOK, HD), shape(BLOCKS, pack * SLOTS, HD)),
        [pltpu.VMEM((TOK, GROUPS, HD), F32), pltpu.VMEM((pack * SLOTS, HD), F32)],
        10**9,
        block_start, freqs, keys, values, depth_k, point_k, depth_v, point_v,
    )
    prev = lax.ppermute(own, "ctx", [((i - WIN) % BLOCKS, i) for i in range(BLOCKS)])
    mem = lax.all_to_all(mem, "ctx", 0, 0)
    rotq = call(
        query_kernel, shape(HEADS * TOK, HD), [pltpu.VMEM((TOK, HEADS, HD), F32)], 10**9,
        block_start, freqs, queries,
    )
    sent = call(octet_kernel, shape(8, pack * TOK, HD), [], 10**8, own, prev)
    recv = lax.all_to_all(sent, "ctx", 0, 0, axis_index_groups=octets)
    raw = (WIN + 1) * TOK
    acc, high = call(
        window_kernel,
        (shape(HEADS * TOK, 2 * HD, dtype=F32), shape(HEADS * TOK, HD, dtype=F32)),
        [pltpu.VMEM((GROUPS, raw, 2 * HD), BF), pltpu.VMEM((GROUPS, raw, 2 * HD), BF)],
        10**10,
        block_start, rotq, recv, prev,
    )
    slots = BLOCKS * SLOTS
    out = call(
        memory_kernel,
        shape(KV, TOK // KV, HEADS * HD),
        [
            pltpu.VMEM((BLOCKS, pack * SLOTS, HD), F32),
            pltpu.VMEM((GROUPS, slots, 2 * HD), BF),
            pltpu.VMEM((GROUPS, slots, 2 * HD), BF),
        ],
        5 * 10**9,
        block_start, rotq, mem, acc, high,
    )
    got = lax.all_to_all(out, "kv", 0, 0)
    return got.transpose(1, 0, 2).reshape(TOK // KV, KV * HEADS * HD)


def solution(mesh):
    placed = (
        P("ctx", "kv", None),
        P("ctx", "kv", None),
        P("ctx", "kv", None),
        P(),
        P(),
        P(),
        P(),
        P(),
    )
    return jax.shard_map(
        shards, mesh=mesh, in_specs=placed, out_specs=P(("ctx", "kv"), None), check_vma=False
    )
```

time: 882 us -> 99.9 us (0.11)
  blocking collectives: 767 us -> 31.7 us
  waiting for transfers between devices: 49.1 us -> 24.1 us
  starting transfers between devices: 35.5 us -> 19.1 us
  other arithmetic: 15.4 us -> 0 us
  Pallas kernels: 0 us -> 12.2 us
  matrix products: 10.9 us -> 0 us
  local copies, waits for them, and re-layouts: 2.98 us -> 12.1 us
    all_gather x2 -> x0, blocking collectives: 638 us -> none  [the longest x1 325 us: shards(): lax.all_gather(mem_k, 'ctx', axis=0, tiled=True)]
    all_to_all x1 -> x2, blocking collectives: 129 us -> 31.7 us  [the longest x1 17.3 us: shards(): recv = lax.all_to_all(sent, 'ctx', 0, 0, axis_index_groups=octets)]
    ppermute x16 -> x1, waiting for transfers between devices: 49.1 us -> 13.5 us  [shards(): lax.ppermute(own, 'ctx', [((i - WIN) % BLOCKS, i) for i in range(BLOCKS)])]
    ppermute x16 -> x1, starting transfers between devices: 35.5 us -> 6.76 us  [shards(): lax.ppermute(own, 'ctx', [((i - WIN) % BLOCKS, i) for i in range(BLOCKS)])]
    all_to_all x0 -> x1, starting transfers between devices: none -> 12.3 us  [shards(): mem = lax.all_to_all(mem, 'ctx', 0, 0)]
    pallas_call x0 -> x5, Pallas kernels: none -> 12.2 us  [call(): pl.pallas_call(kernel, out_shape=out_shape, in_specs=specs, out_specs=(vm...]
    dot_general x22 -> x0, matrix products: 10.9 us -> none  [the longest x10 7 us: take_tile(): jnp.einsum('tgqs,sgd->tgqd', weight.astype(jnp.bfloat16), tile_values, pr...]
    all_to_all x0 -> x1, waiting for transfers between devices: none -> 10.6 us  [shards(): mem = lax.all_to_all(mem, 'ctx', 0, 0)]
  transfers between devices with their start and end apart: 16 -> 2, of which waited for: 13 -> 2; matrix products, arithmetic and copies ran while one was open for 3% -> 0% of each run, Pallas kernels for 0% -> 6%
where the time goes in v1:
time: 99.9 us; the launch traced here: 99.3 us
  blocking collectives  31.7 us (32%)
  waiting for transfers between devices  24.1 us (24%)
  starting transfers between devices  19.1 us (19%)
  Pallas kernels  12.2 us (12%)
  local copies, waits for them, and re-layouts  12.1 us (12%)
    all_to_all x1, blocking collectives, shards(): recv = lax.all_to_all(sent, 'ctx', 0, 0, axis_index_groups=octets)  17.3 us
    all_to_all x1, blocking collectives, shards(): got = lax.all_to_all(out, 'kv', 0, 0)  14.4 us
    ppermute x1, waiting for transfers between devices, shards(): lax.ppermute(own, 'ctx', [((i - WIN) % BLOCKS, i) for i in range(BLOCKS)])  13.5 us
    all_to_all x1, starting transfers between devices, shards(): mem = lax.all_to_all(mem, 'ctx', 0, 0)  12.3 us
    pallas_call x5, Pallas kernels, call(): pl.pallas_call(kernel, out_shape=out_shape, in_specs=specs, out_specs=(vm...  12.2 us
    unnamed x30, local copies, waits for them, and re-layouts  11.3 us
    all_to_all x1, waiting for transfers between devices, shards(): mem = lax.all_to_all(mem, 'ctx', 0, 0)  10.6 us
    ppermute x1, starting transfers between devices, shards(): lax.ppermute(own, 'ctx', [((i - WIN) % BLOCKS, i) for i in range(BLOCKS)])  6.76 us
  transfers between devices with their start and end apart: 2, of which 2 were waited for; matrix products, arithmetic and copies ran while one was open for 0% of the time, Pallas kernels for 6%

profile of v1, /device:TPU:1, one launch (start us, length us, event | category | flops | bytes accessed | tf_op | source)
XLA Modules:
  0.0 99.3 jit_solution(13522290690656348597)
XLA Ops:
  0.0 0.0 copy-start.1
  0.0 0.8 copy-done.1
  0.8 0.0 copy-start.2
  0.8 0.8 copy-done.2
  1.7 0.0 copy-start.3
  1.7 0.8 copy-done.3
  2.5 0.0 copy-start.4
  2.5 0.8 copy-done.4
  3.4 0.0 copy-start.5
  3.4 0.7 copy-done.5
  4.1 0.0 copy-start.6
  4.1 0.7 copy-done.6
  4.8 0.0 copy-start.7
  4.8 0.7 copy-done.7
  5.5 0.0 copy-start.9
  5.5 0.7 copy-done.9
  6.1 2.2 %shard_map.92 = (bf16[512,128]{1,0:T(8,128)(2,1)S(1)}, bf16[128,16,128]{2,1,0:T(8,128)(2,1)}) custom-call(s32[128]{0:T(128)S(1)} %copy-done.7, f32[8,128]{1,0:T(8,128)S(1)} %copy-done.9, bf16[128,2,128]{2,1,0:T(2,128)(2,1)S(1)} %copy-done.1, bf16[128,2,128]{2,1,0:T(2,128)(2,1)S(1)} %copy-done.2, f32[32,128]{1,0:T(8,128)S(1)} %copy-done.5, ...), custom_call_target="tpu_custom_call" | custom-call | flops 1000000000 | bytes 1048576 | tf_op jit(solution)/shard_map/pallas_call | solution.py:184
  8.4 0.0 copy-start
  8.4 0.0 copy-start.8
  8.4 0.0 copy-start.10
  8.4 6.8 %collective-permute-start = (bf16[512,128]{1,0:T(8,128)(2,1)S(1)}, bf16[512,128]{1,0:T(8,128)(2,1)S(1)}, u32[]{:S(2)}, u32[]{:S(2)}) collective-permute-start(bf16[512,128]{1,0:T(8,128)(2,1)S(1)} %get-tuple-element.10.own), channel_id=1, source_target_pairs={{480,0},{484,4},{488,8},{492,12},{496,16},{500,20},{504,24},{508,2... | collective-permute-start | bytes 393224 | tf_op jit(solution)/shard_map/ppermute | solution.py:212
  15.2 13.5 %collective-permute-done.prev = bf16[512,128]{1,0:T(8,128)(2,1)S(1)} collective-permute-done((bf16[512,128]{1,0:T(8,128)(2,1)S(1)}, bf16[512,128]{1,0:T(8,128)(2,1)S(1)}, u32[]{:S(2)}, u32[]{:S(2)}) %collective-permute-start) | collective-permute-done | bytes 131104 | tf_op jit(solution)/shard_map/ppermute | solution.py:212
  28.7 0.1 shard_map.93
  28.8 17.3 %all_to_all.15.recv = bf16[8,512,128]{2,1,0:T(8,128)(2,1)S(1)} all-to-all(bf16[8,512,128]{2,1,0:T(8,128)(2,1)S(1)} %shard_map.93), channel_id=1, replica_groups={{0,4,8,12,16,20,24,28},{32,36,40,44,48,52,56,60},{64,68,72,76,80,84,88,..., dimensions={0} | all-to-all | bytes 2097152 | tf_op jit(solution)/shard_map/all_to_all | solution.py:219
  46.1 12.3 %all-to-all-start = ((bf16[128,16,128]{2,1,0:T(8,128)(2,1)}), bf16[128,16,128]{2,1,0:T(8,128)(2,1)S(1)}, u32[]{:S(2)}, u32[]{:S(2)}) async-start(bf16[128,16,128]{2,1,0:T(8,128)(2,1)} %get-tuple-element.9), calls=%async_computation | async-start | bytes 1048576 | tf_op jit(solution)/shard_map/all_to_all | solution.py:213
  58.4 0.0 copy-done
  58.4 0.0 copy-done.8
  58.4 0.0 copy-done.10
  58.5 1.6 %shard_map.91.rotq = bf16[2048,128]{1,0:T(8,128)(2,1)S(1)} custom-call(s32[128]{0:T(128)S(1)} %copy-done.8, f32[8,128]{1,0:T(8,128)S(1)} %copy-done.10, bf16[128,16,128]{2,1,0:T(8,128)(2,1)S(1)} %copy-done), custom_call_target="tpu_custom_call" | custom-call | flops 1000000000 | bytes 1048576 | tf_op jit(solution)/shard_map/pallas_call | solution.py:184
  60.0 4.3 %shard_map.94 = (f32[2048,256]{1,0:T(8,128)S(1)}, f32[2048,128]{1,0:T(8,128)S(1)}) custom-call(s32[128]{0:T(128)S(1)} %copy-done.8, bf16[2048,128]{1,0:T(8,128)(2,1)S(1)} %shard_map.91.rotq, bf16[8,512,128]{2,1,0:T(8,128)(2,1)S(1)} %all_to_all.15.recv, bf16[512,128]{1,0:T(8,128)(2,1)S(1)} %collective-permute-done.prev), custom_call_target="tpu_custom_call" | custom-call | flops 10000000000 | bytes 1048576 | tf_op jit(solution)/shard_map/pallas_call | solution.py:184
  64.4 0.0 copy-start.11
  64.4 1.3 %copy-done.11 = f32[2048,256]{1,0:T(8,128)} copy-done((f32[2048,256]{1,0:T(8,128)}, f32[2048,256]{1,0:T(8,128)S(1)}, u32[]{:S(2)}) %copy-start.11) | copy-done | bytes 2097176
  65.7 0.0 copy-start.13
  65.7 1.0 copy-done.13
  66.7 10.6 %all-to-all-done.mem = bf16[128,16,128]{2,1,0:T(8,128)(2,1)S(1)} async-done(((bf16[128,16,128]{2,1,0:T(8,128)(2,1)}), bf16[128,16,128]{2,1,0:T(8,128)(2,1)S(1)}, u32[]{:S(2)}, u32[]{:S(2)}) %all-to-all-start) | async-done | bytes 524320 | tf_op jit(solution)/shard_map/all_to_all | solution.py:213
  77.3 0.0 copy-start.12
  77.3 1.6 %copy-done.12 = f32[2048,256]{1,0:T(8,128)S(1)} copy-done((f32[2048,256]{1,0:T(8,128)S(1)}, f32[2048,256]{1,0:T(8,128)}, u32[]{:S(2)}) %copy-start.12) | copy-done | bytes 2097176
  78.9 0.0 copy-start.14
  78.9 1.2 %copy-done.14 = f32[2048,128]{1,0:T(8,128)S(1)} copy-done((f32[2048,128]{1,0:T(8,128)S(1)}, f32[2048,128]{1,0:T(8,128)}, u32[]{:S(2)}) %copy-start.14) | copy-done | bytes 1048600
  80.1 3.9 %shard_map.95 = bf16[4,32,2048]{2,1,0:T(8,128)(2,1)S(1)} custom-call(s32[128]{0:T(128)S(1)} %copy-done.8, bf16[2048,128]{1,0:T(8,128)(2,1)S(1)} %shard_map.91.rotq, bf16[128,16,128]{2,1,0:T(8,128)(2,1)S(1)} %all-to-all-done.mem, f32[2048,256]{1,0:T(8,128)S(1)} %copy-done.12, f32[2048,128]{1,0:T(8,128)S(1)} %copy-done.14), custom_call_target="tpu_custom_call" | custom-call | flops 5000000000 | bytes 1048576 | tf_op jit(solution)/shard_map/pallas_call | solution.py:184
  84.1 14.4 %all_to_all.16 = bf16[4,32,2048]{2,1,0:T(8,128)(2,1)S(1)} all-to-all(bf16[4,32,2048]{2,1,0:T(8,128)(2,1)S(1)} %shard_map.95), channel_id=1, replica_groups=mesh['ctx'=128,'kv'=4] {'kv'}, dimensions={0} | all-to-all | bytes 1048576 | tf_op jit(solution)/shard_map/all_to_all | solution.py:240
  98.4 0.8 copy.11
Async XLA Ops:
  0.0 0.8 copy-start.1
  0.8 0.8 copy-start.2
  1.7 0.8 copy-start.3
  2.5 0.8 copy-start.4
  3.4 0.7 copy-start.5
  4.1 0.7 copy-start.6
  4.8 0.7 copy-start.7
  5.5 0.7 copy-start.9
  8.4 50.0 %copy-start = (bf16[128,16,128]{2,1,0:T(8,128)(2,1)S(1)}, bf16[128,16,128]{2,1,0:T(8,128)(2,1)}, u32[]{:S(2)}) copy-start(bf16[128,16,128]{2,1,0:T(8,128)(2,1)} %q.1) | copy-start | bytes 1572868
  8.4 50.0 %copy-start.8 = (s32[128]{0:T(128)S(1)}, s32[128]{0:T(128)}, u32[]{:S(2)}) copy-start(s32[128]{0:T(128)} %bs.7) | copy-start | bytes 1540
  8.4 50.0 %copy-start.10 = (f32[8,128]{1,0:T(8,128)S(1)}, f32[8,128]{1,0:T(8,128)}, u32[]{:S(2)}) copy-start(f32[8,128]{1,0:T(8,128)} %constant.2.clone.freqs) | copy-start | bytes 12292
  8.4 20.3 %collective-permute-start = (bf16[512,128]{1,0:T(8,128)(2,1)S(1)}, bf16[512,128]{1,0:T(8,128)(2,1)S(1)}, u32[]{:S(2)}, u32[]{:S(2)}) collective-permute-start(bf16[512,128]{1,0:T(8,128)(2,1)S(1)} %get-tuple-element.10.own), channel_id=1, source_target_pairs={{480,0},{484,4},{488,8},{492,12},{496,16},{500,20},{504,24},{508,2... | collective-permute-start | bytes 393224 | tf_op jit(solution)/shard_map/ppermute | solution.py:212
  46.1 31.2 %all-to-all-start = ((bf16[128,16,128]{2,1,0:T(8,128)(2,1)}), bf16[128,16,128]{2,1,0:T(8,128)(2,1)S(1)}, u32[]{:S(2)}, u32[]{:S(2)}) async-start(bf16[128,16,128]{2,1,0:T(8,128)(2,1)} %get-tuple-element.9), calls=%async_computation | async-start | bytes 1048576 | tf_op jit(solution)/shard_map/all_to_all | solution.py:213
  64.4 1.3 %copy-start.11 = (f32[2048,256]{1,0:T(8,128)}, f32[2048,256]{1,0:T(8,128)S(1)}, u32[]{:S(2)}) copy-start(f32[2048,256]{1,0:T(8,128)S(1)} %get-tuple-element.11.acc) | copy-start | bytes 6291460
  65.7 1.0 copy-start.13
  77.3 1.6 %copy-start.12 = (f32[2048,256]{1,0:T(8,128)S(1)}, f32[2048,256]{1,0:T(8,128)}, u32[]{:S(2)}) copy-start(f32[2048,256]{1,0:T(8,128)} %copy-done.11) | copy-start | bytes 6291460
  78.9 1.2 %copy-start.14 = (f32[2048,128]{1,0:T(8,128)S(1)}, f32[2048,128]{1,0:T(8,128)}, u32[]{:S(2)}) copy-start(f32[2048,128]{1,0:T(8,128)} %copy-done.13) | copy-start | bytes 3145732

commit v2 on v1

v2 whole, which is shorter than its diff:
```python
import functools
import math

import jax
import jax.numpy as jnp
import numpy as np
from jax import lax
from jax.experimental import pallas as pl
from jax.experimental.pallas import tpu as pltpu
from jax.sharding import PartitionSpec as P

HD = 128
TOK = 128
STRIDE = 32
SLOTS = TOK // STRIDE
WIN = 8
WINDOW = WIN * TOK
BLOCKS = 128
SEQ = BLOCKS * TOK
HEADS = 16
GROUPS = 2
KV = 4
OCT = 8
NOCT = BLOCKS // OCT
ROWS = TOK // KV
RAW = (WIN + 1) * TOK
MSCALE = 1.0 + 0.1 * math.log(16.0)
SCALE2 = math.log2(math.e) / math.sqrt(HD)
NEG = -1e30
BF = jnp.bfloat16
F32 = jnp.float32


def yarn_freqs():
    index = np.arange(HD // 2, dtype=np.float32)
    inverse = np.exp(np.float32(-(2.0 / HD) * math.log(500000.0)) * index).astype(np.float32)
    ratio = np.float32(8192.0) * inverse / np.float32(2.0 * math.pi)
    ramp = np.clip((ratio - 1.0) / 31.0, 0.0, 1.0).astype(np.float32)
    freqs = inverse * (ramp + (1.0 - ramp) / np.float32(16.0))
    return np.tile(np.concatenate([freqs, freqs])[None, :], (8, 1)).astype(np.float32)


def turn_tables(place0, freqs):
    places = (place0 + lax.broadcasted_iota(jnp.int32, (TOK, HD), 0)).astype(F32)
    angle = places * freqs
    first = lax.broadcasted_iota(jnp.int32, (TOK, HD), 1) < HD // 2
    sine = jnp.sin(angle)
    return jnp.cos(angle), jnp.where(first, -sine, sine)


def turn(x, cosine, sine):
    return ((x * cosine + pltpu.roll(x, HD // 2, 1) * sine) * MSCALE).astype(BF)


def prep_kernel(bs, freqs, k, v, dk, pk, dv, pv, own, mem, *scratch):
    scr, pool, s_bs, s_freqs, s_k, s_v, s_dk, s_pk, s_dv, s_pv, sem = scratch
    pairs = (
        (bs, s_bs), (freqs, s_freqs), (k, s_k), (v, s_v),
        (dk, s_dk), (pk, s_pk), (dv, s_dv), (pv, s_pv),
    )
    copies = [pltpu.make_async_copy(a, b, sem.at[i]) for i, (a, b) in enumerate(pairs)]
    for c in copies:
        c.start()
    for c in copies:
        c.wait()
    me = lax.axis_index("ctx")
    cosine, sine = turn_tables(s_bs[me], s_freqs[0:1, :])
    scr[...] = s_k[...].astype(F32)
    for g in range(GROUPS):
        rot = turn(scr[:, g, :], cosine, sine)
        own[g * TOK : (g + 1) * TOK, :] = rot
        grouped = rot.astype(F32).reshape(SLOTS, STRIDE, HD)
        pool[g * SLOTS : (g + 1) * SLOTS, :] = jnp.sum(grouped * s_dk[...][None], axis=1)
    scr[...] = s_v[...].astype(F32)
    for g in range(GROUPS):
        val = scr[:, g, :]
        own[(GROUPS + g) * TOK : (GROUPS + g + 1) * TOK, :] = val.astype(BF)
        grouped = val.reshape(SLOTS, STRIDE, HD)
        at = (GROUPS + g) * SLOTS
        pool[at : at + SLOTS, :] = jnp.sum(grouped * s_dv[...][None], axis=1)
    half = GROUPS * SLOTS
    mk = jnp.dot(pool[:half, :], s_pk[...], precision=lax.Precision.HIGHEST, preferred_element_type=F32)
    mv = jnp.dot(pool[half:, :], s_pv[...], precision=lax.Precision.HIGHEST, preferred_element_type=F32)
    both = jnp.concatenate([mk, mv], axis=0).astype(BF)
    mem[...] = jnp.broadcast_to(both[None], mem.shape)


def query_kernel(bs, freqs, q, rotq, scr):
    me = lax.axis_index("ctx")
    cosine, sine = turn_tables(bs[me], freqs[0:1, :])
    scr[...] = q[...].astype(F32)
    for h in range(HEADS):
        rotq[h] = turn(scr[:, h, :], cosine, sine)


def octet_kernel(own, prev, mem, out, scr):
    me = lax.rem(lax.axis_index("ctx"), OCT)
    scr[...] = mem[...].astype(F32)
    kinds = 2 * GROUPS * SLOTS
    slots = jnp.concatenate([scr[:, r, :] for r in range(kinds)], axis=0).astype(BF)
    raw = own.shape[0]
    for d in range(OCT):
        out[d, raw:, :] = slots

        @pl.when(me <= d)
        def _():
            out[d, :raw, :] = own[...]

        @pl.when(me > d)
        def _():
            out[d, :raw, :] = prev[...]


def build_kernel(bs, recv, prev, kaug, vaug):
    me = lax.axis_index("ctx")
    pos = lax.rem(me, OCT)
    place = bs[me] + lax.broadcasted_iota(jnp.int32, (TOK, TOK), 1)
    row = lax.broadcasted_iota(jnp.int32, (TOK, TOK), 0)
    ones = jnp.ones((TOK, HD), BF)
    for b in range(WIN + 1):
        back = WIN if b == WIN else lax.rem(pos - b + OCT, OCT)
        there = bs[lax.rem(me - back + BLOCKS, BLOCKS)] + row
        ok = (there <= place) & (there > place - WINDOW)
        bias = jnp.where(ok, 0.0, NEG).astype(BF)
        span = slice(b * TOK, (b + 1) * TOK)
        for g in range(GROUPS):
            ks = slice(g * TOK, (g + 1) * TOK)
            vs = slice((GROUPS + g) * TOK, (GROUPS + g + 1) * TOK)
            kaug[g, span, :HD] = prev[ks, :] if b == WIN else recv[b, ks, :]
            kaug[g, span, HD:] = bias
            vaug[g, span, :HD] = prev[vs, :] if b == WIN else recv[b, vs, :]
            vaug[g, span, HD:] = ones
    many = SLOTS * NOCT
    slot = lax.broadcasted_iota(jnp.int32, (many, TOK), 0) // NOCT
    octet = lax.broadcasted_iota(jnp.int32, (many, TOK), 0) & (NOCT - 1)
    place = bs[me] + lax.broadcasted_iota(jnp.int32, (many, TOK), 1)
    for p in range(OCT):
        end = ((bs[p] + OCT * TOK * octet) & (SEQ - 1)) + (slot + 1) * STRIDE
        bias = jnp.where(end <= place + 1, 0.0, NEG).astype(BF)
        lo = RAW + p * many
        span = slice(lo, lo + many)
        for g in range(GROUPS):
            at = 2 * GROUPS * TOK + g * many
            kaug[g, span, :HD] = recv[p, at : at + many, :]
            kaug[g, span, HD:] = bias
            at += GROUPS * many
            vaug[g, span, :HD] = recv[p, at : at + many, :]
            vaug[g, span, HD:] = ones[:many, :]


def chunk_kernel(off, rotq, kaug, vaug, *rest):
    out = rest[-1]
    dest = lax.axis_index("kv") ^ off
    first = pl.multiple_of(dest * ROWS, ROWS)
    heads = HEADS // GROUPS
    r = lax.broadcasted_iota(jnp.int32, (heads * ROWS, TOK), 0) & (ROWS - 1)
    c = lax.broadcasted_iota(jnp.int32, (heads * ROWS, TOK), 1)
    unit = jnp.where(r + first == c, 1.0, 0.0).astype(BF)
    for g in range(GROUPS):
        q = jnp.concatenate(
            [rotq[g * heads + i, pl.ds(first, ROWS), :] for i in range(heads)], axis=0
        )
        qa = jnp.concatenate([q, unit], axis=1)
        s = lax.dot_general(qa, kaug[g], (((1,), (1,)), ((), ())), preferred_element_type=F32)
        top = jnp.max(s, axis=1, keepdims=True)
        w = jnp.exp2((s - top) * SCALE2).astype(BF)
        mixed = jnp.dot(w, vaug[g], preferred_element_type=F32)
        res = (mixed[:, :HD] / mixed[:, HD:]).astype(BF)
        for i in range(heads):
            h = g * heads + i
            out[:, h * HD : (h + 1) * HD] = res[i * ROWS : (i + 1) * ROWS, :]


def join_kernel(a, b, c, d, out, sem):
    me = lax.axis_index("kv")
    wide = HEADS * HD
    copies = []
    for off, part in enumerate((a, b, c, d)):
        lane = pl.multiple_of((me ^ off) * wide, wide)
        copies.append(pltpu.make_async_copy(part, out.at[:, pl.ds(lane, wide)], sem.at[off]))
    for x in copies:
        x.start()
    for x in copies:
        x.wait()


def call(kernel, out_shape, scratch, flops, spaces, *args, out_space=pltpu.VMEM, grant=32):
    multi = isinstance(out_shape, tuple)
    vm = pl.BlockSpec(memory_space=out_space)
    return pl.pallas_call(
        kernel,
        out_shape=out_shape,
        in_specs=[pl.BlockSpec(memory_space=s) for s in spaces],
        out_specs=(vm,) * len(out_shape) if multi else vm,
        scratch_shapes=scratch,
        compiler_params=pltpu.CompilerParams(vmem_limit_bytes=grant * 2**20),
        cost_estimate=pl.CostEstimate(flops=flops, bytes_accessed=2**10, transcendentals=0),
    )(*args)


def shape(*dims, dtype=BF):
    return jax.ShapeDtypeStruct(dims, dtype)


octets = [[OCT * o + p for p in range(OCT)] for o in range(NOCT)]
strided = [[OCT * o + p for o in range(NOCT)] for p in range(OCT)]
SM, VM, HB = pltpu.SMEM, pltpu.VMEM, pltpu.HBM


def shards(queries, keys, values, block_start, depth_k, point_k, depth_v, point_v):
    freqs = jnp.asarray(yarn_freqs())
    pack = 2 * GROUPS
    params = (block_start, freqs, keys, values, depth_k, point_k, depth_v, point_v)
    own, mem = call(
        prep_kernel,
        (shape(pack * TOK, HD), shape(NOCT, pack * SLOTS, HD)),
        [pltpu.VMEM((TOK, GROUPS, HD), F32), pltpu.VMEM((pack * SLOTS, HD), F32)]
        + [(pltpu.SMEM if i == 0 else pltpu.VMEM)(x.shape, x.dtype) for i, x in enumerate(params)]
        + [pltpu.SemaphoreType.DMA((len(params),))],
        10**9,
        (HB,) * len(params),
        *params,
        grant=60,
    )
    prev = lax.ppermute(own, "ctx", [((i - WIN) % BLOCKS, i) for i in range(BLOCKS)])
    mem = lax.all_to_all(mem, "ctx", 0, 0, axis_index_groups=strided)
    rotq = call(
        query_kernel, shape(HEADS, TOK, HD), [pltpu.VMEM((TOK, HEADS, HD), F32)], 10**9,
        (SM, VM, VM),
        block_start, freqs, queries,
    )
    rows = pack * TOK + pack * SLOTS * NOCT
    sent = call(
        octet_kernel, shape(OCT, rows, HD), [pltpu.VMEM((NOCT, pack * SLOTS, HD), F32)], 10**8,
        (VM,) * 3, own, prev, mem,
    )
    recv = lax.all_to_all(sent, "ctx", 0, 0, axis_index_groups=octets)
    wide = shape(GROUPS, RAW + BLOCKS * SLOTS, 2 * HD)
    kaug, vaug = call(build_kernel, (wide, wide), [], 10**9, (SM, VM, VM), block_start, recv, prev)
    parts = []
    for off in (3, 2, 1, 0):
        after = parts[-2:-1]
        part = call(
            functools.partial(chunk_kernel, off), shape(ROWS, HEADS * HD), [], 10**6,
            (VM,) * 3 + (pl.ANY,) * len(after), rotq, kaug, vaug, *after,
        )
        if off:
            part = lax.ppermute(part, "kv", [(i, i ^ off) for i in range(KV)])
        parts.append(part)
    return call(
        join_kernel, shape(ROWS, KV * HEADS * HD), [pltpu.SemaphoreType.DMA((KV,))], 10**8,
        (VM,) * 4, *parts[::-1], out_space=HB,
    )


def solution(mesh):
    placed = (
        P("ctx", "kv", None),
        P("ctx", "kv", None),
        P("ctx", "kv", None),
        P(),
        P(),
        P(),
        P(),
        P(),
    )
    return jax.shard_map(
        shards, mesh=mesh, in_specs=placed, out_specs=P(("ctx", "kv"), None), check_vma=False
    )
```

time: 99.9 us -> 80.2 us (0.80)
  local copies, waits for them, and re-layouts: 12.1 us -> 0.92 us
  blocking collectives: 31.7 us -> 25 us
  waiting for transfers between devices: 24.1 us -> 18.7 us
  Pallas kernels: 12.2 us -> 14.8 us
  starting transfers between devices: 19.1 us -> 20.2 us
    ppermute x1, waiting for transfers between devices: 13.5 us -> 0.01 us  [shards(): lax.ppermute(own, 'ctx', [((i - WIN) % BLOCKS, i) for i in range(BLOCKS)])]
    unnamed x30 -> x8, local copies, waits for them, and re-layouts: 11.3 us -> 0.92 us
    ppermute x0 -> x3, starting transfers between devices: none -> 8.48 us  [shards(): part = lax.ppermute(part, 'kv', [(i, i ^ off) for i in range(KV)])]
    all_to_all x1, waiting for transfers between devices: 10.6 us -> 18.4 us  [shards(): recv = lax.all_to_all(sent, 'ctx', 0, 0, axis_index_groups=octets)]
    all_to_all x1, starting transfers between devices: 12.3 us -> 5.05 us  [shards(): recv = lax.all_to_all(sent, 'ctx', 0, 0, axis_index_groups=octets)]
    all_to_all x2 -> x1, blocking collectives: 31.7 us -> 25 us  [shards(): mem = lax.all_to_all(mem, 'ctx', 0, 0, axis_index_groups=strided)]
    pallas_call x5 -> x9, Pallas kernels: 12.2 us -> 14.8 us  [call(): pl.pallas_call(kernel, out_shape=out_shape, in_specs=[pl.BlockSpec(memory...]
  transfers between devices with their start and end apart: 2 -> 5, of which waited for: 2 -> 2; matrix products, arithmetic and copies ran while one was open for 0% -> 0% of each run, Pallas kernels for 6% -> 9%
where the time goes in v2:
time: 80.2 us; the launch traced here: 79.8 us
  blocking collectives  25 us (31%)
  starting transfers between devices  20.2 us (25%)
  waiting for transfers between devices  18.7 us (23%)
  Pallas kernels  14.8 us (18%)
  local copies, waits for them, and re-layouts  0.92 us (1%)
    all_to_all x1, blocking collectives, shards(): mem = lax.all_to_all(mem, 'ctx', 0, 0, axis_index_groups=strided)  25 us
    all_to_all x1, waiting for transfers between devices, shards(): recv = lax.all_to_all(sent, 'ctx', 0, 0, axis_index_groups=octets)  18.4 us
    pallas_call x9, Pallas kernels, call(): pl.pallas_call(kernel, out_shape=out_shape, in_specs=[pl.BlockSpec(memory...  14.8 us
    ppermute x3, starting transfers between devices, shards(): part = lax.ppermute(part, 'kv', [(i, i ^ off) for i in range(KV)])  8.48 us
    ppermute x1, starting transfers between devices, shards(): lax.ppermute(own, 'ctx', [((i - WIN) % BLOCKS, i) for i in range(BLOCKS)])  6.64 us
    all_to_all x1, starting transfers between devices, shards(): recv = lax.all_to_all(sent, 'ctx', 0, 0, axis_index_groups=octets)  5.05 us
  transfers between devices with their start and end apart: 5, of which 2 were waited for; matrix products, arithmetic and copies ran while one was open for 0% of the time, Pallas kernels for 9%

profile of v2, /device:TPU:1, one launch (start us, length us, event | category | flops | bytes accessed | tf_op | source)
XLA Modules:
  0.0 79.8 jit_solution(1986859490225746728)
XLA Ops:
  0.0 2.5 %shard_map.92 = (bf16[512,128]{1,0:T(8,128)(2,1)}, bf16[16,16,128]{2,1,0:T(8,128)(2,1)}) custom-call(s32[128]{0:T(128)} %bs.5, f32[8,128]{1,0:T(8,128)} %constant.2.clone.freqs, bf16[128,2,128]{2,1,0:T(2,128)(2,1)} %k.1, bf16[128,2,128]{2,1,0:T(2,128)(2,1)} %v.1, f32[32,128]{1,0:T(8,128)} %dk.1, f32[128,128]{1,0:T(8,128)} %pk.1, f32[32,128]{1,0:T(8,128)} %dv.1, ...), custom_call_target="tpu_custom_call" | custom-call | flops 1000000000 | bytes 1024 | tf_op jit(solution)/shard_map/pallas_call | solution.py:190
  2.5 6.6 %collective-permute-start = (bf16[512,128]{1,0:T(8,128)(2,1)}, bf16[512,128]{1,0:T(8,128)(2,1)S(1)}, u32[]{:S(2)}, u32[]{:S(2)}) collective-permute-start(bf16[512,128]{1,0:T(8,128)(2,1)} %get-tuple-element.9.own), channel_id=1, source_target_pairs={{480,0},{484,4},{488,8},{492,12},{496,16},{500,20},{504,24},{508,2... | collective-permute-start | bytes 393224 | tf_op jit(solution)/shard_map/ppermute | solution.py:225
  9.2 25.0 %all_to_all.10.mem = bf16[16,16,128]{2,1,0:T(8,128)(2,1)S(1)} all-to-all(bf16[16,16,128]{2,1,0:T(8,128)(2,1)} %get-tuple-element.10), channel_id=1, replica_groups={{0,32,64,96,128,160,192,224,256,288,320,352,384,416,448,480},{4,36,68,1..., dimensions={0} | all-to-all | bytes 131072 | tf_op jit(solution)/shard_map/all_to_all | solution.py:226
  34.2 0.0 collective-permute-done.prev
  34.2 0.0 copy-start
  34.2 0.9 %copy-done = bf16[512,128]{1,0:T(8,128)(2,1)S(1)} copy-done((bf16[512,128]{1,0:T(8,128)(2,1)S(1)}, bf16[512,128]{1,0:T(8,128)(2,1)}, u32[]{:S(2)}) %copy-start) | copy-done | bytes 131096
  35.1 1.4 %shard_map.93 = bf16[8,768,128]{2,1,0:T(8,128)(2,1)} custom-call(bf16[512,128]{1,0:T(8,128)(2,1)S(1)} %copy-done, bf16[512,128]{1,0:T(8,128)(2,1)S(1)} %collective-permute-done.prev, bf16[16,16,128]{2,1,0:T(8,128)(2,1)S(1)} %all_to_all.10.mem), custom_call_target="tpu_custom_call" | custom-call | flops 100000000 | bytes 1024 | tf_op jit(solution)/shard_map/pallas_call | solution.py:190
  36.5 0.0 copy-start.1
  36.5 0.0 copy-start.2
  36.5 0.0 copy-start.3
  36.5 5.1 %all-to-all-start.1 = ((bf16[8,768,128]{2,1,0:T(8,128)(2,1)}), bf16[8,768,128]{2,1,0:T(8,128)(2,1)S(1)}, u32[]{:S(2)}, u32[]{:S(2)}) async-start(bf16[8,768,128]{2,1,0:T(8,128)(2,1)} %shard_map.93), calls=%async_computation.1 | async-start | bytes 3145728 | tf_op jit(solution)/shard_map/all_to_all | solution.py:237
  41.5 0.0 copy-done.1
  41.6 0.0 copy-done.2
  41.6 0.0 copy-done.3
  41.6 1.6 %shard_map.91.rotq = bf16[16,128,128]{2,1,0:T(8,128)(2,1)S(1)} custom-call(s32[128]{0:T(128)S(1)} %copy-done.2, f32[8,128]{1,0:T(8,128)S(1)} %copy-done.3, bf16[128,16,128]{2,1,0:T(8,128)(2,1)S(1)} %copy-done.1), custom_call_target="tpu_custom_call" | custom-call | flops 1000000000 | bytes 1024 | tf_op jit(solution)/shard_map/pallas_call | solution.py:190
  43.2 18.4 %all-to-all-done.1.recv = bf16[8,768,128]{2,1,0:T(8,128)(2,1)S(1)} async-done(((bf16[8,768,128]{2,1,0:T(8,128)(2,1)}), bf16[8,768,128]{2,1,0:T(8,128)(2,1)S(1)}, u32[]{:S(2)}, u32[]{:S(2)}) %all-to-all-start.1) | async-done | bytes 1572896 | tf_op jit(solution)/shard_map/all_to_all | solution.py:237
  61.5 1.1 %shard_map.94 = (bf16[2,1664,256]{2,1,0:T(8,128)(2,1)S(1)}, bf16[2,1664,256]{2,1,0:T(8,128)(2,1)S(1)}) custom-call(s32[128]{0:T(128)S(1)} %copy-done.2, bf16[8,768,128]{2,1,0:T(8,128)(2,1)S(1)} %all-to-all-done.1.recv, bf16[512,128]{1,0:T(8,128)(2,1)S(1)} %collective-permute-done.prev), custom_call_target="tpu_custom_call" | custom-call | flops 1000000000 | bytes 1024 | tf_op jit(solution)/shard_map/pallas_call | solution.py:190
  62.6 1.9 %shard_map.97 = bf16[32,2048]{1,0:T(8,128)(2,1)S(1)} custom-call(bf16[16,128,128]{2,1,0:T(8,128)(2,1)S(1)} %shard_map.91.rotq, bf16[2,1664,256]{2,1,0:T(8,128)(2,1)S(1)} %get-tuple-element.11.kaug, bf16[2,1664,256]{2,1,0:T(8,128)(2,1)S(1)} %get-tuple-element.12.vaug), custom_call_target="tpu_custom_call" | custom-call | flops 1000000 | bytes 1024 | tf_op jit(solution)/shard_map/pallas_call | solution.py:190
  64.5 3.5 %collective-permute-start.2 = (bf16[32,2048]{1,0:T(8,128)(2,1)S(1)}, bf16[32,2048]{1,0:T(8,128)(2,1)S(1)}, u32[]{:S(2)}, u32[]{:S(2)}) collective-permute-start(bf16[32,2048]{1,0:T(8,128)(2,1)S(1)} %shard_map.97), channel_id=1, source_target_pairs={{0,3},{1,2},{2,1},{3,0},{4,7},{5,6},{6,5},{7,4},{8,11},{9,10},{10,... | collective-permute-start | bytes 393224 | tf_op jit(solution)/shard_map/ppermute | solution.py:248
  68.0 1.9 %shard_map.95 = bf16[32,2048]{1,0:T(8,128)(2,1)S(1)} custom-call(bf16[16,128,128]{2,1,0:T(8,128)(2,1)S(1)} %shard_map.91.rotq, bf16[2,1664,256]{2,1,0:T(8,128)(2,1)S(1)} %get-tuple-element.11.kaug, bf16[2,1664,256]{2,1,0:T(8,128)(2,1)S(1)} %get-tuple-element.12.vaug), custom_call_target="tpu_custom_call" | custom-call | flops 1000000 | bytes 1024 | tf_op jit(solution)/shard_map/pallas_call | solution.py:190
  69.9 3.0 %collective-permute-start.1 = (bf16[32,2048]{1,0:T(8,128)(2,1)S(1)}, bf16[32,2048]{1,0:T(8,128)(2,1)S(1)}, u32[]{:S(2)}, u32[]{:S(2)}) collective-permute-start(bf16[32,2048]{1,0:T(8,128)(2,1)S(1)} %shard_map.95), channel_id=1, source_target_pairs={{0,2},{1,3},{2,0},{3,1},{4,6},{5,7},{6,4},{7,5},{8,10},{9,11},{10,... | collective-permute-start | bytes 393224 | tf_op jit(solution)/shard_map/ppermute | solution.py:248
  72.9 0.0 collective-permute-done.2.rest_0_.d
  72.9 1.9 %shard_map.98 = bf16[32,2048]{1,0:T(8,128)(2,1)S(1)} custom-call(bf16[16,128,128]{2,1,0:T(8,128)(2,1)S(1)} %shard_map.91.rotq, bf16[2,1664,256]{2,1,0:T(8,128)(2,1)S(1)} %get-tuple-element.11.kaug, bf16[2,1664,256]{2,1,0:T(8,128)(2,1)S(1)} %get-tuple-element.12.vaug, bf16[32,2048]{1,0:T(8,128)(2,1)S(1)} %collective-permute-done.2.rest_0_.d), custom_call_target="tpu_custom_call" | custom-call | flops 1000000 | bytes 1024 | tf_op jit(solution)/shard_map/pallas_call | solution.py:190
  74.8 1.9 %collective-permute-start.3 = (bf16[32,2048]{1,0:T(8,128)(2,1)S(1)}, bf16[32,2048]{1,0:T(8,128)(2,1)S(1)}, u32[]{:S(2)}, u32[]{:S(2)}) collective-permute-start(bf16[32,2048]{1,0:T(8,128)(2,1)S(1)} %shard_map.98), channel_id=1, source_target_pairs={{0,1},{1,0},{2,3},{3,2},{4,5},{5,4},{6,7},{7,6},{8,9},{9,8},{10,11... | collective-permute-start | bytes 393224 | tf_op jit(solution)/shard_map/ppermute | solution.py:248
  76.7 0.3 collective-permute-done.1.rest_0_.c
  77.0 1.9 %shard_map.96.a = bf16[32,2048]{1,0:T(8,128)(2,1)S(1)} custom-call(bf16[16,128,128]{2,1,0:T(8,128)(2,1)S(1)} %shard_map.91.rotq, bf16[2,1664,256]{2,1,0:T(8,128)(2,1)S(1)} %get-tuple-element.11.kaug, bf16[2,1664,256]{2,1,0:T(8,128)(2,1)S(1)} %get-tuple-element.12.vaug, bf16[32,2048]{1,0:T(8,128)(2,1)S(1)} %collective-permute-done.1.rest_0_.c), custom_call_target="tpu_custom_call" | custom-call | flops 1000000 | bytes 1024 | tf_op jit(solution)/shard_map/pallas_call | solution.py:190
  78.9 0.0 collective-permute-done.3.b
  78.9 0.8 %shard_map.99 = bf16[32,8192]{1,0:T(8,128)(2,1)} custom-call(bf16[32,2048]{1,0:T(8,128)(2,1)S(1)} %shard_map.96.a, bf16[32,2048]{1,0:T(8,128)(2,1)S(1)} %collective-permute-done.3.b, bf16[32,2048]{1,0:T(8,128)(2,1)S(1)} %collective-permute-done.1.rest_0_.c, bf16[32,2048]{1,0:T(8,128)(2,1)S(1)} %collective-permute-done.2.rest_0_.d), custom_call_target="tpu_custom_call" | custom-call | flops 100000000 | bytes 1024 | tf_op jit(solution)/shard_map/pallas_call | solution.py:190
Async XLA Ops:
  2.5 31.7 %collective-permute-start = (bf16[512,128]{1,0:T(8,128)(2,1)}, bf16[512,128]{1,0:T(8,128)(2,1)S(1)}, u32[]{:S(2)}, u32[]{:S(2)}) collective-permute-start(bf16[512,128]{1,0:T(8,128)(2,1)} %get-tuple-element.9.own), channel_id=1, source_target_pairs={{480,0},{484,4},{488,8},{492,12},{496,16},{500,20},{504,24},{508,2... | collective-permute-start | bytes 393224 | tf_op jit(solution)/shard_map/ppermute | solution.py:225
  34.2 0.9 %copy-start = (bf16[512,128]{1,0:T(8,128)(2,1)S(1)}, bf16[512,128]{1,0:T(8,128)(2,1)}, u32[]{:S(2)}) copy-start(bf16[512,128]{1,0:T(8,128)(2,1)} %get-tuple-element.9.own) | copy-start | bytes 393220
  36.5 5.1 %copy-start.1 = (bf16[128,16,128]{2,1,0:T(8,128)(2,1)S(1)}, bf16[128,16,128]{2,1,0:T(8,128)(2,1)}, u32[]{:S(2)}) copy-start(bf16[128,16,128]{2,1,0:T(8,128)(2,1)} %q.1) | copy-start | bytes 1572868
  36.5 5.1 %copy-start.2 = (s32[128]{0:T(128)S(1)}, s32[128]{0:T(128)}, u32[]{:S(2)}) copy-start(s32[128]{0:T(128)} %bs.5) | copy-start | bytes 1540
  36.5 5.1 %copy-start.3 = (f32[8,128]{1,0:T(8,128)S(1)}, f32[8,128]{1,0:T(8,128)}, u32[]{:S(2)}) copy-start(f32[8,128]{1,0:T(8,128)} %constant.2.clone.freqs) | copy-start | bytes 12292
  36.5 25.0 %all-to-all-start.1 = ((bf16[8,768,128]{2,1,0:T(8,128)(2,1)}), bf16[8,768,128]{2,1,0:T(8,128)(2,1)S(1)}, u32[]{:S(2)}, u32[]{:S(2)}) async-start(bf16[8,768,128]{2,1,0:T(8,128)(2,1)} %shard_map.93), calls=%async_computation.1 | async-start | bytes 3145728 | tf_op jit(solution)/shard_map/all_to_all | solution.py:237
  64.5 8.4 %collective-permute-start.2 = (bf16[32,2048]{1,0:T(8,128)(2,1)S(1)}, bf16[32,2048]{1,0:T(8,128)(2,1)S(1)}, u32[]{:S(2)}, u32[]{:S(2)}) collective-permute-start(bf16[32,2048]{1,0:T(8,128)(2,1)S(1)} %shard_map.97), channel_id=1, source_target_pairs={{0,3},{1,2},{2,1},{3,0},{4,7},{5,6},{6,5},{7,4},{8,11},{9,10},{10,... | collective-permute-start | bytes 393224 | tf_op jit(solution)/shard_map/ppermute | solution.py:248
  69.9 7.2 %collective-permute-start.1 = (bf16[32,2048]{1,0:T(8,128)(2,1)S(1)}, bf16[32,2048]{1,0:T(8,128)(2,1)S(1)}, u32[]{:S(2)}, u32[]{:S(2)}) collective-permute-start(bf16[32,2048]{1,0:T(8,128)(2,1)S(1)} %shard_map.95), channel_id=1, source_target_pairs={{0,2},{1,3},{2,0},{3,1},{4,6},{5,7},{6,4},{7,5},{8,10},{9,11},{10,... | collective-permute-start | bytes 393224 | tf_op jit(solution)/shard_map/ppermute | solution.py:248
  74.8 4.1 %collective-permute-start.3 = (bf16[32,2048]{1,0:T(8,128)(2,1)S(1)}, bf16[32,2048]{1,0:T(8,128)(2,1)S(1)}, u32[]{:S(2)}, u32[]{:S(2)}) collective-permute-start(bf16[32,2048]{1,0:T(8,128)(2,1)S(1)} %shard_map.98), channel_id=1, source_target_pairs={{0,1},{1,0},{2,3},{3,2},{4,5},{5,4},{6,7},{7,6},{8,9},{9,8},{10,11... | collective-permute-start | bytes 393224 | tf_op jit(solution)/shard_map/ppermute | solution.py:248

commit v3 on v2

--- a/solution.py
+++ b/solution.py
@@ -24,6 +24,9 @@
 NOCT = BLOCKS // OCT
 ROWS = TOK // KV
 RAW = (WIN + 1) * TOK
+MANY = SLOTS * NOCT
+KEYS = RAW + BLOCKS * SLOTS
+TILE = 256
 MSCALE = 1.0 + 0.1 * math.log(16.0)
 SCALE2 = math.log2(math.e) / math.sqrt(HD)
 NEG = -1e30
@@ -93,78 +96,104 @@
         rotq[h] = turn(scr[:, h, :], cosine, sine)
 
 
-def octet_kernel(own, prev, mem, out, scr):
+def raw_kernel(own, prev, rotq, bias, out):
     me = lax.rem(lax.axis_index("ctx"), OCT)
+    raw = own.shape[0]
+    for d in range(OCT):
+
+        @pl.when(me <= d)
+        def _():
+            out[d, :raw, :] = own[...]
+
+        @pl.when(me > d)
+        def _():
+            out[d, :raw, :] = prev[...]
+
+
+def slot_kernel(mem, sent, out, scr):
     scr[...] = mem[...].astype(F32)
     kinds = 2 * GROUPS * SLOTS
     slots = jnp.concatenate([scr[:, r, :] for r in range(kinds)], axis=0).astype(BF)
-    raw = own.shape[0]
+    raw = 2 * GROUPS * TOK
     for d in range(OCT):
         out[d, raw:, :] = slots
 
-        @pl.when(me <= d)
-        def _():
-            out[d, :raw, :] = own[...]
-
-        @pl.when(me > d)
-        def _():
-            out[d, :raw, :] = prev[...]
-
-
-def build_kernel(bs, recv, prev, kaug, vaug):
+
+def bias_kernel(bs, bias):
     me = lax.axis_index("ctx")
     pos = lax.rem(me, OCT)
     place = bs[me] + lax.broadcasted_iota(jnp.int32, (TOK, TOK), 1)
     row = lax.broadcasted_iota(jnp.int32, (TOK, TOK), 0)
-    ones = jnp.ones((TOK, HD), BF)
     for b in range(WIN + 1):
         back = WIN if b == WIN else lax.rem(pos - b + OCT, OCT)
         there = bs[lax.rem(me - back + BLOCKS, BLOCKS)] + row
         ok = (there <= place) & (there > place - WINDOW)
-        bias = jnp.where(ok, 0.0, NEG).astype(BF)
-        span = slice(b * TOK, (b + 1) * TOK)
-        for g in range(GROUPS):
-            ks = slice(g * TOK, (g + 1) * TOK)
-            vs = slice((GROUPS + g) * TOK, (GROUPS + g + 1) * TOK)
-            kaug[g, span, :HD] = prev[ks, :] if b == WIN else recv[b, ks, :]
-            kaug[g, span, HD:] = bias
-            vaug[g, span, :HD] = prev[vs, :] if b == WIN else recv[b, vs, :]
-            vaug[g, span, HD:] = ones
-    many = SLOTS * NOCT
-    slot = lax.broadcasted_iota(jnp.int32, (many, TOK), 0) // NOCT
-    octet = lax.broadcasted_iota(jnp.int32, (many, TOK), 0) & (NOCT - 1)
-    place = bs[me] + lax.broadcasted_iota(jnp.int32, (many, TOK), 1)
+        bias[b * TOK : (b + 1) * TOK, :] = jnp.where(ok, 0.0, NEG).astype(BF)
+    slot = lax.broadcasted_iota(jnp.int32, (MANY, TOK), 0) // NOCT
+    octet = lax.broadcasted_iota(jnp.int32, (MANY, TOK), 0) & (NOCT - 1)
+    place = bs[me] + lax.broadcasted_iota(jnp.int32, (MANY, TOK), 1)
     for p in range(OCT):
         end = ((bs[p] + OCT * TOK * octet) & (SEQ - 1)) + (slot + 1) * STRIDE
-        bias = jnp.where(end <= place + 1, 0.0, NEG).astype(BF)
-        lo = RAW + p * many
-        span = slice(lo, lo + many)
-        for g in range(GROUPS):
-            at = 2 * GROUPS * TOK + g * many
-            kaug[g, span, :HD] = recv[p, at : at + many, :]
-            kaug[g, span, HD:] = bias
-            at += GROUPS * many
-            vaug[g, span, :HD] = recv[p, at : at + many, :]
-            vaug[g, span, HD:] = ones[:many, :]
-
-
-def chunk_kernel(off, rotq, kaug, vaug, *rest):
-    out = rest[-1]
+        lo = RAW + p * MANY
+        bias[lo : lo + MANY, :] = jnp.where(end <= place + 1, 0.0, NEG).astype(BF)
+
+
+def key_tiles():
+    raw = [("r", b) for b in range(OCT)] + [("p", 0)]
+    rows = [(x, TOK) for x in raw] + [(("m", p), MANY) for p in range(OCT)]
+    tiles, tile, size, lo, start = [], [], 0, 0, 0
+    for x, n in rows:
+        tile.append(x)
+        size += n
+        if size == TILE or x == ("m", OCT - 1):
+            tiles.append((lo, size, tile))
+            lo, size, tile = lo + size, 0, []
+    return tiles
+
+
+def gather_tile(recv, prev, tile, raw_at, slot_at):
+    parts = []
+    for kind, i in tile:
+        if kind == "r":
+            parts.append(recv[i, raw_at : raw_at + TOK, :])
+        elif kind == "p":
+            parts.append(prev[raw_at : raw_at + TOK, :])
+        else:
+            parts.append(recv[i, slot_at : slot_at + MANY, :])
+    return jnp.concatenate(parts, axis=0)
+
+
+def chunk_kernel(off, rotq, bias, recv, prev, *rest):
+    out, s = rest[-2:]
     dest = lax.axis_index("kv") ^ off
     first = pl.multiple_of(dest * ROWS, ROWS)
     heads = HEADS // GROUPS
     r = lax.broadcasted_iota(jnp.int32, (heads * ROWS, TOK), 0) & (ROWS - 1)
     c = lax.broadcasted_iota(jnp.int32, (heads * ROWS, TOK), 1)
     unit = jnp.where(r + first == c, 1.0, 0.0).astype(BF)
+    slots = 2 * GROUPS * TOK
     for g in range(GROUPS):
         q = jnp.concatenate(
             [rotq[g * heads + i, pl.ds(first, ROWS), :] for i in range(heads)], axis=0
         )
         qa = jnp.concatenate([q, unit], axis=1)
-        s = lax.dot_general(qa, kaug[g], (((1,), (1,)), ((), ())), preferred_element_type=F32)
-        top = jnp.max(s, axis=1, keepdims=True)
-        w = jnp.exp2((s - top) * SCALE2).astype(BF)
-        mixed = jnp.dot(w, vaug[g], preferred_element_type=F32)
+        high = None
+        for lo, size, tile in key_tiles():
+            k = gather_tile(recv, prev, tile, g * TOK, slots + g * MANY)
+            ka = jnp.concatenate([k, bias[lo : lo + size, :]], axis=1)
+            x = lax.dot_general(qa, ka, (((1,), (1,)), ((), ())), preferred_element_type=F32)
+            s[g, :, lo : lo + size] = x
+            for i in range(size // HD):
+                part = x[:, i * HD : (i + 1) * HD]
+                high = part if high is None else jnp.maximum(high, part)
+        top = jnp.max(high, axis=1, keepdims=True)
+        mixed = None
+        for lo, size, tile in key_tiles():
+            w = jnp.exp2((s[g, :, lo : lo + size] - top) * SCALE2).astype(BF)
+            v = gather_tile(recv, prev, tile, (GROUPS + g) * TOK, slots + (GROUPS + g) * MANY)
+            va = jnp.concatenate([v, jnp.ones((size, HD), BF)], axis=1)
+            part = jnp.dot(w, va, preferred_element_type=F32)
+            mixed = part if mixed is None else mixed + part
         res = (mixed[:, :HD] / mixed[:, HD:]).astype(BF)
         for i in range(heads):
             h = g * heads + i
@@ -184,7 +213,7 @@
         x.wait()
 
 
-def call(kernel, out_shape, scratch, flops, spaces, *args, out_space=pltpu.VMEM, grant=32):
+def call(kernel, out_shape, scratch, flops, spaces, *args, out_space=pltpu.VMEM, grant=32, alias=None):
     multi = isinstance(out_shape, tuple)
     vm = pl.BlockSpec(memory_space=out_space)
     return pl.pallas_call(
@@ -193,6 +222,7 @@
         in_specs=[pl.BlockSpec(memory_space=s) for s in spaces],
         out_specs=(vm,) * len(out_shape) if multi else vm,
         scratch_shapes=scratch,
+        input_output_aliases=alias or {},
         compiler_params=pltpu.CompilerParams(vmem_limit_bytes=grant * 2**20),
         cost_estimate=pl.CostEstimate(flops=flops, bytes_accessed=2**10, transcendentals=0),
     )(*args)
@@ -229,20 +259,23 @@
         (SM, VM, VM),
         block_start, freqs, queries,
     )
-    rows = pack * TOK + pack * SLOTS * NOCT
+    bias = call(bias_kernel, shape(KEYS, TOK), [], 10**8, (SM,), block_start)
+    rows = pack * TOK + pack * MANY
     sent = call(
-        octet_kernel, shape(OCT, rows, HD), [pltpu.VMEM((NOCT, pack * SLOTS, HD), F32)], 10**8,
-        (VM,) * 3, own, prev, mem,
+        raw_kernel, shape(OCT, rows, HD), [], 10**8, (VM, VM, pl.ANY, pl.ANY), own, prev, rotq, bias
+    )
+    sent = call(
+        slot_kernel, shape(OCT, rows, HD), [pltpu.VMEM((NOCT, pack * SLOTS, HD), F32)], 10**8,
+        (VM, VM), mem, sent, alias={1: 0},
     )
     recv = lax.all_to_all(sent, "ctx", 0, 0, axis_index_groups=octets)
-    wide = shape(GROUPS, RAW + BLOCKS * SLOTS, 2 * HD)
-    kaug, vaug = call(build_kernel, (wide, wide), [], 10**9, (SM, VM, VM), block_start, recv, prev)
     parts = []
     for off in (3, 2, 1, 0):
         after = parts[-2:-1]
         part = call(
-            functools.partial(chunk_kernel, off), shape(ROWS, HEADS * HD), [], 10**6,
-            (VM,) * 3 + (pl.ANY,) * len(after), rotq, kaug, vaug, *after,
+            functools.partial(chunk_kernel, off), shape(ROWS, HEADS * HD),
+            [pltpu.VMEM((GROUPS, HEADS // GROUPS * ROWS, KEYS), F32)], 10**6,
+            (VM,) * 4 + (pl.ANY,) * len(after), rotq, bias, recv, prev, *after,
         )
         if off:
             part = lax.ppermute(part, "kv", [(i, i ^ off) for i in range(KV)])

time: 80.2 us -> 77.3 us (0.964)
  starting transfers between devices: 20.2 us -> 31.4 us
  waiting for transfers between devices: 18.7 us -> 9.27 us
  blocking collectives: 25 us -> 22.9 us
  Pallas kernels: 14.8 us -> 13.2 us
  local copies, waits for them, and re-layouts: 0.92 us -> 0.02 us
    all_to_all x1, waiting for transfers between devices: 18.4 us -> 8.93 us  [shards(): mem = lax.all_to_all(mem, 'ctx', 0, 0, axis_index_groups=strided)]
    all_to_all x1, starting transfers between devices: 5.05 us -> 13.6 us  [shards(): mem = lax.all_to_all(mem, 'ctx', 0, 0, axis_index_groups=strided)]
    ppermute x3, starting transfers between devices: 8.48 us -> 11.2 us  [shards(): part = lax.ppermute(part, 'kv', [(i, i ^ off) for i in range(KV)])]
    all_to_all x1, blocking collectives: 25 us -> 22.9 us  [shards(): recv = lax.all_to_all(sent, 'ctx', 0, 0, axis_index_groups=octets)]
    pallas_call x9 -> x10, Pallas kernels: 14.8 us -> 13.2 us  [call(): pl.pallas_call(kernel, out_shape=out_shape, in_specs=[pl.BlockSpec(memory...]
    unnamed x8, local copies, waits for them, and re-layouts: 0.92 us -> 0.02 us
  transfers between devices with their start and end apart: 5 -> 5, of which waited for: 2 -> 2; matrix products, arithmetic and copies ran while one was open for 0% -> 0% of each run, Pallas kernels for 9% -> 10%
where the time goes in v3:
time: 77.3 us; the launch traced here: 77 us
  starting transfers between devices  31.4 us (41%)
  blocking collectives  22.9 us (30%)
  Pallas kernels  13.2 us (17%)
  waiting for transfers between devices  9.27 us (12%)
    all_to_all x1, blocking collectives, shards(): recv = lax.all_to_all(sent, 'ctx', 0, 0, axis_index_groups=octets)  22.9 us
    all_to_all x1, starting transfers between devices, shards(): mem = lax.all_to_all(mem, 'ctx', 0, 0, axis_index_groups=strided)  13.6 us
    pallas_call x10, Pallas kernels, call(): pl.pallas_call(kernel, out_shape=out_shape, in_specs=[pl.BlockSpec(memory...  13.2 us
    ppermute x3, starting transfers between devices, shards(): part = lax.ppermute(part, 'kv', [(i, i ^ off) for i in range(KV)])  11.2 us
    all_to_all x1, waiting for transfers between devices, shards(): mem = lax.all_to_all(mem, 'ctx', 0, 0, axis_index_groups=strided)  8.93 us
    ppermute x1, starting transfers between devices, shards(): lax.ppermute(own, 'ctx', [((i - WIN) % BLOCKS, i) for i in range(BLOCKS)])  6.64 us
  transfers between devices with their start and end apart: 5, of which 2 were waited for; matrix products, arithmetic and copies ran while one was open for 0% of the time, Pallas kernels for 10%

profile of v3, /device:TPU:1, one launch (start us, length us, event | category | flops | bytes accessed | tf_op | source)
XLA Modules:
  0.0 77.0 jit_solution(18212895746194720342)
XLA Ops:
  0.0 0.0 copy-start.3
  0.0 0.0 copy-start.1
  0.0 0.0 copy-start.2
  0.0 2.6 %shard_map.93 = (bf16[512,128]{1,0:T(8,128)(2,1)}, bf16[16,16,128]{2,1,0:T(8,128)(2,1)}) custom-call(s32[128]{0:T(128)} %bs.5, f32[8,128]{1,0:T(8,128)} %constant.2.clone.freqs, bf16[128,2,128]{2,1,0:T(2,128)(2,1)} %k.1, bf16[128,2,128]{2,1,0:T(2,128)(2,1)} %v.1, f32[32,128]{1,0:T(8,128)} %dk.1, f32[128,128]{1,0:T(8,128)} %pk.1, f32[32,128]{1,0:T(8,128)} %dv.1, ...), custom_call_target="tpu_custom_call" | custom-call | flops 1000000000 | bytes 1024 | tf_op jit(solution)/shard_map/pallas_call | solution.py:219
  2.6 6.6 %collective-permute-start = (bf16[512,128]{1,0:T(8,128)(2,1)}, bf16[512,128]{1,0:T(8,128)(2,1)S(1)}, u32[]{:S(2)}, u32[]{:S(2)}) collective-permute-start(bf16[512,128]{1,0:T(8,128)(2,1)} %get-tuple-element.8.own), channel_id=1, source_target_pairs={{480,0},{484,4},{488,8},{492,12},{496,16},{500,20},{504,24},{508,2... | collective-permute-start | bytes 393224 | tf_op jit(solution)/shard_map/ppermute | solution.py:255
  9.3 13.6 %all-to-all-start = ((bf16[16,16,128]{2,1,0:T(8,128)(2,1)}), bf16[16,16,128]{2,1,0:T(8,128)(2,1)S(1)}, u32[]{:S(2)}, u32[]{:S(2)}) async-start(bf16[16,16,128]{2,1,0:T(8,128)(2,1)} %get-tuple-element.7), calls=%async_computation | async-start | bytes 131072 | tf_op jit(solution)/shard_map/all_to_all | solution.py:256
  22.9 0.0 copy-done.1
  22.9 0.7 shard_map.92.bias
  23.6 0.0 copy-done.3
  23.6 0.0 copy-done.2
  23.6 0.0 copy-start
  23.6 1.6 %shard_map.91.rotq = bf16[16,128,128]{2,1,0:T(8,128)(2,1)S(1)} custom-call(s32[128]{0:T(128)S(1)} %copy-done.1, f32[8,128]{1,0:T(8,128)S(1)} %copy-done.3, bf16[128,16,128]{2,1,0:T(8,128)(2,1)S(1)} %copy-done.2), custom_call_target="tpu_custom_call" | custom-call | flops 1000000000 | bytes 1024 | tf_op jit(solution)/shard_map/pallas_call | solution.py:219
  25.2 0.0 collective-permute-done.prev
  25.2 0.0 copy-done
  25.2 0.1 shard_map.94.sent
  25.4 8.9 %all-to-all-done.mem = bf16[16,16,128]{2,1,0:T(8,128)(2,1)S(1)} async-done(((bf16[16,16,128]{2,1,0:T(8,128)(2,1)}), bf16[16,16,128]{2,1,0:T(8,128)(2,1)S(1)}, u32[]{:S(2)}, u32[]{:S(2)}) %all-to-all-start) | async-done | bytes 65568 | tf_op jit(solution)/shard_map/all_to_all | solution.py:256
  34.3 0.1 shard_map.95
  34.4 22.9 %all_to_all.10.recv = bf16[8,768,128]{2,1,0:T(8,128)(2,1)S(1)} all-to-all(bf16[8,768,128]{2,1,0:T(8,128)(2,1)S(1)} %shard_map.95), channel_id=1, replica_groups={{0,4,8,12,16,20,24,28},{32,36,40,44,48,52,56,60},{64,68,72,76,80,84,88,..., dimensions={0} | all-to-all | bytes 3145728 | tf_op jit(solution)/shard_map/all_to_all | solution.py:271
  57.3 1.8 %shard_map.98 = bf16[32,2048]{1,0:T(8,128)(2,1)S(1)} custom-call(bf16[16,128,128]{2,1,0:T(8,128)(2,1)S(1)} %shard_map.91.rotq, bf16[1664,128]{1,0:T(8,128)(2,1)S(1)} %shard_map.92.bias, bf16[8,768,128]{2,1,0:T(8,128)(2,1)S(1)} %all_to_all.10.recv, bf16[512,128]{1,0:T(8,128)(2,1)S(1)} %collective-permute-done.prev), custom_call_target="tpu_custom_call" | custom-call | flops 1000000 | bytes 1024 | tf_op jit(solution)/shard_map/pallas_call | solution.py:219
  59.1 6.2 %collective-permute-start.2 = (bf16[32,2048]{1,0:T(8,128)(2,1)S(1)}, bf16[32,2048]{1,0:T(8,128)(2,1)S(1)}, u32[]{:S(2)}, u32[]{:S(2)}) collective-permute-start(bf16[32,2048]{1,0:T(8,128)(2,1)S(1)} %shard_map.98), channel_id=1, source_target_pairs={{0,3},{1,2},{2,1},{3,0},{4,7},{5,6},{6,5},{7,4},{8,11},{9,10},{10,... | collective-permute-start | bytes 393224 | tf_op jit(solution)/shard_map/ppermute | solution.py:281
  65.3 1.8 %shard_map.96 = bf16[32,2048]{1,0:T(8,128)(2,1)S(1)} custom-call(bf16[16,128,128]{2,1,0:T(8,128)(2,1)S(1)} %shard_map.91.rotq, bf16[1664,128]{1,0:T(8,128)(2,1)S(1)} %shard_map.92.bias, bf16[8,768,128]{2,1,0:T(8,128)(2,1)S(1)} %all_to_all.10.recv, bf16[512,128]{1,0:T(8,128)(2,1)S(1)} %collective-permute-done.prev), custom_call_target="tpu_custom_call" | custom-call | flops 1000000 | bytes 1024 | tf_op jit(solution)/shard_map/pallas_call | solution.py:219
  67.1 3.0 %collective-permute-start.1 = (bf16[32,2048]{1,0:T(8,128)(2,1)S(1)}, bf16[32,2048]{1,0:T(8,128)(2,1)S(1)}, u32[]{:S(2)}, u32[]{:S(2)}) collective-permute-start(bf16[32,2048]{1,0:T(8,128)(2,1)S(1)} %shard_map.96), channel_id=1, source_target_pairs={{0,2},{1,3},{2,0},{3,1},{4,6},{5,7},{6,4},{7,5},{8,10},{9,11},{10,... | collective-permute-start | bytes 393224 | tf_op jit(solution)/shard_map/ppermute | solution.py:281
  70.2 0.0 collective-permute-done.2.rest_0_.d
  70.2 1.8 %shard_map.99 = bf16[32,2048]{1,0:T(8,128)(2,1)S(1)} custom-call(bf16[16,128,128]{2,1,0:T(8,128)(2,1)S(1)} %shard_map.91.rotq, bf16[1664,128]{1,0:T(8,128)(2,1)S(1)} %shard_map.92.bias, bf16[8,768,128]{2,1,0:T(8,128)(2,1)S(1)} %all_to_all.10.recv, bf16[512,128]{1,0:T(8,128)(2,1)S(1)} %collective-permute-done.prev, ...), custom_call_target="tpu_custom_call" | custom-call | flops 1000000 | bytes 1024 | tf_op jit(solution)/shard_map/pallas_call | solution.py:219
  72.0 1.9 %collective-permute-start.3 = (bf16[32,2048]{1,0:T(8,128)(2,1)S(1)}, bf16[32,2048]{1,0:T(8,128)(2,1)S(1)}, u32[]{:S(2)}, u32[]{:S(2)}) collective-permute-start(bf16[32,2048]{1,0:T(8,128)(2,1)S(1)} %shard_map.99), channel_id=1, source_target_pairs={{0,1},{1,0},{2,3},{3,2},{4,5},{5,4},{6,7},{7,6},{8,9},{9,8},{10,11... | collective-permute-start | bytes 393224 | tf_op jit(solution)/shard_map/ppermute | solution.py:281
  74.0 0.3 collective-permute-done.1.rest_0_.c
  74.3 1.8 %shard_map.97.a = bf16[32,2048]{1,0:T(8,128)(2,1)S(1)} custom-call(bf16[16,128,128]{2,1,0:T(8,128)(2,1)S(1)} %shard_map.91.rotq, bf16[1664,128]{1,0:T(8,128)(2,1)S(1)} %shard_map.92.bias, bf16[8,768,128]{2,1,0:T(8,128)(2,1)S(1)} %all_to_all.10.recv, bf16[512,128]{1,0:T(8,128)(2,1)S(1)} %collective-permute-done.prev, ...), custom_call_target="tpu_custom_call" | custom-call | flops 1000000 | bytes 1024 | tf_op jit(solution)/shard_map/pallas_call | solution.py:219
  76.1 0.0 collective-permute-done.3.b
  76.1 0.8 %shard_map.100 = bf16[32,8192]{1,0:T(8,128)(2,1)} custom-call(bf16[32,2048]{1,0:T(8,128)(2,1)S(1)} %shard_map.97.a, bf16[32,2048]{1,0:T(8,128)(2,1)S(1)} %collective-permute-done.3.b, bf16[32,2048]{1,0:T(8,128)(2,1)S(1)} %collective-permute-done.1.rest_0_.c, bf16[32,2048]{1,0:T(8,128)(2,1)S(1)} %collective-permute-done.2.rest_0_.d), custom_call_target="tpu_custom_call" | custom-call | flops 100000000 | bytes 1024 | tf_op jit(solution)/shard_map/pallas_call | solution.py:219
Async XLA Ops:
  0.0 23.6 %copy-start.3 = (f32[8,128]{1,0:T(8,128)S(1)}, f32[8,128]{1,0:T(8,128)}, u32[]{:S(2)}) copy-start(f32[8,128]{1,0:T(8,128)} %constant.2.clone.freqs) | copy-start | bytes 12292
  0.0 22.9 %copy-start.1 = (s32[128]{0:T(128)S(1)}, s32[128]{0:T(128)}, u32[]{:S(2)}) copy-start(s32[128]{0:T(128)} %bs.5) | copy-start | bytes 1540
  0.0 23.6 %copy-start.2 = (bf16[128,16,128]{2,1,0:T(8,128)(2,1)S(1)}, bf16[128,16,128]{2,1,0:T(8,128)(2,1)}, u32[]{:S(2)}) copy-start(bf16[128,16,128]{2,1,0:T(8,128)(2,1)} %q.1) | copy-start | bytes 1572868
  2.6 22.6 %collective-permute-start = (bf16[512,128]{1,0:T(8,128)(2,1)}, bf16[512,128]{1,0:T(8,128)(2,1)S(1)}, u32[]{:S(2)}, u32[]{:S(2)}) collective-permute-start(bf16[512,128]{1,0:T(8,128)(2,1)} %get-tuple-element.8.own), channel_id=1, source_target_pairs={{480,0},{484,4},{488,8},{492,12},{496,16},{500,20},{504,24},{508,2... | collective-permute-start | bytes 393224 | tf_op jit(solution)/shard_map/ppermute | solution.py:255
  9.3 25.0 %all-to-all-start = ((bf16[16,16,128]{2,1,0:T(8,128)(2,1)}), bf16[16,16,128]{2,1,0:T(8,128)(2,1)S(1)}, u32[]{:S(2)}, u32[]{:S(2)}) async-start(bf16[16,16,128]{2,1,0:T(8,128)(2,1)} %get-tuple-element.7), calls=%async_computation | async-start | bytes 131072 | tf_op jit(solution)/shard_map/all_to_all | solution.py:256
  23.6 1.6 %copy-start = (bf16[512,128]{1,0:T(8,128)(2,1)S(1)}, bf16[512,128]{1,0:T(8,128)(2,1)}, u32[]{:S(2)}) copy-start(bf16[512,128]{1,0:T(8,128)(2,1)} %get-tuple-element.8.own) | copy-start | bytes 393220
  59.1 11.1 %collective-permute-start.2 = (bf16[32,2048]{1,0:T(8,128)(2,1)S(1)}, bf16[32,2048]{1,0:T(8,128)(2,1)S(1)}, u32[]{:S(2)}, u32[]{:S(2)}) collective-permute-start(bf16[32,2048]{1,0:T(8,128)(2,1)S(1)} %shard_map.98), channel_id=1, source_target_pairs={{0,3},{1,2},{2,1},{3,0},{4,7},{5,6},{6,5},{7,4},{8,11},{9,10},{10,... | collective-permute-start | bytes 393224 | tf_op jit(solution)/shard_map/ppermute | solution.py:281
  67.1 7.1 %collective-permute-start.1 = (bf16[32,2048]{1,0:T(8,128)(2,1)S(1)}, bf16[32,2048]{1,0:T(8,128)(2,1)S(1)}, u32[]{:S(2)}, u32[]{:S(2)}) collective-permute-start(bf16[32,2048]{1,0:T(8,128)(2,1)S(1)} %shard_map.96), channel_id=1, source_target_pairs={{0,2},{1,3},{2,0},{3,1},{4,6},{5,7},{6,4},{7,5},{8,10},{9,11},{10,... | collective-permute-start | bytes 393224 | tf_op jit(solution)/shard_map/ppermute | solution.py:281
  72.0 4.1 %collective-permute-start.3 = (bf16[32,2048]{1,0:T(8,128)(2,1)S(1)}, bf16[32,2048]{1,0:T(8,128)(2,1)S(1)}, u32[]{:S(2)}, u32[]{:S(2)}) collective-permute-start(bf16[32,2048]{1,0:T(8,128)(2,1)S(1)} %shard_map.99), channel_id=1, source_target_pairs={{0,1},{1,0},{2,3},{3,2},{4,5},{5,4},{6,7},{7,6},{8,9},{9,8},{10,11... | collective-permute-start | bytes 393224 | tf_op jit(solution)/shard_map/ppermute | solution.py:281

commit v4 on v3

--- a/solution.py
+++ b/solution.py
@@ -20,13 +20,11 @@
 HEADS = 16
 GROUPS = 2
 KV = 4
-OCT = 8
-NOCT = BLOCKS // OCT
+RING = 4
 ROWS = TOK // KV
 RAW = (WIN + 1) * TOK
-MANY = SLOTS * NOCT
+TOKP = 2 * GROUPS * TOK
 KEYS = RAW + BLOCKS * SLOTS
-TILE = 256
 MSCALE = 1.0 + 0.1 * math.log(16.0)
 SCALE2 = math.log2(math.e) / math.sqrt(HD)
 NEG = -1e30
@@ -96,74 +94,72 @@
         rotq[h] = turn(scr[:, h, :], cosine, sine)
 
 
-def raw_kernel(own, prev, rotq, bias, out):
-    me = lax.rem(lax.axis_index("ctx"), OCT)
-    raw = own.shape[0]
-    for d in range(OCT):
-
-        @pl.when(me <= d)
+def ring_kernel(own, row1, row2, rotq, bias, *outs):
+    me = lax.rem(lax.axis_index("ctx"), RING)
+    for s, out in enumerate(outs, 1):
+        out[TOKP:, :] = row1[...]
+
+        @pl.when(me + s < RING)
         def _():
-            out[d, :raw, :] = own[...]
-
-        @pl.when(me > d)
+            out[:TOKP, :] = own[...]
+
+        @pl.when(me + s >= RING)
         def _():
-            out[d, :raw, :] = prev[...]
-
-
-def slot_kernel(mem, sent, out, scr):
+            out[:TOKP, :] = row2[...]
+
+
+def slot_kernel(mem, out, scr):
     scr[...] = mem[...].astype(F32)
-    kinds = 2 * GROUPS * SLOTS
-    slots = jnp.concatenate([scr[:, r, :] for r in range(kinds)], axis=0).astype(BF)
-    raw = 2 * GROUPS * TOK
-    for d in range(OCT):
-        out[d, raw:, :] = slots
+    for kind in range(2 * GROUPS):
+        for j in range(SLOTS):
+            out[kind, j * BLOCKS : (j + 1) * BLOCKS, :] = scr[:, kind * SLOTS + j, :].astype(BF)
 
 
 def bias_kernel(bs, bias):
     me = lax.axis_index("ctx")
-    pos = lax.rem(me, OCT)
+    pos = lax.rem(me, RING)
     place = bs[me] + lax.broadcasted_iota(jnp.int32, (TOK, TOK), 1)
     row = lax.broadcasted_iota(jnp.int32, (TOK, TOK), 0)
-    for b in range(WIN + 1):
-        back = WIN if b == WIN else lax.rem(pos - b + OCT, OCT)
+    backs = [0, RING]
+    for s in range(1, RING):
+        wrapped = pos < s
+        backs += [jnp.where(wrapped, RING + s, s), jnp.where(wrapped, s, RING + s)]
+    backs += [WIN]
+    for b, back in enumerate(backs):
         there = bs[lax.rem(me - back + BLOCKS, BLOCKS)] + row
         ok = (there <= place) & (there > place - WINDOW)
         bias[b * TOK : (b + 1) * TOK, :] = jnp.where(ok, 0.0, NEG).astype(BF)
-    slot = lax.broadcasted_iota(jnp.int32, (MANY, TOK), 0) // NOCT
-    octet = lax.broadcasted_iota(jnp.int32, (MANY, TOK), 0) & (NOCT - 1)
-    place = bs[me] + lax.broadcasted_iota(jnp.int32, (MANY, TOK), 1)
-    for p in range(OCT):
-        end = ((bs[p] + OCT * TOK * octet) & (SEQ - 1)) + (slot + 1) * STRIDE
-        lo = RAW + p * MANY
-        bias[lo : lo + MANY, :] = jnp.where(end <= place + 1, 0.0, NEG).astype(BF)
+    start = (bs[0] + TOK * row) & (SEQ - 1)
+    for j in range(SLOTS):
+        ok = start + (j + 1) * STRIDE <= place + 1
+        lo = RAW + j * BLOCKS
+        bias[lo : lo + BLOCKS, :] = jnp.where(ok, 0.0, NEG).astype(BF)
 
 
 def key_tiles():
-    raw = [("r", b) for b in range(OCT)] + [("p", 0)]
-    rows = [(x, TOK) for x in raw] + [(("m", p), MANY) for p in range(OCT)]
-    tiles, tile, size, lo, start = [], [], 0, 0, 0
-    for x, n in rows:
-        tile.append(x)
-        size += n
-        if size == TILE or x == ("m", OCT - 1):
-            tiles.append((lo, size, tile))
-            lo, size, tile = lo + size, 0, []
-    return tiles
-
-
-def gather_tile(recv, prev, tile, raw_at, slot_at):
+    half = SLOTS * BLOCKS // 2
+    tiles = [(0, [("own", 0, TOK), ("row1", 0, TOK)])]
+    for s in range(1, RING):
+        tiles.append((2 * s * TOK, [(s, 0, TOK), (s, TOKP, TOK)]))
+    tiles.append((RAW, [("mem", 0, half)]))
+    tiles.append((RAW + half, [("mem", half, half)]))
+    tiles.append((RAW - TOK, [("row2", 0, TOK)]))
+    return [(lo, sum(n for _, _, n in tile), tile) for lo, tile in tiles]
+
+
+def gather_tile(refs, tile, kind):
     parts = []
-    for kind, i in tile:
-        if kind == "r":
-            parts.append(recv[i, raw_at : raw_at + TOK, :])
-        elif kind == "p":
-            parts.append(prev[raw_at : raw_at + TOK, :])
+    for name, lo, n in tile:
+        if name == "mem":
+            parts.append(refs[name][kind, lo : lo + n, :])
         else:
-            parts.append(recv[i, slot_at : slot_at + MANY, :])
-    return jnp.concatenate(parts, axis=0)
-
-
-def chunk_kernel(off, rotq, bias, recv, prev, *rest):
+            at = lo + kind * TOK
+            parts.append(refs[name][at : at + n, :])
+    return parts[0] if len(parts) == 1 else jnp.concatenate(parts, axis=0)
+
+
+def chunk_kernel(off, rotq, bias, own, row1, row2, r1, r2, r3, mem, *rest):
+    refs = {"own": own, "row1": row1, "row2": row2, 1: r1, 2: r2, 3: r3, "mem": mem}
     out, s = rest[-2:]
     dest = lax.axis_index("kv") ^ off
     first = pl.multiple_of(dest * ROWS, ROWS)
@@ -171,7 +167,6 @@
     r = lax.broadcasted_iota(jnp.int32, (heads * ROWS, TOK), 0) & (ROWS - 1)
     c = lax.broadcasted_iota(jnp.int32, (heads * ROWS, TOK), 1)
     unit = jnp.where(r + first == c, 1.0, 0.0).astype(BF)
-    slots = 2 * GROUPS * TOK
     for g in range(GROUPS):
         q = jnp.concatenate(
             [rotq[g * heads + i, pl.ds(first, ROWS), :] for i in range(heads)], axis=0
@@ -179,7 +174,7 @@
         qa = jnp.concatenate([q, unit], axis=1)
         high = None
         for lo, size, tile in key_tiles():
-            k = gather_tile(recv, prev, tile, g * TOK, slots + g * MANY)
+            k = gather_tile(refs, tile, g)
             ka = jnp.concatenate([k, bias[lo : lo + size, :]], axis=1)
             x = lax.dot_general(qa, ka, (((1,), (1,)), ((), ())), preferred_element_type=F32)
             s[g, :, lo : lo + size] = x
@@ -190,7 +185,7 @@
         mixed = None
         for lo, size, tile in key_tiles():
             w = jnp.exp2((s[g, :, lo : lo + size] - top) * SCALE2).astype(BF)
-            v = gather_tile(recv, prev, tile, (GROUPS + g) * TOK, slots + (GROUPS + g) * MANY)
+            v = gather_tile(refs, tile, GROUPS + g)
             va = jnp.concatenate([v, jnp.ones((size, HD), BF)], axis=1)
             part = jnp.dot(w, va, preferred_element_type=F32)
             mixed = part if mixed is None else mixed + part
@@ -232,8 +227,6 @@
     return jax.ShapeDtypeStruct(dims, dtype)
 
 
-octets = [[OCT * o + p for p in range(OCT)] for o in range(NOCT)]
-strided = [[OCT * o + p for o in range(NOCT)] for p in range(OCT)]
 SM, VM, HB = pltpu.SMEM, pltpu.VMEM, pltpu.HBM
 
 
@@ -243,7 +236,7 @@
     params = (block_start, freqs, keys, values, depth_k, point_k, depth_v, point_v)
     own, mem = call(
         prep_kernel,
-        (shape(pack * TOK, HD), shape(NOCT, pack * SLOTS, HD)),
+        (shape(pack * TOK, HD), shape(BLOCKS, pack * SLOTS, HD)),
         [pltpu.VMEM((TOK, GROUPS, HD), F32), pltpu.VMEM((pack * SLOTS, HD), F32)]
         + [(pltpu.SMEM if i == 0 else pltpu.VMEM)(x.shape, x.dtype) for i, x in enumerate(params)]
         + [pltpu.SemaphoreType.DMA((len(params),))],
@@ -252,30 +245,36 @@
         *params,
         grant=60,
     )
-    prev = lax.ppermute(own, "ctx", [((i - WIN) % BLOCKS, i) for i in range(BLOCKS)])
-    mem = lax.all_to_all(mem, "ctx", 0, 0, axis_index_groups=strided)
+    row1, row2 = (
+        lax.ppermute(own, "ctx", [((i - d) % BLOCKS, i) for i in range(BLOCKS)])
+        for d in (RING, 2 * RING)
+    )
+    mem = lax.all_to_all(mem, "ctx", 0, 0)
     rotq = call(
-        query_kernel, shape(HEADS, TOK, HD), [pltpu.VMEM((TOK, HEADS, HD), F32)], 10**9,
+        query_kernel, shape(HEADS, TOK, HD), [pltpu.VMEM((TOK, HEADS, HD), F32)], 10**3,
         (SM, VM, VM),
         block_start, freqs, queries,
     )
-    bias = call(bias_kernel, shape(KEYS, TOK), [], 10**8, (SM,), block_start)
-    rows = pack * TOK + pack * MANY
-    sent = call(
-        raw_kernel, shape(OCT, rows, HD), [], 10**8, (VM, VM, pl.ANY, pl.ANY), own, prev, rotq, bias
-    )
-    sent = call(
-        slot_kernel, shape(OCT, rows, HD), [pltpu.VMEM((NOCT, pack * SLOTS, HD), F32)], 10**8,
-        (VM, VM), mem, sent, alias={1: 0},
-    )
-    recv = lax.all_to_all(sent, "ctx", 0, 0, axis_index_groups=octets)
+    bias = call(bias_kernel, shape(KEYS, TOK), [], 10**3, (SM,), block_start)
+    rings = call(
+        ring_kernel, (shape(2 * TOKP, HD),) * (RING - 1), [], 10**3, (VM,) * 3 + (pl.ANY,) * 2,
+        own, row1, row2, rotq, bias,
+    )
+    rings = [
+        lax.ppermute(x, "ctx", [(i, i // RING * RING + (i + s) % RING) for i in range(BLOCKS)])
+        for s, x in enumerate(rings, 1)
+    ]
+    mem = call(
+        slot_kernel, shape(pack, BLOCKS * SLOTS, HD),
+        [pltpu.VMEM((BLOCKS, pack * SLOTS, HD), F32)], 10**6, (VM,), mem,
+    )
     parts = []
     for off in (3, 2, 1, 0):
         after = parts[-2:-1]
         part = call(
             functools.partial(chunk_kernel, off), shape(ROWS, HEADS * HD),
             [pltpu.VMEM((GROUPS, HEADS // GROUPS * ROWS, KEYS), F32)], 10**6,
-            (VM,) * 4 + (pl.ANY,) * len(after), rotq, bias, recv, prev, *after,
+            (VM,) * 9 + (pl.ANY,) * len(after), rotq, bias, own, row1, row2, *rings, mem, *after,
         )
         if off:
             part = lax.ppermute(part, "kv", [(i, i ^ off) for i in range(KV)])

time: 77.3 us -> 86.3 us (1.12)
  blocking collectives: 22.9 us -> 0 us
  starting transfers between devices: 31.4 us -> 47.3 us
  waiting for transfers between devices: 9.27 us -> 23.5 us
  Pallas kernels: 13.2 us -> 14.6 us
    ppermute x1 -> x5, waiting for transfers between devices: 0.01 us -> 23.5 us  [the longest x2 17.7 us: shards(): lax.ppermute(own, 'ctx', [((i - d) % BLOCKS, i) for i in range(BLOCKS)])]
    all_to_all x1 -> x0, blocking collectives: 22.9 us -> none  [shards(): recv = lax.all_to_all(sent, 'ctx', 0, 0, axis_index_groups=octets)]
    ppermute x1 -> x5, starting transfers between devices: 6.64 us -> 17.1 us  [the longest x3 10.6 us: shards(): lax.ppermute(x, 'ctx', [(i, i // RING * RING + (i + s) % RING) for i in r...]
    all_to_all x1, waiting for transfers between devices: 8.93 us -> 0.01 us  [shards(): mem = lax.all_to_all(mem, 'ctx', 0, 0)]
    all_to_all x1, starting transfers between devices: 13.6 us -> 21 us  [shards(): mem = lax.all_to_all(mem, 'ctx', 0, 0)]
    ppermute x3, starting transfers between devices: 11.2 us -> 9.21 us  [shards(): part = lax.ppermute(part, 'kv', [(i, i ^ off) for i in range(KV)])]
    pallas_call x10, Pallas kernels: 13.2 us -> 14.6 us  [call(): pl.pallas_call(kernel, out_shape=out_shape, in_specs=[pl.BlockSpec(memory...]
  transfers between devices with their start and end apart: 5 -> 9, of which waited for: 2 -> 4; matrix products, arithmetic and copies ran while one was open for 0% -> 0% of each run, Pallas kernels for 10% -> 11%
where the time goes in v4:
time: 86.3 us; the launch traced here: 85.6 us
  starting transfers between devices  47.3 us (55%)
  waiting for transfers between devices  23.5 us (27%)
  Pallas kernels  14.6 us (17%)
    all_to_all x1, starting transfers between devices, shards(): mem = lax.all_to_all(mem, 'ctx', 0, 0)  21 us
    ppermute x2, waiting for transfers between devices, shards(): lax.ppermute(own, 'ctx', [((i - d) % BLOCKS, i) for i in range(BLOCKS)])  17.7 us
    pallas_call x10, Pallas kernels, call(): pl.pallas_call(kernel, out_shape=out_shape, in_specs=[pl.BlockSpec(memory...  14.6 us
    ppermute x3, starting transfers between devices, shards(): lax.ppermute(x, 'ctx', [(i, i // RING * RING + (i + s) % RING) for i in r...  10.6 us
    ppermute x3, starting transfers between devices, shards(): part = lax.ppermute(part, 'kv', [(i, i ^ off) for i in range(KV)])  9.21 us
    ppermute x2, starting transfers between devices, shards(): lax.ppermute(own, 'ctx', [((i - d) % BLOCKS, i) for i in range(BLOCKS)])  6.48 us
    ppermute x3, waiting for transfers between devices, shards(): lax.ppermute(x, 'ctx', [(i, i // RING * RING + (i + s) % RING) for i in r...  5.74 us
  transfers between devices with their start and end apart: 9, of which 4 were waited for; matrix products, arithmetic and copies ran while one was open for 0% of the time, Pallas kernels for 11%

profile of v4, /device:TPU:1, one launch (start us, length us, event | category | flops | bytes accessed | tf_op | source)
XLA Modules:
  0.0 85.6 jit_solution(16628281998580342283)
XLA Ops:
  0.0 2.7 %shard_map.93 = (bf16[512,128]{1,0:T(8,128)(2,1)}, bf16[128,16,128]{2,1,0:T(8,128)(2,1)}) custom-call(s32[128]{0:T(128)} %bs.5, f32[8,128]{1,0:T(8,128)} %constant.2.clone.freqs, bf16[128,2,128]{2,1,0:T(2,128)(2,1)} %k.1, bf16[128,2,128]{2,1,0:T(2,128)(2,1)} %v.1, f32[32,128]{1,0:T(8,128)} %dk.1, f32[128,128]{1,0:T(8,128)} %pk.1, f32[32,128]{1,0:T(8,128)} %dv.1, ...), custom_call_target="tpu_custom_call" | custom-call | flops 1000000000 | bytes 1024 | tf_op jit(solution)/shard_map/pallas_call | solution.py:214
  2.8 0.0 copy-start
  2.8 0.0 copy-start.1
  2.8 21.0 %all-to-all-start = ((bf16[128,16,128]{2,1,0:T(8,128)(2,1)}), bf16[128,16,128]{2,1,0:T(8,128)(2,1)S(1)}, u32[]{:S(2)}, u32[]{:S(2)}) async-start(bf16[128,16,128]{2,1,0:T(8,128)(2,1)} %get-tuple-element.14), calls=%async_computation | async-start | bytes 1048576 | tf_op jit(solution)/shard_map/all_to_all | solution.py:252
  23.7 0.0 copy-start.3
  23.8 0.0 copy-done
  23.8 0.0 copy-start.2
  23.8 3.4 %collective-permute-start.1 = (bf16[512,128]{1,0:T(8,128)(2,1)S(1)}, bf16[512,128]{1,0:T(8,128)(2,1)S(1)}, u32[]{:S(2)}, u32[]{:S(2)}) collective-permute-start(bf16[512,128]{1,0:T(8,128)(2,1)S(1)} %copy-done), channel_id=1, source_target_pairs={{480,0},{484,4},{488,8},{492,12},{496,16},{500,20},{504,24},{508,2... | collective-permute-start | bytes 393224 | tf_op jit(solution)/shard_map/ppermute | solution.py:249
  27.2 3.1 %collective-permute-start = (bf16[512,128]{1,0:T(8,128)(2,1)S(1)}, bf16[512,128]{1,0:T(8,128)(2,1)S(1)}, u32[]{:S(2)}, u32[]{:S(2)}) collective-permute-start(bf16[512,128]{1,0:T(8,128)(2,1)S(1)} %copy-done), channel_id=1, source_target_pairs={{496,0},{500,4},{504,8},{508,12},{0,16},{4,20},{8,24},{12,28},{16,... | collective-permute-start | bytes 393224 | tf_op jit(solution)/shard_map/ppermute | solution.py:249
  30.3 0.0 copy-done.3
  30.3 0.7 shard_map.92.bias
  31.0 0.0 copy-done.1
  31.0 0.0 copy-done.2
  31.0 1.6 %shard_map.91.rotq = bf16[16,128,128]{2,1,0:T(8,128)(2,1)S(1)} custom-call(s32[128]{0:T(128)S(1)} %copy-done.3, f32[8,128]{1,0:T(8,128)S(1)} %copy-done.2, bf16[128,16,128]{2,1,0:T(8,128)(2,1)S(1)} %copy-done.1), custom_call_target="tpu_custom_call" | custom-call | flops 1000 | bytes 1024 | tf_op jit(solution)/shard_map/pallas_call | solution.py:214
  32.6 13.7 %collective-permute-done.1.row2 = bf16[512,128]{1,0:T(8,128)(2,1)S(1)} collective-permute-done((bf16[512,128]{1,0:T(8,128)(2,1)S(1)}, bf16[512,128]{1,0:T(8,128)(2,1)S(1)}, u32[]{:S(2)}, u32[]{:S(2)}) %collective-permute-start.1) | collective-permute-done | bytes 131104 | tf_op jit(solution)/shard_map/ppermute | solution.py:249
  46.3 4.1 %collective-permute-done.row1 = bf16[512,128]{1,0:T(8,128)(2,1)S(1)} collective-permute-done((bf16[512,128]{1,0:T(8,128)(2,1)S(1)}, bf16[512,128]{1,0:T(8,128)(2,1)S(1)}, u32[]{:S(2)}, u32[]{:S(2)}) %collective-permute-start) | collective-permute-done | bytes 131104 | tf_op jit(solution)/shard_map/ppermute | solution.py:249
  50.3 0.1 shard_map.94
  50.4 3.1 %collective-permute-start.2 = (bf16[1024,128]{1,0:T(8,128)(2,1)S(1)}, bf16[1024,128]{1,0:T(8,128)(2,1)S(1)}, u32[]{:S(2)}, u32[]{:S(2)}) collective-permute-start(bf16[1024,128]{1,0:T(8,128)(2,1)S(1)} %get-tuple-element.11), channel_id=1, source_target_pairs={{0,4},{4,8},{8,12},{12,0},{16,20},{20,24},{24,28},{28,16},{32,36},... | collective-permute-start | bytes 786440 | tf_op jit(solution)/shard_map/ppermute | solution.py:264
  53.5 4.5 %collective-permute-start.3 = (bf16[1024,128]{1,0:T(8,128)(2,1)S(1)}, bf16[1024,128]{1,0:T(8,128)(2,1)S(1)}, u32[]{:S(2)}, u32[]{:S(2)}) collective-permute-start(bf16[1024,128]{1,0:T(8,128)(2,1)S(1)} %get-tuple-element.12), channel_id=1, source_target_pairs={{0,8},{4,12},{8,0},{12,4},{16,24},{20,28},{24,16},{28,20},{32,40},... | collective-permute-start | bytes 786440 | tf_op jit(solution)/shard_map/ppermute | solution.py:264
  58.0 3.0 %collective-permute-start.4 = (bf16[1024,128]{1,0:T(8,128)(2,1)S(1)}, bf16[1024,128]{1,0:T(8,128)(2,1)S(1)}, u32[]{:S(2)}, u32[]{:S(2)}) collective-permute-start(bf16[1024,128]{1,0:T(8,128)(2,1)S(1)} %get-tuple-element.13), channel_id=1, source_target_pairs={{0,12},{4,0},{8,4},{12,8},{16,28},{20,16},{24,20},{28,24},{32,44},... | collective-permute-start | bytes 786440 | tf_op jit(solution)/shard_map/ppermute | solution.py:264
  61.0 0.0 all-to-all-done.mem
  61.1 1.4 %shard_map.95.mem = bf16[4,512,128]{2,1,0:T(8,128)(2,1)S(1)} custom-call(bf16[128,16,128]{2,1,0:T(8,128)(2,1)S(1)} %all-to-all-done.mem), custom_call_target="tpu_custom_call" | custom-call | flops 1000000 | bytes 1024 | tf_op jit(solution)/shard_map/pallas_call | solution.py:214
  62.5 0.0 collective-permute-done.2.r1
  62.5 3.5 %collective-permute-done.3.r2 = bf16[1024,128]{1,0:T(8,128)(2,1)S(1)} collective-permute-done((bf16[1024,128]{1,0:T(8,128)(2,1)S(1)}, bf16[1024,128]{1,0:T(8,128)(2,1)S(1)}, u32[]{:S(2)}, u32[]{:S(2)}) %collective-permute-start.3) | collective-permute-done | bytes 262176 | tf_op jit(solution)/shard_map/ppermute | solution.py:264
  65.9 2.3 %collective-permute-done.4.r3 = bf16[1024,128]{1,0:T(8,128)(2,1)S(1)} collective-permute-done((bf16[1024,128]{1,0:T(8,128)(2,1)S(1)}, bf16[1024,128]{1,0:T(8,128)(2,1)S(1)}, u32[]{:S(2)}, u32[]{:S(2)}) %collective-permute-start.4) | collective-permute-done | bytes 262176 | tf_op jit(solution)/shard_map/ppermute | solution.py:264
  68.2 1.8 %shard_map.98 = bf16[32,2048]{1,0:T(8,128)(2,1)S(1)} custom-call(bf16[16,128,128]{2,1,0:T(8,128)(2,1)S(1)} %shard_map.91.rotq, bf16[1664,128]{1,0:T(8,128)(2,1)S(1)} %shard_map.92.bias, bf16[512,128]{1,0:T(8,128)(2,1)S(1)} %copy-done, bf16[512,128]{1,0:T(8,128)(2,1)S(1)} %collective-permute-done.row1, bf16[512,128]{1,0:T(8,128)(2,1)S(1)} %collective-permute-done.1.row2, ...), custom_call_target="tpu_custom_call" | custom-call | flops 1000000 | bytes 1024 | tf_op jit(solution)/shard_map/pallas_call | solution.py:214
  70.0 4.0 %collective-permute-start.6 = (bf16[32,2048]{1,0:T(8,128)(2,1)S(1)}, bf16[32,2048]{1,0:T(8,128)(2,1)S(1)}, u32[]{:S(2)}, u32[]{:S(2)}) collective-permute-start(bf16[32,2048]{1,0:T(8,128)(2,1)S(1)} %shard_map.98), channel_id=1, source_target_pairs={{0,3},{1,2},{2,1},{3,0},{4,7},{5,6},{6,5},{7,4},{8,11},{9,10},{10,... | collective-permute-start | bytes 393224 | tf_op jit(solution)/shard_map/ppermute | solution.py:280
  74.0 1.8 %shard_map.96 = bf16[32,2048]{1,0:T(8,128)(2,1)S(1)} custom-call(bf16[16,128,128]{2,1,0:T(8,128)(2,1)S(1)} %shard_map.91.rotq, bf16[1664,128]{1,0:T(8,128)(2,1)S(1)} %shard_map.92.bias, bf16[512,128]{1,0:T(8,128)(2,1)S(1)} %copy-done, bf16[512,128]{1,0:T(8,128)(2,1)S(1)} %collective-permute-done.row1, bf16[512,128]{1,0:T(8,128)(2,1)S(1)} %collective-permute-done.1.row2, ...), custom_call_target="tpu_custom_call" | custom-call | flops 1000000 | bytes 1024 | tf_op jit(solution)/shard_map/pallas_call | solution.py:214
  75.8 3.3 %collective-permute-start.5 = (bf16[32,2048]{1,0:T(8,128)(2,1)S(1)}, bf16[32,2048]{1,0:T(8,128)(2,1)S(1)}, u32[]{:S(2)}, u32[]{:S(2)}) collective-permute-start(bf16[32,2048]{1,0:T(8,128)(2,1)S(1)} %shard_map.96), channel_id=1, source_target_pairs={{0,2},{1,3},{2,0},{3,1},{4,6},{5,7},{6,4},{7,5},{8,10},{9,11},{10,... | collective-permute-start | bytes 393224 | tf_op jit(solution)/shard_map/ppermute | solution.py:280
  79.2 0.0 collective-permute-done.6.rest_0_.d
  79.2 1.8 %shard_map.99 = bf16[32,2048]{1,0:T(8,128)(2,1)S(1)} custom-call(bf16[16,128,128]{2,1,0:T(8,128)(2,1)S(1)} %shard_map.91.rotq, bf16[1664,128]{1,0:T(8,128)(2,1)S(1)} %shard_map.92.bias, bf16[512,128]{1,0:T(8,128)(2,1)S(1)} %copy-done, bf16[512,128]{1,0:T(8,128)(2,1)S(1)} %collective-permute-done.row1, bf16[512,128]{1,0:T(8,128)(2,1)S(1)} %collective-permute-done.1.row2, ...), custom_call_target="tpu_custom_call" | custom-call | flops 1000000 | bytes 1024 | tf_op jit(solution)/shard_map/pallas_call | solution.py:214
  81.0 1.9 %collective-permute-start.7 = (bf16[32,2048]{1,0:T(8,128)(2,1)S(1)}, bf16[32,2048]{1,0:T(8,128)(2,1)S(1)}, u32[]{:S(2)}, u32[]{:S(2)}) collective-permute-start(bf16[32,2048]{1,0:T(8,128)(2,1)S(1)} %shard_map.99), channel_id=1, source_target_pairs={{0,1},{1,0},{2,3},{3,2},{4,5},{5,4},{6,7},{7,6},{8,9},{9,8},{10,11... | collective-permute-start | bytes 393224 | tf_op jit(solution)/shard_map/ppermute | solution.py:280
  82.9 0.0 collective-permute-done.5.rest_0_.c
  82.9 1.8 %shard_map.97.a = bf16[32,2048]{1,0:T(8,128)(2,1)S(1)} custom-call(bf16[16,128,128]{2,1,0:T(8,128)(2,1)S(1)} %shard_map.91.rotq, bf16[1664,128]{1,0:T(8,128)(2,1)S(1)} %shard_map.92.bias, bf16[512,128]{1,0:T(8,128)(2,1)S(1)} %copy-done, bf16[512,128]{1,0:T(8,128)(2,1)S(1)} %collective-permute-done.row1, bf16[512,128]{1,0:T(8,128)(2,1)S(1)} %collective-permute-done.1.row2, ...), custom_call_target="tpu_custom_call" | custom-call | flops 1000000 | bytes 1024 | tf_op jit(solution)/shard_map/pallas_call | solution.py:214
  84.7 0.0 collective-permute-done.7.b
  84.7 0.8 shard_map.100
Async XLA Ops:
  2.8 21.0 %copy-start = (bf16[512,128]{1,0:T(8,128)(2,1)S(1)}, bf16[512,128]{1,0:T(8,128)(2,1)}, u32[]{:S(2)}) copy-start(bf16[512,128]{1,0:T(8,128)(2,1)} %get-tuple-element.10.own) | copy-start | bytes 393220
  2.8 28.2 %copy-start.1 = (bf16[128,16,128]{2,1,0:T(8,128)(2,1)S(1)}, bf16[128,16,128]{2,1,0:T(8,128)(2,1)}, u32[]{:S(2)}) copy-start(bf16[128,16,128]{2,1,0:T(8,128)(2,1)} %q.1) | copy-start | bytes 1572868
  2.8 58.3 %all-to-all-start = ((bf16[128,16,128]{2,1,0:T(8,128)(2,1)}), bf16[128,16,128]{2,1,0:T(8,128)(2,1)S(1)}, u32[]{:S(2)}, u32[]{:S(2)}) async-start(bf16[128,16,128]{2,1,0:T(8,128)(2,1)} %get-tuple-element.14), calls=%async_computation | async-start | bytes 1048576 | tf_op jit(solution)/shard_map/all_to_all | solution.py:252
  23.7 6.5 %copy-start.3 = (s32[128]{0:T(128)S(1)}, s32[128]{0:T(128)}, u32[]{:S(2)}) copy-start(s32[128]{0:T(128)} %bs.5) | copy-start | bytes 1540
  23.8 7.2 %copy-start.2 = (f32[8,128]{1,0:T(8,128)S(1)}, f32[8,128]{1,0:T(8,128)}, u32[]{:S(2)}) copy-start(f32[8,128]{1,0:T(8,128)} %constant.2.clone.freqs) | copy-start | bytes 12292
  23.8 22.5 %collective-permute-start.1 = (bf16[512,128]{1,0:T(8,128)(2,1)S(1)}, bf16[512,128]{1,0:T(8,128)(2,1)S(1)}, u32[]{:S(2)}, u32[]{:S(2)}) collective-permute-start(bf16[512,128]{1,0:T(8,128)(2,1)S(1)} %copy-done), channel_id=1, source_target_pairs={{480,0},{484,4},{488,8},{492,12},{496,16},{500,20},{504,24},{508,2... | collective-permute-start | bytes 393224 | tf_op jit(solution)/shard_map/ppermute | solution.py:249
  27.2 23.1 %collective-permute-start = (bf16[512,128]{1,0:T(8,128)(2,1)S(1)}, bf16[512,128]{1,0:T(8,128)(2,1)S(1)}, u32[]{:S(2)}, u32[]{:S(2)}) collective-permute-start(bf16[512,128]{1,0:T(8,128)(2,1)S(1)} %copy-done), channel_id=1, source_target_pairs={{496,0},{500,4},{504,8},{508,12},{0,16},{4,20},{8,24},{12,28},{16,... | collective-permute-start | bytes 393224 | tf_op jit(solution)/shard_map/ppermute | solution.py:249
  50.4 12.1 %collective-permute-start.2 = (bf16[1024,128]{1,0:T(8,128)(2,1)S(1)}, bf16[1024,128]{1,0:T(8,128)(2,1)S(1)}, u32[]{:S(2)}, u32[]{:S(2)}) collective-permute-start(bf16[1024,128]{1,0:T(8,128)(2,1)S(1)} %get-tuple-element.11), channel_id=1, source_target_pairs={{0,4},{4,8},{8,12},{12,0},{16,20},{20,24},{24,28},{28,16},{32,36},... | collective-permute-start | bytes 786440 | tf_op jit(solution)/shard_map/ppermute | solution.py:264
  53.5 12.4 %collective-permute-start.3 = (bf16[1024,128]{1,0:T(8,128)(2,1)S(1)}, bf16[1024,128]{1,0:T(8,128)(2,1)S(1)}, u32[]{:S(2)}, u32[]{:S(2)}) collective-permute-start(bf16[1024,128]{1,0:T(8,128)(2,1)S(1)} %get-tuple-element.12), channel_id=1, source_target_pairs={{0,8},{4,12},{8,0},{12,4},{16,24},{20,28},{24,16},{28,20},{32,40},... | collective-permute-start | bytes 786440 | tf_op jit(solution)/shard_map/ppermute | solution.py:264
  58.0 10.2 %collective-permute-start.4 = (bf16[1024,128]{1,0:T(8,128)(2,1)S(1)}, bf16[1024,128]{1,0:T(8,128)(2,1)S(1)}, u32[]{:S(2)}, u32[]{:S(2)}) collective-permute-start(bf16[1024,128]{1,0:T(8,128)(2,1)S(1)} %get-tuple-element.13), channel_id=1, source_target_pairs={{0,12},{4,0},{8,4},{12,8},{16,28},{20,16},{24,20},{28,24},{32,44},... | collective-permute-start | bytes 786440 | tf_op jit(solution)/shard_map/ppermute | solution.py:264
  70.0 9.1 %collective-permute-start.6 = (bf16[32,2048]{1,0:T(8,128)(2,1)S(1)}, bf16[32,2048]{1,0:T(8,128)(2,1)S(1)}, u32[]{:S(2)}, u32[]{:S(2)}) collective-permute-start(bf16[32,2048]{1,0:T(8,128)(2,1)S(1)} %shard_map.98), channel_id=1, source_target_pairs={{0,3},{1,2},{2,1},{3,0},{4,7},{5,6},{6,5},{7,4},{8,11},{9,10},{10,... | collective-permute-start | bytes 393224 | tf_op jit(solution)/shard_map/ppermute | solution.py:280
  75.8 7.1 %collective-permute-start.5 = (bf16[32,2048]{1,0:T(8,128)(2,1)S(1)}, bf16[32,2048]{1,0:T(8,128)(2,1)S(1)}, u32[]{:S(2)}, u32[]{:S(2)}) collective-permute-start(bf16[32,2048]{1,0:T(8,128)(2,1)S(1)} %shard_map.96), channel_id=1, source_target_pairs={{0,2},{1,3},{2,0},{3,1},{4,6},{5,7},{6,4},{7,5},{8,10},{9,11},{10,... | collective-permute-start | bytes 393224 | tf_op jit(solution)/shard_map/ppermute | solution.py:280
  81.0 3.8 %collective-permute-start.7 = (bf16[32,2048]{1,0:T(8,128)(2,1)S(1)}, bf16[32,2048]{1,0:T(8,128)(2,1)S(1)}, u32[]{:S(2)}, u32[]{:S(2)}) collective-permute-start(bf16[32,2048]{1,0:T(8,128)(2,1)S(1)} %shard_map.99), channel_id=1, source_target_pairs={{0,1},{1,0},{2,3},{3,2},{4,5},{5,4},{6,7},{7,6},{8,9},{9,8},{10,11... | collective-permute-start | bytes 393224 | tf_op jit(solution)/shard_map/ppermute | solution.py:280

commit v5 on v4

--- a/solution.py
+++ b/solution.py
@@ -21,9 +21,12 @@
 GROUPS = 2
 KV = 4
 RING = 4
+NEAR = 8
+FAR = BLOCKS // NEAR
 ROWS = TOK // KV
 RAW = (WIN + 1) * TOK
 TOKP = 2 * GROUPS * TOK
+PIECE = SLOTS * NEAR
 KEYS = RAW + BLOCKS * SLOTS
 MSCALE = 1.0 + 0.1 * math.log(16.0)
 SCALE2 = math.log2(math.e) / math.sqrt(HD)
@@ -94,9 +97,13 @@
         rotq[h] = turn(scr[:, h, :], cosine, sine)
 
 
-def ring_kernel(own, row1, row2, rotq, bias, *outs):
+def ring_kernel(own, row1, row2, mem, r1, r2, r3, far, scr):
     me = lax.rem(lax.axis_index("ctx"), RING)
-    for s, out in enumerate(outs, 1):
+    scr[...] = mem[...].astype(F32)
+    kinds = 2 * GROUPS * SLOTS
+    slots = jnp.concatenate([scr[:, r, :] for r in range(kinds)], axis=0).astype(BF)
+    far[...] = jnp.broadcast_to(slots[None], far.shape)
+    for s, out in enumerate((r1, r2, r3), 1):
         out[TOKP:, :] = row1[...]
 
         @pl.when(me + s < RING)
@@ -106,13 +113,6 @@
         @pl.when(me + s >= RING)
         def _():
             out[:TOKP, :] = row2[...]
-
-
-def slot_kernel(mem, out, scr):
-    scr[...] = mem[...].astype(F32)
-    for kind in range(2 * GROUPS):
-        for j in range(SLOTS):
-            out[kind, j * BLOCKS : (j + 1) * BLOCKS, :] = scr[:, kind * SLOTS + j, :].astype(BF)
 
 
 def bias_kernel(bs, bias):
@@ -129,11 +129,12 @@
         there = bs[lax.rem(me - back + BLOCKS, BLOCKS)] + row
         ok = (there <= place) & (there > place - WINDOW)
         bias[b * TOK : (b + 1) * TOK, :] = jnp.where(ok, 0.0, NEG).astype(BF)
-    start = (bs[0] + TOK * row) & (SEQ - 1)
-    for j in range(SLOTS):
-        ok = start + (j + 1) * STRIDE <= place + 1
-        lo = RAW + j * BLOCKS
-        bias[lo : lo + BLOCKS, :] = jnp.where(ok, 0.0, NEG).astype(BF)
+    for lo in range(0, BLOCKS * SLOTS, TOK):
+        at = lo + row
+        block = at // PIECE * NEAR + (at & (NEAR - 1))
+        slot = (at & (PIECE - 1)) // NEAR
+        ok = ((bs[0] + TOK * block) & (SEQ - 1)) + (slot + 1) * STRIDE <= place + 1
+        bias[RAW + lo : RAW + lo + TOK, :] = jnp.where(ok, 0.0, NEG).astype(BF)
 
 
 def key_tiles():
@@ -151,7 +152,8 @@
     parts = []
     for name, lo, n in tile:
         if name == "mem":
-            parts.append(refs[name][kind, lo : lo + n, :])
+            rows = slice(kind * PIECE, (kind + 1) * PIECE)
+            parts += [refs[name][i, rows, :] for i in range(lo // PIECE, (lo + n) // PIECE)]
         else:
             at = lo + kind * TOK
             parts.append(refs[name][at : at + n, :])
@@ -227,6 +229,8 @@
     return jax.ShapeDtypeStruct(dims, dtype)
 
 
+near = [[NEAR * o + p for p in range(NEAR)] for o in range(FAR)]
+strided = [[NEAR * o + p for o in range(FAR)] for p in range(NEAR)]
 SM, VM, HB = pltpu.SMEM, pltpu.VMEM, pltpu.HBM
 
 
@@ -236,7 +240,7 @@
     params = (block_start, freqs, keys, values, depth_k, point_k, depth_v, point_v)
     own, mem = call(
         prep_kernel,
-        (shape(pack * TOK, HD), shape(BLOCKS, pack * SLOTS, HD)),
+        (shape(pack * TOK, HD), shape(NEAR, pack * SLOTS, HD)),
         [pltpu.VMEM((TOK, GROUPS, HD), F32), pltpu.VMEM((pack * SLOTS, HD), F32)]
         + [(pltpu.SMEM if i == 0 else pltpu.VMEM)(x.shape, x.dtype) for i, x in enumerate(params)]
         + [pltpu.SemaphoreType.DMA((len(params),))],
@@ -249,25 +253,24 @@
         lax.ppermute(own, "ctx", [((i - d) % BLOCKS, i) for i in range(BLOCKS)])
         for d in (RING, 2 * RING)
     )
-    mem = lax.all_to_all(mem, "ctx", 0, 0)
+    mem = lax.all_to_all(mem, "ctx", 0, 0, axis_index_groups=near)
     rotq = call(
         query_kernel, shape(HEADS, TOK, HD), [pltpu.VMEM((TOK, HEADS, HD), F32)], 10**3,
         (SM, VM, VM),
         block_start, freqs, queries,
     )
     bias = call(bias_kernel, shape(KEYS, TOK), [], 10**3, (SM,), block_start)
-    rings = call(
-        ring_kernel, (shape(2 * TOKP, HD),) * (RING - 1), [], 10**3, (VM,) * 3 + (pl.ANY,) * 2,
-        own, row1, row2, rotq, bias,
-    )
+    *rings, far = call(
+        ring_kernel,
+        (shape(2 * TOKP, HD),) * (RING - 1) + (shape(FAR, pack * PIECE, HD),),
+        [pltpu.VMEM((NEAR, pack * SLOTS, HD), F32)], 10**3, (VM,) * 4,
+        own, row1, row2, mem,
+    )
+    mem = lax.all_to_all(far, "ctx", 0, 0, axis_index_groups=strided)
     rings = [
         lax.ppermute(x, "ctx", [(i, i // RING * RING + (i + s) % RING) for i in range(BLOCKS)])
         for s, x in enumerate(rings, 1)
     ]
-    mem = call(
-        slot_kernel, shape(pack, BLOCKS * SLOTS, HD),
-        [pltpu.VMEM((BLOCKS, pack * SLOTS, HD), F32)], 10**6, (VM,), mem,
-    )
     parts = []
     for off in (3, 2, 1, 0):
         after = parts[-2:-1]

time: 86.3 us -> 74.1 us (0.86)
  waiting for transfers between devices: 23.5 us -> 7.17 us
  blocking collectives: 0 us -> 12.5 us
  starting transfers between devices: 47.3 us -> 38.8 us
  local copies, waits for them, and re-layouts: 0.02 us -> 0.93 us
    ppermute x2, waiting for transfers between devices: 17.7 us -> 0.46 us  [shards(): lax.ppermute(own, 'ctx', [((i - d) % BLOCKS, i) for i in range(BLOCKS)])]
    all_to_all x0 -> x1, blocking collectives: none -> 12.5 us  [shards(): mem = lax.all_to_all(mem, 'ctx', 0, 0, axis_index_groups=near)]
    all_to_all x1, starting transfers between devices: 21 us -> 9.04 us  [shards(): mem = lax.all_to_all(far, 'ctx', 0, 0, axis_index_groups=strided)]
    ppermute x2, starting transfers between devices: 6.48 us -> 10.6 us  [shards(): lax.ppermute(own, 'ctx', [((i - d) % BLOCKS, i) for i in range(BLOCKS)])]
    all_to_all x1, waiting for transfers between devices: 0.01 us -> 1.6 us  [shards(): mem = lax.all_to_all(far, 'ctx', 0, 0, axis_index_groups=strided)]
    ppermute x3, starting transfers between devices: 10.6 us -> 9.06 us  [shards(): lax.ppermute(x, 'ctx', [(i, i // RING * RING + (i + s) % RING) for i in r...]
    unnamed x8 -> x10, local copies, waits for them, and re-layouts: 0.02 us -> 0.93 us
    pallas_call x10 -> x9, Pallas kernels: 14.6 us -> 14.1 us  [call(): pl.pallas_call(kernel, out_shape=out_shape, in_specs=[pl.BlockSpec(memory...]
where the time goes in v5:
time: 74.1 us; the launch traced here: 73.6 us
  starting transfers between devices  38.8 us (52%)
  Pallas kernels  14.1 us (19%)
  blocking collectives  12.5 us (17%)
  waiting for transfers between devices  7.17 us (10%)
  local copies, waits for them, and re-layouts  0.93 us (1%)
    pallas_call x9, Pallas kernels, call(): pl.pallas_call(kernel, out_shape=out_shape, in_specs=[pl.BlockSpec(memory...  14.1 us
    all_to_all x1, blocking collectives, shards(): mem = lax.all_to_all(mem, 'ctx', 0, 0, axis_index_groups=near)  12.5 us
    ppermute x2, starting transfers between devices, shards(): lax.ppermute(own, 'ctx', [((i - d) % BLOCKS, i) for i in range(BLOCKS)])  10.6 us
    ppermute x3, starting transfers between devices, shards(): part = lax.ppermute(part, 'kv', [(i, i ^ off) for i in range(KV)])  10 us
    ppermute x3, starting transfers between devices, shards(): lax.ppermute(x, 'ctx', [(i, i // RING * RING + (i + s) % RING) for i in r...  9.06 us
    all_to_all x1, starting transfers between devices, shards(): mem = lax.all_to_all(far, 'ctx', 0, 0, axis_index_groups=strided)  9.04 us
    ppermute x3, waiting for transfers between devices, shards(): lax.ppermute(x, 'ctx', [(i, i // RING * RING + (i + s) % RING) for i in r...  5.1 us
    all_to_all x1, waiting for transfers between devices, shards(): mem = lax.all_to_all(far, 'ctx', 0, 0, axis_index_groups=strided)  1.6 us
  transfers between devices with their start and end apart: 9, of which 4 were waited for; matrix products, arithmetic and copies ran while one was open for 0% of the time, Pallas kernels for 11%

profile of v5, /device:TPU:1, one launch (start us, length us, event | category | flops | bytes accessed | tf_op | source)
XLA Modules:
  0.0 73.6 jit_solution(5989604850553218607)
XLA Ops:
  0.0 2.5 %shard_map.93 = (bf16[512,128]{1,0:T(8,128)(2,1)}, bf16[8,16,128]{2,1,0:T(8,128)(2,1)}) custom-call(s32[128]{0:T(128)} %bs.5, f32[8,128]{1,0:T(8,128)} %constant.2.clone.freqs, bf16[128,2,128]{2,1,0:T(2,128)(2,1)} %k.1, bf16[128,2,128]{2,1,0:T(2,128)(2,1)} %v.1, f32[32,128]{1,0:T(8,128)} %dk.1, f32[128,128]{1,0:T(8,128)} %pk.1, f32[32,128]{1,0:T(8,128)} %dv.1, ...), custom_call_target="tpu_custom_call" | custom-call | flops 1000000000 | bytes 1024 | tf_op jit(solution)/shard_map/pallas_call | solution.py:216
  2.5 4.8 %collective-permute-start = (bf16[512,128]{1,0:T(8,128)(2,1)}, bf16[512,128]{1,0:T(8,128)(2,1)S(1)}, u32[]{:S(2)}, u32[]{:S(2)}) collective-permute-start(bf16[512,128]{1,0:T(8,128)(2,1)} %get-tuple-element.11.own), channel_id=1, source_target_pairs={{496,0},{500,4},{504,8},{508,12},{0,16},{4,20},{8,24},{12,28},{16,... | collective-permute-start | bytes 393224 | tf_op jit(solution)/shard_map/ppermute | solution.py:253
  7.4 5.8 %collective-permute-start.1 = (bf16[512,128]{1,0:T(8,128)(2,1)}, bf16[512,128]{1,0:T(8,128)(2,1)S(1)}, u32[]{:S(2)}, u32[]{:S(2)}) collective-permute-start(bf16[512,128]{1,0:T(8,128)(2,1)} %get-tuple-element.11.own), channel_id=1, source_target_pairs={{480,0},{484,4},{488,8},{492,12},{496,16},{500,20},{504,24},{508,2... | collective-permute-start | bytes 393224 | tf_op jit(solution)/shard_map/ppermute | solution.py:253
  13.2 12.5 %all_to_all.10.mem = bf16[8,16,128]{2,1,0:T(8,128)(2,1)S(1)} all-to-all(bf16[8,16,128]{2,1,0:T(8,128)(2,1)} %get-tuple-element.12), channel_id=1, replica_groups={{0,4,8,12,16,20,24,28},{32,36,40,44,48,52,56,60},{64,68,72,76,80,84,88,..., dimensions={0} | all-to-all | bytes 65536 | tf_op jit(solution)/shard_map/all_to_all | solution.py:256
  25.6 0.0 collective-permute-done.row1
  25.7 0.5 collective-permute-done.1.row2
  26.1 0.0 copy-start
  26.1 0.9 %copy-done = bf16[512,128]{1,0:T(8,128)(2,1)S(1)} copy-done((bf16[512,128]{1,0:T(8,128)(2,1)S(1)}, bf16[512,128]{1,0:T(8,128)(2,1)}, u32[]{:S(2)}) %copy-start) | copy-done | bytes 131096
  27.0 1.1 %shard_map.94 = (bf16[1024,128]{1,0:T(8,128)(2,1)}, bf16[1024,128]{1,0:T(8,128)(2,1)}, bf16[1024,128]{1,0:T(8,128)(2,1)S(1)}, bf16[16,128,128]{2,1,0:T(8,128)(2,1)}) custom-call(bf16[512,128]{1,0:T(8,128)(2,1)S(1)} %copy-done, bf16[512,128]{1,0:T(8,128)(2,1)S(1)} %collective-permute-done.row1, bf16[512,128]{1,0:T(8,128)(2,1)S(1)} %collective-permute-done.1.row2, ...), custom_call_target="tpu_custom_call" | custom-call | flops 1000 | bytes 1024 | tf_op jit(solution)/shard_map/pallas_call | solution.py:216
  28.1 0.0 copy-start.2
  28.1 9.0 %all-to-all-start.1 = ((bf16[16,128,128]{2,1,0:T(8,128)(2,1)}), bf16[16,128,128]{2,1,0:T(8,128)(2,1)S(1)}, u32[]{:S(2)}, u32[]{:S(2)}) async-start(bf16[16,128,128]{2,1,0:T(8,128)(2,1)} %get-tuple-element.16), calls=%async_computation.1 | async-start | bytes 1048576 | tf_op jit(solution)/shard_map/all_to_all | solution.py:269
  37.2 2.5 %collective-permute-start.2 = (bf16[1024,128]{1,0:T(8,128)(2,1)}, bf16[1024,128]{1,0:T(8,128)(2,1)S(1)}, u32[]{:S(2)}, u32[]{:S(2)}) collective-permute-start(bf16[1024,128]{1,0:T(8,128)(2,1)} %get-tuple-element.13), channel_id=1, source_target_pairs={{0,4},{4,8},{8,12},{12,0},{16,20},{20,24},{24,28},{28,16},{32,36},... | collective-permute-start | bytes 786440 | tf_op jit(solution)/shard_map/ppermute | solution.py:271
  39.7 0.0 copy-start.4
  39.7 3.5 %collective-permute-start.3 = (bf16[1024,128]{1,0:T(8,128)(2,1)}, bf16[1024,128]{1,0:T(8,128)(2,1)S(1)}, u32[]{:S(2)}, u32[]{:S(2)}) collective-permute-start(bf16[1024,128]{1,0:T(8,128)(2,1)} %get-tuple-element.14), channel_id=1, source_target_pairs={{0,8},{4,12},{8,0},{12,4},{16,24},{20,28},{24,16},{28,20},{32,40},... | collective-permute-start | bytes 786440 | tf_op jit(solution)/shard_map/ppermute | solution.py:271
  43.2 0.0 copy-start.3
  43.2 3.1 %collective-permute-start.4 = (bf16[1024,128]{1,0:T(8,128)(2,1)S(1)}, bf16[1024,128]{1,0:T(8,128)(2,1)S(1)}, u32[]{:S(2)}, u32[]{:S(2)}) collective-permute-start(bf16[1024,128]{1,0:T(8,128)(2,1)S(1)} %get-tuple-element.15), channel_id=1, source_target_pairs={{0,12},{4,0},{8,4},{12,8},{16,28},{20,16},{24,20},{28,24},{32,44},... | collective-permute-start | bytes 786440 | tf_op jit(solution)/shard_map/ppermute | solution.py:271
  46.3 0.0 copy-done.4
  46.3 0.8 %shard_map.92.bias = bf16[1664,128]{1,0:T(8,128)(2,1)S(1)} custom-call(s32[128]{0:T(128)S(1)} %copy-done.4), custom_call_target="tpu_custom_call" | custom-call | flops 1000 | bytes 1024 | tf_op jit(solution)/shard_map/pallas_call | solution.py:216
  47.1 0.0 copy-done.2
  47.1 0.0 copy-done.3
  47.1 0.0 copy-start.1
  47.1 1.6 %shard_map.91.rotq = bf16[16,128,128]{2,1,0:T(8,128)(2,1)S(1)} custom-call(s32[128]{0:T(128)S(1)} %copy-done.4, f32[8,128]{1,0:T(8,128)S(1)} %copy-done.3, bf16[128,16,128]{2,1,0:T(8,128)(2,1)S(1)} %copy-done.2), custom_call_target="tpu_custom_call" | custom-call | flops 1000 | bytes 1024 | tf_op jit(solution)/shard_map/pallas_call | solution.py:216
  48.7 0.0 collective-permute-done.2.r1
  48.7 2.9 %collective-permute-done.3.r2 = bf16[1024,128]{1,0:T(8,128)(2,1)S(1)} collective-permute-done((bf16[1024,128]{1,0:T(8,128)(2,1)}, bf16[1024,128]{1,0:T(8,128)(2,1)S(1)}, u32[]{:S(2)}, u32[]{:S(2)}) %collective-permute-start.3) | collective-permute-done | bytes 262176 | tf_op jit(solution)/shard_map/ppermute | solution.py:271
  51.6 2.2 %collective-permute-done.4.r3 = bf16[1024,128]{1,0:T(8,128)(2,1)S(1)} collective-permute-done((bf16[1024,128]{1,0:T(8,128)(2,1)S(1)}, bf16[1024,128]{1,0:T(8,128)(2,1)S(1)}, u32[]{:S(2)}, u32[]{:S(2)}) %collective-permute-start.4) | collective-permute-done | bytes 262176 | tf_op jit(solution)/shard_map/ppermute | solution.py:271
  53.8 1.6 %all-to-all-done.1.mem = bf16[16,128,128]{2,1,0:T(8,128)(2,1)S(1)} async-done(((bf16[16,128,128]{2,1,0:T(8,128)(2,1)}), bf16[16,128,128]{2,1,0:T(8,128)(2,1)S(1)}, u32[]{:S(2)}, u32[]{:S(2)}) %all-to-all-start.1) | async-done | bytes 524320 | tf_op jit(solution)/shard_map/all_to_all | solution.py:269
  55.4 0.0 copy-done.1
  55.4 1.8 %shard_map.97 = bf16[32,2048]{1,0:T(8,128)(2,1)S(1)} custom-call(bf16[16,128,128]{2,1,0:T(8,128)(2,1)S(1)} %shard_map.91.rotq, bf16[1664,128]{1,0:T(8,128)(2,1)S(1)} %shard_map.92.bias, bf16[512,128]{1,0:T(8,128)(2,1)S(1)} %copy-done.1, bf16[512,128]{1,0:T(8,128)(2,1)S(1)} %collective-permute-done.row1, bf16[512,128]{1,0:T(8,128)(2,1)S(1)} %collective-permute-done.1.row2, ...), custom_call_target="tpu_custom_call" | custom-call | flops 1000000 | bytes 1024 | tf_op jit(solution)/shard_map/pallas_call | solution.py:216
  57.2 4.4 %collective-permute-start.6 = (bf16[32,2048]{1,0:T(8,128)(2,1)S(1)}, bf16[32,2048]{1,0:T(8,128)(2,1)S(1)}, u32[]{:S(2)}, u32[]{:S(2)}) collective-permute-start(bf16[32,2048]{1,0:T(8,128)(2,1)S(1)} %shard_map.97), channel_id=1, source_target_pairs={{0,3},{1,2},{2,1},{3,0},{4,7},{5,6},{6,5},{7,4},{8,11},{9,10},{10,... | collective-permute-start | bytes 393224 | tf_op jit(solution)/shard_map/ppermute | solution.py:283
  61.6 1.8 %shard_map.95 = bf16[32,2048]{1,0:T(8,128)(2,1)S(1)} custom-call(bf16[16,128,128]{2,1,0:T(8,128)(2,1)S(1)} %shard_map.91.rotq, bf16[1664,128]{1,0:T(8,128)(2,1)S(1)} %shard_map.92.bias, bf16[512,128]{1,0:T(8,128)(2,1)S(1)} %copy-done.1, bf16[512,128]{1,0:T(8,128)(2,1)S(1)} %collective-permute-done.row1, bf16[512,128]{1,0:T(8,128)(2,1)S(1)} %collective-permute-done.1.row2, ...), custom_call_target="tpu_custom_call" | custom-call | flops 1000000 | bytes 1024 | tf_op jit(solution)/shard_map/pallas_call | solution.py:216
  63.5 3.7 %collective-permute-start.5 = (bf16[32,2048]{1,0:T(8,128)(2,1)S(1)}, bf16[32,2048]{1,0:T(8,128)(2,1)S(1)}, u32[]{:S(2)}, u32[]{:S(2)}) collective-permute-start(bf16[32,2048]{1,0:T(8,128)(2,1)S(1)} %shard_map.95), channel_id=1, source_target_pairs={{0,2},{1,3},{2,0},{3,1},{4,6},{5,7},{6,4},{7,5},{8,10},{9,11},{10,... | collective-permute-start | bytes 393224 | tf_op jit(solution)/shard_map/ppermute | solution.py:283
  67.2 0.0 collective-permute-done.6.rest_0_.d
  67.2 1.8 %shard_map.98 = bf16[32,2048]{1,0:T(8,128)(2,1)S(1)} custom-call(bf16[16,128,128]{2,1,0:T(8,128)(2,1)S(1)} %shard_map.91.rotq, bf16[1664,128]{1,0:T(8,128)(2,1)S(1)} %shard_map.92.bias, bf16[512,128]{1,0:T(8,128)(2,1)S(1)} %copy-done.1, bf16[512,128]{1,0:T(8,128)(2,1)S(1)} %collective-permute-done.row1, bf16[512,128]{1,0:T(8,128)(2,1)S(1)} %collective-permute-done.1.row2, ...), custom_call_target="tpu_custom_call" | custom-call | flops 1000000 | bytes 1024 | tf_op jit(solution)/shard_map/pallas_call | solution.py:216
  69.0 1.9 %collective-permute-start.7 = (bf16[32,2048]{1,0:T(8,128)(2,1)S(1)}, bf16[32,2048]{1,0:T(8,128)(2,1)S(1)}, u32[]{:S(2)}, u32[]{:S(2)}) collective-permute-start(bf16[32,2048]{1,0:T(8,128)(2,1)S(1)} %shard_map.98), channel_id=1, source_target_pairs={{0,1},{1,0},{2,3},{3,2},{4,5},{5,4},{6,7},{7,6},{8,9},{9,8},{10,11... | collective-permute-start | bytes 393224 | tf_op jit(solution)/shard_map/ppermute | solution.py:283
  70.9 0.0 collective-permute-done.5.rest_0_.c
  70.9 1.8 %shard_map.96.a = bf16[32,2048]{1,0:T(8,128)(2,1)S(1)} custom-call(bf16[16,128,128]{2,1,0:T(8,128)(2,1)S(1)} %shard_map.91.rotq, bf16[1664,128]{1,0:T(8,128)(2,1)S(1)} %shard_map.92.bias, bf16[512,128]{1,0:T(8,128)(2,1)S(1)} %copy-done.1, bf16[512,128]{1,0:T(8,128)(2,1)S(1)} %collective-permute-done.row1, bf16[512,128]{1,0:T(8,128)(2,1)S(1)} %collective-permute-done.1.row2, ...), custom_call_target="tpu_custom_call" | custom-call | flops 1000000 | bytes 1024 | tf_op jit(solution)/shard_map/pallas_call | solution.py:216
  72.7 0.0 collective-permute-done.7.b
  72.7 0.8 %shard_map.99 = bf16[32,8192]{1,0:T(8,128)(2,1)} custom-call(bf16[32,2048]{1,0:T(8,128)(2,1)S(1)} %shard_map.96.a, bf16[32,2048]{1,0:T(8,128)(2,1)S(1)} %collective-permute-done.7.b, bf16[32,2048]{1,0:T(8,128)(2,1)S(1)} %collective-permute-done.5.rest_0_.c, bf16[32,2048]{1,0:T(8,128)(2,1)S(1)} %collective-permute-done.6.rest_0_.d), custom_call_target="tpu_custom_call" | custom-call | flops 100000000 | bytes 1024 | tf_op jit(solution)/shard_map/pallas_call | solution.py:216
Async XLA Ops:
  2.5 23.1 %collective-permute-start = (bf16[512,128]{1,0:T(8,128)(2,1)}, bf16[512,128]{1,0:T(8,128)(2,1)S(1)}, u32[]{:S(2)}, u32[]{:S(2)}) collective-permute-start(bf16[512,128]{1,0:T(8,128)(2,1)} %get-tuple-element.11.own), channel_id=1, source_target_pairs={{496,0},{500,4},{504,8},{508,12},{0,16},{4,20},{8,24},{12,28},{16,... | collective-permute-start | bytes 393224 | tf_op jit(solution)/shard_map/ppermute | solution.py:253
  7.4 18.7 %collective-permute-start.1 = (bf16[512,128]{1,0:T(8,128)(2,1)}, bf16[512,128]{1,0:T(8,128)(2,1)S(1)}, u32[]{:S(2)}, u32[]{:S(2)}) collective-permute-start(bf16[512,128]{1,0:T(8,128)(2,1)} %get-tuple-element.11.own), channel_id=1, source_target_pairs={{480,0},{484,4},{488,8},{492,12},{496,16},{500,20},{504,24},{508,2... | collective-permute-start | bytes 393224 | tf_op jit(solution)/shard_map/ppermute | solution.py:253
  26.1 0.9 %copy-start = (bf16[512,128]{1,0:T(8,128)(2,1)S(1)}, bf16[512,128]{1,0:T(8,128)(2,1)}, u32[]{:S(2)}) copy-start(bf16[512,128]{1,0:T(8,128)(2,1)} %get-tuple-element.11.own) | copy-start | bytes 393220
  28.1 19.0 %copy-start.2 = (bf16[128,16,128]{2,1,0:T(8,128)(2,1)S(1)}, bf16[128,16,128]{2,1,0:T(8,128)(2,1)}, u32[]{:S(2)}) copy-start(bf16[128,16,128]{2,1,0:T(8,128)(2,1)} %q.1) | copy-start | bytes 1572868
  28.1 27.3 %all-to-all-start.1 = ((bf16[16,128,128]{2,1,0:T(8,128)(2,1)}), bf16[16,128,128]{2,1,0:T(8,128)(2,1)S(1)}, u32[]{:S(2)}, u32[]{:S(2)}) async-start(bf16[16,128,128]{2,1,0:T(8,128)(2,1)} %get-tuple-element.16), calls=%async_computation.1 | async-start | bytes 1048576 | tf_op jit(solution)/shard_map/all_to_all | solution.py:269
  37.2 11.6 %collective-permute-start.2 = (bf16[1024,128]{1,0:T(8,128)(2,1)}, bf16[1024,128]{1,0:T(8,128)(2,1)S(1)}, u32[]{:S(2)}, u32[]{:S(2)}) collective-permute-start(bf16[1024,128]{1,0:T(8,128)(2,1)} %get-tuple-element.13), channel_id=1, source_target_pairs={{0,4},{4,8},{8,12},{12,0},{16,20},{20,24},{24,28},{28,16},{32,36},... | collective-permute-start | bytes 786440 | tf_op jit(solution)/shard_map/ppermute | solution.py:271
  39.7 6.6 %copy-start.4 = (s32[128]{0:T(128)S(1)}, s32[128]{0:T(128)}, u32[]{:S(2)}) copy-start(s32[128]{0:T(128)} %bs.5) | copy-start | bytes 1540
  39.7 11.9 %collective-permute-start.3 = (bf16[1024,128]{1,0:T(8,128)(2,1)}, bf16[1024,128]{1,0:T(8,128)(2,1)S(1)}, u32[]{:S(2)}, u32[]{:S(2)}) collective-permute-start(bf16[1024,128]{1,0:T(8,128)(2,1)} %get-tuple-element.14), channel_id=1, source_target_pairs={{0,8},{4,12},{8,0},{12,4},{16,24},{20,28},{24,16},{28,20},{32,40},... | collective-permute-start | bytes 786440 | tf_op jit(solution)/shard_map/ppermute | solution.py:271
  43.2 3.9 %copy-start.3 = (f32[8,128]{1,0:T(8,128)S(1)}, f32[8,128]{1,0:T(8,128)}, u32[]{:S(2)}) copy-start(f32[8,128]{1,0:T(8,128)} %constant.2.clone.freqs) | copy-start | bytes 12292
  43.2 10.6 %collective-permute-start.4 = (bf16[1024,128]{1,0:T(8,128)(2,1)S(1)}, bf16[1024,128]{1,0:T(8,128)(2,1)S(1)}, u32[]{:S(2)}, u32[]{:S(2)}) collective-permute-start(bf16[1024,128]{1,0:T(8,128)(2,1)S(1)} %get-tuple-element.15), channel_id=1, source_target_pairs={{0,12},{4,0},{8,4},{12,8},{16,28},{20,16},{24,20},{28,24},{32,44},... | collective-permute-start | bytes 786440 | tf_op jit(solution)/shard_map/ppermute | solution.py:271
  47.1 8.3 %copy-start.1 = (bf16[512,128]{1,0:T(8,128)(2,1)S(1)}, bf16[512,128]{1,0:T(8,128)(2,1)}, u32[]{:S(2)}) copy-start(bf16[512,128]{1,0:T(8,128)(2,1)} %get-tuple-element.11.own) | copy-start | bytes 393220
  57.2 9.9 %collective-permute-start.6 = (bf16[32,2048]{1,0:T(8,128)(2,1)S(1)}, bf16[32,2048]{1,0:T(8,128)(2,1)S(1)}, u32[]{:S(2)}, u32[]{:S(2)}) collective-permute-start(bf16[32,2048]{1,0:T(8,128)(2,1)S(1)} %shard_map.97), channel_id=1, source_target_pairs={{0,3},{1,2},{2,1},{3,0},{4,7},{5,6},{6,5},{7,4},{8,11},{9,10},{10,... | collective-permute-start | bytes 393224 | tf_op jit(solution)/shard_map/ppermute | solution.py:283
  63.5 7.4 %collective-permute-start.5 = (bf16[32,2048]{1,0:T(8,128)(2,1)S(1)}, bf16[32,2048]{1,0:T(8,128)(2,1)S(1)}, u32[]{:S(2)}, u32[]{:S(2)}) collective-permute-start(bf16[32,2048]{1,0:T(8,128)(2,1)S(1)} %shard_map.95), channel_id=1, source_target_pairs={{0,2},{1,3},{2,0},{3,1},{4,6},{5,7},{6,4},{7,5},{8,10},{9,11},{10,... | collective-permute-start | bytes 393224 | tf_op jit(solution)/shard_map/ppermute | solution.py:283
  69.0 3.8 %collective-permute-start.7 = (bf16[32,2048]{1,0:T(8,128)(2,1)S(1)}, bf16[32,2048]{1,0:T(8,128)(2,1)S(1)}, u32[]{:S(2)}, u32[]{:S(2)}) collective-permute-start(bf16[32,2048]{1,0:T(8,128)(2,1)S(1)} %shard_map.98), channel_id=1, source_target_pairs={{0,1},{1,0},{2,3},{3,2},{4,5},{5,4},{6,7},{7,6},{8,9},{9,8},{10,11... | collective-permute-start | bytes 393224 | tf_op jit(solution)/shard_map/ppermute | solution.py:283

commit v6 on v5

--- a/solution.py
+++ b/solution.py
@@ -21,6 +21,7 @@
 GROUPS = 2
 KV = 4
 RING = 4
+BATCH = 4
 NEAR = 8
 FAR = BLOCKS // NEAR
 ROWS = TOK // KV
@@ -137,61 +138,97 @@
         bias[RAW + lo : RAW + lo + TOK, :] = jnp.where(ok, 0.0, NEG).astype(BF)
 
 
-def key_tiles():
-    half = SLOTS * BLOCKS // 2
-    tiles = [(0, [("own", 0, TOK), ("row1", 0, TOK)])]
-    for s in range(1, RING):
-        tiles.append((2 * s * TOK, [(s, 0, TOK), (s, TOKP, TOK)]))
-    tiles.append((RAW, [("mem", 0, half)]))
-    tiles.append((RAW + half, [("mem", half, half)]))
-    tiles.append((RAW - TOK, [("row2", 0, TOK)]))
-    return [(lo, sum(n for _, _, n in tile), tile) for lo, tile in tiles]
-
-
-def gather_tile(refs, tile, kind):
-    parts = []
-    for name, lo, n in tile:
-        if name == "mem":
-            rows = slice(kind * PIECE, (kind + 1) * PIECE)
-            parts += [refs[name][i, rows, :] for i in range(lo // PIECE, (lo + n) // PIECE)]
-        else:
-            at = lo + kind * TOK
-            parts.append(refs[name][at : at + n, :])
-    return parts[0] if len(parts) == 1 else jnp.concatenate(parts, axis=0)
-
-
-def chunk_kernel(off, rotq, bias, own, row1, row2, r1, r2, r3, mem, *rest):
-    refs = {"own": own, "row1": row1, "row2": row2, 1: r1, 2: r2, 3: r3, "mem": mem}
-    out, s = rest[-2:]
+def score(qa, k, bias):
+    ka = jnp.concatenate([k, bias], axis=1)
+    return lax.dot_general(qa, ka, (((1,), (1,)), ((), ())), preferred_element_type=F32)
+
+
+def tile_max(high, x):
+    for i in range(x.shape[1] // HD):
+        part = x[:, i * HD : (i + 1) * HD]
+        high = part if high is None else jnp.maximum(high, part)
+    return high
+
+
+def weigh(x, top, v):
+    w = jnp.exp2((x - top) * SCALE2).astype(BF)
+    va = jnp.concatenate([v, jnp.ones(v.shape, BF)], axis=1)
+    return jnp.dot(w, va, preferred_element_type=F32)
+
+
+def window_kernel(rotq, bias, own, row1, row2, r1, r2, r3, acc, high, s):
+    tiles = [(0, ((own, 0), (row1, 0)))]
+    for i, r in enumerate((r1, r2, r3), 1):
+        tiles.append((2 * i * TOK, ((r, 0), (r, TOKP))))
+    tiles.append((RAW - TOK, ((row2, 0),)))
+
+    def rows_of(parts, kind):
+        got = [r[lo + kind * TOK : lo + (kind + 1) * TOK, :] for r, lo in parts]
+        return jnp.concatenate(got, axis=0) if len(got) > 1 else got[0]
+
+    r = lax.broadcasted_iota(jnp.int32, (BATCH * TOK, TOK), 0) & (TOK - 1)
+    c = lax.broadcasted_iota(jnp.int32, (BATCH * TOK, TOK), 1)
+    unit = jnp.where(r == c, 1.0, 0.0).astype(BF)
+    for first in range(0, HEADS, BATCH):
+        g = first // (HEADS // GROUPS)
+        slot = first // BATCH % 2
+        q = rotq[first : first + BATCH].reshape(BATCH * TOK, HD)
+        qa = jnp.concatenate([q, unit], axis=1)
+        top = None
+        for lo, parts in tiles:
+            size = len(parts) * TOK
+            x = score(qa, rows_of(parts, g), bias[lo : lo + size, :])
+            s[slot, :, lo : lo + size] = x
+            top = tile_max(top, x)
+        top = jnp.max(top, axis=1, keepdims=True)
+        mixed = None
+        for lo, parts in tiles:
+            size = len(parts) * TOK
+            part = weigh(s[slot, :, lo : lo + size], top, rows_of(parts, GROUPS + g))
+            mixed = part if mixed is None else mixed + part
+        acc[first : first + BATCH] = mixed.reshape(BATCH, TOK, 2 * HD)
+        high[first : first + BATCH] = jnp.broadcast_to(top, (BATCH * TOK, HD)).reshape(
+            BATCH, TOK, HD
+        )
+
+
+def chunk_kernel(off, rotq, bias, mem, acc, high, *rest):
+    out = rest[-1]
     dest = lax.axis_index("kv") ^ off
     first = pl.multiple_of(dest * ROWS, ROWS)
     heads = HEADS // GROUPS
     r = lax.broadcasted_iota(jnp.int32, (heads * ROWS, TOK), 0) & (ROWS - 1)
     c = lax.broadcasted_iota(jnp.int32, (heads * ROWS, TOK), 1)
     unit = jnp.where(r + first == c, 1.0, 0.0).astype(BF)
+    half = BLOCKS * SLOTS // 2
+
+    def rows_of(lo, kind):
+        span = slice(kind * PIECE, (kind + 1) * PIECE)
+        return jnp.concatenate(
+            [mem[i, span, :] for i in range(lo // PIECE, (lo + half) // PIECE)], axis=0
+        )
+
+    def heads_of(ref, g):
+        return jnp.concatenate(
+            [ref[g * heads + i, pl.ds(first, ROWS), :] for i in range(heads)], axis=0
+        )
+
     for g in range(GROUPS):
-        q = jnp.concatenate(
-            [rotq[g * heads + i, pl.ds(first, ROWS), :] for i in range(heads)], axis=0
-        )
-        qa = jnp.concatenate([q, unit], axis=1)
-        high = None
-        for lo, size, tile in key_tiles():
-            k = gather_tile(refs, tile, g)
-            ka = jnp.concatenate([k, bias[lo : lo + size, :]], axis=1)
-            x = lax.dot_general(qa, ka, (((1,), (1,)), ((), ())), preferred_element_type=F32)
-            s[g, :, lo : lo + size] = x
-            for i in range(size // HD):
-                part = x[:, i * HD : (i + 1) * HD]
-                high = part if high is None else jnp.maximum(high, part)
-        top = jnp.max(high, axis=1, keepdims=True)
-        mixed = None
-        for lo, size, tile in key_tiles():
-            w = jnp.exp2((s[g, :, lo : lo + size] - top) * SCALE2).astype(BF)
-            v = gather_tile(refs, tile, GROUPS + g)
-            va = jnp.concatenate([v, jnp.ones((size, HD), BF)], axis=1)
-            part = jnp.dot(w, va, preferred_element_type=F32)
-            mixed = part if mixed is None else mixed + part
-        res = (mixed[:, :HD] / mixed[:, HD:]).astype(BF)
+        qa = jnp.concatenate([heads_of(rotq, g), unit], axis=1)
+        xs = [
+            score(qa, rows_of(lo, g), bias[RAW + lo : RAW + lo + half, :]) for lo in (0, half)
+        ]
+        top = tile_max(tile_max(None, xs[0]), xs[1])
+        before = heads_of(high, g)
+        top = jnp.maximum(jnp.max(top, axis=1, keepdims=True), before)
+        keep = jnp.exp2((before - top) * SCALE2)
+        old = heads_of(acc, g)
+        mixed, total = old[:, :HD] * keep, old[:, HD:] * keep
+        wide = jnp.concatenate([top] * (half // HD), axis=1)
+        new = weigh(xs[0], wide, rows_of(0, GROUPS + g)) + weigh(
+            xs[1], wide, rows_of(half, GROUPS + g)
+        )
+        res = ((mixed + new[:, :HD]) / (total + new[:, HD:])).astype(BF)
         for i in range(heads):
             h = g * heads + i
             out[:, h * HD : (h + 1) * HD] = res[i * ROWS : (i + 1) * ROWS, :]
@@ -271,13 +308,18 @@
         lax.ppermute(x, "ctx", [(i, i // RING * RING + (i + s) % RING) for i in range(BLOCKS)])
         for s, x in enumerate(rings, 1)
     ]
+    acc, high = call(
+        window_kernel,
+        (shape(HEADS, TOK, 2 * HD, dtype=F32), shape(HEADS, TOK, HD, dtype=F32)),
+        [pltpu.VMEM((2, BATCH * TOK, RAW), F32)], 10**10, (VM,) * 8,
+        rotq, bias, own, row1, row2, *rings, grant=16,
+    )
     parts = []
     for off in (3, 2, 1, 0):
         after = parts[-2:-1]
         part = call(
-            functools.partial(chunk_kernel, off), shape(ROWS, HEADS * HD),
-            [pltpu.VMEM((GROUPS, HEADS // GROUPS * ROWS, KEYS), F32)], 10**6,
-            (VM,) * 9 + (pl.ANY,) * len(after), rotq, bias, own, row1, row2, *rings, mem, *after,
+            functools.partial(chunk_kernel, off), shape(ROWS, HEADS * HD), [], 10**6,
+            (VM,) * 5 + (pl.ANY,) * len(after), rotq, bias, mem, acc, high, *after, grant=16,
         )
         if off:
             part = lax.ppermute(part, "kv", [(i, i ^ off) for i in range(KV)])

time: 74.1 us -> 85.8 us (1.16)
  local copies, waits for them, and re-layouts: 0.93 us -> 8.7 us
  Pallas kernels: 14.1 us -> 17.9 us
  starting transfers between devices: 38.8 us -> 37.8 us
  waiting for transfers between devices: 7.17 us -> 8.17 us
    unnamed x10 -> x30, local copies, waits for them, and re-layouts: 0.93 us -> 8.7 us
    ppermute x3, waiting for transfers between devices: 5.1 us -> 0.01 us  [shards(): lax.ppermute(x, 'ctx', [(i, i // RING * RING + (i + s) % RING) for i in r...]
    all_to_all x1, waiting for transfers between devices: 1.6 us -> 5.91 us  [shards(): mem = lax.all_to_all(far, 'ctx', 0, 0, axis_index_groups=strided)]
    pallas_call x9 -> x10, Pallas kernels: 14.1 us -> 17.9 us  [call(): pl.pallas_call(kernel, out_shape=out_shape, in_specs=[pl.BlockSpec(memory...]
    all_to_all x1, starting transfers between devices: 9.04 us -> 6.5 us  [shards(): mem = lax.all_to_all(far, 'ctx', 0, 0, axis_index_groups=strided)]
    ppermute x2, waiting for transfers between devices: 0.46 us -> 2.24 us  [shards(): lax.ppermute(own, 'ctx', [((i - d) % BLOCKS, i) for i in range(BLOCKS)])]
    ppermute x3, starting transfers between devices: 9.06 us -> 10.5 us  [shards(): lax.ppermute(x, 'ctx', [(i, i // RING * RING + (i + s) % RING) for i in r...]
  transfers between devices with their start and end apart: 9 -> 9, of which waited for: 4 -> 2; matrix products, arithmetic and copies ran while one was open for 0% -> 0% of each run, Pallas kernels for 11% -> 14%
where the time goes in v6:
time: 85.8 us; the launch traced here: 85 us
  starting transfers between devices  37.8 us (44%)
  Pallas kernels  17.9 us (21%)
  blocking collectives  12.2 us (14%)
  local copies, waits for them, and re-layouts  8.7 us (10%)
  waiting for transfers between devices  8.17 us (10%)
    pallas_call x10, Pallas kernels, call(): pl.pallas_call(kernel, out_shape=out_shape, in_specs=[pl.BlockSpec(memory...  17.9 us
    all_to_all x1, blocking collectives, shards(): mem = lax.all_to_all(mem, 'ctx', 0, 0, axis_index_groups=near)  12.2 us
    ppermute x2, starting transfers between devices, shards(): lax.ppermute(own, 'ctx', [((i - d) % BLOCKS, i) for i in range(BLOCKS)])  10.6 us
    ppermute x3, starting transfers between devices, shards(): lax.ppermute(x, 'ctx', [(i, i // RING * RING + (i + s) % RING) for i in r...  10.5 us
    ppermute x3, starting transfers between devices, shards(): part = lax.ppermute(part, 'kv', [(i, i ^ off) for i in range(KV)])  10.2 us
    unnamed x30, local copies, waits for them, and re-layouts  8.7 us
    all_to_all x1, starting transfers between devices, shards(): mem = lax.all_to_all(far, 'ctx', 0, 0, axis_index_groups=strided)  6.5 us
    all_to_all x1, waiting for transfers between devices, shards(): mem = lax.all_to_all(far, 'ctx', 0, 0, axis_index_groups=strided)  5.91 us
  transfers between devices with their start and end apart: 9, of which 2 were waited for; matrix products, arithmetic and copies ran while one was open for 0% of the time, Pallas kernels for 14%

profile of v6, /device:TPU:1, one launch (start us, length us, event | category | flops | bytes accessed | tf_op | source)
XLA Modules:
  0.0 85.0 jit_solution(12570317993384018183)
XLA Ops:
  0.0 0.0 copy-start.7
  0.0 0.0 copy-start.8
  0.0 0.0 copy-start.4
  0.0 2.6 %shard_map.93 = (bf16[512,128]{1,0:T(8,128)(2,1)}, bf16[8,16,128]{2,1,0:T(8,128)(2,1)}) custom-call(s32[128]{0:T(128)} %bs.5, f32[8,128]{1,0:T(8,128)} %constant.2.clone.freqs, bf16[128,2,128]{2,1,0:T(2,128)(2,1)} %k.1, bf16[128,2,128]{2,1,0:T(2,128)(2,1)} %v.1, f32[32,128]{1,0:T(8,128)} %dk.1, f32[128,128]{1,0:T(8,128)} %pk.1, f32[32,128]{1,0:T(8,128)} %dv.1, ...), custom_call_target="tpu_custom_call" | custom-call | flops 1000000000 | bytes 1024 | tf_op jit(solution)/shard_map/pallas_call | solution.py:253
  2.6 6.6 %collective-permute-start.1 = (bf16[512,128]{1,0:T(8,128)(2,1)}, bf16[512,128]{1,0:T(8,128)(2,1)S(1)}, u32[]{:S(2)}, u32[]{:S(2)}) collective-permute-start(bf16[512,128]{1,0:T(8,128)(2,1)} %get-tuple-element.13.own), channel_id=1, source_target_pairs={{480,0},{484,4},{488,8},{492,12},{496,16},{500,20},{504,24},{508,2... | collective-permute-start | bytes 393224 | tf_op jit(solution)/shard_map/ppermute | solution.py:290
  9.3 4.0 %collective-permute-start = (bf16[512,128]{1,0:T(8,128)(2,1)}, bf16[512,128]{1,0:T(8,128)(2,1)S(1)}, u32[]{:S(2)}, u32[]{:S(2)}) collective-permute-start(bf16[512,128]{1,0:T(8,128)(2,1)} %get-tuple-element.13.own), channel_id=1, source_target_pairs={{496,0},{500,4},{504,8},{508,12},{0,16},{4,20},{8,24},{12,28},{16,... | collective-permute-start | bytes 393224 | tf_op jit(solution)/shard_map/ppermute | solution.py:290
  13.3 12.2 %all_to_all.10.mem = bf16[8,16,128]{2,1,0:T(8,128)(2,1)S(1)} all-to-all(bf16[8,16,128]{2,1,0:T(8,128)(2,1)} %get-tuple-element.14), channel_id=1, replica_groups={{0,4,8,12,16,20,24,28},{32,36,40,44,48,52,56,60},{64,68,72,76,80,84,88,..., dimensions={0} | all-to-all | bytes 65536 | tf_op jit(solution)/shard_map/all_to_all | solution.py:293
  25.4 0.0 collective-permute-done.1.row2
  25.4 2.2 %collective-permute-done.row1 = bf16[512,128]{1,0:T(8,128)(2,1)S(1)} collective-permute-done((bf16[512,128]{1,0:T(8,128)(2,1)}, bf16[512,128]{1,0:T(8,128)(2,1)S(1)}, u32[]{:S(2)}, u32[]{:S(2)}) %collective-permute-start) | collective-permute-done | bytes 131104 | tf_op jit(solution)/shard_map/ppermute | solution.py:290
  27.7 0.0 copy-start.5
  27.7 0.9 %copy-done.5 = bf16[512,128]{1,0:T(8,128)(2,1)S(1)} copy-done((bf16[512,128]{1,0:T(8,128)(2,1)S(1)}, bf16[512,128]{1,0:T(8,128)(2,1)}, u32[]{:S(2)}) %copy-start.5) | copy-done | bytes 131096
  28.6 0.0 copy-start.6
  28.6 0.9 %shard_map.94 = (bf16[1024,128]{1,0:T(8,128)(2,1)S(1)}, bf16[1024,128]{1,0:T(8,128)(2,1)S(1)}, bf16[1024,128]{1,0:T(8,128)(2,1)S(1)}, bf16[16,128,128]{2,1,0:T(8,128)(2,1)}) custom-call(bf16[512,128]{1,0:T(8,128)(2,1)S(1)} %copy-done.5, bf16[512,128]{1,0:T(8,128)(2,1)S(1)} %collective-permute-done.row1, bf16[512,128]{1,0:T(8,128)(2,1)S(1)} %collective-permute-done.1.row2, ...), custom_call_target="tpu_custom_call" | custom-call | flops 1000 | bytes 1024 | tf_op jit(solution)/shard_map/pallas_call | solution.py:253
  29.5 3.1 %collective-permute-start.2 = (bf16[1024,128]{1,0:T(8,128)(2,1)S(1)}, bf16[1024,128]{1,0:T(8,128)(2,1)S(1)}, u32[]{:S(2)}, u32[]{:S(2)}) collective-permute-start(bf16[1024,128]{1,0:T(8,128)(2,1)S(1)} %get-tuple-element.16), channel_id=1, source_target_pairs={{0,4},{4,8},{8,12},{12,0},{16,20},{20,24},{24,28},{28,16},{32,36},... | collective-permute-start | bytes 786440 | tf_op jit(solution)/shard_map/ppermute | solution.py:308
  32.6 4.4 %collective-permute-start.3 = (bf16[1024,128]{1,0:T(8,128)(2,1)S(1)}, bf16[1024,128]{1,0:T(8,128)(2,1)S(1)}, u32[]{:S(2)}, u32[]{:S(2)}) collective-permute-start(bf16[1024,128]{1,0:T(8,128)(2,1)S(1)} %get-tuple-element.17), channel_id=1, source_target_pairs={{0,8},{4,12},{8,0},{12,4},{16,24},{20,28},{24,16},{28,20},{32,40},... | collective-permute-start | bytes 786440 | tf_op jit(solution)/shard_map/ppermute | solution.py:308
  37.0 3.1 %collective-permute-start.4 = (bf16[1024,128]{1,0:T(8,128)(2,1)S(1)}, bf16[1024,128]{1,0:T(8,128)(2,1)S(1)}, u32[]{:S(2)}, u32[]{:S(2)}) collective-permute-start(bf16[1024,128]{1,0:T(8,128)(2,1)S(1)} %get-tuple-element.18), channel_id=1, source_target_pairs={{0,12},{4,0},{8,4},{12,8},{16,28},{20,16},{24,20},{28,24},{32,44},... | collective-permute-start | bytes 786440 | tf_op jit(solution)/shard_map/ppermute | solution.py:308
  40.1 6.5 %all-to-all-start.1 = ((bf16[16,128,128]{2,1,0:T(8,128)(2,1)}), bf16[16,128,128]{2,1,0:T(8,128)(2,1)}, u32[]{:S(2)}, u32[]{:S(2)}) async-start(bf16[16,128,128]{2,1,0:T(8,128)(2,1)} %get-tuple-element.15), calls=%async_computation.1 | async-start | bytes 1048576 | tf_op jit(solution)/shard_map/all_to_all | solution.py:306
  46.6 0.0 copy-done.8
  46.6 0.8 shard_map.92.bias
  47.4 0.0 copy-done.7
  47.4 0.0 copy-done.4
  47.4 0.0 copy-start.2
  47.4 1.6 %shard_map.91.rotq = bf16[16,128,128]{2,1,0:T(8,128)(2,1)S(1)} custom-call(s32[128]{0:T(128)S(1)} %copy-done.8, f32[8,128]{1,0:T(8,128)S(1)} %copy-done.7, bf16[128,16,128]{2,1,0:T(8,128)(2,1)S(1)} %copy-done.4), custom_call_target="tpu_custom_call" | custom-call | flops 1000 | bytes 1024 | tf_op jit(solution)/shard_map/pallas_call | solution.py:253
  49.0 0.0 collective-permute-done.2.r1
  49.0 0.0 copy-start.9
  49.0 0.7 copy-done.9
  49.7 0.0 collective-permute-done.3.r2
  49.7 0.0 copy-start.11
  49.7 0.7 copy-done.11
  50.4 0.0 collective-permute-done.4.r3
  50.4 0.0 copy-done.2
  50.4 0.0 copy-start.13
  50.4 0.7 copy-done.13
  51.1 0.0 copy-done.6
  51.1 0.0 copy-start.10
  51.1 0.9 %copy-done.10 = bf16[1024,128]{1,0:T(8,128)(2,1)S(1)} copy-done((bf16[1024,128]{1,0:T(8,128)(2,1)S(1)}, bf16[1024,128]{1,0:T(8,128)(2,1)}, u32[]{:S(2)}) %copy-start.10) | copy-done | bytes 262168
  52.1 0.0 copy-start.12
  52.1 0.9 %copy-done.12 = bf16[1024,128]{1,0:T(8,128)(2,1)S(1)} copy-done((bf16[1024,128]{1,0:T(8,128)(2,1)S(1)}, bf16[1024,128]{1,0:T(8,128)(2,1)}, u32[]{:S(2)}) %copy-start.12) | copy-done | bytes 262168
  53.0 0.0 copy-start.14
  53.0 0.9 %copy-done.14 = bf16[1024,128]{1,0:T(8,128)(2,1)S(1)} copy-done((bf16[1024,128]{1,0:T(8,128)(2,1)S(1)}, bf16[1024,128]{1,0:T(8,128)(2,1)}, u32[]{:S(2)}) %copy-start.14) | copy-done | bytes 262168
  54.0 3.9 %shard_map.95 = (f32[16,128,256]{2,1,0:T(8,128)S(1)}, f32[16,128,128]{2,1,0:T(8,128)S(1)}) custom-call(bf16[16,128,128]{2,1,0:T(8,128)(2,1)S(1)} %shard_map.91.rotq, bf16[1664,128]{1,0:T(8,128)(2,1)S(1)} %shard_map.92.bias, bf16[512,128]{1,0:T(8,128)(2,1)S(1)} %copy-done.6, bf16[512,128]{1,0:T(8,128)(2,1)S(1)} %collective-permute-done.row1, ...), custom_call_target="tpu_custom_call" | custom-call | flops 10000000000 | bytes 1024 | tf_op jit(solution)/shard_map/pallas_call | solution.py:253
  57.9 0.0 copy-start
  57.9 0.8 copy-done
  58.7 5.9 %all-to-all-done.1.mem = bf16[16,128,128]{2,1,0:T(8,128)(2,1)} async-done(((bf16[16,128,128]{2,1,0:T(8,128)(2,1)}), bf16[16,128,128]{2,1,0:T(8,128)(2,1)}, u32[]{:S(2)}, u32[]{:S(2)}) %all-to-all-start.1) | async-done | bytes 524320 | tf_op jit(solution)/shard_map/all_to_all | solution.py:306
  64.6 0.0 copy-start.1
  64.6 1.0 %copy-done.1 = bf16[16,128,128]{2,1,0:T(8,128)(2,1)S(1)} copy-done((bf16[16,128,128]{2,1,0:T(8,128)(2,1)S(1)}, bf16[16,128,128]{2,1,0:T(8,128)(2,1)}, u32[]{:S(2)}) %copy-start.1) | copy-done | bytes 524312
  65.6 0.0 copy-start.3
  65.6 1.0 %copy-done.3 = bf16[1664,128]{1,0:T(8,128)(2,1)S(1)} copy-done((bf16[1664,128]{1,0:T(8,128)(2,1)S(1)}, bf16[1664,128]{1,0:T(8,128)(2,1)}, u32[]{:S(2)}) %copy-start.3) | copy-done | bytes 426008
  66.7 1.8 %shard_map.98 = bf16[32,2048]{1,0:T(8,128)(2,1)S(1)} custom-call(bf16[16,128,128]{2,1,0:T(8,128)(2,1)S(1)} %copy-done.1, bf16[1664,128]{1,0:T(8,128)(2,1)S(1)} %copy-done.3, bf16[16,128,128]{2,1,0:T(8,128)(2,1)} %all-to-all-done.1.mem, f32[16,128,256]{2,1,0:T(8,128)S(1)} %get-tuple-element.19.acc, f32[16,128,128]{2,1,0:T(8,128)S(1)} %get-tuple-element.20.high), custom_call_target="tpu_custom_call" | custom-call | flops 1000000 | bytes 1024 | tf_op jit(solution)/shard_map/pallas_call | solution.py:253
  68.5 4.8 %collective-permute-start.6 = (bf16[32,2048]{1,0:T(8,128)(2,1)S(1)}, bf16[32,2048]{1,0:T(8,128)(2,1)S(1)}, u32[]{:S(2)}, u32[]{:S(2)}) collective-permute-start(bf16[32,2048]{1,0:T(8,128)(2,1)S(1)} %shard_map.98), channel_id=1, source_target_pairs={{0,3},{1,2},{2,1},{3,0},{4,7},{5,6},{6,5},{7,4},{8,11},{9,10},{10,... | collective-permute-start | bytes 393224 | tf_op jit(solution)/shard_map/ppermute | solution.py:325
  73.3 1.8 %shard_map.96 = bf16[32,2048]{1,0:T(8,128)(2,1)S(1)} custom-call(bf16[16,128,128]{2,1,0:T(8,128)(2,1)S(1)} %copy-done.1, bf16[1664,128]{1,0:T(8,128)(2,1)S(1)} %copy-done.3, bf16[16,128,128]{2,1,0:T(8,128)(2,1)} %all-to-all-done.1.mem, f32[16,128,256]{2,1,0:T(8,128)S(1)} %get-tuple-element.19.acc, f32[16,128,128]{2,1,0:T(8,128)S(1)} %get-tuple-element.20.high), custom_call_target="tpu_custom_call" | custom-call | flops 1000000 | bytes 1024 | tf_op jit(solution)/shard_map/pallas_call | solution.py:253
  75.1 3.4 %collective-permute-start.5 = (bf16[32,2048]{1,0:T(8,128)(2,1)S(1)}, bf16[32,2048]{1,0:T(8,128)(2,1)S(1)}, u32[]{:S(2)}, u32[]{:S(2)}) collective-permute-start(bf16[32,2048]{1,0:T(8,128)(2,1)S(1)} %shard_map.96), channel_id=1, source_target_pairs={{0,2},{1,3},{2,0},{3,1},{4,6},{5,7},{6,4},{7,5},{8,10},{9,11},{10,... | collective-permute-start | bytes 393224 | tf_op jit(solution)/shard_map/ppermute | solution.py:325
  78.5 0.0 collective-permute-done.6.rest_0_.d
  78.6 1.8 %shard_map.99 = bf16[32,2048]{1,0:T(8,128)(2,1)S(1)} custom-call(bf16[16,128,128]{2,1,0:T(8,128)(2,1)S(1)} %copy-done.1, bf16[1664,128]{1,0:T(8,128)(2,1)S(1)} %copy-done.3, bf16[16,128,128]{2,1,0:T(8,128)(2,1)} %all-to-all-done.1.mem, f32[16,128,256]{2,1,0:T(8,128)S(1)} %get-tuple-element.19.acc, f32[16,128,128]{2,1,0:T(8,128)S(1)} %get-tuple-element.20.high, ...), custom_call_target="tpu_custom_call" | custom-call | flops 1000000 | bytes 1024 | tf_op jit(solution)/shard_map/pallas_call | solution.py:253
  80.4 1.9 %collective-permute-start.7 = (bf16[32,2048]{1,0:T(8,128)(2,1)S(1)}, bf16[32,2048]{1,0:T(8,128)(2,1)S(1)}, u32[]{:S(2)}, u32[]{:S(2)}) collective-permute-start(bf16[32,2048]{1,0:T(8,128)(2,1)S(1)} %shard_map.99), channel_id=1, source_target_pairs={{0,1},{1,0},{2,3},{3,2},{4,5},{5,4},{6,7},{7,6},{8,9},{9,8},{10,11... | collective-permute-start | bytes 393224 | tf_op jit(solution)/shard_map/ppermute | solution.py:325
  82.3 0.0 collective-permute-done.5.rest_0_.c
  82.3 1.8 %shard_map.97.a = bf16[32,2048]{1,0:T(8,128)(2,1)S(1)} custom-call(bf16[16,128,128]{2,1,0:T(8,128)(2,1)S(1)} %copy-done.1, bf16[1664,128]{1,0:T(8,128)(2,1)S(1)} %copy-done.3, bf16[16,128,128]{2,1,0:T(8,128)(2,1)} %all-to-all-done.1.mem, f32[16,128,256]{2,1,0:T(8,128)S(1)} %get-tuple-element.19.acc, f32[16,128,128]{2,1,0:T(8,128)S(1)} %get-tuple-element.20.high, ...), custom_call_target="tpu_custom_call" | custom-call | flops 1000000 | bytes 1024 | tf_op jit(solution)/shard_map/pallas_call | solution.py:253
  84.1 0.0 collective-permute-done.7.b
  84.1 0.8 shard_map.100
Async XLA Ops:
  0.0 47.4 %copy-start.7 = (f32[8,128]{1,0:T(8,128)S(1)}, f32[8,128]{1,0:T(8,128)}, u32[]{:S(2)}) copy-start(f32[8,128]{1,0:T(8,128)} %constant.2.clone.freqs) | copy-start | bytes 12292
  0.0 46.6 %copy-start.8 = (s32[128]{0:T(128)S(1)}, s32[128]{0:T(128)}, u32[]{:S(2)}) copy-start(s32[128]{0:T(128)} %bs.5) | copy-start | bytes 1540
  0.0 47.4 %copy-start.4 = (bf16[128,16,128]{2,1,0:T(8,128)(2,1)S(1)}, bf16[128,16,128]{2,1,0:T(8,128)(2,1)}, u32[]{:S(2)}) copy-start(bf16[128,16,128]{2,1,0:T(8,128)(2,1)} %q.1) | copy-start | bytes 1572868
  2.6 22.8 %collective-permute-start.1 = (bf16[512,128]{1,0:T(8,128)(2,1)}, bf16[512,128]{1,0:T(8,128)(2,1)S(1)}, u32[]{:S(2)}, u32[]{:S(2)}) collective-permute-start(bf16[512,128]{1,0:T(8,128)(2,1)} %get-tuple-element.13.own), channel_id=1, source_target_pairs={{480,0},{484,4},{488,8},{492,12},{496,16},{500,20},{504,24},{508,2... | collective-permute-start | bytes 393224 | tf_op jit(solution)/shard_map/ppermute | solution.py:290
  9.3 18.4 %collective-permute-start = (bf16[512,128]{1,0:T(8,128)(2,1)}, bf16[512,128]{1,0:T(8,128)(2,1)S(1)}, u32[]{:S(2)}, u32[]{:S(2)}) collective-permute-start(bf16[512,128]{1,0:T(8,128)(2,1)} %get-tuple-element.13.own), channel_id=1, source_target_pairs={{496,0},{500,4},{504,8},{508,12},{0,16},{4,20},{8,24},{12,28},{16,... | collective-permute-start | bytes 393224 | tf_op jit(solution)/shard_map/ppermute | solution.py:290
  27.7 0.9 %copy-start.5 = (bf16[512,128]{1,0:T(8,128)(2,1)S(1)}, bf16[512,128]{1,0:T(8,128)(2,1)}, u32[]{:S(2)}) copy-start(bf16[512,128]{1,0:T(8,128)(2,1)} %get-tuple-element.13.own) | copy-start | bytes 393220
  28.6 22.6 %copy-start.6 = (bf16[512,128]{1,0:T(8,128)(2,1)S(1)}, bf16[512,128]{1,0:T(8,128)(2,1)}, u32[]{:S(2)}) copy-start(bf16[512,128]{1,0:T(8,128)(2,1)} %get-tuple-element.13.own) | copy-start | bytes 393220
  29.5 19.5 %collective-permute-start.2 = (bf16[1024,128]{1,0:T(8,128)(2,1)S(1)}, bf16[1024,128]{1,0:T(8,128)(2,1)S(1)}, u32[]{:S(2)}, u32[]{:S(2)}) collective-permute-start(bf16[1024,128]{1,0:T(8,128)(2,1)S(1)} %get-tuple-element.16), channel_id=1, source_target_pairs={{0,4},{4,8},{8,12},{12,0},{16,20},{20,24},{24,28},{28,16},{32,36},... | collective-permute-start | bytes 786440 | tf_op jit(solution)/shard_map/ppermute | solution.py:308
  32.6 17.1 %collective-permute-start.3 = (bf16[1024,128]{1,0:T(8,128)(2,1)S(1)}, bf16[1024,128]{1,0:T(8,128)(2,1)S(1)}, u32[]{:S(2)}, u32[]{:S(2)}) collective-permute-start(bf16[1024,128]{1,0:T(8,128)(2,1)S(1)} %get-tuple-element.17), channel_id=1, source_target_pairs={{0,8},{4,12},{8,0},{12,4},{16,24},{20,28},{24,16},{28,20},{32,40},... | collective-permute-start | bytes 786440 | tf_op jit(solution)/shard_map/ppermute | solution.py:308
  37.0 13.4 %collective-permute-start.4 = (bf16[1024,128]{1,0:T(8,128)(2,1)S(1)}, bf16[1024,128]{1,0:T(8,128)(2,1)S(1)}, u32[]{:S(2)}, u32[]{:S(2)}) collective-permute-start(bf16[1024,128]{1,0:T(8,128)(2,1)S(1)} %get-tuple-element.18), channel_id=1, source_target_pairs={{0,12},{4,0},{8,4},{12,8},{16,28},{20,16},{24,20},{28,24},{32,44},... | collective-permute-start | bytes 786440 | tf_op jit(solution)/shard_map/ppermute | solution.py:308
  40.1 24.5 %all-to-all-start.1 = ((bf16[16,128,128]{2,1,0:T(8,128)(2,1)}), bf16[16,128,128]{2,1,0:T(8,128)(2,1)}, u32[]{:S(2)}, u32[]{:S(2)}) async-start(bf16[16,128,128]{2,1,0:T(8,128)(2,1)} %get-tuple-element.15), calls=%async_computation.1 | async-start | bytes 1048576 | tf_op jit(solution)/shard_map/all_to_all | solution.py:306
  47.4 3.0 %copy-start.2 = (bf16[1664,128]{1,0:T(8,128)(2,1)}, bf16[1664,128]{1,0:T(8,128)(2,1)S(1)}, u32[]{:S(2)}) copy-start(bf16[1664,128]{1,0:T(8,128)(2,1)S(1)} %shard_map.92.bias) | copy-start | bytes 1277956
  49.0 0.7 copy-start.9
  49.7 0.7 copy-start.11
  50.4 0.7 copy-start.13
  51.1 1.0 %copy-start.10 = (bf16[1024,128]{1,0:T(8,128)(2,1)S(1)}, bf16[1024,128]{1,0:T(8,128)(2,1)}, u32[]{:S(2)}) copy-start(bf16[1024,128]{1,0:T(8,128)(2,1)} %copy-done.9) | copy-start | bytes 786436
  52.1 0.9 %copy-start.12 = (bf16[1024,128]{1,0:T(8,128)(2,1)S(1)}, bf16[1024,128]{1,0:T(8,128)(2,1)}, u32[]{:S(2)}) copy-start(bf16[1024,128]{1,0:T(8,128)(2,1)} %copy-done.11) | copy-start | bytes 786436
  53.0 0.9 %copy-start.14 = (bf16[1024,128]{1,0:T(8,128)(2,1)S(1)}, bf16[1024,128]{1,0:T(8,128)(2,1)}, u32[]{:S(2)}) copy-start(bf16[1024,128]{1,0:T(8,128)(2,1)} %copy-done.13) | copy-start | bytes 786436
  57.9 0.8 copy-start
  64.6 1.0 %copy-start.1 = (bf16[16,128,128]{2,1,0:T(8,128)(2,1)S(1)}, bf16[16,128,128]{2,1,0:T(8,128)(2,1)}, u32[]{:S(2)}) copy-start(bf16[16,128,128]{2,1,0:T(8,128)(2,1)} %copy-done) | copy-start | bytes 1572868
  65.6 1.0 %copy-start.3 = (bf16[1664,128]{1,0:T(8,128)(2,1)S(1)}, bf16[1664,128]{1,0:T(8,128)(2,1)}, u32[]{:S(2)}) copy-start(bf16[1664,128]{1,0:T(8,128)(2,1)} %copy-done.2) | copy-start | bytes 1277956
  68.5 10.1 %collective-permute-start.6 = (bf16[32,2048]{1,0:T(8,128)(2,1)S(1)}, bf16[32,2048]{1,0:T(8,128)(2,1)S(1)}, u32[]{:S(2)}, u32[]{:S(2)}) collective-permute-start(bf16[32,2048]{1,0:T(8,128)(2,1)S(1)} %shard_map.98), channel_id=1, source_target_pairs={{0,3},{1,2},{2,1},{3,0},{4,7},{5,6},{6,5},{7,4},{8,11},{9,10},{10,... | collective-permute-start | bytes 393224 | tf_op jit(solution)/shard_map/ppermute | solution.py:325
  75.1 7.2 %collective-permute-start.5 = (bf16[32,2048]{1,0:T(8,128)(2,1)S(1)}, bf16[32,2048]{1,0:T(8,128)(2,1)S(1)}, u32[]{:S(2)}, u32[]{:S(2)}) collective-permute-start(bf16[32,2048]{1,0:T(8,128)(2,1)S(1)} %shard_map.96), channel_id=1, source_target_pairs={{0,2},{1,3},{2,0},{3,1},{4,6},{5,7},{6,4},{7,5},{8,10},{9,11},{10,... | collective-permute-start | bytes 393224 | tf_op jit(solution)/shard_map/ppermute | solution.py:325
  80.4 3.8 %collective-permute-start.7 = (bf16[32,2048]{1,0:T(8,128)(2,1)S(1)}, bf16[32,2048]{1,0:T(8,128)(2,1)S(1)}, u32[]{:S(2)}, u32[]{:S(2)}) collective-permute-start(bf16[32,2048]{1,0:T(8,128)(2,1)S(1)} %shard_map.99), channel_id=1, source_target_pairs={{0,1},{1,0},{2,3},{3,2},{4,5},{5,4},{6,7},{7,6},{8,9},{9,8},{10,11... | collective-permute-start | bytes 393224 | tf_op jit(solution)/shard_map/ppermute | solution.py:325

commit v7 on v5

--- a/solution.py
+++ b/solution.py
@@ -52,8 +52,8 @@
     return jnp.cos(angle), jnp.where(first, -sine, sine)
 
 
-def turn(x, cosine, sine):
-    return ((x * cosine + pltpu.roll(x, HD // 2, 1) * sine) * MSCALE).astype(BF)
+def turn(x, cosine, sine, scale=MSCALE):
+    return ((x * cosine + pltpu.roll(x, HD // 2, 1) * sine) * scale).astype(BF)
 
 
 def prep_kernel(bs, freqs, k, v, dk, pk, dv, pv, own, mem, *scratch):
@@ -89,12 +89,12 @@
     mem[...] = jnp.broadcast_to(both[None], mem.shape)
 
 
-def query_kernel(bs, freqs, q, rotq, scr):
+def query_kernel(bs, freqs, q, after, rotq, scr):
     me = lax.axis_index("ctx")
     cosine, sine = turn_tables(bs[me], freqs[0:1, :])
     scr[...] = q[...].astype(F32)
     for h in range(HEADS):
-        rotq[h] = turn(scr[:, h, :], cosine, sine)
+        rotq[h] = turn(scr[:, h, :], cosine, sine, MSCALE * SCALE2)
 
 
 def ring_kernel(own, row1, row2, mem, r1, r2, r3, far, scr):
@@ -186,7 +186,7 @@
         top = jnp.max(high, axis=1, keepdims=True)
         mixed = None
         for lo, size, tile in key_tiles():
-            w = jnp.exp2((s[g, :, lo : lo + size] - top) * SCALE2).astype(BF)
+            w = jnp.exp2((s[g, :, lo : lo + size] - top).astype(BF))
             v = gather_tile(refs, tile, GROUPS + g)
             va = jnp.concatenate([v, jnp.ones((size, HD), BF)], axis=1)
             part = jnp.dot(w, va, preferred_element_type=F32)
@@ -254,11 +254,6 @@
         for d in (RING, 2 * RING)
     )
     mem = lax.all_to_all(mem, "ctx", 0, 0, axis_index_groups=near)
-    rotq = call(
-        query_kernel, shape(HEADS, TOK, HD), [pltpu.VMEM((TOK, HEADS, HD), F32)], 10**3,
-        (SM, VM, VM),
-        block_start, freqs, queries,
-    )
     bias = call(bias_kernel, shape(KEYS, TOK), [], 10**3, (SM,), block_start)
     *rings, far = call(
         ring_kernel,
@@ -267,10 +262,18 @@
         own, row1, row2, mem,
     )
     mem = lax.all_to_all(far, "ctx", 0, 0, axis_index_groups=strided)
-    rings = [
-        lax.ppermute(x, "ctx", [(i, i // RING * RING + (i + s) % RING) for i in range(BLOCKS)])
-        for s, x in enumerate(rings, 1)
-    ]
+    turned = {
+        s: lax.ppermute(
+            rings[s - 1], "ctx", [(i, i // RING * RING + (i + s) % RING) for i in range(BLOCKS)]
+        )
+        for s in (2, 1, 3)
+    }
+    rings = [turned[s] for s in (1, 2, 3)]
+    rotq = call(
+        query_kernel, shape(HEADS, TOK, HD), [pltpu.VMEM((TOK, HEADS, HD), F32)], 10**10,
+        (SM, VM, VM, pl.ANY),
+        block_start, freqs, queries, turned[2],
+    )
     parts = []
     for off in (3, 2, 1, 0):
         after = parts[-2:-1]

time: 74.1 us -> 77.2 us (1.042)
  waiting for transfers between devices: 7.17 us -> 11.3 us
    all_to_all x1, waiting for transfers between devices: 1.6 us -> 7.42 us  [shards(): mem = lax.all_to_all(far, 'ctx', 0, 0, axis_index_groups=strided)]
    ppermute x3, waiting for transfers between devices: 5.1 us -> 1.68 us  [shards(): lax.ppermute(rings[s - 1], 'ctx', [(i, i // RING * RING + (i + s) % RING)...]
    all_to_all x1, starting transfers between devices: 9.04 us -> 6.58 us  [shards(): mem = lax.all_to_all(far, 'ctx', 0, 0, axis_index_groups=strided)]
    ppermute x3, starting transfers between devices: 9.06 us -> 11.3 us  [shards(): lax.ppermute(rings[s - 1], 'ctx', [(i, i // RING * RING + (i + s) % RING)...]
    ppermute x2, waiting for transfers between devices: 0.46 us -> 2.24 us  [shards(): lax.ppermute(own, 'ctx', [((i - d) % BLOCKS, i) for i in range(BLOCKS)])]
  transfers between devices with their start and end apart: 9 -> 9, of which waited for: 4 -> 4; matrix products, arithmetic and copies ran while one was open for 0% -> 0% of each run, Pallas kernels for 11% -> 10%
where the time goes in v7:
time: 77.2 us; the launch traced here: 76.7 us
  starting transfers between devices  38.1 us (49%)
  Pallas kernels  13.9 us (18%)
  blocking collectives  12.2 us (16%)
  waiting for transfers between devices  11.3 us (15%)
  local copies, waits for them, and re-layouts  0.93 us (1%)
    pallas_call x9, Pallas kernels, call(): pl.pallas_call(kernel, out_shape=out_shape, in_specs=[pl.BlockSpec(memory...  13.9 us
    all_to_all x1, blocking collectives, shards(): mem = lax.all_to_all(mem, 'ctx', 0, 0, axis_index_groups=near)  12.2 us
    ppermute x3, starting transfers between devices, shards(): lax.ppermute(rings[s - 1], 'ctx', [(i, i // RING * RING + (i + s) % RING)...  11.3 us
    ppermute x2, starting transfers between devices, shards(): lax.ppermute(own, 'ctx', [((i - d) % BLOCKS, i) for i in range(BLOCKS)])  10.6 us
    ppermute x3, starting transfers between devices, shards(): part = lax.ppermute(part, 'kv', [(i, i ^ off) for i in range(KV)])  9.64 us
    all_to_all x1, waiting for transfers between devices, shards(): mem = lax.all_to_all(far, 'ctx', 0, 0, axis_index_groups=strided)  7.42 us
    all_to_all x1, starting transfers between devices, shards(): mem = lax.all_to_all(far, 'ctx', 0, 0, axis_index_groups=strided)  6.58 us
    ppermute x2, waiting for transfers between devices, shards(): lax.ppermute(own, 'ctx', [((i - d) % BLOCKS, i) for i in range(BLOCKS)])  2.24 us
  transfers between devices with their start and end apart: 9, of which 4 were waited for; matrix products, arithmetic and copies ran while one was open for 0% of the time, Pallas kernels for 10%

profile of v7, /device:TPU:1, one launch (start us, length us, event | category | flops | bytes accessed | tf_op | source)
XLA Modules:
  0.0 76.7 jit_solution(15940485516721254077)
XLA Ops:
  0.0 2.5 %shard_map.91 = (bf16[512,128]{1,0:T(8,128)(2,1)}, bf16[8,16,128]{2,1,0:T(8,128)(2,1)}) custom-call(s32[128]{0:T(128)} %bs.5, f32[8,128]{1,0:T(8,128)} %constant.2.clone.freqs, bf16[128,2,128]{2,1,0:T(2,128)(2,1)} %k.1, bf16[128,2,128]{2,1,0:T(2,128)(2,1)} %v.1, f32[32,128]{1,0:T(8,128)} %dk.1, f32[128,128]{1,0:T(8,128)} %pk.1, f32[32,128]{1,0:T(8,128)} %dv.1, ...), custom_call_target="tpu_custom_call" | custom-call | flops 1000000000 | bytes 1024 | tf_op jit(solution)/shard_map/pallas_call | solution.py:216
  2.5 6.6 %collective-permute-start.1 = (bf16[512,128]{1,0:T(8,128)(2,1)}, bf16[512,128]{1,0:T(8,128)(2,1)S(1)}, u32[]{:S(2)}, u32[]{:S(2)}) collective-permute-start(bf16[512,128]{1,0:T(8,128)(2,1)} %get-tuple-element.11.own), channel_id=1, source_target_pairs={{480,0},{484,4},{488,8},{492,12},{496,16},{500,20},{504,24},{508,2... | collective-permute-start | bytes 393224 | tf_op jit(solution)/shard_map/ppermute | solution.py:253
  9.2 4.0 %collective-permute-start = (bf16[512,128]{1,0:T(8,128)(2,1)}, bf16[512,128]{1,0:T(8,128)(2,1)S(1)}, u32[]{:S(2)}, u32[]{:S(2)}) collective-permute-start(bf16[512,128]{1,0:T(8,128)(2,1)} %get-tuple-element.11.own), channel_id=1, source_target_pairs={{496,0},{500,4},{504,8},{508,12},{0,16},{4,20},{8,24},{12,28},{16,... | collective-permute-start | bytes 393224 | tf_op jit(solution)/shard_map/ppermute | solution.py:253
  13.2 12.2 %all_to_all.10.mem = bf16[8,16,128]{2,1,0:T(8,128)(2,1)S(1)} all-to-all(bf16[8,16,128]{2,1,0:T(8,128)(2,1)} %get-tuple-element.12), channel_id=1, replica_groups={{0,4,8,12,16,20,24,28},{32,36,40,44,48,52,56,60},{64,68,72,76,80,84,88,..., dimensions={0} | all-to-all | bytes 65536 | tf_op jit(solution)/shard_map/all_to_all | solution.py:256
  25.4 0.0 collective-permute-done.1.row2
  25.4 2.2 %collective-permute-done.row1 = bf16[512,128]{1,0:T(8,128)(2,1)S(1)} collective-permute-done((bf16[512,128]{1,0:T(8,128)(2,1)}, bf16[512,128]{1,0:T(8,128)(2,1)S(1)}, u32[]{:S(2)}, u32[]{:S(2)}) %collective-permute-start) | collective-permute-done | bytes 131104 | tf_op jit(solution)/shard_map/ppermute | solution.py:253
  27.6 0.0 copy-start
  27.6 0.9 %copy-done = bf16[512,128]{1,0:T(8,128)(2,1)S(1)} copy-done((bf16[512,128]{1,0:T(8,128)(2,1)S(1)}, bf16[512,128]{1,0:T(8,128)(2,1)}, u32[]{:S(2)}) %copy-start) | copy-done | bytes 131096
  28.5 1.0 %shard_map.92 = (bf16[1024,128]{1,0:T(8,128)(2,1)}, bf16[1024,128]{1,0:T(8,128)(2,1)S(1)}, bf16[1024,128]{1,0:T(8,128)(2,1)S(1)}, bf16[16,128,128]{2,1,0:T(8,128)(2,1)}) custom-call(bf16[512,128]{1,0:T(8,128)(2,1)S(1)} %copy-done, bf16[512,128]{1,0:T(8,128)(2,1)S(1)} %collective-permute-done.row1, bf16[512,128]{1,0:T(8,128)(2,1)S(1)} %collective-permute-done.1.row2, ...), custom_call_target="tpu_custom_call" | custom-call | flops 1000 | bytes 1024 | tf_op jit(solution)/shard_map/pallas_call | solution.py:216
  29.5 4.6 %collective-permute-start.2 = (bf16[1024,128]{1,0:T(8,128)(2,1)S(1)}, bf16[1024,128]{1,0:T(8,128)(2,1)S(1)}, u32[]{:S(2)}, u32[]{:S(2)}) collective-permute-start(bf16[1024,128]{1,0:T(8,128)(2,1)S(1)} %get-tuple-element.13), channel_id=1, source_target_pairs={{0,8},{4,12},{8,0},{12,4},{16,24},{20,28},{24,16},{28,20},{32,40},... | collective-permute-start | bytes 786440 | tf_op jit(solution)/shard_map/ppermute | solution.py:266
  34.2 0.0 copy-start.2
  34.2 0.0 copy-start.3
  34.2 6.6 %all-to-all-start.1 = ((bf16[16,128,128]{2,1,0:T(8,128)(2,1)}), bf16[16,128,128]{2,1,0:T(8,128)(2,1)S(1)}, u32[]{:S(2)}, u32[]{:S(2)}) async-start(bf16[16,128,128]{2,1,0:T(8,128)(2,1)} %get-tuple-element.16), calls=%async_computation.1 | async-start | bytes 1048576 | tf_op jit(solution)/shard_map/all_to_all | solution.py:264
  40.8 0.0 copy-done.2
  40.8 0.0 copy-start.4
  40.8 0.8 %shard_map.94.bias = bf16[1664,128]{1,0:T(8,128)(2,1)S(1)} custom-call(s32[128]{0:T(128)S(1)} %copy-done.2), custom_call_target="tpu_custom_call" | custom-call | flops 1000 | bytes 1024 | tf_op jit(solution)/shard_map/pallas_call | solution.py:216
  41.6 2.2 %collective-permute-start.3 = (bf16[1024,128]{1,0:T(8,128)(2,1)}, bf16[1024,128]{1,0:T(8,128)(2,1)S(1)}, u32[]{:S(2)}, u32[]{:S(2)}) collective-permute-start(bf16[1024,128]{1,0:T(8,128)(2,1)} %get-tuple-element.14), channel_id=1, source_target_pairs={{0,4},{4,8},{8,12},{12,0},{16,20},{20,24},{24,28},{28,16},{32,36},... | collective-permute-start | bytes 786440 | tf_op jit(solution)/shard_map/ppermute | solution.py:266
  43.8 0.0 copy-start.1
  43.8 4.4 %collective-permute-start.4 = (bf16[1024,128]{1,0:T(8,128)(2,1)S(1)}, bf16[1024,128]{1,0:T(8,128)(2,1)S(1)}, u32[]{:S(2)}, u32[]{:S(2)}) collective-permute-start(bf16[1024,128]{1,0:T(8,128)(2,1)S(1)} %get-tuple-element.15), channel_id=1, source_target_pairs={{0,12},{4,0},{8,4},{12,8},{16,28},{20,16},{24,20},{28,24},{32,44},... | collective-permute-start | bytes 786440 | tf_op jit(solution)/shard_map/ppermute | solution.py:266
  48.3 0.0 collective-permute-done.2.after.r2
  48.3 0.0 copy-done.3
  48.3 0.0 copy-done.4
  48.3 1.6 %shard_map.93.rotq = bf16[16,128,128]{2,1,0:T(8,128)(2,1)S(1)} custom-call(s32[128]{0:T(128)S(1)} %copy-done.2, f32[8,128]{1,0:T(8,128)S(1)} %copy-done.4, bf16[128,16,128]{2,1,0:T(8,128)(2,1)S(1)} %copy-done.3, bf16[1024,128]{1,0:T(8,128)(2,1)S(1)} %collective-permute-done.2.after.r2), custom_call_target="tpu_custom_call" | custom-call | flops 10000000000 | bytes 1024 | tf_op jit(solution)/shard_map/pallas_call | solution.py:216
  49.9 0.6 collective-permute-done.3.r1
  50.4 1.1 %collective-permute-done.4.r3 = bf16[1024,128]{1,0:T(8,128)(2,1)S(1)} collective-permute-done((bf16[1024,128]{1,0:T(8,128)(2,1)S(1)}, bf16[1024,128]{1,0:T(8,128)(2,1)S(1)}, u32[]{:S(2)}, u32[]{:S(2)}) %collective-permute-start.4) | collective-permute-done | bytes 262176 | tf_op jit(solution)/shard_map/ppermute | solution.py:266
  51.6 7.4 %all-to-all-done.1.mem = bf16[16,128,128]{2,1,0:T(8,128)(2,1)S(1)} async-done(((bf16[16,128,128]{2,1,0:T(8,128)(2,1)}), bf16[16,128,128]{2,1,0:T(8,128)(2,1)S(1)}, u32[]{:S(2)}, u32[]{:S(2)}) %all-to-all-start.1) | async-done | bytes 524320 | tf_op jit(solution)/shard_map/all_to_all | solution.py:264
  59.0 0.0 copy-done.1
  59.0 1.8 %shard_map.97 = bf16[32,2048]{1,0:T(8,128)(2,1)S(1)} custom-call(bf16[16,128,128]{2,1,0:T(8,128)(2,1)S(1)} %shard_map.93.rotq, bf16[1664,128]{1,0:T(8,128)(2,1)S(1)} %shard_map.94.bias, bf16[512,128]{1,0:T(8,128)(2,1)S(1)} %copy-done.1, bf16[512,128]{1,0:T(8,128)(2,1)S(1)} %collective-permute-done.row1, bf16[512,128]{1,0:T(8,128)(2,1)S(1)} %collective-permute-done.1.row2, ...), custom_call_target="tpu_custom_call" | custom-call | flops 1000000 | bytes 1024 | tf_op jit(solution)/shard_map/pallas_call | solution.py:216
  60.8 4.3 %collective-permute-start.6 = (bf16[32,2048]{1,0:T(8,128)(2,1)S(1)}, bf16[32,2048]{1,0:T(8,128)(2,1)S(1)}, u32[]{:S(2)}, u32[]{:S(2)}) collective-permute-start(bf16[32,2048]{1,0:T(8,128)(2,1)S(1)} %shard_map.97), channel_id=1, source_target_pairs={{0,3},{1,2},{2,1},{3,0},{4,7},{5,6},{6,5},{7,4},{8,11},{9,10},{10,... | collective-permute-start | bytes 393224 | tf_op jit(solution)/shard_map/ppermute | solution.py:286
  65.1 1.8 %shard_map.95 = bf16[32,2048]{1,0:T(8,128)(2,1)S(1)} custom-call(bf16[16,128,128]{2,1,0:T(8,128)(2,1)S(1)} %shard_map.93.rotq, bf16[1664,128]{1,0:T(8,128)(2,1)S(1)} %shard_map.94.bias, bf16[512,128]{1,0:T(8,128)(2,1)S(1)} %copy-done.1, bf16[512,128]{1,0:T(8,128)(2,1)S(1)} %collective-permute-done.row1, bf16[512,128]{1,0:T(8,128)(2,1)S(1)} %collective-permute-done.1.row2, ...), custom_call_target="tpu_custom_call" | custom-call | flops 1000000 | bytes 1024 | tf_op jit(solution)/shard_map/pallas_call | solution.py:216
  66.9 3.4 %collective-permute-start.5 = (bf16[32,2048]{1,0:T(8,128)(2,1)S(1)}, bf16[32,2048]{1,0:T(8,128)(2,1)S(1)}, u32[]{:S(2)}, u32[]{:S(2)}) collective-permute-start(bf16[32,2048]{1,0:T(8,128)(2,1)S(1)} %shard_map.95), channel_id=1, source_target_pairs={{0,2},{1,3},{2,0},{3,1},{4,6},{5,7},{6,4},{7,5},{8,10},{9,11},{10,... | collective-permute-start | bytes 393224 | tf_op jit(solution)/shard_map/ppermute | solution.py:286
  70.3 0.0 collective-permute-done.6.rest_0_.d
  70.3 1.8 %shard_map.98 = bf16[32,2048]{1,0:T(8,128)(2,1)S(1)} custom-call(bf16[16,128,128]{2,1,0:T(8,128)(2,1)S(1)} %shard_map.93.rotq, bf16[1664,128]{1,0:T(8,128)(2,1)S(1)} %shard_map.94.bias, bf16[512,128]{1,0:T(8,128)(2,1)S(1)} %copy-done.1, bf16[512,128]{1,0:T(8,128)(2,1)S(1)} %collective-permute-done.row1, bf16[512,128]{1,0:T(8,128)(2,1)S(1)} %collective-permute-done.1.row2, ...), custom_call_target="tpu_custom_call" | custom-call | flops 1000000 | bytes 1024 | tf_op jit(solution)/shard_map/pallas_call | solution.py:216
  72.1 1.9 %collective-permute-start.7 = (bf16[32,2048]{1,0:T(8,128)(2,1)S(1)}, bf16[32,2048]{1,0:T(8,128)(2,1)S(1)}, u32[]{:S(2)}, u32[]{:S(2)}) collective-permute-start(bf16[32,2048]{1,0:T(8,128)(2,1)S(1)} %shard_map.98), channel_id=1, source_target_pairs={{0,1},{1,0},{2,3},{3,2},{4,5},{5,4},{6,7},{7,6},{8,9},{9,8},{10,11... | collective-permute-start | bytes 393224 | tf_op jit(solution)/shard_map/ppermute | solution.py:286
  74.0 0.0 collective-permute-done.5.rest_0_.c
  74.0 1.8 %shard_map.96.a = bf16[32,2048]{1,0:T(8,128)(2,1)S(1)} custom-call(bf16[16,128,128]{2,1,0:T(8,128)(2,1)S(1)} %shard_map.93.rotq, bf16[1664,128]{1,0:T(8,128)(2,1)S(1)} %shard_map.94.bias, bf16[512,128]{1,0:T(8,128)(2,1)S(1)} %copy-done.1, bf16[512,128]{1,0:T(8,128)(2,1)S(1)} %collective-permute-done.row1, bf16[512,128]{1,0:T(8,128)(2,1)S(1)} %collective-permute-done.1.row2, ...), custom_call_target="tpu_custom_call" | custom-call | flops 1000000 | bytes 1024 | tf_op jit(solution)/shard_map/pallas_call | solution.py:216
  75.8 0.0 collective-permute-done.7.b
  75.8 0.8 %shard_map.99 = bf16[32,8192]{1,0:T(8,128)(2,1)} custom-call(bf16[32,2048]{1,0:T(8,128)(2,1)S(1)} %shard_map.96.a, bf16[32,2048]{1,0:T(8,128)(2,1)S(1)} %collective-permute-done.7.b, bf16[32,2048]{1,0:T(8,128)(2,1)S(1)} %collective-permute-done.5.rest_0_.c, bf16[32,2048]{1,0:T(8,128)(2,1)S(1)} %collective-permute-done.6.rest_0_.d), custom_call_target="tpu_custom_call" | custom-call | flops 100000000 | bytes 1024 | tf_op jit(solution)/shard_map/pallas_call | solution.py:216
Async XLA Ops:
  2.5 22.8 %collective-permute-start.1 = (bf16[512,128]{1,0:T(8,128)(2,1)}, bf16[512,128]{1,0:T(8,128)(2,1)S(1)}, u32[]{:S(2)}, u32[]{:S(2)}) collective-permute-start(bf16[512,128]{1,0:T(8,128)(2,1)} %get-tuple-element.11.own), channel_id=1, source_target_pairs={{480,0},{484,4},{488,8},{492,12},{496,16},{500,20},{504,24},{508,2... | collective-permute-start | bytes 393224 | tf_op jit(solution)/shard_map/ppermute | solution.py:253
  9.2 18.4 %collective-permute-start = (bf16[512,128]{1,0:T(8,128)(2,1)}, bf16[512,128]{1,0:T(8,128)(2,1)S(1)}, u32[]{:S(2)}, u32[]{:S(2)}) collective-permute-start(bf16[512,128]{1,0:T(8,128)(2,1)} %get-tuple-element.11.own), channel_id=1, source_target_pairs={{496,0},{500,4},{504,8},{508,12},{0,16},{4,20},{8,24},{12,28},{16,... | collective-permute-start | bytes 393224 | tf_op jit(solution)/shard_map/ppermute | solution.py:253
  27.6 0.9 %copy-start = (bf16[512,128]{1,0:T(8,128)(2,1)S(1)}, bf16[512,128]{1,0:T(8,128)(2,1)}, u32[]{:S(2)}) copy-start(bf16[512,128]{1,0:T(8,128)(2,1)} %get-tuple-element.11.own) | copy-start | bytes 393220
  29.5 18.7 %collective-permute-start.2 = (bf16[1024,128]{1,0:T(8,128)(2,1)S(1)}, bf16[1024,128]{1,0:T(8,128)(2,1)S(1)}, u32[]{:S(2)}, u32[]{:S(2)}) collective-permute-start(bf16[1024,128]{1,0:T(8,128)(2,1)S(1)} %get-tuple-element.13), channel_id=1, source_target_pairs={{0,8},{4,12},{8,0},{12,4},{16,24},{20,28},{24,16},{28,20},{32,40},... | collective-permute-start | bytes 786440 | tf_op jit(solution)/shard_map/ppermute | solution.py:266
  34.2 6.6 %copy-start.2 = (s32[128]{0:T(128)S(1)}, s32[128]{0:T(128)}, u32[]{:S(2)}) copy-start(s32[128]{0:T(128)} %bs.5) | copy-start | bytes 1540
  34.2 14.1 %copy-start.3 = (bf16[128,16,128]{2,1,0:T(8,128)(2,1)S(1)}, bf16[128,16,128]{2,1,0:T(8,128)(2,1)}, u32[]{:S(2)}) copy-start(bf16[128,16,128]{2,1,0:T(8,128)(2,1)} %q.1) | copy-start | bytes 1572868
  34.2 24.8 %all-to-all-start.1 = ((bf16[16,128,128]{2,1,0:T(8,128)(2,1)}), bf16[16,128,128]{2,1,0:T(8,128)(2,1)S(1)}, u32[]{:S(2)}, u32[]{:S(2)}) async-start(bf16[16,128,128]{2,1,0:T(8,128)(2,1)} %get-tuple-element.16), calls=%async_computation.1 | async-start | bytes 1048576 | tf_op jit(solution)/shard_map/all_to_all | solution.py:264
  40.8 7.5 %copy-start.4 = (f32[8,128]{1,0:T(8,128)S(1)}, f32[8,128]{1,0:T(8,128)}, u32[]{:S(2)}) copy-start(f32[8,128]{1,0:T(8,128)} %constant.2.clone.freqs) | copy-start | bytes 12292
  41.6 8.8 %collective-permute-start.3 = (bf16[1024,128]{1,0:T(8,128)(2,1)}, bf16[1024,128]{1,0:T(8,128)(2,1)S(1)}, u32[]{:S(2)}, u32[]{:S(2)}) collective-permute-start(bf16[1024,128]{1,0:T(8,128)(2,1)} %get-tuple-element.14), channel_id=1, source_target_pairs={{0,4},{4,8},{8,12},{12,0},{16,20},{20,24},{24,28},{28,16},{32,36},... | collective-permute-start | bytes 786440 | tf_op jit(solution)/shard_map/ppermute | solution.py:266
  43.8 15.1 %copy-start.1 = (bf16[512,128]{1,0:T(8,128)(2,1)S(1)}, bf16[512,128]{1,0:T(8,128)(2,1)}, u32[]{:S(2)}) copy-start(bf16[512,128]{1,0:T(8,128)(2,1)} %get-tuple-element.11.own) | copy-start | bytes 393220
  43.8 7.7 %collective-permute-start.4 = (bf16[1024,128]{1,0:T(8,128)(2,1)S(1)}, bf16[1024,128]{1,0:T(8,128)(2,1)S(1)}, u32[]{:S(2)}, u32[]{:S(2)}) collective-permute-start(bf16[1024,128]{1,0:T(8,128)(2,1)S(1)} %get-tuple-element.15), channel_id=1, source_target_pairs={{0,12},{4,0},{8,4},{12,8},{16,28},{20,16},{24,20},{28,24},{32,44},... | collective-permute-start | bytes 786440 | tf_op jit(solution)/shard_map/ppermute | solution.py:266
  60.8 9.5 %collective-permute-start.6 = (bf16[32,2048]{1,0:T(8,128)(2,1)S(1)}, bf16[32,2048]{1,0:T(8,128)(2,1)S(1)}, u32[]{:S(2)}, u32[]{:S(2)}) collective-permute-start(bf16[32,2048]{1,0:T(8,128)(2,1)S(1)} %shard_map.97), channel_id=1, source_target_pairs={{0,3},{1,2},{2,1},{3,0},{4,7},{5,6},{6,5},{7,4},{8,11},{9,10},{10,... | collective-permute-start | bytes 393224 | tf_op jit(solution)/shard_map/ppermute | solution.py:286
  66.9 7.1 %collective-permute-start.5 = (bf16[32,2048]{1,0:T(8,128)(2,1)S(1)}, bf16[32,2048]{1,0:T(8,128)(2,1)S(1)}, u32[]{:S(2)}, u32[]{:S(2)}) collective-permute-start(bf16[32,2048]{1,0:T(8,128)(2,1)S(1)} %shard_map.95), channel_id=1, source_target_pairs={{0,2},{1,3},{2,0},{3,1},{4,6},{5,7},{6,4},{7,5},{8,10},{9,11},{10,... | collective-permute-start | bytes 393224 | tf_op jit(solution)/shard_map/ppermute | solution.py:286
  72.1 3.7 %collective-permute-start.7 = (bf16[32,2048]{1,0:T(8,128)(2,1)S(1)}, bf16[32,2048]{1,0:T(8,128)(2,1)S(1)}, u32[]{:S(2)}, u32[]{:S(2)}) collective-permute-start(bf16[32,2048]{1,0:T(8,128)(2,1)S(1)} %shard_map.98), channel_id=1, source_target_pairs={{0,1},{1,0},{2,3},{3,2},{4,5},{5,4},{6,7},{7,6},{8,9},{9,8},{10,11... | collective-permute-start | bytes 393224 | tf_op jit(solution)/shard_map/ppermute | solution.py:286

commit v8 on v7

--- a/solution.py
+++ b/solution.py
@@ -21,6 +21,7 @@
 GROUPS = 2
 KV = 4
 RING = 4
+ORDER = (2, 1, 3)
 NEAR = 8
 FAR = BLOCKS // NEAR
 ROWS = TOK // KV
@@ -89,7 +90,7 @@
     mem[...] = jnp.broadcast_to(both[None], mem.shape)
 
 
-def query_kernel(bs, freqs, q, after, rotq, scr):
+def query_kernel(bs, freqs, q, rotq, scr):
     me = lax.axis_index("ctx")
     cosine, sine = turn_tables(bs[me], freqs[0:1, :])
     scr[...] = q[...].astype(F32)
@@ -97,13 +98,13 @@
         rotq[h] = turn(scr[:, h, :], cosine, sine, MSCALE * SCALE2)
 
 
-def ring_kernel(own, row1, row2, mem, r1, r2, r3, far, scr):
+def ring_kernel(own, row1, row2, mem, ra, rb, rc, far, scr):
     me = lax.rem(lax.axis_index("ctx"), RING)
     scr[...] = mem[...].astype(F32)
     kinds = 2 * GROUPS * SLOTS
     slots = jnp.concatenate([scr[:, r, :] for r in range(kinds)], axis=0).astype(BF)
     far[...] = jnp.broadcast_to(slots[None], far.shape)
-    for s, out in enumerate((r1, r2, r3), 1):
+    for s, out in zip(ORDER, (ra, rb, rc)):
         out[TOKP:, :] = row1[...]
 
         @pl.when(me + s < RING)
@@ -160,18 +161,17 @@
     return parts[0] if len(parts) == 1 else jnp.concatenate(parts, axis=0)
 
 
-def chunk_kernel(off, rotq, bias, own, row1, row2, r1, r2, r3, mem, *rest):
+def chunk_kernel(offs, rotq, bias, own, row1, row2, r1, r2, r3, mem, *rest):
     refs = {"own": own, "row1": row1, "row2": row2, 1: r1, 2: r2, 3: r3, "mem": mem}
-    out, s = rest[-2:]
-    dest = lax.axis_index("kv") ^ off
-    first = pl.multiple_of(dest * ROWS, ROWS)
+    outs, s = rest[-1 - len(offs) : -1], rest[-1]
+    firsts = [pl.multiple_of((lax.axis_index("kv") ^ o) * ROWS, ROWS) for o in offs]
     heads = HEADS // GROUPS
     r = lax.broadcasted_iota(jnp.int32, (heads * ROWS, TOK), 0) & (ROWS - 1)
     c = lax.broadcasted_iota(jnp.int32, (heads * ROWS, TOK), 1)
-    unit = jnp.where(r + first == c, 1.0, 0.0).astype(BF)
+    unit = jnp.concatenate([jnp.where(r + f == c, 1.0, 0.0).astype(BF) for f in firsts], axis=0)
     for g in range(GROUPS):
         q = jnp.concatenate(
-            [rotq[g * heads + i, pl.ds(first, ROWS), :] for i in range(heads)], axis=0
+            [rotq[g * heads + i, pl.ds(f, ROWS), :] for f in firsts for i in range(heads)], axis=0
         )
         qa = jnp.concatenate([q, unit], axis=1)
         high = None
@@ -186,15 +186,16 @@
         top = jnp.max(high, axis=1, keepdims=True)
         mixed = None
         for lo, size, tile in key_tiles():
-            w = jnp.exp2((s[g, :, lo : lo + size] - top).astype(BF))
+            w = jnp.exp2(s[g, :, lo : lo + size] - top).astype(BF)
             v = gather_tile(refs, tile, GROUPS + g)
             va = jnp.concatenate([v, jnp.ones((size, HD), BF)], axis=1)
             part = jnp.dot(w, va, preferred_element_type=F32)
             mixed = part if mixed is None else mixed + part
         res = (mixed[:, :HD] / mixed[:, HD:]).astype(BF)
-        for i in range(heads):
-            h = g * heads + i
-            out[:, h * HD : (h + 1) * HD] = res[i * ROWS : (i + 1) * ROWS, :]
+        for n, out in enumerate(outs):
+            for i in range(heads):
+                h, at = g * heads + i, (n * heads + i) * ROWS
+                out[:, h * HD : (h + 1) * HD] = res[at : at + ROWS, :]
 
 
 def join_kernel(a, b, c, d, out, sem):
@@ -254,6 +255,11 @@
         for d in (RING, 2 * RING)
     )
     mem = lax.all_to_all(mem, "ctx", 0, 0, axis_index_groups=near)
+    rotq = call(
+        query_kernel, shape(HEADS, TOK, HD), [pltpu.VMEM((TOK, HEADS, HD), F32)], 10**3,
+        (SM, VM, VM),
+        block_start, freqs, queries,
+    )
     bias = call(bias_kernel, shape(KEYS, TOK), [], 10**3, (SM,), block_start)
     *rings, far = call(
         ring_kernel,
@@ -264,30 +270,28 @@
     mem = lax.all_to_all(far, "ctx", 0, 0, axis_index_groups=strided)
     turned = {
         s: lax.ppermute(
-            rings[s - 1], "ctx", [(i, i // RING * RING + (i + s) % RING) for i in range(BLOCKS)]
+            x, "ctx", [(i, i // RING * RING + (i + s) % RING) for i in range(BLOCKS)]
         )
-        for s in (2, 1, 3)
+        for s, x in zip(ORDER, rings)
     }
     rings = [turned[s] for s in (1, 2, 3)]
-    rotq = call(
-        query_kernel, shape(HEADS, TOK, HD), [pltpu.VMEM((TOK, HEADS, HD), F32)], 10**10,
-        (SM, VM, VM, pl.ANY),
-        block_start, freqs, queries, turned[2],
-    )
-    parts = []
-    for off in (3, 2, 1, 0):
-        after = parts[-2:-1]
-        part = call(
-            functools.partial(chunk_kernel, off), shape(ROWS, HEADS * HD),
-            [pltpu.VMEM((GROUPS, HEADS // GROUPS * ROWS, KEYS), F32)], 10**6,
-            (VM,) * 9 + (pl.ANY,) * len(after), rotq, bias, own, row1, row2, *rings, mem, *after,
+    parts = {}
+    part = None
+    for offs in ((3, 2), (1, 0)):
+        got = call(
+            functools.partial(chunk_kernel, offs), (shape(ROWS, HEADS * HD),) * len(offs),
+            [pltpu.VMEM((GROUPS, len(offs) * HEADS // GROUPS * ROWS, KEYS), F32)], 10**6,
+            (VM,) * 9 + (pl.ANY,) * (part is not None),
+            rotq, bias, own, row1, row2, *rings, mem, *([] if part is None else [part]),
         )
-        if off:
-            part = lax.ppermute(part, "kv", [(i, i ^ off) for i in range(KV)])
-        parts.append(part)
+        for off, part in zip(offs, got):
+            if off:
+                part = lax.ppermute(part, "kv", [(i, i ^ off) for i in range(KV)])
+            parts[off] = part
+        part = parts[offs[0]]
     return call(
         join_kernel, shape(ROWS, KV * HEADS * HD), [pltpu.SemaphoreType.DMA((KV,))], 10**8,
-        (VM,) * 4, *parts[::-1], out_space=HB,
+        (VM,) * 4, *(parts[i] for i in range(KV)), out_space=HB,
     )
 
 

time: 77.2 us -> 75.2 us (0.974)
  waiting for transfers between devices: 11.3 us -> 8.12 us
  starting transfers between devices: 38.1 us -> 39.8 us
  Pallas kernels: 13.9 us -> 13.1 us
    all_to_all x1, waiting for transfers between devices: 7.42 us -> 1.61 us  [shards(): mem = lax.all_to_all(far, 'ctx', 0, 0, axis_index_groups=strided)]
    ppermute x3, waiting for transfers between devices: 1.68 us -> 5.09 us  [shards(): lax.ppermute(x, 'ctx', [(i, i // RING * RING + (i + s) % RING) for i in r...]
    all_to_all x1, starting transfers between devices: 6.58 us -> 9.04 us  [shards(): mem = lax.all_to_all(far, 'ctx', 0, 0, axis_index_groups=strided)]
    ppermute x3, starting transfers between devices: 11.3 us -> 9.06 us  [shards(): lax.ppermute(x, 'ctx', [(i, i // RING * RING + (i + s) % RING) for i in r...]
    ppermute x2, waiting for transfers between devices: 2.24 us -> 0.46 us  [shards(): lax.ppermute(own, 'ctx', [((i - d) % BLOCKS, i) for i in range(BLOCKS)])]
    ppermute x3, starting transfers between devices: 9.64 us -> 11.1 us  [shards(): part = lax.ppermute(part, 'kv', [(i, i ^ off) for i in range(KV)])]
    ppermute x3, waiting for transfers between devices: 0.01 us -> 0.96 us  [shards(): part = lax.ppermute(part, 'kv', [(i, i ^ off) for i in range(KV)])]
    pallas_call x9 -> x7, Pallas kernels: 13.9 us -> 13.1 us  [call(): pl.pallas_call(kernel, out_shape=out_shape, in_specs=[pl.BlockSpec(memory...]
  transfers between devices with their start and end apart: 9 -> 9, of which waited for: 4 -> 5; matrix products, arithmetic and copies ran while one was open for 0% -> 0% of each run, Pallas kernels for 10% -> 7%
where the time goes in v8:
time: 75.2 us; the launch traced here: 74.7 us
  starting transfers between devices  39.8 us (53%)
  Pallas kernels  13.1 us (17%)
  blocking collectives  12.5 us (17%)
  waiting for transfers between devices  8.12 us (11%)
  local copies, waits for them, and re-layouts  0.93 us (1%)
    pallas_call x7, Pallas kernels, call(): pl.pallas_call(kernel, out_shape=out_shape, in_specs=[pl.BlockSpec(memory...  13.1 us
    all_to_all x1, blocking collectives, shards(): mem = lax.all_to_all(mem, 'ctx', 0, 0, axis_index_groups=near)  12.5 us
    ppermute x3, starting transfers between devices, shards(): part = lax.ppermute(part, 'kv', [(i, i ^ off) for i in range(KV)])  11.1 us
    ppermute x2, starting transfers between devices, shards(): lax.ppermute(own, 'ctx', [((i - d) % BLOCKS, i) for i in range(BLOCKS)])  10.6 us
    ppermute x3, starting transfers between devices, shards(): lax.ppermute(x, 'ctx', [(i, i // RING * RING + (i + s) % RING) for i in r...  9.06 us
    all_to_all x1, starting transfers between devices, shards(): mem = lax.all_to_all(far, 'ctx', 0, 0, axis_index_groups=strided)  9.04 us
    ppermute x3, waiting for transfers between devices, shards(): lax.ppermute(x, 'ctx', [(i, i // RING * RING + (i + s) % RING) for i in r...  5.09 us
    all_to_all x1, waiting for transfers between devices, shards(): mem = lax.all_to_all(far, 'ctx', 0, 0, axis_index_groups=strided)  1.61 us
  transfers between devices with their start and end apart: 9, of which 5 were waited for; matrix products, arithmetic and copies ran while one was open for 0% of the time, Pallas kernels for 7%

profile of v8, /device:TPU:1, one launch (start us, length us, event | category | flops | bytes accessed | tf_op | source)
XLA Modules:
  0.0 74.7 jit_solution(4991472707751497002)
XLA Ops:
  0.0 2.5 %shard_map.93 = (bf16[512,128]{1,0:T(8,128)(2,1)}, bf16[8,16,128]{2,1,0:T(8,128)(2,1)}) custom-call(s32[128]{0:T(128)} %bs.5, f32[8,128]{1,0:T(8,128)} %constant.2.clone.freqs, bf16[128,2,128]{2,1,0:T(2,128)(2,1)} %k.1, bf16[128,2,128]{2,1,0:T(2,128)(2,1)} %v.1, f32[32,128]{1,0:T(8,128)} %dk.1, f32[128,128]{1,0:T(8,128)} %pk.1, f32[32,128]{1,0:T(8,128)} %dv.1, ...), custom_call_target="tpu_custom_call" | custom-call | flops 1000000000 | bytes 1024 | tf_op jit(solution)/shard_map/pallas_call | solution.py:217
  2.5 4.8 %collective-permute-start = (bf16[512,128]{1,0:T(8,128)(2,1)}, bf16[512,128]{1,0:T(8,128)(2,1)S(1)}, u32[]{:S(2)}, u32[]{:S(2)}) collective-permute-start(bf16[512,128]{1,0:T(8,128)(2,1)} %get-tuple-element.15.own), channel_id=1, source_target_pairs={{496,0},{500,4},{504,8},{508,12},{0,16},{4,20},{8,24},{12,28},{16,... | collective-permute-start | bytes 393224 | tf_op jit(solution)/shard_map/ppermute | solution.py:254
  7.4 5.8 %collective-permute-start.1 = (bf16[512,128]{1,0:T(8,128)(2,1)}, bf16[512,128]{1,0:T(8,128)(2,1)S(1)}, u32[]{:S(2)}, u32[]{:S(2)}) collective-permute-start(bf16[512,128]{1,0:T(8,128)(2,1)} %get-tuple-element.15.own), channel_id=1, source_target_pairs={{480,0},{484,4},{488,8},{492,12},{496,16},{500,20},{504,24},{508,2... | collective-permute-start | bytes 393224 | tf_op jit(solution)/shard_map/ppermute | solution.py:254
  13.2 12.5 %all_to_all.10.mem = bf16[8,16,128]{2,1,0:T(8,128)(2,1)S(1)} all-to-all(bf16[8,16,128]{2,1,0:T(8,128)(2,1)} %get-tuple-element.16), channel_id=1, replica_groups={{0,4,8,12,16,20,24,28},{32,36,40,44,48,52,56,60},{64,68,72,76,80,84,88,..., dimensions={0} | all-to-all | bytes 65536 | tf_op jit(solution)/shard_map/all_to_all | solution.py:257
  25.6 0.0 collective-permute-done.row1
  25.7 0.5 collective-permute-done.1.row2
  26.1 0.0 copy-start
  26.1 0.9 %copy-done = bf16[512,128]{1,0:T(8,128)(2,1)S(1)} copy-done((bf16[512,128]{1,0:T(8,128)(2,1)S(1)}, bf16[512,128]{1,0:T(8,128)(2,1)}, u32[]{:S(2)}) %copy-start) | copy-done | bytes 131096
  27.0 1.1 %shard_map.94 = (bf16[1024,128]{1,0:T(8,128)(2,1)}, bf16[1024,128]{1,0:T(8,128)(2,1)}, bf16[1024,128]{1,0:T(8,128)(2,1)S(1)}, bf16[16,128,128]{2,1,0:T(8,128)(2,1)}) custom-call(bf16[512,128]{1,0:T(8,128)(2,1)S(1)} %copy-done, bf16[512,128]{1,0:T(8,128)(2,1)S(1)} %collective-permute-done.row1, bf16[512,128]{1,0:T(8,128)(2,1)S(1)} %collective-permute-done.1.row2, ...), custom_call_target="tpu_custom_call" | custom-call | flops 1000 | bytes 1024 | tf_op jit(solution)/shard_map/pallas_call | solution.py:217
  28.1 0.0 copy-start.2
  28.1 9.0 %all-to-all-start.1 = ((bf16[16,128,128]{2,1,0:T(8,128)(2,1)}), bf16[16,128,128]{2,1,0:T(8,128)(2,1)S(1)}, u32[]{:S(2)}, u32[]{:S(2)}) async-start(bf16[16,128,128]{2,1,0:T(8,128)(2,1)} %get-tuple-element.20), calls=%async_computation.1 | async-start | bytes 1048576 | tf_op jit(solution)/shard_map/all_to_all | solution.py:270
  37.2 2.5 %collective-permute-start.2 = (bf16[1024,128]{1,0:T(8,128)(2,1)}, bf16[1024,128]{1,0:T(8,128)(2,1)S(1)}, u32[]{:S(2)}, u32[]{:S(2)}) collective-permute-start(bf16[1024,128]{1,0:T(8,128)(2,1)} %get-tuple-element.17), channel_id=1, source_target_pairs={{0,4},{4,8},{8,12},{12,0},{16,20},{20,24},{24,28},{28,16},{32,36},... | collective-permute-start | bytes 786440 | tf_op jit(solution)/shard_map/ppermute | solution.py:272
  39.7 0.0 copy-start.4
  39.7 3.5 %collective-permute-start.3 = (bf16[1024,128]{1,0:T(8,128)(2,1)}, bf16[1024,128]{1,0:T(8,128)(2,1)S(1)}, u32[]{:S(2)}, u32[]{:S(2)}) collective-permute-start(bf16[1024,128]{1,0:T(8,128)(2,1)} %get-tuple-element.18), channel_id=1, source_target_pairs={{0,8},{4,12},{8,0},{12,4},{16,24},{20,28},{24,16},{28,20},{32,40},... | collective-permute-start | bytes 786440 | tf_op jit(solution)/shard_map/ppermute | solution.py:272
  43.2 0.0 copy-start.3
  43.2 3.1 %collective-permute-start.4 = (bf16[1024,128]{1,0:T(8,128)(2,1)S(1)}, bf16[1024,128]{1,0:T(8,128)(2,1)S(1)}, u32[]{:S(2)}, u32[]{:S(2)}) collective-permute-start(bf16[1024,128]{1,0:T(8,128)(2,1)S(1)} %get-tuple-element.19), channel_id=1, source_target_pairs={{0,12},{4,0},{8,4},{12,8},{16,28},{20,16},{24,20},{28,24},{32,44},... | collective-permute-start | bytes 786440 | tf_op jit(solution)/shard_map/ppermute | solution.py:272
  46.3 0.0 copy-done.4
  46.3 0.8 %shard_map.92.bias = bf16[1664,128]{1,0:T(8,128)(2,1)S(1)} custom-call(s32[128]{0:T(128)S(1)} %copy-done.4), custom_call_target="tpu_custom_call" | custom-call | flops 1000 | bytes 1024 | tf_op jit(solution)/shard_map/pallas_call | solution.py:217
  47.1 0.0 copy-done.2
  47.1 0.0 copy-done.3
  47.1 0.0 copy-start.1
  47.1 1.6 %shard_map.91.rotq = bf16[16,128,128]{2,1,0:T(8,128)(2,1)S(1)} custom-call(s32[128]{0:T(128)S(1)} %copy-done.4, f32[8,128]{1,0:T(8,128)S(1)} %copy-done.3, bf16[128,16,128]{2,1,0:T(8,128)(2,1)S(1)} %copy-done.2), custom_call_target="tpu_custom_call" | custom-call | flops 1000 | bytes 1024 | tf_op jit(solution)/shard_map/pallas_call | solution.py:217
  48.7 0.0 collective-permute-done.2.r1
  48.7 2.9 %collective-permute-done.3.r2 = bf16[1024,128]{1,0:T(8,128)(2,1)S(1)} collective-permute-done((bf16[1024,128]{1,0:T(8,128)(2,1)}, bf16[1024,128]{1,0:T(8,128)(2,1)S(1)}, u32[]{:S(2)}, u32[]{:S(2)}) %collective-permute-start.3) | collective-permute-done | bytes 262176 | tf_op jit(solution)/shard_map/ppermute | solution.py:272
  51.6 2.2 %collective-permute-done.4.r3 = bf16[1024,128]{1,0:T(8,128)(2,1)S(1)} collective-permute-done((bf16[1024,128]{1,0:T(8,128)(2,1)S(1)}, bf16[1024,128]{1,0:T(8,128)(2,1)S(1)}, u32[]{:S(2)}, u32[]{:S(2)}) %collective-permute-start.4) | collective-permute-done | bytes 262176 | tf_op jit(solution)/shard_map/ppermute | solution.py:272
  53.8 1.6 %all-to-all-done.1.mem = bf16[16,128,128]{2,1,0:T(8,128)(2,1)S(1)} async-done(((bf16[16,128,128]{2,1,0:T(8,128)(2,1)}), bf16[16,128,128]{2,1,0:T(8,128)(2,1)S(1)}, u32[]{:S(2)}, u32[]{:S(2)}) %all-to-all-start.1) | async-done | bytes 524320 | tf_op jit(solution)/shard_map/all_to_all | solution.py:270
  55.4 0.0 copy-done.1
  55.4 3.1 %shard_map.95 = (bf16[32,2048]{1,0:T(8,128)(2,1)S(1)}, bf16[32,2048]{1,0:T(8,128)(2,1)S(1)}) custom-call(bf16[16,128,128]{2,1,0:T(8,128)(2,1)S(1)} %shard_map.91.rotq, bf16[1664,128]{1,0:T(8,128)(2,1)S(1)} %shard_map.92.bias, bf16[512,128]{1,0:T(8,128)(2,1)S(1)} %copy-done.1, bf16[512,128]{1,0:T(8,128)(2,1)S(1)} %collective-permute-done.row1, ...), custom_call_target="tpu_custom_call" | custom-call | flops 1000000 | bytes 1024 | tf_op jit(solution)/shard_map/pallas_call | solution.py:217
  58.6 4.4 %collective-permute-start.5 = (bf16[32,2048]{1,0:T(8,128)(2,1)S(1)}, bf16[32,2048]{1,0:T(8,128)(2,1)S(1)}, u32[]{:S(2)}, u32[]{:S(2)}) collective-permute-start(bf16[32,2048]{1,0:T(8,128)(2,1)S(1)} %get-tuple-element.21), channel_id=1, source_target_pairs={{0,3},{1,2},{2,1},{3,0},{4,7},{5,6},{6,5},{7,4},{8,11},{9,10},{10,... | collective-permute-start | bytes 393224 | tf_op jit(solution)/shard_map/ppermute | solution.py:289
  63.0 3.7 %collective-permute-start.7 = (bf16[32,2048]{1,0:T(8,128)(2,1)S(1)}, bf16[32,2048]{1,0:T(8,128)(2,1)S(1)}, u32[]{:S(2)}, u32[]{:S(2)}) collective-permute-start(bf16[32,2048]{1,0:T(8,128)(2,1)S(1)} %get-tuple-element.24), channel_id=1, source_target_pairs={{0,2},{1,3},{2,0},{3,1},{4,6},{5,7},{6,4},{7,5},{8,10},{9,11},{10,... | collective-permute-start | bytes 393224 | tf_op jit(solution)/shard_map/ppermute | solution.py:289
  66.7 0.0 collective-permute-done.5.rest_0_.d
  66.7 3.2 %shard_map.96 = (bf16[32,2048]{1,0:T(8,128)(2,1)S(1)}, bf16[32,2048]{1,0:T(8,128)(2,1)S(1)}) custom-call(bf16[16,128,128]{2,1,0:T(8,128)(2,1)S(1)} %shard_map.91.rotq, bf16[1664,128]{1,0:T(8,128)(2,1)S(1)} %shard_map.92.bias, bf16[512,128]{1,0:T(8,128)(2,1)S(1)} %copy-done.1, bf16[512,128]{1,0:T(8,128)(2,1)S(1)} %collective-permute-done.row1, ...), custom_call_target="tpu_custom_call" | custom-call | flops 1000000 | bytes 1024 | tf_op jit(solution)/shard_map/pallas_call | solution.py:217
  69.9 3.0 %collective-permute-start.6 = (bf16[32,2048]{1,0:T(8,128)(2,1)S(1)}, bf16[32,2048]{1,0:T(8,128)(2,1)S(1)}, u32[]{:S(2)}, u32[]{:S(2)}) collective-permute-start(bf16[32,2048]{1,0:T(8,128)(2,1)S(1)} %get-tuple-element.23), channel_id=1, source_target_pairs={{0,1},{1,0},{2,3},{3,2},{4,5},{5,4},{6,7},{7,6},{8,9},{9,8},{10,11... | collective-permute-start | bytes 393224 | tf_op jit(solution)/shard_map/ppermute | solution.py:289
  72.9 0.0 collective-permute-done.7.c
  72.9 1.0 %collective-permute-done.6.b = bf16[32,2048]{1,0:T(8,128)(2,1)S(1)} collective-permute-done((bf16[32,2048]{1,0:T(8,128)(2,1)S(1)}, bf16[32,2048]{1,0:T(8,128)(2,1)S(1)}, u32[]{:S(2)}, u32[]{:S(2)}) %collective-permute-start.6) | collective-permute-done | bytes 131104 | tf_op jit(solution)/shard_map/ppermute | solution.py:289
  73.8 0.8 %shard_map.97 = bf16[32,8192]{1,0:T(8,128)(2,1)} custom-call(bf16[32,2048]{1,0:T(8,128)(2,1)S(1)} %get-tuple-element.22.a, bf16[32,2048]{1,0:T(8,128)(2,1)S(1)} %collective-permute-done.6.b, bf16[32,2048]{1,0:T(8,128)(2,1)S(1)} %collective-permute-done.7.c, bf16[32,2048]{1,0:T(8,128)(2,1)S(1)} %collective-permute-done.5.rest_0_.d), custom_call_target="tpu_custom_call" | custom-call | flops 100000000 | bytes 1024 | tf_op jit(solution)/shard_map/pallas_call | solution.py:217
Async XLA Ops:
  2.5 23.1 %collective-permute-start = (bf16[512,128]{1,0:T(8,128)(2,1)}, bf16[512,128]{1,0:T(8,128)(2,1)S(1)}, u32[]{:S(2)}, u32[]{:S(2)}) collective-permute-start(bf16[512,128]{1,0:T(8,128)(2,1)} %get-tuple-element.15.own), channel_id=1, source_target_pairs={{496,0},{500,4},{504,8},{508,12},{0,16},{4,20},{8,24},{12,28},{16,... | collective-permute-start | bytes 393224 | tf_op jit(solution)/shard_map/ppermute | solution.py:254
  7.4 18.7 %collective-permute-start.1 = (bf16[512,128]{1,0:T(8,128)(2,1)}, bf16[512,128]{1,0:T(8,128)(2,1)S(1)}, u32[]{:S(2)}, u32[]{:S(2)}) collective-permute-start(bf16[512,128]{1,0:T(8,128)(2,1)} %get-tuple-element.15.own), channel_id=1, source_target_pairs={{480,0},{484,4},{488,8},{492,12},{496,16},{500,20},{504,24},{508,2... | collective-permute-start | bytes 393224 | tf_op jit(solution)/shard_map/ppermute | solution.py:254
  26.1 0.9 %copy-start = (bf16[512,128]{1,0:T(8,128)(2,1)S(1)}, bf16[512,128]{1,0:T(8,128)(2,1)}, u32[]{:S(2)}) copy-start(bf16[512,128]{1,0:T(8,128)(2,1)} %get-tuple-element.15.own) | copy-start | bytes 393220
  28.1 19.0 %copy-start.2 = (bf16[128,16,128]{2,1,0:T(8,128)(2,1)S(1)}, bf16[128,16,128]{2,1,0:T(8,128)(2,1)}, u32[]{:S(2)}) copy-start(bf16[128,16,128]{2,1,0:T(8,128)(2,1)} %q.1) | copy-start | bytes 1572868
  28.1 27.3 %all-to-all-start.1 = ((bf16[16,128,128]{2,1,0:T(8,128)(2,1)}), bf16[16,128,128]{2,1,0:T(8,128)(2,1)S(1)}, u32[]{:S(2)}, u32[]{:S(2)}) async-start(bf16[16,128,128]{2,1,0:T(8,128)(2,1)} %get-tuple-element.20), calls=%async_computation.1 | async-start | bytes 1048576 | tf_op jit(solution)/shard_map/all_to_all | solution.py:270
  37.2 11.6 %collective-permute-start.2 = (bf16[1024,128]{1,0:T(8,128)(2,1)}, bf16[1024,128]{1,0:T(8,128)(2,1)S(1)}, u32[]{:S(2)}, u32[]{:S(2)}) collective-permute-start(bf16[1024,128]{1,0:T(8,128)(2,1)} %get-tuple-element.17), channel_id=1, source_target_pairs={{0,4},{4,8},{8,12},{12,0},{16,20},{20,24},{24,28},{28,16},{32,36},... | collective-permute-start | bytes 786440 | tf_op jit(solution)/shard_map/ppermute | solution.py:272
  39.7 6.6 %copy-start.4 = (s32[128]{0:T(128)S(1)}, s32[128]{0:T(128)}, u32[]{:S(2)}) copy-start(s32[128]{0:T(128)} %bs.5) | copy-start | bytes 1540
  39.7 11.9 %collective-permute-start.3 = (bf16[1024,128]{1,0:T(8,128)(2,1)}, bf16[1024,128]{1,0:T(8,128)(2,1)S(1)}, u32[]{:S(2)}, u32[]{:S(2)}) collective-permute-start(bf16[1024,128]{1,0:T(8,128)(2,1)} %get-tuple-element.18), channel_id=1, source_target_pairs={{0,8},{4,12},{8,0},{12,4},{16,24},{20,28},{24,16},{28,20},{32,40},... | collective-permute-start | bytes 786440 | tf_op jit(solution)/shard_map/ppermute | solution.py:272
  43.2 3.9 %copy-start.3 = (f32[8,128]{1,0:T(8,128)S(1)}, f32[8,128]{1,0:T(8,128)}, u32[]{:S(2)}) copy-start(f32[8,128]{1,0:T(8,128)} %constant.2.clone.freqs) | copy-start | bytes 12292
  43.2 10.6 %collective-permute-start.4 = (bf16[1024,128]{1,0:T(8,128)(2,1)S(1)}, bf16[1024,128]{1,0:T(8,128)(2,1)S(1)}, u32[]{:S(2)}, u32[]{:S(2)}) collective-permute-start(bf16[1024,128]{1,0:T(8,128)(2,1)S(1)} %get-tuple-element.19), channel_id=1, source_target_pairs={{0,12},{4,0},{8,4},{12,8},{16,28},{20,16},{24,20},{28,24},{32,44},... | collective-permute-start | bytes 786440 | tf_op jit(solution)/shard_map/ppermute | solution.py:272
  47.1 8.3 %copy-start.1 = (bf16[512,128]{1,0:T(8,128)(2,1)S(1)}, bf16[512,128]{1,0:T(8,128)(2,1)}, u32[]{:S(2)}) copy-start(bf16[512,128]{1,0:T(8,128)(2,1)} %get-tuple-element.15.own) | copy-start | bytes 393220
  58.6 8.1 %collective-permute-start.5 = (bf16[32,2048]{1,0:T(8,128)(2,1)S(1)}, bf16[32,2048]{1,0:T(8,128)(2,1)S(1)}, u32[]{:S(2)}, u32[]{:S(2)}) collective-permute-start(bf16[32,2048]{1,0:T(8,128)(2,1)S(1)} %get-tuple-element.21), channel_id=1, source_target_pairs={{0,3},{1,2},{2,1},{3,0},{4,7},{5,6},{6,5},{7,4},{8,11},{9,10},{10,... | collective-permute-start | bytes 393224 | tf_op jit(solution)/shard_map/ppermute | solution.py:289
  63.0 9.9 %collective-permute-start.7 = (bf16[32,2048]{1,0:T(8,128)(2,1)S(1)}, bf16[32,2048]{1,0:T(8,128)(2,1)S(1)}, u32[]{:S(2)}, u32[]{:S(2)}) collective-permute-start(bf16[32,2048]{1,0:T(8,128)(2,1)S(1)} %get-tuple-element.24), channel_id=1, source_target_pairs={{0,2},{1,3},{2,0},{3,1},{4,6},{5,7},{6,4},{7,5},{8,10},{9,11},{10,... | collective-permute-start | bytes 393224 | tf_op jit(solution)/shard_map/ppermute | solution.py:289
  69.9 4.0 %collective-permute-start.6 = (bf16[32,2048]{1,0:T(8,128)(2,1)S(1)}, bf16[32,2048]{1,0:T(8,128)(2,1)S(1)}, u32[]{:S(2)}, u32[]{:S(2)}) collective-permute-start(bf16[32,2048]{1,0:T(8,128)(2,1)S(1)} %get-tuple-element.23), channel_id=1, source_target_pairs={{0,1},{1,0},{2,3},{3,2},{4,5},{5,4},{6,7},{7,6},{8,9},{9,8},{10,11... | collective-permute-start | bytes 393224 | tf_op jit(solution)/shard_map/ppermute | solution.py:289

commit v9 on v3

--- a/solution.py
+++ b/solution.py
@@ -163,18 +163,18 @@
     return jnp.concatenate(parts, axis=0)
 
 
-def chunk_kernel(off, rotq, bias, recv, prev, *rest):
-    out, s = rest[-2:]
-    dest = lax.axis_index("kv") ^ off
-    first = pl.multiple_of(dest * ROWS, ROWS)
+def chunk_kernel(offs, rotq, bias, recv, prev, *rest):
+    outs, s = rest[:-1], rest[-1]
+    firsts = [pl.multiple_of((lax.axis_index("kv") ^ o) * ROWS, ROWS) for o in offs]
     heads = HEADS // GROUPS
     r = lax.broadcasted_iota(jnp.int32, (heads * ROWS, TOK), 0) & (ROWS - 1)
     c = lax.broadcasted_iota(jnp.int32, (heads * ROWS, TOK), 1)
-    unit = jnp.where(r + first == c, 1.0, 0.0).astype(BF)
+    unit = jnp.concatenate([jnp.where(r + f == c, 1.0, 0.0).astype(BF) for f in firsts], axis=0)
     slots = 2 * GROUPS * TOK
+    tops = []
     for g in range(GROUPS):
         q = jnp.concatenate(
-            [rotq[g * heads + i, pl.ds(first, ROWS), :] for i in range(heads)], axis=0
+            [rotq[g * heads + i, pl.ds(f, ROWS), :] for f in firsts for i in range(heads)], axis=0
         )
         qa = jnp.concatenate([q, unit], axis=1)
         high = None
@@ -186,18 +186,20 @@
             for i in range(size // HD):
                 part = x[:, i * HD : (i + 1) * HD]
                 high = part if high is None else jnp.maximum(high, part)
-        top = jnp.max(high, axis=1, keepdims=True)
+        tops.append(jnp.max(high, axis=1, keepdims=True))
+    for g in range(GROUPS):
         mixed = None
         for lo, size, tile in key_tiles():
-            w = jnp.exp2((s[g, :, lo : lo + size] - top) * SCALE2).astype(BF)
+            w = jnp.exp2((s[g, :, lo : lo + size] - tops[g]) * SCALE2).astype(BF)
             v = gather_tile(recv, prev, tile, (GROUPS + g) * TOK, slots + (GROUPS + g) * MANY)
             va = jnp.concatenate([v, jnp.ones((size, HD), BF)], axis=1)
             part = jnp.dot(w, va, preferred_element_type=F32)
             mixed = part if mixed is None else mixed + part
         res = (mixed[:, :HD] / mixed[:, HD:]).astype(BF)
-        for i in range(heads):
-            h = g * heads + i
-            out[:, h * HD : (h + 1) * HD] = res[i * ROWS : (i + 1) * ROWS, :]
+        for n, out in enumerate(outs):
+            for i in range(heads):
+                h, at = g * heads + i, (n * heads + i) * ROWS
+                out[:, h * HD : (h + 1) * HD] = res[at : at + ROWS, :]
 
 
 def join_kernel(a, b, c, d, out, sem):
@@ -269,20 +271,20 @@
         (VM, VM), mem, sent, alias={1: 0},
     )
     recv = lax.all_to_all(sent, "ctx", 0, 0, axis_index_groups=octets)
-    parts = []
-    for off in (3, 2, 1, 0):
-        after = parts[-2:-1]
-        part = call(
-            functools.partial(chunk_kernel, off), shape(ROWS, HEADS * HD),
-            [pltpu.VMEM((GROUPS, HEADS // GROUPS * ROWS, KEYS), F32)], 10**6,
-            (VM,) * 4 + (pl.ANY,) * len(after), rotq, bias, recv, prev, *after,
+    parts = {}
+    for offs in ((3, 2), (1, 0)):
+        got = call(
+            functools.partial(chunk_kernel, offs), (shape(ROWS, HEADS * HD),) * len(offs),
+            [pltpu.VMEM((GROUPS, len(offs) * HEADS // GROUPS * ROWS, KEYS), F32)], 10**6,
+            (VM,) * 4, rotq, bias, recv, prev,
         )
-        if off:
-            part = lax.ppermute(part, "kv", [(i, i ^ off) for i in range(KV)])
-        parts.append(part)
+        for off, part in zip(offs, got):
+            if off:
+                part = lax.ppermute(part, "kv", [(i, i ^ off) for i in range(KV)])
+            parts[off] = part
     return call(
         join_kernel, shape(ROWS, KV * HEADS * HD), [pltpu.SemaphoreType.DMA((KV,))], 10**8,
-        (VM,) * 4, *parts[::-1], out_space=HB,
+        (VM,) * 4, *(parts[i] for i in range(KV)), out_space=HB,
     )
 
 

time: 77.3 us -> 75.7 us (0.979)
  Pallas kernels: 13.2 us -> 10.4 us
  waiting for transfers between devices: 9.27 us -> 10.2 us
    pallas_call x10 -> x8, Pallas kernels: 13.2 us -> 10.4 us  [call(): pl.pallas_call(kernel, out_shape=out_shape, in_specs=[pl.BlockSpec(memory...]
    ppermute x3, waiting for transfers between devices: 0.34 us -> 1.31 us  [shards(): part = lax.ppermute(part, 'kv', [(i, i ^ off) for i in range(KV)])]
  transfers between devices with their start and end apart: 5 -> 5, of which waited for: 2 -> 3; matrix products, arithmetic and copies ran while one was open for 0% -> 0% of each run, Pallas kernels for 10% -> 6%
where the time goes in v9:
time: 75.7 us; the launch traced here: 75.4 us
  starting transfers between devices  31.7 us (42%)
  blocking collectives  22.9 us (30%)
  Pallas kernels  10.4 us (14%)
  waiting for transfers between devices  10.2 us (13%)
    all_to_all x1, blocking collectives, shards(): recv = lax.all_to_all(sent, 'ctx', 0, 0, axis_index_groups=octets)  22.9 us
    all_to_all x1, starting transfers between devices, shards(): mem = lax.all_to_all(mem, 'ctx', 0, 0, axis_index_groups=strided)  13.6 us
    ppermute x3, starting transfers between devices, shards(): part = lax.ppermute(part, 'kv', [(i, i ^ off) for i in range(KV)])  11.5 us
    pallas_call x8, Pallas kernels, call(): pl.pallas_call(kernel, out_shape=out_shape, in_specs=[pl.BlockSpec(memory...  10.4 us
    all_to_all x1, waiting for transfers between devices, shards(): mem = lax.all_to_all(mem, 'ctx', 0, 0, axis_index_groups=strided)  8.93 us
    ppermute x1, starting transfers between devices, shards(): lax.ppermute(own, 'ctx', [((i - WIN) % BLOCKS, i) for i in range(BLOCKS)])  6.64 us
  transfers between devices with their start and end apart: 5, of which 3 were waited for; matrix products, arithmetic and copies ran while one was open for 0% of the time, Pallas kernels for 6%

profile of v9, /device:TPU:1, one launch (start us, length us, event | category | flops | bytes accessed | tf_op | source)
XLA Modules:
  0.0 75.4 jit_solution(14012353851904996386)
XLA Ops:
  0.0 0.0 copy-start.3
  0.0 0.0 copy-start.1
  0.0 0.0 copy-start.2
  0.0 2.6 %shard_map.93 = (bf16[512,128]{1,0:T(8,128)(2,1)}, bf16[16,16,128]{2,1,0:T(8,128)(2,1)}) custom-call(s32[128]{0:T(128)} %bs.5, f32[8,128]{1,0:T(8,128)} %constant.2.clone.freqs, bf16[128,2,128]{2,1,0:T(2,128)(2,1)} %k.1, bf16[128,2,128]{2,1,0:T(2,128)(2,1)} %v.1, f32[32,128]{1,0:T(8,128)} %dk.1, f32[128,128]{1,0:T(8,128)} %pk.1, f32[32,128]{1,0:T(8,128)} %dv.1, ...), custom_call_target="tpu_custom_call" | custom-call | flops 1000000000 | bytes 1024 | tf_op jit(solution)/shard_map/pallas_call | solution.py:221
  2.6 6.6 %collective-permute-start = (bf16[512,128]{1,0:T(8,128)(2,1)}, bf16[512,128]{1,0:T(8,128)(2,1)S(1)}, u32[]{:S(2)}, u32[]{:S(2)}) collective-permute-start(bf16[512,128]{1,0:T(8,128)(2,1)} %get-tuple-element.12.own), channel_id=1, source_target_pairs={{480,0},{484,4},{488,8},{492,12},{496,16},{500,20},{504,24},{508,2... | collective-permute-start | bytes 393224 | tf_op jit(solution)/shard_map/ppermute | solution.py:257
  9.3 13.6 %all-to-all-start = ((bf16[16,16,128]{2,1,0:T(8,128)(2,1)}), bf16[16,16,128]{2,1,0:T(8,128)(2,1)S(1)}, u32[]{:S(2)}, u32[]{:S(2)}) async-start(bf16[16,16,128]{2,1,0:T(8,128)(2,1)} %get-tuple-element.11), calls=%async_computation | async-start | bytes 131072 | tf_op jit(solution)/shard_map/all_to_all | solution.py:258
  22.9 0.0 copy-done.1
  22.9 0.7 shard_map.92.bias
  23.6 0.0 copy-done.3
  23.6 0.0 copy-done.2
  23.6 0.0 copy-start
  23.6 1.6 %shard_map.91.rotq = bf16[16,128,128]{2,1,0:T(8,128)(2,1)S(1)} custom-call(s32[128]{0:T(128)S(1)} %copy-done.1, f32[8,128]{1,0:T(8,128)S(1)} %copy-done.3, bf16[128,16,128]{2,1,0:T(8,128)(2,1)S(1)} %copy-done.2), custom_call_target="tpu_custom_call" | custom-call | flops 1000000000 | bytes 1024 | tf_op jit(solution)/shard_map/pallas_call | solution.py:221
  25.2 0.0 collective-permute-done.prev
  25.2 0.0 copy-done
  25.3 0.1 shard_map.94.sent
  25.4 8.9 %all-to-all-done.mem = bf16[16,16,128]{2,1,0:T(8,128)(2,1)S(1)} async-done(((bf16[16,16,128]{2,1,0:T(8,128)(2,1)}), bf16[16,16,128]{2,1,0:T(8,128)(2,1)S(1)}, u32[]{:S(2)}, u32[]{:S(2)}) %all-to-all-start) | async-done | bytes 65568 | tf_op jit(solution)/shard_map/all_to_all | solution.py:258
  34.3 0.1 shard_map.95
  34.4 22.9 %all_to_all.10.recv = bf16[8,768,128]{2,1,0:T(8,128)(2,1)S(1)} all-to-all(bf16[8,768,128]{2,1,0:T(8,128)(2,1)S(1)} %shard_map.95), channel_id=1, replica_groups={{0,4,8,12,16,20,24,28},{32,36,40,44,48,52,56,60},{64,68,72,76,80,84,88,..., dimensions={0} | all-to-all | bytes 3145728 | tf_op jit(solution)/shard_map/all_to_all | solution.py:273
  57.3 2.2 %shard_map.97 = (bf16[32,2048]{1,0:T(8,128)(2,1)S(1)}, bf16[32,2048]{1,0:T(8,128)(2,1)S(1)}) custom-call(bf16[16,128,128]{2,1,0:T(8,128)(2,1)S(1)} %shard_map.91.rotq, bf16[1664,128]{1,0:T(8,128)(2,1)S(1)} %shard_map.92.bias, bf16[8,768,128]{2,1,0:T(8,128)(2,1)S(1)} %all_to_all.10.recv, bf16[512,128]{1,0:T(8,128)(2,1)S(1)} %collective-permute-done.prev), custom_call_target="tpu_custom_call" | custom-call | flops 1000000 | bytes 1024 | tf_op jit(solution)/shard_map/pallas_call | solution.py:221
  59.5 2.1 %collective-permute-start.2 = (bf16[32,2048]{1,0:T(8,128)(2,1)S(1)}, bf16[32,2048]{1,0:T(8,128)(2,1)S(1)}, u32[]{:S(2)}, u32[]{:S(2)}) collective-permute-start(bf16[32,2048]{1,0:T(8,128)(2,1)S(1)} %get-tuple-element.15), channel_id=1, source_target_pairs={{0,2},{1,3},{2,0},{3,1},{4,6},{5,7},{6,4},{7,5},{8,10},{9,11},{10,... | collective-permute-start | bytes 393224 | tf_op jit(solution)/shard_map/ppermute | solution.py:283
  61.6 7.5 %collective-permute-start.3 = (bf16[32,2048]{1,0:T(8,128)(2,1)S(1)}, bf16[32,2048]{1,0:T(8,128)(2,1)S(1)}, u32[]{:S(2)}, u32[]{:S(2)}) collective-permute-start(bf16[32,2048]{1,0:T(8,128)(2,1)S(1)} %get-tuple-element.16), channel_id=1, source_target_pairs={{0,3},{1,2},{2,1},{3,0},{4,7},{5,6},{6,5},{7,4},{8,11},{9,10},{10,... | collective-permute-start | bytes 393224 | tf_op jit(solution)/shard_map/ppermute | solution.py:283
  69.1 2.2 %shard_map.96 = (bf16[32,2048]{1,0:T(8,128)(2,1)S(1)}, bf16[32,2048]{1,0:T(8,128)(2,1)S(1)}) custom-call(bf16[16,128,128]{2,1,0:T(8,128)(2,1)S(1)} %shard_map.91.rotq, bf16[1664,128]{1,0:T(8,128)(2,1)S(1)} %shard_map.92.bias, bf16[8,768,128]{2,1,0:T(8,128)(2,1)S(1)} %all_to_all.10.recv, bf16[512,128]{1,0:T(8,128)(2,1)S(1)} %collective-permute-done.prev), custom_call_target="tpu_custom_call" | custom-call | flops 1000000 | bytes 1024 | tf_op jit(solution)/shard_map/pallas_call | solution.py:221
  71.3 1.9 %collective-permute-start.1 = (bf16[32,2048]{1,0:T(8,128)(2,1)S(1)}, bf16[32,2048]{1,0:T(8,128)(2,1)S(1)}, u32[]{:S(2)}, u32[]{:S(2)}) collective-permute-start(bf16[32,2048]{1,0:T(8,128)(2,1)S(1)} %get-tuple-element.14), channel_id=1, source_target_pairs={{0,1},{1,0},{2,3},{3,2},{4,5},{5,4},{6,7},{7,6},{8,9},{9,8},{10,11... | collective-permute-start | bytes 393224 | tf_op jit(solution)/shard_map/ppermute | solution.py:283
  73.2 0.0 collective-permute-done.2.c
  73.2 0.1 collective-permute-done.3.d
  73.4 1.2 %collective-permute-done.1.b = bf16[32,2048]{1,0:T(8,128)(2,1)S(1)} collective-permute-done((bf16[32,2048]{1,0:T(8,128)(2,1)S(1)}, bf16[32,2048]{1,0:T(8,128)(2,1)S(1)}, u32[]{:S(2)}, u32[]{:S(2)}) %collective-permute-start.1) | collective-permute-done | bytes 131104 | tf_op jit(solution)/shard_map/ppermute | solution.py:283
  74.5 0.8 %shard_map.98 = bf16[32,8192]{1,0:T(8,128)(2,1)} custom-call(bf16[32,2048]{1,0:T(8,128)(2,1)S(1)} %get-tuple-element.13.a, bf16[32,2048]{1,0:T(8,128)(2,1)S(1)} %collective-permute-done.1.b, bf16[32,2048]{1,0:T(8,128)(2,1)S(1)} %collective-permute-done.2.c, bf16[32,2048]{1,0:T(8,128)(2,1)S(1)} %collective-permute-done.3.d), custom_call_target="tpu_custom_call" | custom-call | flops 100000000 | bytes 1024 | tf_op jit(solution)/shard_map/pallas_call | solution.py:221
Async XLA Ops:
  0.0 23.6 %copy-start.3 = (f32[8,128]{1,0:T(8,128)S(1)}, f32[8,128]{1,0:T(8,128)}, u32[]{:S(2)}) copy-start(f32[8,128]{1,0:T(8,128)} %constant.2.clone.freqs) | copy-start | bytes 12292
  0.0 22.9 %copy-start.1 = (s32[128]{0:T(128)S(1)}, s32[128]{0:T(128)}, u32[]{:S(2)}) copy-start(s32[128]{0:T(128)} %bs.5) | copy-start | bytes 1540
  0.0 23.6 %copy-start.2 = (bf16[128,16,128]{2,1,0:T(8,128)(2,1)S(1)}, bf16[128,16,128]{2,1,0:T(8,128)(2,1)}, u32[]{:S(2)}) copy-start(bf16[128,16,128]{2,1,0:T(8,128)(2,1)} %q.1) | copy-start | bytes 1572868
  2.6 22.6 %collective-permute-start = (bf16[512,128]{1,0:T(8,128)(2,1)}, bf16[512,128]{1,0:T(8,128)(2,1)S(1)}, u32[]{:S(2)}, u32[]{:S(2)}) collective-permute-start(bf16[512,128]{1,0:T(8,128)(2,1)} %get-tuple-element.12.own), channel_id=1, source_target_pairs={{480,0},{484,4},{488,8},{492,12},{496,16},{500,20},{504,24},{508,2... | collective-permute-start | bytes 393224 | tf_op jit(solution)/shard_map/ppermute | solution.py:257
  9.3 25.0 %all-to-all-start = ((bf16[16,16,128]{2,1,0:T(8,128)(2,1)}), bf16[16,16,128]{2,1,0:T(8,128)(2,1)S(1)}, u32[]{:S(2)}, u32[]{:S(2)}) async-start(bf16[16,16,128]{2,1,0:T(8,128)(2,1)} %get-tuple-element.11), calls=%async_computation | async-start | bytes 131072 | tf_op jit(solution)/shard_map/all_to_all | solution.py:258
  23.6 1.6 %copy-start = (bf16[512,128]{1,0:T(8,128)(2,1)S(1)}, bf16[512,128]{1,0:T(8,128)(2,1)}, u32[]{:S(2)}) copy-start(bf16[512,128]{1,0:T(8,128)(2,1)} %get-tuple-element.12.own) | copy-start | bytes 393220
  59.5 13.7 %collective-permute-start.2 = (bf16[32,2048]{1,0:T(8,128)(2,1)S(1)}, bf16[32,2048]{1,0:T(8,128)(2,1)S(1)}, u32[]{:S(2)}, u32[]{:S(2)}) collective-permute-start(bf16[32,2048]{1,0:T(8,128)(2,1)S(1)} %get-tuple-element.15), channel_id=1, source_target_pairs={{0,2},{1,3},{2,0},{3,1},{4,6},{5,7},{6,4},{7,5},{8,10},{9,11},{10,... | collective-permute-start | bytes 393224 | tf_op jit(solution)/shard_map/ppermute | solution.py:283
  61.6 11.8 %collective-permute-start.3 = (bf16[32,2048]{1,0:T(8,128)(2,1)S(1)}, bf16[32,2048]{1,0:T(8,128)(2,1)S(1)}, u32[]{:S(2)}, u32[]{:S(2)}) collective-permute-start(bf16[32,2048]{1,0:T(8,128)(2,1)S(1)} %get-tuple-element.16), channel_id=1, source_target_pairs={{0,3},{1,2},{2,1},{3,0},{4,7},{5,6},{6,5},{7,4},{8,11},{9,10},{10,... | collective-permute-start | bytes 393224 | tf_op jit(solution)/shard_map/ppermute | solution.py:283
  71.3 3.2 %collective-permute-start.1 = (bf16[32,2048]{1,0:T(8,128)(2,1)S(1)}, bf16[32,2048]{1,0:T(8,128)(2,1)S(1)}, u32[]{:S(2)}, u32[]{:S(2)}) collective-permute-start(bf16[32,2048]{1,0:T(8,128)(2,1)S(1)} %get-tuple-element.14), channel_id=1, source_target_pairs={{0,1},{1,0},{2,3},{3,2},{4,5},{5,4},{6,7},{7,6},{8,9},{9,8},{10,11... | collective-permute-start | bytes 393224 | tf_op jit(solution)/shard_map/ppermute | solution.py:283

commit v10 on v8

--- a/solution.py
+++ b/solution.py
@@ -95,15 +95,18 @@
     cosine, sine = turn_tables(bs[me], freqs[0:1, :])
     scr[...] = q[...].astype(F32)
     for h in range(HEADS):
-        rotq[h] = turn(scr[:, h, :], cosine, sine, MSCALE * SCALE2)
-
-
-def ring_kernel(own, row1, row2, mem, ra, rb, rc, far, scr):
-    me = lax.rem(lax.axis_index("ctx"), RING)
+        rotq[h] = turn(scr[:, h, :], cosine, sine)
+
+
+def far_kernel(mem, row1, row2, far, scr):
     scr[...] = mem[...].astype(F32)
     kinds = 2 * GROUPS * SLOTS
     slots = jnp.concatenate([scr[:, r, :] for r in range(kinds)], axis=0).astype(BF)
     far[...] = jnp.broadcast_to(slots[None], far.shape)
+
+
+def ring_kernel(own, row1, row2, far, ra, rb, rc):
+    me = lax.rem(lax.axis_index("ctx"), RING)
     for s, out in zip(ORDER, (ra, rb, rc)):
         out[TOKP:, :] = row1[...]
 
@@ -163,12 +166,13 @@
 
 def chunk_kernel(offs, rotq, bias, own, row1, row2, r1, r2, r3, mem, *rest):
     refs = {"own": own, "row1": row1, "row2": row2, 1: r1, 2: r2, 3: r3, "mem": mem}
-    outs, s = rest[-1 - len(offs) : -1], rest[-1]
+    outs, s = rest[:-1], rest[-1]
     firsts = [pl.multiple_of((lax.axis_index("kv") ^ o) * ROWS, ROWS) for o in offs]
     heads = HEADS // GROUPS
     r = lax.broadcasted_iota(jnp.int32, (heads * ROWS, TOK), 0) & (ROWS - 1)
     c = lax.broadcasted_iota(jnp.int32, (heads * ROWS, TOK), 1)
     unit = jnp.concatenate([jnp.where(r + f == c, 1.0, 0.0).astype(BF) for f in firsts], axis=0)
+    tops = []
     for g in range(GROUPS):
         q = jnp.concatenate(
             [rotq[g * heads + i, pl.ds(f, ROWS), :] for f in firsts for i in range(heads)], axis=0
@@ -183,10 +187,11 @@
             for i in range(size // HD):
                 part = x[:, i * HD : (i + 1) * HD]
                 high = part if high is None else jnp.maximum(high, part)
-        top = jnp.max(high, axis=1, keepdims=True)
+        tops.append(jnp.max(high, axis=1, keepdims=True))
+    for g in range(GROUPS):
         mixed = None
         for lo, size, tile in key_tiles():
-            w = jnp.exp2(s[g, :, lo : lo + size] - top).astype(BF)
+            w = jnp.exp2((s[g, :, lo : lo + size] - tops[g]) * SCALE2).astype(BF)
             v = gather_tile(refs, tile, GROUPS + g)
             va = jnp.concatenate([v, jnp.ones((size, HD), BF)], axis=1)
             part = jnp.dot(w, va, preferred_element_type=F32)
@@ -261,13 +266,15 @@
         block_start, freqs, queries,
     )
     bias = call(bias_kernel, shape(KEYS, TOK), [], 10**3, (SM,), block_start)
-    *rings, far = call(
-        ring_kernel,
-        (shape(2 * TOKP, HD),) * (RING - 1) + (shape(FAR, pack * PIECE, HD),),
-        [pltpu.VMEM((NEAR, pack * SLOTS, HD), F32)], 10**3, (VM,) * 4,
-        own, row1, row2, mem,
+    far = call(
+        far_kernel, shape(FAR, pack * PIECE, HD),
+        [pltpu.VMEM((NEAR, pack * SLOTS, HD), F32)], 10**3, (VM, pl.ANY, pl.ANY), mem, row1, row2,
     )
     mem = lax.all_to_all(far, "ctx", 0, 0, axis_index_groups=strided)
+    rings = call(
+        ring_kernel, (shape(2 * TOKP, HD),) * (RING - 1), [], 10**3, (VM,) * 3 + (pl.ANY,),
+        own, row1, row2, far,
+    )
     turned = {
         s: lax.ppermute(
             x, "ctx", [(i, i // RING * RING + (i + s) % RING) for i in range(BLOCKS)]
@@ -276,19 +283,16 @@
     }
     rings = [turned[s] for s in (1, 2, 3)]
     parts = {}
-    part = None
     for offs in ((3, 2), (1, 0)):
         got = call(
             functools.partial(chunk_kernel, offs), (shape(ROWS, HEADS * HD),) * len(offs),
             [pltpu.VMEM((GROUPS, len(offs) * HEADS // GROUPS * ROWS, KEYS), F32)], 10**6,
-            (VM,) * 9 + (pl.ANY,) * (part is not None),
-            rotq, bias, own, row1, row2, *rings, mem, *([] if part is None else [part]),
+            (VM,) * 9, rotq, bias, own, row1, row2, *rings, mem,
         )
         for off, part in zip(offs, got):
             if off:
                 part = lax.ppermute(part, "kv", [(i, i ^ off) for i in range(KV)])
             parts[off] = part
-        part = parts[offs[0]]
     return call(
         join_kernel, shape(ROWS, KV * HEADS * HD), [pltpu.SemaphoreType.DMA((KV,))], 10**8,
         (VM,) * 4, *(parts[i] for i in range(KV)), out_space=HB,

time: 75.2 us -> 71.7 us (0.953)
  Pallas kernels: 13.1 us -> 11.1 us
  local copies, waits for them, and re-layouts: 0.93 us -> 0.02 us
    pallas_call x7 -> x8, Pallas kernels: 13.1 us -> 11.1 us  [call(): pl.pallas_call(kernel, out_shape=out_shape, in_specs=[pl.BlockSpec(memory...]
    unnamed x10 -> x8, local copies, waits for them, and re-layouts: 0.93 us -> 0.02 us
    ppermute x3, starting transfers between devices: 11.1 us -> 10.3 us  [shards(): part = lax.ppermute(part, 'kv', [(i, i ^ off) for i in range(KV)])]
where the time goes in v10:
time: 71.7 us; the launch traced here: 71.2 us
  starting transfers between devices  39.2 us (55%)
  blocking collectives  12.5 us (17%)
  Pallas kernels  11.1 us (15%)
  waiting for transfers between devices  8.23 us (11%)
    all_to_all x1, blocking collectives, shards(): mem = lax.all_to_all(mem, 'ctx', 0, 0, axis_index_groups=near)  12.5 us
    pallas_call x8, Pallas kernels, call(): pl.pallas_call(kernel, out_shape=out_shape, in_specs=[pl.BlockSpec(memory...  11.1 us
    ppermute x2, starting transfers between devices, shards(): lax.ppermute(own, 'ctx', [((i - d) % BLOCKS, i) for i in range(BLOCKS)])  10.6 us
    ppermute x3, starting transfers between devices, shards(): part = lax.ppermute(part, 'kv', [(i, i ^ off) for i in range(KV)])  10.3 us
    ppermute x3, starting transfers between devices, shards(): lax.ppermute(x, 'ctx', [(i, i // RING * RING + (i + s) % RING) for i in r...  9.2 us
    all_to_all x1, starting transfers between devices, shards(): mem = lax.all_to_all(far, 'ctx', 0, 0, axis_index_groups=strided)  9.04 us
    ppermute x3, waiting for transfers between devices, shards(): lax.ppermute(x, 'ctx', [(i, i // RING * RING + (i + s) % RING) for i in r...  4.79 us
    all_to_all x1, waiting for transfers between devices, shards(): mem = lax.all_to_all(far, 'ctx', 0, 0, axis_index_groups=strided)  1.69 us
  transfers between devices with their start and end apart: 9, of which 5 were waited for; matrix products, arithmetic and copies ran while one was open for 0% of the time, Pallas kernels for 7%

profile of v10, /device:TPU:1, one launch (start us, length us, event | category | flops | bytes accessed | tf_op | source)
XLA Modules:
  0.0 71.2 jit_solution(10411606029355900365)
XLA Ops:
  0.0 2.5 %shard_map.93 = (bf16[512,128]{1,0:T(8,128)(2,1)}, bf16[8,16,128]{2,1,0:T(8,128)(2,1)}) custom-call(s32[128]{0:T(128)} %bs.5, f32[8,128]{1,0:T(8,128)} %constant.2.clone.freqs, bf16[128,2,128]{2,1,0:T(2,128)(2,1)} %k.1, bf16[128,2,128]{2,1,0:T(2,128)(2,1)} %v.1, f32[32,128]{1,0:T(8,128)} %dk.1, f32[128,128]{1,0:T(8,128)} %pk.1, f32[32,128]{1,0:T(8,128)} %dv.1, ...), custom_call_target="tpu_custom_call" | custom-call | flops 1000000000 | bytes 1024 | tf_op jit(solution)/shard_map/pallas_call | solution.py:222
  2.5 4.8 %collective-permute-start = (bf16[512,128]{1,0:T(8,128)(2,1)}, bf16[512,128]{1,0:T(8,128)(2,1)S(1)}, u32[]{:S(2)}, u32[]{:S(2)}) collective-permute-start(bf16[512,128]{1,0:T(8,128)(2,1)} %get-tuple-element.14.own), channel_id=1, source_target_pairs={{496,0},{500,4},{504,8},{508,12},{0,16},{4,20},{8,24},{12,28},{16,... | collective-permute-start | bytes 393224 | tf_op jit(solution)/shard_map/ppermute | solution.py:259
  7.4 5.8 %collective-permute-start.1 = (bf16[512,128]{1,0:T(8,128)(2,1)}, bf16[512,128]{1,0:T(8,128)(2,1)S(1)}, u32[]{:S(2)}, u32[]{:S(2)}) collective-permute-start(bf16[512,128]{1,0:T(8,128)(2,1)} %get-tuple-element.14.own), channel_id=1, source_target_pairs={{480,0},{484,4},{488,8},{492,12},{496,16},{500,20},{504,24},{508,2... | collective-permute-start | bytes 393224 | tf_op jit(solution)/shard_map/ppermute | solution.py:259
  13.2 12.5 %all_to_all.10.mem = bf16[8,16,128]{2,1,0:T(8,128)(2,1)S(1)} all-to-all(bf16[8,16,128]{2,1,0:T(8,128)(2,1)} %get-tuple-element.15), channel_id=1, replica_groups={{0,4,8,12,16,20,24,28},{32,36,40,44,48,52,56,60},{64,68,72,76,80,84,88,..., dimensions={0} | all-to-all | bytes 65536 | tf_op jit(solution)/shard_map/all_to_all | solution.py:262
  25.6 0.0 collective-permute-done.row1
  25.7 0.5 collective-permute-done.1.row2
  26.1 0.9 %shard_map.94.far = bf16[16,128,128]{2,1,0:T(8,128)(2,1)} custom-call(bf16[8,16,128]{2,1,0:T(8,128)(2,1)S(1)} %all_to_all.10.mem, bf16[512,128]{1,0:T(8,128)(2,1)S(1)} %collective-permute-done.row1, bf16[512,128]{1,0:T(8,128)(2,1)S(1)} %collective-permute-done.1.row2), custom_call_target="tpu_custom_call" | custom-call | flops 1000 | bytes 1024 | tf_op jit(solution)/shard_map/pallas_call | solution.py:222
  27.0 0.0 copy-start
  27.0 9.0 %all-to-all-start.1 = ((bf16[16,128,128]{2,1,0:T(8,128)(2,1)}), bf16[16,128,128]{2,1,0:T(8,128)(2,1)S(1)}, u32[]{:S(2)}, u32[]{:S(2)}) async-start(bf16[16,128,128]{2,1,0:T(8,128)(2,1)} %shard_map.94.far), calls=%async_computation.1 | async-start | bytes 1048576 | tf_op jit(solution)/shard_map/all_to_all | solution.py:273
  36.0 0.0 copy-done
  36.0 0.0 copy-start.1
  36.1 0.1 shard_map.95
  36.1 2.6 %collective-permute-start.2 = (bf16[1024,128]{1,0:T(8,128)(2,1)S(1)}, bf16[1024,128]{1,0:T(8,128)(2,1)S(1)}, u32[]{:S(2)}, u32[]{:S(2)}) collective-permute-start(bf16[1024,128]{1,0:T(8,128)(2,1)S(1)} %get-tuple-element.16), channel_id=1, source_target_pairs={{0,4},{4,8},{8,12},{12,0},{16,20},{20,24},{24,28},{28,16},{32,36},... | collective-permute-start | bytes 786440 | tf_op jit(solution)/shard_map/ppermute | solution.py:279
  38.8 0.0 copy-start.3
  38.8 3.5 %collective-permute-start.3 = (bf16[1024,128]{1,0:T(8,128)(2,1)S(1)}, bf16[1024,128]{1,0:T(8,128)(2,1)S(1)}, u32[]{:S(2)}, u32[]{:S(2)}) collective-permute-start(bf16[1024,128]{1,0:T(8,128)(2,1)S(1)} %get-tuple-element.17), channel_id=1, source_target_pairs={{0,8},{4,12},{8,0},{12,4},{16,24},{20,28},{24,16},{28,20},{32,40},... | collective-permute-start | bytes 786440 | tf_op jit(solution)/shard_map/ppermute | solution.py:279
  42.3 0.0 copy-start.2
  42.3 3.1 %collective-permute-start.4 = (bf16[1024,128]{1,0:T(8,128)(2,1)S(1)}, bf16[1024,128]{1,0:T(8,128)(2,1)S(1)}, u32[]{:S(2)}, u32[]{:S(2)}) collective-permute-start(bf16[1024,128]{1,0:T(8,128)(2,1)S(1)} %get-tuple-element.18), channel_id=1, source_target_pairs={{0,12},{4,0},{8,4},{12,8},{16,28},{20,16},{24,20},{28,24},{32,44},... | collective-permute-start | bytes 786440 | tf_op jit(solution)/shard_map/ppermute | solution.py:279
  45.4 0.0 copy-done.3
  45.4 0.8 %shard_map.92.bias = bf16[1664,128]{1,0:T(8,128)(2,1)S(1)} custom-call(s32[128]{0:T(128)S(1)} %copy-done.3), custom_call_target="tpu_custom_call" | custom-call | flops 1000 | bytes 1024 | tf_op jit(solution)/shard_map/pallas_call | solution.py:222
  46.2 0.0 copy-done.1
  46.2 0.0 copy-done.2
  46.2 1.6 %shard_map.91.rotq = bf16[16,128,128]{2,1,0:T(8,128)(2,1)S(1)} custom-call(s32[128]{0:T(128)S(1)} %copy-done.3, f32[8,128]{1,0:T(8,128)S(1)} %copy-done.2, bf16[128,16,128]{2,1,0:T(8,128)(2,1)S(1)} %copy-done.1), custom_call_target="tpu_custom_call" | custom-call | flops 1000 | bytes 1024 | tf_op jit(solution)/shard_map/pallas_call | solution.py:222
  47.8 0.0 collective-permute-done.2.r1
  47.8 2.7 %collective-permute-done.3.r2 = bf16[1024,128]{1,0:T(8,128)(2,1)S(1)} collective-permute-done((bf16[1024,128]{1,0:T(8,128)(2,1)S(1)}, bf16[1024,128]{1,0:T(8,128)(2,1)S(1)}, u32[]{:S(2)}, u32[]{:S(2)}) %collective-permute-start.3) | collective-permute-done | bytes 262176 | tf_op jit(solution)/shard_map/ppermute | solution.py:279
  50.5 2.1 %collective-permute-done.4.r3 = bf16[1024,128]{1,0:T(8,128)(2,1)S(1)} collective-permute-done((bf16[1024,128]{1,0:T(8,128)(2,1)S(1)}, bf16[1024,128]{1,0:T(8,128)(2,1)S(1)}, u32[]{:S(2)}, u32[]{:S(2)}) %collective-permute-start.4) | collective-permute-done | bytes 262176 | tf_op jit(solution)/shard_map/ppermute | solution.py:279
  52.6 1.7 %all-to-all-done.1.mem = bf16[16,128,128]{2,1,0:T(8,128)(2,1)S(1)} async-done(((bf16[16,128,128]{2,1,0:T(8,128)(2,1)}), bf16[16,128,128]{2,1,0:T(8,128)(2,1)S(1)}, u32[]{:S(2)}, u32[]{:S(2)}) %all-to-all-start.1) | async-done | bytes 524320 | tf_op jit(solution)/shard_map/all_to_all | solution.py:273
  54.3 2.2 %shard_map.97 = (bf16[32,2048]{1,0:T(8,128)(2,1)S(1)}, bf16[32,2048]{1,0:T(8,128)(2,1)S(1)}) custom-call(bf16[16,128,128]{2,1,0:T(8,128)(2,1)S(1)} %shard_map.91.rotq, bf16[1664,128]{1,0:T(8,128)(2,1)S(1)} %shard_map.92.bias, bf16[512,128]{1,0:T(8,128)(2,1)S(1)} %copy-done, bf16[512,128]{1,0:T(8,128)(2,1)S(1)} %collective-permute-done.row1, ...), custom_call_target="tpu_custom_call" | custom-call | flops 1000000 | bytes 1024 | tf_op jit(solution)/shard_map/pallas_call | solution.py:222
  56.5 1.9 %collective-permute-start.6 = (bf16[32,2048]{1,0:T(8,128)(2,1)S(1)}, bf16[32,2048]{1,0:T(8,128)(2,1)S(1)}, u32[]{:S(2)}, u32[]{:S(2)}) collective-permute-start(bf16[32,2048]{1,0:T(8,128)(2,1)S(1)} %get-tuple-element.21), channel_id=1, source_target_pairs={{0,2},{1,3},{2,0},{3,1},{4,6},{5,7},{6,4},{7,5},{8,10},{9,11},{10,... | collective-permute-start | bytes 393224 | tf_op jit(solution)/shard_map/ppermute | solution.py:294
  58.4 6.4 %collective-permute-start.7 = (bf16[32,2048]{1,0:T(8,128)(2,1)S(1)}, bf16[32,2048]{1,0:T(8,128)(2,1)S(1)}, u32[]{:S(2)}, u32[]{:S(2)}) collective-permute-start(bf16[32,2048]{1,0:T(8,128)(2,1)S(1)} %get-tuple-element.22), channel_id=1, source_target_pairs={{0,3},{1,2},{2,1},{3,0},{4,7},{5,6},{6,5},{7,4},{8,11},{9,10},{10,... | collective-permute-start | bytes 393224 | tf_op jit(solution)/shard_map/ppermute | solution.py:294
  64.9 2.2 %shard_map.96 = (bf16[32,2048]{1,0:T(8,128)(2,1)S(1)}, bf16[32,2048]{1,0:T(8,128)(2,1)S(1)}) custom-call(bf16[16,128,128]{2,1,0:T(8,128)(2,1)S(1)} %shard_map.91.rotq, bf16[1664,128]{1,0:T(8,128)(2,1)S(1)} %shard_map.92.bias, bf16[512,128]{1,0:T(8,128)(2,1)S(1)} %copy-done, bf16[512,128]{1,0:T(8,128)(2,1)S(1)} %collective-permute-done.row1, ...), custom_call_target="tpu_custom_call" | custom-call | flops 1000000 | bytes 1024 | tf_op jit(solution)/shard_map/pallas_call | solution.py:222
  67.1 1.9 %collective-permute-start.5 = (bf16[32,2048]{1,0:T(8,128)(2,1)S(1)}, bf16[32,2048]{1,0:T(8,128)(2,1)S(1)}, u32[]{:S(2)}, u32[]{:S(2)}) collective-permute-start(bf16[32,2048]{1,0:T(8,128)(2,1)S(1)} %get-tuple-element.20), channel_id=1, source_target_pairs={{0,1},{1,0},{2,3},{3,2},{4,5},{5,4},{6,7},{7,6},{8,9},{9,8},{10,11... | collective-permute-start | bytes 393224 | tf_op jit(solution)/shard_map/ppermute | solution.py:294
  69.0 0.0 collective-permute-done.6.c
  69.0 0.0 collective-permute-done.7.d
  69.1 1.3 %collective-permute-done.5.b = bf16[32,2048]{1,0:T(8,128)(2,1)S(1)} collective-permute-done((bf16[32,2048]{1,0:T(8,128)(2,1)S(1)}, bf16[32,2048]{1,0:T(8,128)(2,1)S(1)}, u32[]{:S(2)}, u32[]{:S(2)}) %collective-permute-start.5) | collective-permute-done | bytes 131104 | tf_op jit(solution)/shard_map/ppermute | solution.py:294
  70.3 0.8 %shard_map.98 = bf16[32,8192]{1,0:T(8,128)(2,1)} custom-call(bf16[32,2048]{1,0:T(8,128)(2,1)S(1)} %get-tuple-element.19.a, bf16[32,2048]{1,0:T(8,128)(2,1)S(1)} %collective-permute-done.5.b, bf16[32,2048]{1,0:T(8,128)(2,1)S(1)} %collective-permute-done.6.c, bf16[32,2048]{1,0:T(8,128)(2,1)S(1)} %collective-permute-done.7.d), custom_call_target="tpu_custom_call" | custom-call | flops 100000000 | bytes 1024 | tf_op jit(solution)/shard_map/pallas_call | solution.py:222
Async XLA Ops:
  2.5 23.1 %collective-permute-start = (bf16[512,128]{1,0:T(8,128)(2,1)}, bf16[512,128]{1,0:T(8,128)(2,1)S(1)}, u32[]{:S(2)}, u32[]{:S(2)}) collective-permute-start(bf16[512,128]{1,0:T(8,128)(2,1)} %get-tuple-element.14.own), channel_id=1, source_target_pairs={{496,0},{500,4},{504,8},{508,12},{0,16},{4,20},{8,24},{12,28},{16,... | collective-permute-start | bytes 393224 | tf_op jit(solution)/shard_map/ppermute | solution.py:259
  7.4 18.7 %collective-permute-start.1 = (bf16[512,128]{1,0:T(8,128)(2,1)}, bf16[512,128]{1,0:T(8,128)(2,1)S(1)}, u32[]{:S(2)}, u32[]{:S(2)}) collective-permute-start(bf16[512,128]{1,0:T(8,128)(2,1)} %get-tuple-element.14.own), channel_id=1, source_target_pairs={{480,0},{484,4},{488,8},{492,12},{496,16},{500,20},{504,24},{508,2... | collective-permute-start | bytes 393224 | tf_op jit(solution)/shard_map/ppermute | solution.py:259
  27.0 9.1 %copy-start = (bf16[512,128]{1,0:T(8,128)(2,1)S(1)}, bf16[512,128]{1,0:T(8,128)(2,1)}, u32[]{:S(2)}) copy-start(bf16[512,128]{1,0:T(8,128)(2,1)} %get-tuple-element.14.own) | copy-start | bytes 393220
  27.0 27.3 %all-to-all-start.1 = ((bf16[16,128,128]{2,1,0:T(8,128)(2,1)}), bf16[16,128,128]{2,1,0:T(8,128)(2,1)S(1)}, u32[]{:S(2)}, u32[]{:S(2)}) async-start(bf16[16,128,128]{2,1,0:T(8,128)(2,1)} %shard_map.94.far), calls=%async_computation.1 | async-start | bytes 1048576 | tf_op jit(solution)/shard_map/all_to_all | solution.py:273
  36.0 10.2 %copy-start.1 = (bf16[128,16,128]{2,1,0:T(8,128)(2,1)S(1)}, bf16[128,16,128]{2,1,0:T(8,128)(2,1)}, u32[]{:S(2)}) copy-start(bf16[128,16,128]{2,1,0:T(8,128)(2,1)} %q.1) | copy-start | bytes 1572868
  36.1 11.7 %collective-permute-start.2 = (bf16[1024,128]{1,0:T(8,128)(2,1)S(1)}, bf16[1024,128]{1,0:T(8,128)(2,1)S(1)}, u32[]{:S(2)}, u32[]{:S(2)}) collective-permute-start(bf16[1024,128]{1,0:T(8,128)(2,1)S(1)} %get-tuple-element.16), channel_id=1, source_target_pairs={{0,4},{4,8},{8,12},{12,0},{16,20},{20,24},{24,28},{28,16},{32,36},... | collective-permute-start | bytes 786440 | tf_op jit(solution)/shard_map/ppermute | solution.py:279
  38.8 6.6 %copy-start.3 = (s32[128]{0:T(128)S(1)}, s32[128]{0:T(128)}, u32[]{:S(2)}) copy-start(s32[128]{0:T(128)} %bs.5) | copy-start | bytes 1540
  38.8 11.7 %collective-permute-start.3 = (bf16[1024,128]{1,0:T(8,128)(2,1)S(1)}, bf16[1024,128]{1,0:T(8,128)(2,1)S(1)}, u32[]{:S(2)}, u32[]{:S(2)}) collective-permute-start(bf16[1024,128]{1,0:T(8,128)(2,1)S(1)} %get-tuple-element.17), channel_id=1, source_target_pairs={{0,8},{4,12},{8,0},{12,4},{16,24},{20,28},{24,16},{28,20},{32,40},... | collective-permute-start | bytes 786440 | tf_op jit(solution)/shard_map/ppermute | solution.py:279
  42.3 3.9 %copy-start.2 = (f32[8,128]{1,0:T(8,128)S(1)}, f32[8,128]{1,0:T(8,128)}, u32[]{:S(2)}) copy-start(f32[8,128]{1,0:T(8,128)} %constant.2.clone.freqs) | copy-start | bytes 12292
  42.3 10.3 %collective-permute-start.4 = (bf16[1024,128]{1,0:T(8,128)(2,1)S(1)}, bf16[1024,128]{1,0:T(8,128)(2,1)S(1)}, u32[]{:S(2)}, u32[]{:S(2)}) collective-permute-start(bf16[1024,128]{1,0:T(8,128)(2,1)S(1)} %get-tuple-element.18), channel_id=1, source_target_pairs={{0,12},{4,0},{8,4},{12,8},{16,28},{20,16},{24,20},{28,24},{32,44},... | collective-permute-start | bytes 786440 | tf_op jit(solution)/shard_map/ppermute | solution.py:279
  56.5 12.5 %collective-permute-start.6 = (bf16[32,2048]{1,0:T(8,128)(2,1)S(1)}, bf16[32,2048]{1,0:T(8,128)(2,1)S(1)}, u32[]{:S(2)}, u32[]{:S(2)}) collective-permute-start(bf16[32,2048]{1,0:T(8,128)(2,1)S(1)} %get-tuple-element.21), channel_id=1, source_target_pairs={{0,2},{1,3},{2,0},{3,1},{4,6},{5,7},{6,4},{7,5},{8,10},{9,11},{10,... | collective-permute-start | bytes 393224 | tf_op jit(solution)/shard_map/ppermute | solution.py:294
  58.4 10.6 %collective-permute-start.7 = (bf16[32,2048]{1,0:T(8,128)(2,1)S(1)}, bf16[32,2048]{1,0:T(8,128)(2,1)S(1)}, u32[]{:S(2)}, u32[]{:S(2)}) collective-permute-start(bf16[32,2048]{1,0:T(8,128)(2,1)S(1)} %get-tuple-element.22), channel_id=1, source_target_pairs={{0,3},{1,2},{2,1},{3,0},{4,7},{5,6},{6,5},{7,4},{8,11},{9,10},{10,... | collective-permute-start | bytes 393224 | tf_op jit(solution)/shard_map/ppermute | solution.py:294
  67.1 3.2 %collective-permute-start.5 = (bf16[32,2048]{1,0:T(8,128)(2,1)S(1)}, bf16[32,2048]{1,0:T(8,128)(2,1)S(1)}, u32[]{:S(2)}, u32[]{:S(2)}) collective-permute-start(bf16[32,2048]{1,0:T(8,128)(2,1)S(1)} %get-tuple-element.20), channel_id=1, source_target_pairs={{0,1},{1,0},{2,3},{3,2},{4,5},{5,4},{6,7},{7,6},{8,9},{9,8},{10,11... | collective-permute-start | bytes 393224 | tf_op jit(solution)/shard_map/ppermute | solution.py:294

commit v11 on v10

--- a/solution.py
+++ b/solution.py
@@ -22,7 +22,7 @@
 KV = 4
 RING = 4
 ORDER = (2, 1, 3)
-NEAR = 8
+NEAR = 4
 FAR = BLOCKS // NEAR
 ROWS = TOK // KV
 RAW = (WIN + 1) * TOK

time: 71.7 us -> 71.5 us (level)
  the two profiles are of different devices: /device:TPU:1 before, /device:TPU:43 now
where the time goes in v11:
time: 71.5 us; the launch traced here: 70.9 us
  starting transfers between devices  37.4 us (52%)
  waiting for transfers between devices  14.6 us (20%)
  Pallas kernels  11.1 us (16%)
  blocking collectives  7.61 us (11%)
    pallas_call x8, Pallas kernels, call(): pl.pallas_call(kernel, out_shape=out_shape, in_specs=[pl.BlockSpec(memory...  11.1 us
    all_to_all x1, starting transfers between devices, shards(): mem = lax.all_to_all(far, 'ctx', 0, 0, axis_index_groups=strided)  9.9 us
    ppermute x2, starting transfers between devices, shards(): lax.ppermute(own, 'ctx', [((i - d) % BLOCKS, i) for i in range(BLOCKS)])  9.81 us
    ppermute x3, starting transfers between devices, shards(): lax.ppermute(x, 'ctx', [(i, i // RING * RING + (i + s) % RING) for i in r...  9.77 us
    ppermute x3, waiting for transfers between devices, shards(): lax.ppermute(x, 'ctx', [(i, i // RING * RING + (i + s) % RING) for i in r...  8.15 us
    ppermute x3, starting transfers between devices, shards(): part = lax.ppermute(part, 'kv', [(i, i ^ off) for i in range(KV)])  7.96 us
    all_to_all x1, blocking collectives, shards(): mem = lax.all_to_all(mem, 'ctx', 0, 0, axis_index_groups=near)  7.61 us
    ppermute x2, waiting for transfers between devices, shards(): lax.ppermute(own, 'ctx', [((i - d) % BLOCKS, i) for i in range(BLOCKS)])  5.11 us
  transfers between devices with their start and end apart: 9, of which 5 were waited for; matrix products, arithmetic and copies ran while one was open for 0% of the time, Pallas kernels for 7%

profile of v11, /device:TPU:43, one launch (start us, length us, event | category | flops | bytes accessed | tf_op | source)
XLA Modules:
  0.0 70.9 jit_solution(14087186010062468511)
XLA Ops:
  0.0 2.5 %shard_map.93 = (bf16[512,128]{1,0:T(8,128)(2,1)}, bf16[4,16,128]{2,1,0:T(8,128)(2,1)}) custom-call(s32[128]{0:T(128)} %bs.5, f32[8,128]{1,0:T(8,128)} %constant.2.clone.freqs, bf16[128,2,128]{2,1,0:T(2,128)(2,1)} %k.1, bf16[128,2,128]{2,1,0:T(2,128)(2,1)} %v.1, f32[32,128]{1,0:T(8,128)} %dk.1, f32[128,128]{1,0:T(8,128)} %pk.1, f32[32,128]{1,0:T(8,128)} %dv.1, ...), custom_call_target="tpu_custom_call" | custom-call | flops 1000000000 | bytes 1024 | tf_op jit(solution)/shard_map/pallas_call | solution.py:222
  2.5 4.0 %collective-permute-start = (bf16[512,128]{1,0:T(8,128)(2,1)}, bf16[512,128]{1,0:T(8,128)(2,1)S(1)}, u32[]{:S(2)}, u32[]{:S(2)}) collective-permute-start(bf16[512,128]{1,0:T(8,128)(2,1)} %get-tuple-element.14.own), channel_id=1, source_target_pairs={{496,0},{500,4},{504,8},{508,12},{0,16},{4,20},{8,24},{12,28},{16,... | collective-permute-start | bytes 393224 | tf_op jit(solution)/shard_map/ppermute | solution.py:259
  6.5 5.8 %collective-permute-start.1 = (bf16[512,128]{1,0:T(8,128)(2,1)}, bf16[512,128]{1,0:T(8,128)(2,1)S(1)}, u32[]{:S(2)}, u32[]{:S(2)}) collective-permute-start(bf16[512,128]{1,0:T(8,128)(2,1)} %get-tuple-element.14.own), channel_id=1, source_target_pairs={{480,0},{484,4},{488,8},{492,12},{496,16},{500,20},{504,24},{508,2... | collective-permute-start | bytes 393224 | tf_op jit(solution)/shard_map/ppermute | solution.py:259
  12.4 7.6 %all_to_all.10.mem = bf16[4,16,128]{2,1,0:T(8,128)(2,1)S(1)} all-to-all(bf16[4,16,128]{2,1,0:T(8,128)(2,1)} %get-tuple-element.15), channel_id=1, replica_groups={{0,4,8,12},{16,20,24,28},{32,36,40,44},{48,52,56,60},{64,68,72,76},{80,..., dimensions={0} | all-to-all | bytes 32768 | tf_op jit(solution)/shard_map/all_to_all | solution.py:262
  20.0 3.4 %collective-permute-done.row1 = bf16[512,128]{1,0:T(8,128)(2,1)S(1)} collective-permute-done((bf16[512,128]{1,0:T(8,128)(2,1)}, bf16[512,128]{1,0:T(8,128)(2,1)S(1)}, u32[]{:S(2)}, u32[]{:S(2)}) %collective-permute-start) | collective-permute-done | bytes 131104 | tf_op jit(solution)/shard_map/ppermute | solution.py:259
  23.4 1.7 %collective-permute-done.1.row2 = bf16[512,128]{1,0:T(8,128)(2,1)S(1)} collective-permute-done((bf16[512,128]{1,0:T(8,128)(2,1)}, bf16[512,128]{1,0:T(8,128)(2,1)S(1)}, u32[]{:S(2)}, u32[]{:S(2)}) %collective-permute-start.1) | collective-permute-done | bytes 131104 | tf_op jit(solution)/shard_map/ppermute | solution.py:259
  25.1 0.9 %shard_map.94.far = bf16[32,64,128]{2,1,0:T(8,128)(2,1)} custom-call(bf16[4,16,128]{2,1,0:T(8,128)(2,1)S(1)} %all_to_all.10.mem, bf16[512,128]{1,0:T(8,128)(2,1)S(1)} %collective-permute-done.row1, bf16[512,128]{1,0:T(8,128)(2,1)S(1)} %collective-permute-done.1.row2), custom_call_target="tpu_custom_call" | custom-call | flops 1000 | bytes 1024 | tf_op jit(solution)/shard_map/pallas_call | solution.py:222
  25.9 0.0 copy-start
  25.9 9.9 %all-to-all-start.1 = ((bf16[32,64,128]{2,1,0:T(8,128)(2,1)}), bf16[32,64,128]{2,1,0:T(8,128)(2,1)S(1)}, u32[]{:S(2)}, u32[]{:S(2)}) async-start(bf16[32,64,128]{2,1,0:T(8,128)(2,1)} %shard_map.94.far), calls=%async_computation.1 | async-start | bytes 1048576 | tf_op jit(solution)/shard_map/all_to_all | solution.py:273
  35.8 0.0 copy-done
  35.9 0.0 copy-start.1
  35.9 0.1 shard_map.95
  35.9 3.3 %collective-permute-start.2 = (bf16[1024,128]{1,0:T(8,128)(2,1)S(1)}, bf16[1024,128]{1,0:T(8,128)(2,1)S(1)}, u32[]{:S(2)}, u32[]{:S(2)}) collective-permute-start(bf16[1024,128]{1,0:T(8,128)(2,1)S(1)} %get-tuple-element.16), channel_id=1, source_target_pairs={{0,4},{4,8},{8,12},{12,0},{16,20},{20,24},{24,28},{28,16},{32,36},... | collective-permute-start | bytes 786440 | tf_op jit(solution)/shard_map/ppermute | solution.py:279
  39.2 0.0 copy-start.3
  39.2 2.7 %collective-permute-start.3 = (bf16[1024,128]{1,0:T(8,128)(2,1)S(1)}, bf16[1024,128]{1,0:T(8,128)(2,1)S(1)}, u32[]{:S(2)}, u32[]{:S(2)}) collective-permute-start(bf16[1024,128]{1,0:T(8,128)(2,1)S(1)} %get-tuple-element.17), channel_id=1, source_target_pairs={{0,8},{4,12},{8,0},{12,4},{16,24},{20,28},{24,16},{28,20},{32,40},... | collective-permute-start | bytes 786440 | tf_op jit(solution)/shard_map/ppermute | solution.py:279
  42.0 0.0 copy-start.2
  42.0 3.8 %collective-permute-start.4 = (bf16[1024,128]{1,0:T(8,128)(2,1)S(1)}, bf16[1024,128]{1,0:T(8,128)(2,1)S(1)}, u32[]{:S(2)}, u32[]{:S(2)}) collective-permute-start(bf16[1024,128]{1,0:T(8,128)(2,1)S(1)} %get-tuple-element.18), channel_id=1, source_target_pairs={{0,12},{4,0},{8,4},{12,8},{16,28},{20,16},{24,20},{28,24},{32,44},... | collective-permute-start | bytes 786440 | tf_op jit(solution)/shard_map/ppermute | solution.py:279
  45.8 0.0 copy-done.3
  45.8 0.8 %shard_map.92.bias = bf16[1664,128]{1,0:T(8,128)(2,1)S(1)} custom-call(s32[128]{0:T(128)S(1)} %copy-done.3), custom_call_target="tpu_custom_call" | custom-call | flops 1000 | bytes 1024 | tf_op jit(solution)/shard_map/pallas_call | solution.py:222
  46.6 0.0 copy-done.1
  46.6 0.0 copy-done.2
  46.6 1.6 %shard_map.91.rotq = bf16[16,128,128]{2,1,0:T(8,128)(2,1)S(1)} custom-call(s32[128]{0:T(128)S(1)} %copy-done.3, f32[8,128]{1,0:T(8,128)S(1)} %copy-done.2, bf16[128,16,128]{2,1,0:T(8,128)(2,1)S(1)} %copy-done.1), custom_call_target="tpu_custom_call" | custom-call | flops 1000 | bytes 1024 | tf_op jit(solution)/shard_map/pallas_call | solution.py:222
  48.2 0.0 collective-permute-done.2.r1
  48.2 0.6 collective-permute-done.3.r2
  48.8 7.5 %collective-permute-done.4.r3 = bf16[1024,128]{1,0:T(8,128)(2,1)S(1)} collective-permute-done((bf16[1024,128]{1,0:T(8,128)(2,1)S(1)}, bf16[1024,128]{1,0:T(8,128)(2,1)S(1)}, u32[]{:S(2)}, u32[]{:S(2)}) %collective-permute-start.4) | collective-permute-done | bytes 262176 | tf_op jit(solution)/shard_map/ppermute | solution.py:279
  56.4 0.0 all-to-all-done.1.mem
  56.4 2.2 %shard_map.97 = (bf16[32,2048]{1,0:T(8,128)(2,1)S(1)}, bf16[32,2048]{1,0:T(8,128)(2,1)S(1)}) custom-call(bf16[16,128,128]{2,1,0:T(8,128)(2,1)S(1)} %shard_map.91.rotq, bf16[1664,128]{1,0:T(8,128)(2,1)S(1)} %shard_map.92.bias, bf16[512,128]{1,0:T(8,128)(2,1)S(1)} %copy-done, bf16[512,128]{1,0:T(8,128)(2,1)S(1)} %collective-permute-done.row1, ...), custom_call_target="tpu_custom_call" | custom-call | flops 1000000 | bytes 1024 | tf_op jit(solution)/shard_map/pallas_call | solution.py:222
  58.6 1.9 %collective-permute-start.6 = (bf16[32,2048]{1,0:T(8,128)(2,1)S(1)}, bf16[32,2048]{1,0:T(8,128)(2,1)S(1)}, u32[]{:S(2)}, u32[]{:S(2)}) collective-permute-start(bf16[32,2048]{1,0:T(8,128)(2,1)S(1)} %get-tuple-element.21), channel_id=1, source_target_pairs={{0,2},{1,3},{2,0},{3,1},{4,6},{5,7},{6,4},{7,5},{8,10},{9,11},{10,... | collective-permute-start | bytes 393224 | tf_op jit(solution)/shard_map/ppermute | solution.py:294
  60.5 4.1 %collective-permute-start.7 = (bf16[32,2048]{1,0:T(8,128)(2,1)S(1)}, bf16[32,2048]{1,0:T(8,128)(2,1)S(1)}, u32[]{:S(2)}, u32[]{:S(2)}) collective-permute-start(bf16[32,2048]{1,0:T(8,128)(2,1)S(1)} %get-tuple-element.22), channel_id=1, source_target_pairs={{0,3},{1,2},{2,1},{3,0},{4,7},{5,6},{6,5},{7,4},{8,11},{9,10},{10,... | collective-permute-start | bytes 393224 | tf_op jit(solution)/shard_map/ppermute | solution.py:294
  64.6 2.2 %shard_map.96 = (bf16[32,2048]{1,0:T(8,128)(2,1)S(1)}, bf16[32,2048]{1,0:T(8,128)(2,1)S(1)}) custom-call(bf16[16,128,128]{2,1,0:T(8,128)(2,1)S(1)} %shard_map.91.rotq, bf16[1664,128]{1,0:T(8,128)(2,1)S(1)} %shard_map.92.bias, bf16[512,128]{1,0:T(8,128)(2,1)S(1)} %copy-done, bf16[512,128]{1,0:T(8,128)(2,1)S(1)} %collective-permute-done.row1, ...), custom_call_target="tpu_custom_call" | custom-call | flops 1000000 | bytes 1024 | tf_op jit(solution)/shard_map/pallas_call | solution.py:222
  66.9 1.9 %collective-permute-start.5 = (bf16[32,2048]{1,0:T(8,128)(2,1)S(1)}, bf16[32,2048]{1,0:T(8,128)(2,1)S(1)}, u32[]{:S(2)}, u32[]{:S(2)}) collective-permute-start(bf16[32,2048]{1,0:T(8,128)(2,1)S(1)} %get-tuple-element.20), channel_id=1, source_target_pairs={{0,1},{1,0},{2,3},{3,2},{4,5},{5,4},{6,7},{7,6},{8,9},{9,8},{10,11... | collective-permute-start | bytes 393224 | tf_op jit(solution)/shard_map/ppermute | solution.py:294
  68.8 0.0 collective-permute-done.6.c
  68.8 0.0 collective-permute-done.7.d
  68.8 1.3 %collective-permute-done.5.b = bf16[32,2048]{1,0:T(8,128)(2,1)S(1)} collective-permute-done((bf16[32,2048]{1,0:T(8,128)(2,1)S(1)}, bf16[32,2048]{1,0:T(8,128)(2,1)S(1)}, u32[]{:S(2)}, u32[]{:S(2)}) %collective-permute-start.5) | collective-permute-done | bytes 131104 | tf_op jit(solution)/shard_map/ppermute | solution.py:294
  70.1 0.8 %shard_map.98 = bf16[32,8192]{1,0:T(8,128)(2,1)} custom-call(bf16[32,2048]{1,0:T(8,128)(2,1)S(1)} %get-tuple-element.19.a, bf16[32,2048]{1,0:T(8,128)(2,1)S(1)} %collective-permute-done.5.b, bf16[32,2048]{1,0:T(8,128)(2,1)S(1)} %collective-permute-done.6.c, bf16[32,2048]{1,0:T(8,128)(2,1)S(1)} %collective-permute-done.7.d), custom_call_target="tpu_custom_call" | custom-call | flops 100000000 | bytes 1024 | tf_op jit(solution)/shard_map/pallas_call | solution.py:222
Async XLA Ops:
  2.5 20.8 %collective-permute-start = (bf16[512,128]{1,0:T(8,128)(2,1)}, bf16[512,128]{1,0:T(8,128)(2,1)S(1)}, u32[]{:S(2)}, u32[]{:S(2)}) collective-permute-start(bf16[512,128]{1,0:T(8,128)(2,1)} %get-tuple-element.14.own), channel_id=1, source_target_pairs={{496,0},{500,4},{504,8},{508,12},{0,16},{4,20},{8,24},{12,28},{16,... | collective-permute-start | bytes 393224 | tf_op jit(solution)/shard_map/ppermute | solution.py:259
  6.5 18.5 %collective-permute-start.1 = (bf16[512,128]{1,0:T(8,128)(2,1)}, bf16[512,128]{1,0:T(8,128)(2,1)S(1)}, u32[]{:S(2)}, u32[]{:S(2)}) collective-permute-start(bf16[512,128]{1,0:T(8,128)(2,1)} %get-tuple-element.14.own), channel_id=1, source_target_pairs={{480,0},{484,4},{488,8},{492,12},{496,16},{500,20},{504,24},{508,2... | collective-permute-start | bytes 393224 | tf_op jit(solution)/shard_map/ppermute | solution.py:259
  25.9 9.9 %copy-start = (bf16[512,128]{1,0:T(8,128)(2,1)S(1)}, bf16[512,128]{1,0:T(8,128)(2,1)}, u32[]{:S(2)}) copy-start(bf16[512,128]{1,0:T(8,128)(2,1)} %get-tuple-element.14.own) | copy-start | bytes 393220
  25.9 30.4 %all-to-all-start.1 = ((bf16[32,64,128]{2,1,0:T(8,128)(2,1)}), bf16[32,64,128]{2,1,0:T(8,128)(2,1)S(1)}, u32[]{:S(2)}, u32[]{:S(2)}) async-start(bf16[32,64,128]{2,1,0:T(8,128)(2,1)} %shard_map.94.far), calls=%async_computation.1 | async-start | bytes 1048576 | tf_op jit(solution)/shard_map/all_to_all | solution.py:273
  35.9 10.7 %copy-start.1 = (bf16[128,16,128]{2,1,0:T(8,128)(2,1)S(1)}, bf16[128,16,128]{2,1,0:T(8,128)(2,1)}, u32[]{:S(2)}) copy-start(bf16[128,16,128]{2,1,0:T(8,128)(2,1)} %q.1) | copy-start | bytes 1572868
  35.9 12.3 %collective-permute-start.2 = (bf16[1024,128]{1,0:T(8,128)(2,1)S(1)}, bf16[1024,128]{1,0:T(8,128)(2,1)S(1)}, u32[]{:S(2)}, u32[]{:S(2)}) collective-permute-start(bf16[1024,128]{1,0:T(8,128)(2,1)S(1)} %get-tuple-element.16), channel_id=1, source_target_pairs={{0,4},{4,8},{8,12},{12,0},{16,20},{20,24},{24,28},{28,16},{32,36},... | collective-permute-start | bytes 786440 | tf_op jit(solution)/shard_map/ppermute | solution.py:279
  39.2 6.6 %copy-start.3 = (s32[128]{0:T(128)S(1)}, s32[128]{0:T(128)}, u32[]{:S(2)}) copy-start(s32[128]{0:T(128)} %bs.5) | copy-start | bytes 1540
  39.2 9.6 %collective-permute-start.3 = (bf16[1024,128]{1,0:T(8,128)(2,1)S(1)}, bf16[1024,128]{1,0:T(8,128)(2,1)S(1)}, u32[]{:S(2)}, u32[]{:S(2)}) collective-permute-start(bf16[1024,128]{1,0:T(8,128)(2,1)S(1)} %get-tuple-element.17), channel_id=1, source_target_pairs={{0,8},{4,12},{8,0},{12,4},{16,24},{20,28},{24,16},{28,20},{32,40},... | collective-permute-start | bytes 786440 | tf_op jit(solution)/shard_map/ppermute | solution.py:279
  42.0 4.6 %copy-start.2 = (f32[8,128]{1,0:T(8,128)S(1)}, f32[8,128]{1,0:T(8,128)}, u32[]{:S(2)}) copy-start(f32[8,128]{1,0:T(8,128)} %constant.2.clone.freqs) | copy-start | bytes 12292
  42.0 14.4 %collective-permute-start.4 = (bf16[1024,128]{1,0:T(8,128)(2,1)S(1)}, bf16[1024,128]{1,0:T(8,128)(2,1)S(1)}, u32[]{:S(2)}, u32[]{:S(2)}) collective-permute-start(bf16[1024,128]{1,0:T(8,128)(2,1)S(1)} %get-tuple-element.18), channel_id=1, source_target_pairs={{0,12},{4,0},{8,4},{12,8},{16,28},{20,16},{24,20},{28,24},{32,44},... | collective-permute-start | bytes 786440 | tf_op jit(solution)/shard_map/ppermute | solution.py:279
  58.6 10.2 %collective-permute-start.6 = (bf16[32,2048]{1,0:T(8,128)(2,1)S(1)}, bf16[32,2048]{1,0:T(8,128)(2,1)S(1)}, u32[]{:S(2)}, u32[]{:S(2)}) collective-permute-start(bf16[32,2048]{1,0:T(8,128)(2,1)S(1)} %get-tuple-element.21), channel_id=1, source_target_pairs={{0,2},{1,3},{2,0},{3,1},{4,6},{5,7},{6,4},{7,5},{8,10},{9,11},{10,... | collective-permute-start | bytes 393224 | tf_op jit(solution)/shard_map/ppermute | solution.py:294
  60.5 8.3 %collective-permute-start.7 = (bf16[32,2048]{1,0:T(8,128)(2,1)S(1)}, bf16[32,2048]{1,0:T(8,128)(2,1)S(1)}, u32[]{:S(2)}, u32[]{:S(2)}) collective-permute-start(bf16[32,2048]{1,0:T(8,128)(2,1)S(1)} %get-tuple-element.22), channel_id=1, source_target_pairs={{0,3},{1,2},{2,1},{3,0},{4,7},{5,6},{6,5},{7,4},{8,11},{9,10},{10,... | collective-permute-start | bytes 393224 | tf_op jit(solution)/shard_map/ppermute | solution.py:294
  66.9 3.2 %collective-permute-start.5 = (bf16[32,2048]{1,0:T(8,128)(2,1)S(1)}, bf16[32,2048]{1,0:T(8,128)(2,1)S(1)}, u32[]{:S(2)}, u32[]{:S(2)}) collective-permute-start(bf16[32,2048]{1,0:T(8,128)(2,1)S(1)} %get-tuple-element.20), channel_id=1, source_target_pairs={{0,1},{1,0},{2,3},{3,2},{4,5},{5,4},{6,7},{7,6},{8,9},{9,8},{10,11... | collective-permute-start | bytes 393224 | tf_op jit(solution)/shard_map/ppermute | solution.py:294

commit v12 on v10

--- a/solution.py
+++ b/solution.py
@@ -21,7 +21,7 @@
 GROUPS = 2
 KV = 4
 RING = 4
-ORDER = (2, 1, 3)
+ORDER = (3, 2, 1)
 NEAR = 8
 FAR = BLOCKS // NEAR
 ROWS = TOK // KV
@@ -108,7 +108,8 @@
 def ring_kernel(own, row1, row2, far, ra, rb, rc):
     me = lax.rem(lax.axis_index("ctx"), RING)
     for s, out in zip(ORDER, (ra, rb, rc)):
-        out[TOKP:, :] = row1[...]
+        if s != 2:
+            out[TOKP:, :] = row1[...]
 
         @pl.when(me + s < RING)
         def _():
@@ -145,7 +146,7 @@
     half = SLOTS * BLOCKS // 2
     tiles = [(0, [("own", 0, TOK), ("row1", 0, TOK)])]
     for s in range(1, RING):
-        tiles.append((2 * s * TOK, [(s, 0, TOK), (s, TOKP, TOK)]))
+        tiles.append((2 * s * TOK, [(s, 0, TOK), ("pass", 0, TOK) if s == 2 else (s, TOKP, TOK)]))
     tiles.append((RAW, [("mem", 0, half)]))
     tiles.append((RAW + half, [("mem", half, half)]))
     tiles.append((RAW - TOK, [("row2", 0, TOK)]))
@@ -164,8 +165,8 @@
     return parts[0] if len(parts) == 1 else jnp.concatenate(parts, axis=0)
 
 
-def chunk_kernel(offs, rotq, bias, own, row1, row2, r1, r2, r3, mem, *rest):
-    refs = {"own": own, "row1": row1, "row2": row2, 1: r1, 2: r2, 3: r3, "mem": mem}
+def chunk_kernel(offs, rotq, bias, own, row1, row2, r1, r2, r3, passed, mem, *rest):
+    refs = {"own": own, "row1": row1, "row2": row2, 1: r1, 2: r2, 3: r3, "pass": passed, "mem": mem}
     outs, s = rest[:-1], rest[-1]
     firsts = [pl.multiple_of((lax.axis_index("kv") ^ o) * ROWS, ROWS) for o in offs]
     heads = HEADS // GROUPS
@@ -272,7 +273,7 @@
     )
     mem = lax.all_to_all(far, "ctx", 0, 0, axis_index_groups=strided)
     rings = call(
-        ring_kernel, (shape(2 * TOKP, HD),) * (RING - 1), [], 10**3, (VM,) * 3 + (pl.ANY,),
+        ring_kernel, tuple(shape(TOKP if s == 2 else 2 * TOKP, HD) for s in ORDER), [], 10**3, (VM,) * 3 + (pl.ANY,),
         own, row1, row2, far,
     )
     turned = {
@@ -281,13 +282,16 @@
         )
         for s, x in zip(ORDER, rings)
     }
-    rings = [turned[s] for s in (1, 2, 3)]
+    passed = lax.ppermute(
+        turned[3][TOKP:], "ctx", [(i, i // RING * RING + (i + 3) % RING) for i in range(BLOCKS)]
+    )
+    rings = [turned[s] for s in (1, 2, 3)] + [passed]
     parts = {}
     for offs in ((3, 2), (1, 0)):
         got = call(
             functools.partial(chunk_kernel, offs), (shape(ROWS, HEADS * HD),) * len(offs),
             [pltpu.VMEM((GROUPS, len(offs) * HEADS // GROUPS * ROWS, KEYS), F32)], 10**6,
-            (VM,) * 9, rotq, bias, own, row1, row2, *rings, mem,
+            (VM,) * 10, rotq, bias, own, row1, row2, *rings, mem,
         )
         for off, part in zip(offs, got):
             if off:

time: 71.7 us -> 71.8 us (level)
  waiting for transfers between devices: 8.23 us -> 5.18 us
  starting transfers between devices: 39.2 us -> 42.2 us
    ppermute x3, waiting for transfers between devices: 4.79 us -> 0.01 us  [shards(): lax.ppermute(x, 'ctx', [(i, i // RING * RING + (i + s) % RING) for i in r...]
    ppermute x0 -> x1, starting transfers between devices: none -> 3.61 us  [shards(): lax.ppermute(turned[3][TOKP:], 'ctx', [(i, i // RING * RING + (i + 3) % R...]
    all_to_all x1, waiting for transfers between devices: 1.69 us -> 3.41 us  [shards(): mem = lax.all_to_all(far, 'ctx', 0, 0, axis_index_groups=strided)]
  transfers between devices with their start and end apart: 9 -> 10, of which waited for: 5 -> 3; matrix products, arithmetic and copies ran while one was open for 0% -> 0% of each run, Pallas kernels for 7% -> 7%
where the time goes in v12:
time: 71.8 us; the launch traced here: 71.2 us
  starting transfers between devices  42.2 us (59%)
  blocking collectives  12.5 us (17%)
  Pallas kernels  11.1 us (15%)
  waiting for transfers between devices  5.18 us (7%)
    all_to_all x1, blocking collectives, shards(): mem = lax.all_to_all(mem, 'ctx', 0, 0, axis_index_groups=near)  12.5 us
    pallas_call x8, Pallas kernels, call(): pl.pallas_call(kernel, out_shape=out_shape, in_specs=[pl.BlockSpec(memory...  11.1 us
    ppermute x2, starting transfers between devices, shards(): lax.ppermute(own, 'ctx', [((i - d) % BLOCKS, i) for i in range(BLOCKS)])  10.6 us
    ppermute x3, starting transfers between devices, shards(): part = lax.ppermute(part, 'kv', [(i, i ^ off) for i in range(KV)])  10.3 us
    all_to_all x1, starting transfers between devices, shards(): mem = lax.all_to_all(far, 'ctx', 0, 0, axis_index_groups=strided)  9.04 us
    ppermute x3, starting transfers between devices, shards(): lax.ppermute(x, 'ctx', [(i, i // RING * RING + (i + s) % RING) for i in r...  8.6 us
    ppermute x1, starting transfers between devices, shards(): lax.ppermute(turned[3][TOKP:], 'ctx', [(i, i // RING * RING + (i + 3) % R...  3.61 us
    all_to_all x1, waiting for transfers between devices, shards(): mem = lax.all_to_all(far, 'ctx', 0, 0, axis_index_groups=strided)  3.41 us
  transfers between devices with their start and end apart: 10, of which 3 were waited for; matrix products, arithmetic and copies ran while one was open for 0% of the time, Pallas kernels for 7%

profile of v12, /device:TPU:1, one launch (start us, length us, event | category | flops | bytes accessed | tf_op | source)
XLA Modules:
  0.0 71.2 jit_solution(1174734782438531631)
XLA Ops:
  0.0 2.5 %shard_map.93 = (bf16[512,128]{1,0:T(8,128)(2,1)}, bf16[8,16,128]{2,1,0:T(8,128)(2,1)}) custom-call(s32[128]{0:T(128)} %bs.5, f32[8,128]{1,0:T(8,128)} %constant.2.clone.freqs, bf16[128,2,128]{2,1,0:T(2,128)(2,1)} %k.1, bf16[128,2,128]{2,1,0:T(2,128)(2,1)} %v.1, f32[32,128]{1,0:T(8,128)} %dk.1, f32[128,128]{1,0:T(8,128)} %pk.1, f32[32,128]{1,0:T(8,128)} %dv.1, ...), custom_call_target="tpu_custom_call" | custom-call | flops 1000000000 | bytes 1024 | tf_op jit(solution)/shard_map/pallas_call | solution.py:223
  2.5 4.8 %collective-permute-start = (bf16[512,128]{1,0:T(8,128)(2,1)}, bf16[512,128]{1,0:T(8,128)(2,1)S(1)}, u32[]{:S(2)}, u32[]{:S(2)}) collective-permute-start(bf16[512,128]{1,0:T(8,128)(2,1)} %get-tuple-element.14.own), channel_id=1, source_target_pairs={{496,0},{500,4},{504,8},{508,12},{0,16},{4,20},{8,24},{12,28},{16,... | collective-permute-start | bytes 393224 | tf_op jit(solution)/shard_map/ppermute | solution.py:260
  7.4 5.8 %collective-permute-start.1 = (bf16[512,128]{1,0:T(8,128)(2,1)}, bf16[512,128]{1,0:T(8,128)(2,1)S(1)}, u32[]{:S(2)}, u32[]{:S(2)}) collective-permute-start(bf16[512,128]{1,0:T(8,128)(2,1)} %get-tuple-element.14.own), channel_id=1, source_target_pairs={{480,0},{484,4},{488,8},{492,12},{496,16},{500,20},{504,24},{508,2... | collective-permute-start | bytes 393224 | tf_op jit(solution)/shard_map/ppermute | solution.py:260
  13.2 12.5 %all_to_all.10.mem = bf16[8,16,128]{2,1,0:T(8,128)(2,1)S(1)} all-to-all(bf16[8,16,128]{2,1,0:T(8,128)(2,1)} %get-tuple-element.15), channel_id=1, replica_groups={{0,4,8,12,16,20,24,28},{32,36,40,44,48,52,56,60},{64,68,72,76,80,84,88,..., dimensions={0} | all-to-all | bytes 65536 | tf_op jit(solution)/shard_map/all_to_all | solution.py:263
  25.6 0.0 collective-permute-done.row1
  25.7 0.5 collective-permute-done.1.row2
  26.1 0.9 %shard_map.94.far = bf16[16,128,128]{2,1,0:T(8,128)(2,1)} custom-call(bf16[8,16,128]{2,1,0:T(8,128)(2,1)S(1)} %all_to_all.10.mem, bf16[512,128]{1,0:T(8,128)(2,1)S(1)} %collective-permute-done.row1, bf16[512,128]{1,0:T(8,128)(2,1)S(1)} %collective-permute-done.1.row2), custom_call_target="tpu_custom_call" | custom-call | flops 1000 | bytes 1024 | tf_op jit(solution)/shard_map/pallas_call | solution.py:223
  27.0 0.0 copy-start
  27.0 9.0 %all-to-all-start.1 = ((bf16[16,128,128]{2,1,0:T(8,128)(2,1)}), bf16[16,128,128]{2,1,0:T(8,128)(2,1)S(1)}, u32[]{:S(2)}, u32[]{:S(2)}) async-start(bf16[16,128,128]{2,1,0:T(8,128)(2,1)} %shard_map.94.far), calls=%async_computation.1 | async-start | bytes 1048576 | tf_op jit(solution)/shard_map/all_to_all | solution.py:274
  36.0 0.0 copy-done
  36.0 0.0 copy-start.3
  36.1 0.1 shard_map.95
  36.1 0.0 copy-start.1
  36.1 3.0 %collective-permute-start.4 = (bf16[1024,128]{1,0:T(8,128)(2,1)S(1)}, bf16[1024,128]{1,0:T(8,128)(2,1)S(1)}, u32[]{:S(2)}, u32[]{:S(2)}) collective-permute-start(bf16[1024,128]{1,0:T(8,128)(2,1)S(1)} %get-tuple-element.18), channel_id=1, source_target_pairs={{0,12},{4,0},{8,4},{12,8},{16,28},{20,16},{24,20},{28,24},{32,44},... | collective-permute-start | bytes 786440 | tf_op jit(solution)/shard_map/ppermute | solution.py:280
  39.2 2.4 %collective-permute-start.2 = (bf16[1024,128]{1,0:T(8,128)(2,1)S(1)}, bf16[1024,128]{1,0:T(8,128)(2,1)S(1)}, u32[]{:S(2)}, u32[]{:S(2)}) collective-permute-start(bf16[1024,128]{1,0:T(8,128)(2,1)S(1)} %get-tuple-element.16), channel_id=1, source_target_pairs={{0,4},{4,8},{8,12},{12,0},{16,20},{20,24},{24,28},{28,16},{32,36},... | collective-permute-start | bytes 786440 | tf_op jit(solution)/shard_map/ppermute | solution.py:280
  41.6 3.2 %collective-permute-start.3 = (bf16[512,128]{1,0:T(8,128)(2,1)S(1)}, bf16[512,128]{1,0:T(8,128)(2,1)S(1)}, u32[]{:S(2)}, u32[]{:S(2)}) collective-permute-start(bf16[512,128]{1,0:T(8,128)(2,1)S(1)} %get-tuple-element.17), channel_id=1, source_target_pairs={{0,8},{4,12},{8,0},{12,4},{16,24},{20,28},{24,16},{28,20},{32,40},... | collective-permute-start | bytes 393224 | tf_op jit(solution)/shard_map/ppermute | solution.py:280
  44.8 0.0 collective-permute-done.4.r3
  44.8 0.0 copy-start.2
  44.8 3.6 %collective-permute-start.5 = (bf16[512,128]{1,0:T(8,128)(2,1)S(1)}, bf16[512,128]{1,0:T(8,128)(2,1)S(1)}, u32[]{:S(2)}, u32[]{:S(2)}) collective-permute-start(bf16[512,128]{1,0:T(8,128)(2,1)S(1)} %slice.4), channel_id=1, source_target_pairs={{0,12},{4,0},{8,4},{12,8},{16,28},{20,16},{24,20},{28,24},{32,44},... | collective-permute-start | bytes 393224 | tf_op jit(solution)/shard_map/ppermute | solution.py:285
  48.4 0.0 copy-done.3
  48.4 0.8 %shard_map.92.bias = bf16[1664,128]{1,0:T(8,128)(2,1)S(1)} custom-call(s32[128]{0:T(128)S(1)} %copy-done.3), custom_call_target="tpu_custom_call" | custom-call | flops 1000 | bytes 1024 | tf_op jit(solution)/shard_map/pallas_call | solution.py:223
  49.2 0.0 copy-done.1
  49.2 0.0 copy-done.2
  49.3 1.6 %shard_map.91.rotq = bf16[16,128,128]{2,1,0:T(8,128)(2,1)S(1)} custom-call(s32[128]{0:T(128)S(1)} %copy-done.3, f32[8,128]{1,0:T(8,128)S(1)} %copy-done.2, bf16[128,16,128]{2,1,0:T(8,128)(2,1)S(1)} %copy-done.1), custom_call_target="tpu_custom_call" | custom-call | flops 1000 | bytes 1024 | tf_op jit(solution)/shard_map/pallas_call | solution.py:223
  50.8 0.0 collective-permute-done.3.r2
  50.9 0.0 collective-permute-done.2.r1
  50.9 0.0 collective-permute-done.5.passed
  50.9 3.4 %all-to-all-done.1.mem = bf16[16,128,128]{2,1,0:T(8,128)(2,1)S(1)} async-done(((bf16[16,128,128]{2,1,0:T(8,128)(2,1)}), bf16[16,128,128]{2,1,0:T(8,128)(2,1)S(1)}, u32[]{:S(2)}, u32[]{:S(2)}) %all-to-all-start.1) | async-done | bytes 524320 | tf_op jit(solution)/shard_map/all_to_all | solution.py:274
  54.3 2.2 %shard_map.97 = (bf16[32,2048]{1,0:T(8,128)(2,1)S(1)}, bf16[32,2048]{1,0:T(8,128)(2,1)S(1)}) custom-call(bf16[16,128,128]{2,1,0:T(8,128)(2,1)S(1)} %shard_map.91.rotq, bf16[1664,128]{1,0:T(8,128)(2,1)S(1)} %shard_map.92.bias, bf16[512,128]{1,0:T(8,128)(2,1)S(1)} %copy-done, bf16[512,128]{1,0:T(8,128)(2,1)S(1)} %collective-permute-done.row1, ...), custom_call_target="tpu_custom_call" | custom-call | flops 1000000 | bytes 1024 | tf_op jit(solution)/shard_map/pallas_call | solution.py:223
  56.5 1.9 %collective-permute-start.7 = (bf16[32,2048]{1,0:T(8,128)(2,1)S(1)}, bf16[32,2048]{1,0:T(8,128)(2,1)S(1)}, u32[]{:S(2)}, u32[]{:S(2)}) collective-permute-start(bf16[32,2048]{1,0:T(8,128)(2,1)S(1)} %get-tuple-element.21), channel_id=1, source_target_pairs={{0,2},{1,3},{2,0},{3,1},{4,6},{5,7},{6,4},{7,5},{8,10},{9,11},{10,... | collective-permute-start | bytes 393224 | tf_op jit(solution)/shard_map/ppermute | solution.py:298
  58.4 6.4 %collective-permute-start.8 = (bf16[32,2048]{1,0:T(8,128)(2,1)S(1)}, bf16[32,2048]{1,0:T(8,128)(2,1)S(1)}, u32[]{:S(2)}, u32[]{:S(2)}) collective-permute-start(bf16[32,2048]{1,0:T(8,128)(2,1)S(1)} %get-tuple-element.22), channel_id=1, source_target_pairs={{0,3},{1,2},{2,1},{3,0},{4,7},{5,6},{6,5},{7,4},{8,11},{9,10},{10,... | collective-permute-start | bytes 393224 | tf_op jit(solution)/shard_map/ppermute | solution.py:298
  64.9 2.2 %shard_map.96 = (bf16[32,2048]{1,0:T(8,128)(2,1)S(1)}, bf16[32,2048]{1,0:T(8,128)(2,1)S(1)}) custom-call(bf16[16,128,128]{2,1,0:T(8,128)(2,1)S(1)} %shard_map.91.rotq, bf16[1664,128]{1,0:T(8,128)(2,1)S(1)} %shard_map.92.bias, bf16[512,128]{1,0:T(8,128)(2,1)S(1)} %copy-done, bf16[512,128]{1,0:T(8,128)(2,1)S(1)} %collective-permute-done.row1, ...), custom_call_target="tpu_custom_call" | custom-call | flops 1000000 | bytes 1024 | tf_op jit(solution)/shard_map/pallas_call | solution.py:223
  67.1 1.9 %collective-permute-start.6 = (bf16[32,2048]{1,0:T(8,128)(2,1)S(1)}, bf16[32,2048]{1,0:T(8,128)(2,1)S(1)}, u32[]{:S(2)}, u32[]{:S(2)}) collective-permute-start(bf16[32,2048]{1,0:T(8,128)(2,1)S(1)} %get-tuple-element.20), channel_id=1, source_target_pairs={{0,1},{1,0},{2,3},{3,2},{4,5},{5,4},{6,7},{7,6},{8,9},{9,8},{10,11... | collective-permute-start | bytes 393224 | tf_op jit(solution)/shard_map/ppermute | solution.py:298
  69.0 0.0 collective-permute-done.7.c
  69.0 0.0 collective-permute-done.8.d
  69.1 1.3 %collective-permute-done.6.b = bf16[32,2048]{1,0:T(8,128)(2,1)S(1)} collective-permute-done((bf16[32,2048]{1,0:T(8,128)(2,1)S(1)}, bf16[32,2048]{1,0:T(8,128)(2,1)S(1)}, u32[]{:S(2)}, u32[]{:S(2)}) %collective-permute-start.6) | collective-permute-done | bytes 131104 | tf_op jit(solution)/shard_map/ppermute | solution.py:298
  70.3 0.8 %shard_map.98 = bf16[32,8192]{1,0:T(8,128)(2,1)} custom-call(bf16[32,2048]{1,0:T(8,128)(2,1)S(1)} %get-tuple-element.19.a, bf16[32,2048]{1,0:T(8,128)(2,1)S(1)} %collective-permute-done.6.b, bf16[32,2048]{1,0:T(8,128)(2,1)S(1)} %collective-permute-done.7.c, bf16[32,2048]{1,0:T(8,128)(2,1)S(1)} %collective-permute-done.8.d), custom_call_target="tpu_custom_call" | custom-call | flops 100000000 | bytes 1024 | tf_op jit(solution)/shard_map/pallas_call | solution.py:223
  (1 shorter events, 0.0 us)
Async XLA Ops:
  2.5 23.1 %collective-permute-start = (bf16[512,128]{1,0:T(8,128)(2,1)}, bf16[512,128]{1,0:T(8,128)(2,1)S(1)}, u32[]{:S(2)}, u32[]{:S(2)}) collective-permute-start(bf16[512,128]{1,0:T(8,128)(2,1)} %get-tuple-element.14.own), channel_id=1, source_target_pairs={{496,0},{500,4},{504,8},{508,12},{0,16},{4,20},{8,24},{12,28},{16,... | collective-permute-start | bytes 393224 | tf_op jit(solution)/shard_map/ppermute | solution.py:260
  7.4 18.7 %collective-permute-start.1 = (bf16[512,128]{1,0:T(8,128)(2,1)}, bf16[512,128]{1,0:T(8,128)(2,1)S(1)}, u32[]{:S(2)}, u32[]{:S(2)}) collective-permute-start(bf16[512,128]{1,0:T(8,128)(2,1)} %get-tuple-element.14.own), channel_id=1, source_target_pairs={{480,0},{484,4},{488,8},{492,12},{496,16},{500,20},{504,24},{508,2... | collective-permute-start | bytes 393224 | tf_op jit(solution)/shard_map/ppermute | solution.py:260
  27.0 9.1 %copy-start = (bf16[512,128]{1,0:T(8,128)(2,1)S(1)}, bf16[512,128]{1,0:T(8,128)(2,1)}, u32[]{:S(2)}) copy-start(bf16[512,128]{1,0:T(8,128)(2,1)} %get-tuple-element.14.own) | copy-start | bytes 393220
  27.0 27.3 %all-to-all-start.1 = ((bf16[16,128,128]{2,1,0:T(8,128)(2,1)}), bf16[16,128,128]{2,1,0:T(8,128)(2,1)S(1)}, u32[]{:S(2)}, u32[]{:S(2)}) async-start(bf16[16,128,128]{2,1,0:T(8,128)(2,1)} %shard_map.94.far), calls=%async_computation.1 | async-start | bytes 1048576 | tf_op jit(solution)/shard_map/all_to_all | solution.py:274
  36.0 12.4 %copy-start.3 = (s32[128]{0:T(128)S(1)}, s32[128]{0:T(128)}, u32[]{:S(2)}) copy-start(s32[128]{0:T(128)} %bs.5) | copy-start | bytes 1540
  36.1 13.1 %copy-start.1 = (bf16[128,16,128]{2,1,0:T(8,128)(2,1)S(1)}, bf16[128,16,128]{2,1,0:T(8,128)(2,1)}, u32[]{:S(2)}) copy-start(bf16[128,16,128]{2,1,0:T(8,128)(2,1)} %q.1) | copy-start | bytes 1572868
  36.1 8.6 %collective-permute-start.4 = (bf16[1024,128]{1,0:T(8,128)(2,1)S(1)}, bf16[1024,128]{1,0:T(8,128)(2,1)S(1)}, u32[]{:S(2)}, u32[]{:S(2)}) collective-permute-start(bf16[1024,128]{1,0:T(8,128)(2,1)S(1)} %get-tuple-element.18), channel_id=1, source_target_pairs={{0,12},{4,0},{8,4},{12,8},{16,28},{20,16},{24,20},{28,24},{32,44},... | collective-permute-start | bytes 786440 | tf_op jit(solution)/shard_map/ppermute | solution.py:280
  39.2 11.7 %collective-permute-start.2 = (bf16[1024,128]{1,0:T(8,128)(2,1)S(1)}, bf16[1024,128]{1,0:T(8,128)(2,1)S(1)}, u32[]{:S(2)}, u32[]{:S(2)}) collective-permute-start(bf16[1024,128]{1,0:T(8,128)(2,1)S(1)} %get-tuple-element.16), channel_id=1, source_target_pairs={{0,4},{4,8},{8,12},{12,0},{16,20},{20,24},{24,28},{28,16},{32,36},... | collective-permute-start | bytes 786440 | tf_op jit(solution)/shard_map/ppermute | solution.py:280
  41.6 9.3 %collective-permute-start.3 = (bf16[512,128]{1,0:T(8,128)(2,1)S(1)}, bf16[512,128]{1,0:T(8,128)(2,1)S(1)}, u32[]{:S(2)}, u32[]{:S(2)}) collective-permute-start(bf16[512,128]{1,0:T(8,128)(2,1)S(1)} %get-tuple-element.17), channel_id=1, source_target_pairs={{0,8},{4,12},{8,0},{12,4},{16,24},{20,28},{24,16},{28,20},{32,40},... | collective-permute-start | bytes 393224 | tf_op jit(solution)/shard_map/ppermute | solution.py:280
  44.8 4.5 %copy-start.2 = (f32[8,128]{1,0:T(8,128)S(1)}, f32[8,128]{1,0:T(8,128)}, u32[]{:S(2)}) copy-start(f32[8,128]{1,0:T(8,128)} %constant.2.clone.freqs) | copy-start | bytes 12292
  44.8 6.1 %collective-permute-start.5 = (bf16[512,128]{1,0:T(8,128)(2,1)S(1)}, bf16[512,128]{1,0:T(8,128)(2,1)S(1)}, u32[]{:S(2)}, u32[]{:S(2)}) collective-permute-start(bf16[512,128]{1,0:T(8,128)(2,1)S(1)} %slice.4), channel_id=1, source_target_pairs={{0,12},{4,0},{8,4},{12,8},{16,28},{20,16},{24,20},{28,24},{32,44},... | collective-permute-start | bytes 393224 | tf_op jit(solution)/shard_map/ppermute | solution.py:285
  56.5 12.5 %collective-permute-start.7 = (bf16[32,2048]{1,0:T(8,128)(2,1)S(1)}, bf16[32,2048]{1,0:T(8,128)(2,1)S(1)}, u32[]{:S(2)}, u32[]{:S(2)}) collective-permute-start(bf16[32,2048]{1,0:T(8,128)(2,1)S(1)} %get-tuple-element.21), channel_id=1, source_target_pairs={{0,2},{1,3},{2,0},{3,1},{4,6},{5,7},{6,4},{7,5},{8,10},{9,11},{10,... | collective-permute-start | bytes 393224 | tf_op jit(solution)/shard_map/ppermute | solution.py:298
  58.4 10.6 %collective-permute-start.8 = (bf16[32,2048]{1,0:T(8,128)(2,1)S(1)}, bf16[32,2048]{1,0:T(8,128)(2,1)S(1)}, u32[]{:S(2)}, u32[]{:S(2)}) collective-permute-start(bf16[32,2048]{1,0:T(8,128)(2,1)S(1)} %get-tuple-element.22), channel_id=1, source_target_pairs={{0,3},{1,2},{2,1},{3,0},{4,7},{5,6},{6,5},{7,4},{8,11},{9,10},{10,... | collective-permute-start | bytes 393224 | tf_op jit(solution)/shard_map/ppermute | solution.py:298
  67.1 3.2 %collective-permute-start.6 = (bf16[32,2048]{1,0:T(8,128)(2,1)S(1)}, bf16[32,2048]{1,0:T(8,128)(2,1)S(1)}, u32[]{:S(2)}, u32[]{:S(2)}) collective-permute-start(bf16[32,2048]{1,0:T(8,128)(2,1)S(1)} %get-tuple-element.20), channel_id=1, source_target_pairs={{0,1},{1,0},{2,3},{3,2},{4,5},{5,4},{6,7},{7,6},{8,9},{9,8},{10,11... | collective-permute-start | bytes 393224 | tf_op jit(solution)/shard_map/ppermute | solution.py:298

commit v13 on v12

--- a/solution.py
+++ b/solution.py
@@ -98,7 +98,7 @@
         rotq[h] = turn(scr[:, h, :], cosine, sine)
 
 
-def far_kernel(mem, row1, row2, far, scr):
+def far_kernel(mem, row1, row2, rotq, bias, far, scr):
     scr[...] = mem[...].astype(F32)
     kinds = 2 * GROUPS * SLOTS
     slots = jnp.concatenate([scr[:, r, :] for r in range(kinds)], axis=0).astype(BF)
@@ -262,14 +262,14 @@
     )
     mem = lax.all_to_all(mem, "ctx", 0, 0, axis_index_groups=near)
     rotq = call(
-        query_kernel, shape(HEADS, TOK, HD), [pltpu.VMEM((TOK, HEADS, HD), F32)], 10**3,
+        query_kernel, shape(HEADS, TOK, HD), [pltpu.VMEM((TOK, HEADS, HD), F32)], 10**9,
         (SM, VM, VM),
         block_start, freqs, queries,
     )
     bias = call(bias_kernel, shape(KEYS, TOK), [], 10**3, (SM,), block_start)
     far = call(
         far_kernel, shape(FAR, pack * PIECE, HD),
-        [pltpu.VMEM((NEAR, pack * SLOTS, HD), F32)], 10**3, (VM, pl.ANY, pl.ANY), mem, row1, row2,
+        [pltpu.VMEM((NEAR, pack * SLOTS, HD), F32)], 10**3, (VM,) + (pl.ANY,) * 4, mem, row1, row2, rotq, bias,
     )
     mem = lax.all_to_all(far, "ctx", 0, 0, axis_index_groups=strided)
     rings = call(

time: 71.8 us -> 71.4 us (level)
  blocking collectives: 12.5 us -> 0 us
  waiting for transfers between devices: 5.18 us -> 12.1 us
  starting transfers between devices: 42.2 us -> 47.4 us
    all_to_all x1 -> x0, blocking collectives: 12.5 us -> none  [shards(): mem = lax.all_to_all(mem, 'ctx', 0, 0, axis_index_groups=near)]
    all_to_all x0 -> x1, starting transfers between devices: none -> 7.05 us  [shards(): mem = lax.all_to_all(mem, 'ctx', 0, 0, axis_index_groups=near)]
    all_to_all x0 -> x1, waiting for transfers between devices: none -> 2.67 us  [shards(): mem = lax.all_to_all(mem, 'ctx', 0, 0, axis_index_groups=near)]
    ppermute x3, waiting for transfers between devices: 0.01 us -> 2.12 us  [shards(): lax.ppermute(x, 'ctx', [(i, i // RING * RING + (i + s) % RING) for i in r...]
    ppermute x2, waiting for transfers between devices: 0.46 us -> 2.23 us  [shards(): lax.ppermute(own, 'ctx', [((i - d) % BLOCKS, i) for i in range(BLOCKS)])]
    all_to_all x1, starting transfers between devices: 9.04 us -> 7.57 us  [shards(): mem = lax.all_to_all(far, 'ctx', 0, 0, axis_index_groups=strided)]
    ppermute x1, waiting for transfers between devices: 0.01 us -> 0.91 us  [shards(): lax.ppermute(turned[3][TOKP:], 'ctx', [(i, i // RING * RING + (i + 3) % R...]
  transfers between devices with their start and end apart: 10 -> 11, of which waited for: 3 -> 6; matrix products, arithmetic and copies ran while one was open for 0% -> 0% of each run, Pallas kernels for 7% -> 7%
where the time goes in v13:
time: 71.4 us; the launch traced here: 70.8 us
  starting transfers between devices  47.4 us (66%)
  waiting for transfers between devices  12.1 us (17%)
  Pallas kernels  11.1 us (16%)
    pallas_call x8, Pallas kernels, call(): pl.pallas_call(kernel, out_shape=out_shape, in_specs=[pl.BlockSpec(memory...  11.1 us
    ppermute x2, starting transfers between devices, shards(): lax.ppermute(own, 'ctx', [((i - d) % BLOCKS, i) for i in range(BLOCKS)])  10.6 us
    ppermute x3, starting transfers between devices, shards(): part = lax.ppermute(part, 'kv', [(i, i ^ off) for i in range(KV)])  10.2 us
    ppermute x3, starting transfers between devices, shards(): lax.ppermute(x, 'ctx', [(i, i // RING * RING + (i + s) % RING) for i in r...  8.93 us
    all_to_all x1, starting transfers between devices, shards(): mem = lax.all_to_all(far, 'ctx', 0, 0, axis_index_groups=strided)  7.57 us
    all_to_all x1, starting transfers between devices, shards(): mem = lax.all_to_all(mem, 'ctx', 0, 0, axis_index_groups=near)  7.05 us
    ppermute x1, starting transfers between devices, shards(): lax.ppermute(turned[3][TOKP:], 'ctx', [(i, i // RING * RING + (i + 3) % R...  3.03 us
    all_to_all x1, waiting for transfers between devices, shards(): mem = lax.all_to_all(far, 'ctx', 0, 0, axis_index_groups=strided)  2.84 us
  transfers between devices with their start and end apart: 11, of which 6 were waited for; matrix products, arithmetic and copies ran while one was open for 0% of the time, Pallas kernels for 7%

profile of v13, /device:TPU:1, one launch (start us, length us, event | category | flops | bytes accessed | tf_op | source)
XLA Modules:
  0.0 70.8 jit_solution(2981803349561850495)
XLA Ops:
  0.0 0.0 copy-start.2
  0.0 2.6 %shard_map.93 = (bf16[512,128]{1,0:T(8,128)(2,1)}, bf16[8,16,128]{2,1,0:T(8,128)(2,1)}) custom-call(s32[128]{0:T(128)} %bs.5, f32[8,128]{1,0:T(8,128)} %constant.2.clone.freqs, bf16[128,2,128]{2,1,0:T(2,128)(2,1)} %k.1, bf16[128,2,128]{2,1,0:T(2,128)(2,1)} %v.1, f32[32,128]{1,0:T(8,128)} %dk.1, f32[128,128]{1,0:T(8,128)} %pk.1, f32[32,128]{1,0:T(8,128)} %dv.1, ...), custom_call_target="tpu_custom_call" | custom-call | flops 1000000000 | bytes 1024 | tf_op jit(solution)/shard_map/pallas_call | solution.py:223
  2.6 6.6 %collective-permute-start.1 = (bf16[512,128]{1,0:T(8,128)(2,1)}, bf16[512,128]{1,0:T(8,128)(2,1)S(1)}, u32[]{:S(2)}, u32[]{:S(2)}) collective-permute-start(bf16[512,128]{1,0:T(8,128)(2,1)} %get-tuple-element.14.own), channel_id=1, source_target_pairs={{480,0},{484,4},{488,8},{492,12},{496,16},{500,20},{504,24},{508,2... | collective-permute-start | bytes 393224 | tf_op jit(solution)/shard_map/ppermute | solution.py:260
  9.2 4.0 %collective-permute-start = (bf16[512,128]{1,0:T(8,128)(2,1)}, bf16[512,128]{1,0:T(8,128)(2,1)S(1)}, u32[]{:S(2)}, u32[]{:S(2)}) collective-permute-start(bf16[512,128]{1,0:T(8,128)(2,1)} %get-tuple-element.14.own), channel_id=1, source_target_pairs={{496,0},{500,4},{504,8},{508,12},{0,16},{4,20},{8,24},{12,28},{16,... | collective-permute-start | bytes 393224 | tf_op jit(solution)/shard_map/ppermute | solution.py:260
  13.3 0.0 copy-start.1
  13.3 7.1 %all-to-all-start = ((bf16[8,16,128]{2,1,0:T(8,128)(2,1)}), bf16[8,16,128]{2,1,0:T(8,128)(2,1)S(1)}, u32[]{:S(2)}, u32[]{:S(2)}) async-start(bf16[8,16,128]{2,1,0:T(8,128)(2,1)} %get-tuple-element.15), calls=%async_computation | async-start | bytes 65536 | tf_op jit(solution)/shard_map/all_to_all | solution.py:263
  20.3 0.0 copy-done.1
  20.3 0.0 copy-start.3
  20.3 0.8 %shard_map.92.bias = bf16[1664,128]{1,0:T(8,128)(2,1)S(1)} custom-call(s32[128]{0:T(128)S(1)} %copy-done.1), custom_call_target="tpu_custom_call" | custom-call | flops 1000 | bytes 1024 | tf_op jit(solution)/shard_map/pallas_call | solution.py:223
  21.2 0.0 copy-done.2
  21.2 0.0 copy-done.3
  21.2 1.6 %shard_map.91.rotq = bf16[16,128,128]{2,1,0:T(8,128)(2,1)S(1)} custom-call(s32[128]{0:T(128)S(1)} %copy-done.1, f32[8,128]{1,0:T(8,128)S(1)} %copy-done.3, bf16[128,16,128]{2,1,0:T(8,128)(2,1)S(1)} %copy-done.2), custom_call_target="tpu_custom_call" | custom-call | flops 1000000000 | bytes 1024 | tf_op jit(solution)/shard_map/pallas_call | solution.py:223
  22.8 2.7 %all-to-all-done.mem = bf16[8,16,128]{2,1,0:T(8,128)(2,1)S(1)} async-done(((bf16[8,16,128]{2,1,0:T(8,128)(2,1)}), bf16[8,16,128]{2,1,0:T(8,128)(2,1)S(1)}, u32[]{:S(2)}, u32[]{:S(2)}) %all-to-all-start) | async-done | bytes 32800 | tf_op jit(solution)/shard_map/all_to_all | solution.py:263
  25.4 0.0 collective-permute-done.1.row2
  25.4 2.2 %collective-permute-done.row1 = bf16[512,128]{1,0:T(8,128)(2,1)S(1)} collective-permute-done((bf16[512,128]{1,0:T(8,128)(2,1)}, bf16[512,128]{1,0:T(8,128)(2,1)S(1)}, u32[]{:S(2)}, u32[]{:S(2)}) %collective-permute-start) | collective-permute-done | bytes 131104 | tf_op jit(solution)/shard_map/ppermute | solution.py:260
  27.7 0.9 %shard_map.94.far = bf16[16,128,128]{2,1,0:T(8,128)(2,1)} custom-call(bf16[8,16,128]{2,1,0:T(8,128)(2,1)S(1)} %all-to-all-done.mem, bf16[512,128]{1,0:T(8,128)(2,1)S(1)} %collective-permute-done.row1, bf16[512,128]{1,0:T(8,128)(2,1)S(1)} %collective-permute-done.1.row2, bf16[16,128,128]{2,1,0:T(8,128)(2,1)S(1)} %shard_map.91.rotq, ...), custom_call_target="tpu_custom_call" | custom-call | flops 1000 | bytes 1024 | tf_op jit(solution)/shard_map/pallas_call | solution.py:223
  28.5 0.0 copy-start
  28.5 7.6 %all-to-all-start.1 = ((bf16[16,128,128]{2,1,0:T(8,128)(2,1)}), bf16[16,128,128]{2,1,0:T(8,128)(2,1)S(1)}, u32[]{:S(2)}, u32[]{:S(2)}) async-start(bf16[16,128,128]{2,1,0:T(8,128)(2,1)} %shard_map.94.far), calls=%async_computation.1 | async-start | bytes 1048576 | tf_op jit(solution)/shard_map/all_to_all | solution.py:274
  36.1 0.0 copy-done
  36.1 0.1 shard_map.95
  36.2 3.4 %collective-permute-start.4 = (bf16[1024,128]{1,0:T(8,128)(2,1)S(1)}, bf16[1024,128]{1,0:T(8,128)(2,1)S(1)}, u32[]{:S(2)}, u32[]{:S(2)}) collective-permute-start(bf16[1024,128]{1,0:T(8,128)(2,1)S(1)} %get-tuple-element.18), channel_id=1, source_target_pairs={{0,12},{4,0},{8,4},{12,8},{16,28},{20,16},{24,20},{28,24},{32,44},... | collective-permute-start | bytes 786440 | tf_op jit(solution)/shard_map/ppermute | solution.py:280
  39.6 1.9 %collective-permute-start.2 = (bf16[1024,128]{1,0:T(8,128)(2,1)S(1)}, bf16[1024,128]{1,0:T(8,128)(2,1)S(1)}, u32[]{:S(2)}, u32[]{:S(2)}) collective-permute-start(bf16[1024,128]{1,0:T(8,128)(2,1)S(1)} %get-tuple-element.16), channel_id=1, source_target_pairs={{0,4},{4,8},{8,12},{12,0},{16,20},{20,24},{24,28},{28,16},{32,36},... | collective-permute-start | bytes 786440 | tf_op jit(solution)/shard_map/ppermute | solution.py:280
  41.5 3.6 %collective-permute-start.3 = (bf16[512,128]{1,0:T(8,128)(2,1)S(1)}, bf16[512,128]{1,0:T(8,128)(2,1)S(1)}, u32[]{:S(2)}, u32[]{:S(2)}) collective-permute-start(bf16[512,128]{1,0:T(8,128)(2,1)S(1)} %get-tuple-element.17), channel_id=1, source_target_pairs={{0,8},{4,12},{8,0},{12,4},{16,24},{20,28},{24,16},{28,20},{32,40},... | collective-permute-start | bytes 393224 | tf_op jit(solution)/shard_map/ppermute | solution.py:280
  45.1 0.0 collective-permute-done.4.r3
  45.2 3.0 %collective-permute-start.5 = (bf16[512,128]{1,0:T(8,128)(2,1)S(1)}, bf16[512,128]{1,0:T(8,128)(2,1)S(1)}, u32[]{:S(2)}, u32[]{:S(2)}) collective-permute-start(bf16[512,128]{1,0:T(8,128)(2,1)S(1)} %slice.4), channel_id=1, source_target_pairs={{0,12},{4,0},{8,4},{12,8},{16,28},{20,16},{24,20},{28,24},{32,44},... | collective-permute-start | bytes 393224 | tf_op jit(solution)/shard_map/ppermute | solution.py:285
  48.2 2.1 %collective-permute-done.3.r2 = bf16[512,128]{1,0:T(8,128)(2,1)S(1)} collective-permute-done((bf16[512,128]{1,0:T(8,128)(2,1)S(1)}, bf16[512,128]{1,0:T(8,128)(2,1)S(1)}, u32[]{:S(2)}, u32[]{:S(2)}) %collective-permute-start.3) | collective-permute-done | bytes 131104 | tf_op jit(solution)/shard_map/ppermute | solution.py:280
  50.3 0.0 collective-permute-done.2.r1
  50.3 0.9 %collective-permute-done.5.passed = bf16[512,128]{1,0:T(8,128)(2,1)S(1)} collective-permute-done((bf16[512,128]{1,0:T(8,128)(2,1)S(1)}, bf16[512,128]{1,0:T(8,128)(2,1)S(1)}, u32[]{:S(2)}, u32[]{:S(2)}) %collective-permute-start.5) | collective-permute-done | bytes 131104 | tf_op jit(solution)/shard_map/ppermute | solution.py:285
  51.2 2.8 %all-to-all-done.1.mem = bf16[16,128,128]{2,1,0:T(8,128)(2,1)S(1)} async-done(((bf16[16,128,128]{2,1,0:T(8,128)(2,1)}), bf16[16,128,128]{2,1,0:T(8,128)(2,1)S(1)}, u32[]{:S(2)}, u32[]{:S(2)}) %all-to-all-start.1) | async-done | bytes 524320 | tf_op jit(solution)/shard_map/all_to_all | solution.py:274
  54.1 2.2 %shard_map.97 = (bf16[32,2048]{1,0:T(8,128)(2,1)S(1)}, bf16[32,2048]{1,0:T(8,128)(2,1)S(1)}) custom-call(bf16[16,128,128]{2,1,0:T(8,128)(2,1)S(1)} %shard_map.91.rotq, bf16[1664,128]{1,0:T(8,128)(2,1)S(1)} %shard_map.92.bias, bf16[512,128]{1,0:T(8,128)(2,1)S(1)} %copy-done, bf16[512,128]{1,0:T(8,128)(2,1)S(1)} %collective-permute-done.row1, ...), custom_call_target="tpu_custom_call" | custom-call | flops 1000000 | bytes 1024 | tf_op jit(solution)/shard_map/pallas_call | solution.py:223
  56.3 1.9 %collective-permute-start.7 = (bf16[32,2048]{1,0:T(8,128)(2,1)S(1)}, bf16[32,2048]{1,0:T(8,128)(2,1)S(1)}, u32[]{:S(2)}, u32[]{:S(2)}) collective-permute-start(bf16[32,2048]{1,0:T(8,128)(2,1)S(1)} %get-tuple-element.21), channel_id=1, source_target_pairs={{0,2},{1,3},{2,0},{3,1},{4,6},{5,7},{6,4},{7,5},{8,10},{9,11},{10,... | collective-permute-start | bytes 393224 | tf_op jit(solution)/shard_map/ppermute | solution.py:298
  58.2 6.3 %collective-permute-start.8 = (bf16[32,2048]{1,0:T(8,128)(2,1)S(1)}, bf16[32,2048]{1,0:T(8,128)(2,1)S(1)}, u32[]{:S(2)}, u32[]{:S(2)}) collective-permute-start(bf16[32,2048]{1,0:T(8,128)(2,1)S(1)} %get-tuple-element.22), channel_id=1, source_target_pairs={{0,3},{1,2},{2,1},{3,0},{4,7},{5,6},{6,5},{7,4},{8,11},{9,10},{10,... | collective-permute-start | bytes 393224 | tf_op jit(solution)/shard_map/ppermute | solution.py:298
  64.6 2.2 %shard_map.96 = (bf16[32,2048]{1,0:T(8,128)(2,1)S(1)}, bf16[32,2048]{1,0:T(8,128)(2,1)S(1)}) custom-call(bf16[16,128,128]{2,1,0:T(8,128)(2,1)S(1)} %shard_map.91.rotq, bf16[1664,128]{1,0:T(8,128)(2,1)S(1)} %shard_map.92.bias, bf16[512,128]{1,0:T(8,128)(2,1)S(1)} %copy-done, bf16[512,128]{1,0:T(8,128)(2,1)S(1)} %collective-permute-done.row1, ...), custom_call_target="tpu_custom_call" | custom-call | flops 1000000 | bytes 1024 | tf_op jit(solution)/shard_map/pallas_call | solution.py:223
  66.8 1.9 %collective-permute-start.6 = (bf16[32,2048]{1,0:T(8,128)(2,1)S(1)}, bf16[32,2048]{1,0:T(8,128)(2,1)S(1)}, u32[]{:S(2)}, u32[]{:S(2)}) collective-permute-start(bf16[32,2048]{1,0:T(8,128)(2,1)S(1)} %get-tuple-element.20), channel_id=1, source_target_pairs={{0,1},{1,0},{2,3},{3,2},{4,5},{5,4},{6,7},{7,6},{8,9},{9,8},{10,11... | collective-permute-start | bytes 393224 | tf_op jit(solution)/shard_map/ppermute | solution.py:298
  68.7 0.0 collective-permute-done.7.c
  68.7 0.0 collective-permute-done.8.d
  68.7 1.3 %collective-permute-done.6.b = bf16[32,2048]{1,0:T(8,128)(2,1)S(1)} collective-permute-done((bf16[32,2048]{1,0:T(8,128)(2,1)S(1)}, bf16[32,2048]{1,0:T(8,128)(2,1)S(1)}, u32[]{:S(2)}, u32[]{:S(2)}) %collective-permute-start.6) | collective-permute-done | bytes 131104 | tf_op jit(solution)/shard_map/ppermute | solution.py:298
  70.0 0.8 %shard_map.98 = bf16[32,8192]{1,0:T(8,128)(2,1)} custom-call(bf16[32,2048]{1,0:T(8,128)(2,1)S(1)} %get-tuple-element.19.a, bf16[32,2048]{1,0:T(8,128)(2,1)S(1)} %collective-permute-done.6.b, bf16[32,2048]{1,0:T(8,128)(2,1)S(1)} %collective-permute-done.7.c, bf16[32,2048]{1,0:T(8,128)(2,1)S(1)} %collective-permute-done.8.d), custom_call_target="tpu_custom_call" | custom-call | flops 100000000 | bytes 1024 | tf_op jit(solution)/shard_map/pallas_call | solution.py:223
  (1 shorter events, 0.0 us)
Async XLA Ops:
  0.0 21.2 %copy-start.2 = (bf16[128,16,128]{2,1,0:T(8,128)(2,1)S(1)}, bf16[128,16,128]{2,1,0:T(8,128)(2,1)}, u32[]{:S(2)}) copy-start(bf16[128,16,128]{2,1,0:T(8,128)(2,1)} %q.1) | copy-start | bytes 1572868
  2.6 22.8 %collective-permute-start.1 = (bf16[512,128]{1,0:T(8,128)(2,1)}, bf16[512,128]{1,0:T(8,128)(2,1)S(1)}, u32[]{:S(2)}, u32[]{:S(2)}) collective-permute-start(bf16[512,128]{1,0:T(8,128)(2,1)} %get-tuple-element.14.own), channel_id=1, source_target_pairs={{480,0},{484,4},{488,8},{492,12},{496,16},{500,20},{504,24},{508,2... | collective-permute-start | bytes 393224 | tf_op jit(solution)/shard_map/ppermute | solution.py:260
  9.2 18.4 %collective-permute-start = (bf16[512,128]{1,0:T(8,128)(2,1)}, bf16[512,128]{1,0:T(8,128)(2,1)S(1)}, u32[]{:S(2)}, u32[]{:S(2)}) collective-permute-start(bf16[512,128]{1,0:T(8,128)(2,1)} %get-tuple-element.14.own), channel_id=1, source_target_pairs={{496,0},{500,4},{504,8},{508,12},{0,16},{4,20},{8,24},{12,28},{16,... | collective-permute-start | bytes 393224 | tf_op jit(solution)/shard_map/ppermute | solution.py:260
  13.3 7.1 %copy-start.1 = (s32[128]{0:T(128)S(1)}, s32[128]{0:T(128)}, u32[]{:S(2)}) copy-start(s32[128]{0:T(128)} %bs.5) | copy-start | bytes 1540
  13.3 12.2 %all-to-all-start = ((bf16[8,16,128]{2,1,0:T(8,128)(2,1)}), bf16[8,16,128]{2,1,0:T(8,128)(2,1)S(1)}, u32[]{:S(2)}, u32[]{:S(2)}) async-start(bf16[8,16,128]{2,1,0:T(8,128)(2,1)} %get-tuple-element.15), calls=%async_computation | async-start | bytes 65536 | tf_op jit(solution)/shard_map/all_to_all | solution.py:263
  20.3 0.8 %copy-start.3 = (f32[8,128]{1,0:T(8,128)S(1)}, f32[8,128]{1,0:T(8,128)}, u32[]{:S(2)}) copy-start(f32[8,128]{1,0:T(8,128)} %constant.2.clone.freqs) | copy-start | bytes 12292
  28.5 7.6 %copy-start = (bf16[512,128]{1,0:T(8,128)(2,1)S(1)}, bf16[512,128]{1,0:T(8,128)(2,1)}, u32[]{:S(2)}) copy-start(bf16[512,128]{1,0:T(8,128)(2,1)} %get-tuple-element.14.own) | copy-start | bytes 393220
  28.5 25.6 %all-to-all-start.1 = ((bf16[16,128,128]{2,1,0:T(8,128)(2,1)}), bf16[16,128,128]{2,1,0:T(8,128)(2,1)S(1)}, u32[]{:S(2)}, u32[]{:S(2)}) async-start(bf16[16,128,128]{2,1,0:T(8,128)(2,1)} %shard_map.94.far), calls=%async_computation.1 | async-start | bytes 1048576 | tf_op jit(solution)/shard_map/all_to_all | solution.py:274
  36.2 9.0 %collective-permute-start.4 = (bf16[1024,128]{1,0:T(8,128)(2,1)S(1)}, bf16[1024,128]{1,0:T(8,128)(2,1)S(1)}, u32[]{:S(2)}, u32[]{:S(2)}) collective-permute-start(bf16[1024,128]{1,0:T(8,128)(2,1)S(1)} %get-tuple-element.18), channel_id=1, source_target_pairs={{0,12},{4,0},{8,4},{12,8},{16,28},{20,16},{24,20},{28,24},{32,44},... | collective-permute-start | bytes 786440 | tf_op jit(solution)/shard_map/ppermute | solution.py:280
  39.6 10.8 %collective-permute-start.2 = (bf16[1024,128]{1,0:T(8,128)(2,1)S(1)}, bf16[1024,128]{1,0:T(8,128)(2,1)S(1)}, u32[]{:S(2)}, u32[]{:S(2)}) collective-permute-start(bf16[1024,128]{1,0:T(8,128)(2,1)S(1)} %get-tuple-element.16), channel_id=1, source_target_pairs={{0,4},{4,8},{8,12},{12,0},{16,20},{20,24},{24,28},{28,16},{32,36},... | collective-permute-start | bytes 786440 | tf_op jit(solution)/shard_map/ppermute | solution.py:280
  41.5 8.8 %collective-permute-start.3 = (bf16[512,128]{1,0:T(8,128)(2,1)S(1)}, bf16[512,128]{1,0:T(8,128)(2,1)S(1)}, u32[]{:S(2)}, u32[]{:S(2)}) collective-permute-start(bf16[512,128]{1,0:T(8,128)(2,1)S(1)} %get-tuple-element.17), channel_id=1, source_target_pairs={{0,8},{4,12},{8,0},{12,4},{16,24},{20,28},{24,16},{28,20},{32,40},... | collective-permute-start | bytes 393224 | tf_op jit(solution)/shard_map/ppermute | solution.py:280
  45.2 6.1 %collective-permute-start.5 = (bf16[512,128]{1,0:T(8,128)(2,1)S(1)}, bf16[512,128]{1,0:T(8,128)(2,1)S(1)}, u32[]{:S(2)}, u32[]{:S(2)}) collective-permute-start(bf16[512,128]{1,0:T(8,128)(2,1)S(1)} %slice.4), channel_id=1, source_target_pairs={{0,12},{4,0},{8,4},{12,8},{16,28},{20,16},{24,20},{28,24},{32,44},... | collective-permute-start | bytes 393224 | tf_op jit(solution)/shard_map/ppermute | solution.py:285
  56.3 12.4 %collective-permute-start.7 = (bf16[32,2048]{1,0:T(8,128)(2,1)S(1)}, bf16[32,2048]{1,0:T(8,128)(2,1)S(1)}, u32[]{:S(2)}, u32[]{:S(2)}) collective-permute-start(bf16[32,2048]{1,0:T(8,128)(2,1)S(1)} %get-tuple-element.21), channel_id=1, source_target_pairs={{0,2},{1,3},{2,0},{3,1},{4,6},{5,7},{6,4},{7,5},{8,10},{9,11},{10,... | collective-permute-start | bytes 393224 | tf_op jit(solution)/shard_map/ppermute | solution.py:298
  58.2 10.5 %collective-permute-start.8 = (bf16[32,2048]{1,0:T(8,128)(2,1)S(1)}, bf16[32,2048]{1,0:T(8,128)(2,1)S(1)}, u32[]{:S(2)}, u32[]{:S(2)}) collective-permute-start(bf16[32,2048]{1,0:T(8,128)(2,1)S(1)} %get-tuple-element.22), channel_id=1, source_target_pairs={{0,3},{1,2},{2,1},{3,0},{4,7},{5,6},{6,5},{7,4},{8,11},{9,10},{10,... | collective-permute-start | bytes 393224 | tf_op jit(solution)/shard_map/ppermute | solution.py:298
  66.8 3.2 %collective-permute-start.6 = (bf16[32,2048]{1,0:T(8,128)(2,1)S(1)}, bf16[32,2048]{1,0:T(8,128)(2,1)S(1)}, u32[]{:S(2)}, u32[]{:S(2)}) collective-permute-start(bf16[32,2048]{1,0:T(8,128)(2,1)S(1)} %get-tuple-element.20), channel_id=1, source_target_pairs={{0,1},{1,0},{2,3},{3,2},{4,5},{5,4},{6,7},{7,6},{8,9},{9,8},{10,11... | collective-permute-start | bytes 393224 | tf_op jit(solution)/shard_map/ppermute | solution.py:298

commit v14 on v13

--- a/solution.py
+++ b/solution.py
@@ -22,7 +22,7 @@
 KV = 4
 RING = 4
 ORDER = (3, 2, 1)
-NEAR = 8
+NEAR = 4
 FAR = BLOCKS // NEAR
 ROWS = TOK // KV
 RAW = (WIN + 1) * TOK

time: 71.4 us -> 70.5 us (0.987)
  starting transfers between devices: 47.4 us -> 46.2 us
    ppermute x2, waiting for transfers between devices: 2.23 us -> 5.84 us  [shards(): lax.ppermute(own, 'ctx', [((i - d) % BLOCKS, i) for i in range(BLOCKS)])]
    all_to_all x1, starting transfers between devices: 7.05 us -> 4.02 us  [shards(): mem = lax.all_to_all(mem, 'ctx', 0, 0, axis_index_groups=near)]
    all_to_all x1, waiting for transfers between devices: 2.84 us -> 0.01 us  [shards(): mem = lax.all_to_all(far, 'ctx', 0, 0, axis_index_groups=strided)]
    ppermute x3, starting transfers between devices: 8.93 us -> 9.82 us  [shards(): lax.ppermute(x, 'ctx', [(i, i // RING * RING + (i + s) % RING) for i in r...]
    ppermute x1, starting transfers between devices: 3.03 us -> 3.84 us  [shards(): lax.ppermute(turned[3][TOKP:], 'ctx', [(i, i // RING * RING + (i + 3) % R...]
    ppermute x3, starting transfers between devices: 10.2 us -> 10.9 us  [shards(): part = lax.ppermute(part, 'kv', [(i, i ^ off) for i in range(KV)])]
where the time goes in v14:
time: 70.5 us; the launch traced here: 70 us
  starting transfers between devices  46.2 us (66%)
  waiting for transfers between devices  12.4 us (18%)
  Pallas kernels  11.1 us (16%)
    pallas_call x8, Pallas kernels, call(): pl.pallas_call(kernel, out_shape=out_shape, in_specs=[pl.BlockSpec(memory...  11.1 us
    ppermute x3, starting transfers between devices, shards(): part = lax.ppermute(part, 'kv', [(i, i ^ off) for i in range(KV)])  10.9 us
    ppermute x2, starting transfers between devices, shards(): lax.ppermute(own, 'ctx', [((i - d) % BLOCKS, i) for i in range(BLOCKS)])  10.6 us
    ppermute x3, starting transfers between devices, shards(): lax.ppermute(x, 'ctx', [(i, i // RING * RING + (i + s) % RING) for i in r...  9.82 us
    all_to_all x1, starting transfers between devices, shards(): mem = lax.all_to_all(far, 'ctx', 0, 0, axis_index_groups=strided)  6.96 us
    ppermute x2, waiting for transfers between devices, shards(): lax.ppermute(own, 'ctx', [((i - d) % BLOCKS, i) for i in range(BLOCKS)])  5.84 us
    all_to_all x1, starting transfers between devices, shards(): mem = lax.all_to_all(mem, 'ctx', 0, 0, axis_index_groups=near)  4.02 us
    ppermute x1, starting transfers between devices, shards(): lax.ppermute(turned[3][TOKP:], 'ctx', [(i, i // RING * RING + (i + 3) % R...  3.84 us
  transfers between devices with their start and end apart: 11, of which 6 were waited for; matrix products, arithmetic and copies ran while one was open for 0% of the time, Pallas kernels for 7%

profile of v14, /device:TPU:1, one launch (start us, length us, event | category | flops | bytes accessed | tf_op | source)
XLA Modules:
  0.0 70.0 jit_solution(16632908246488331499)
XLA Ops:
  0.0 0.0 copy-start.2
  0.0 2.6 %shard_map.93 = (bf16[512,128]{1,0:T(8,128)(2,1)}, bf16[4,16,128]{2,1,0:T(8,128)(2,1)}) custom-call(s32[128]{0:T(128)} %bs.5, f32[8,128]{1,0:T(8,128)} %constant.2.clone.freqs, bf16[128,2,128]{2,1,0:T(2,128)(2,1)} %k.1, bf16[128,2,128]{2,1,0:T(2,128)(2,1)} %v.1, f32[32,128]{1,0:T(8,128)} %dk.1, f32[128,128]{1,0:T(8,128)} %pk.1, f32[32,128]{1,0:T(8,128)} %dv.1, ...), custom_call_target="tpu_custom_call" | custom-call | flops 1000000000 | bytes 1024 | tf_op jit(solution)/shard_map/pallas_call | solution.py:223
  2.6 6.6 %collective-permute-start.1 = (bf16[512,128]{1,0:T(8,128)(2,1)}, bf16[512,128]{1,0:T(8,128)(2,1)S(1)}, u32[]{:S(2)}, u32[]{:S(2)}) collective-permute-start(bf16[512,128]{1,0:T(8,128)(2,1)} %get-tuple-element.14.own), channel_id=1, source_target_pairs={{480,0},{484,4},{488,8},{492,12},{496,16},{500,20},{504,24},{508,2... | collective-permute-start | bytes 393224 | tf_op jit(solution)/shard_map/ppermute | solution.py:260
  9.2 4.0 %collective-permute-start = (bf16[512,128]{1,0:T(8,128)(2,1)}, bf16[512,128]{1,0:T(8,128)(2,1)S(1)}, u32[]{:S(2)}, u32[]{:S(2)}) collective-permute-start(bf16[512,128]{1,0:T(8,128)(2,1)} %get-tuple-element.14.own), channel_id=1, source_target_pairs={{496,0},{500,4},{504,8},{508,12},{0,16},{4,20},{8,24},{12,28},{16,... | collective-permute-start | bytes 393224 | tf_op jit(solution)/shard_map/ppermute | solution.py:260
  13.2 0.0 copy-start.1
  13.3 0.0 copy-start.3
  13.3 4.0 %all-to-all-start = ((bf16[4,16,128]{2,1,0:T(8,128)(2,1)}), bf16[4,16,128]{2,1,0:T(8,128)(2,1)S(1)}, u32[]{:S(2)}, u32[]{:S(2)}) async-start(bf16[4,16,128]{2,1,0:T(8,128)(2,1)} %get-tuple-element.15), calls=%async_computation | async-start | bytes 32768 | tf_op jit(solution)/shard_map/all_to_all | solution.py:263
  17.3 0.0 copy-done.2
  17.3 0.0 copy-done.1
  17.3 0.0 copy-done.3
  17.3 1.6 %shard_map.91.rotq = bf16[16,128,128]{2,1,0:T(8,128)(2,1)S(1)} custom-call(s32[128]{0:T(128)S(1)} %copy-done.1, f32[8,128]{1,0:T(8,128)S(1)} %copy-done.3, bf16[128,16,128]{2,1,0:T(8,128)(2,1)S(1)} %copy-done.2), custom_call_target="tpu_custom_call" | custom-call | flops 1000000000 | bytes 1024 | tf_op jit(solution)/shard_map/pallas_call | solution.py:223
  18.9 0.8 %shard_map.92.bias = bf16[1664,128]{1,0:T(8,128)(2,1)S(1)} custom-call(s32[128]{0:T(128)S(1)} %copy-done.1), custom_call_target="tpu_custom_call" | custom-call | flops 1000 | bytes 1024 | tf_op jit(solution)/shard_map/pallas_call | solution.py:223
  19.7 2.1 %all-to-all-done.mem = bf16[4,16,128]{2,1,0:T(8,128)(2,1)S(1)} async-done(((bf16[4,16,128]{2,1,0:T(8,128)(2,1)}), bf16[4,16,128]{2,1,0:T(8,128)(2,1)S(1)}, u32[]{:S(2)}, u32[]{:S(2)}) %all-to-all-start) | async-done | bytes 16416 | tf_op jit(solution)/shard_map/all_to_all | solution.py:263
  21.8 1.2 %collective-permute-done.1.row2 = bf16[512,128]{1,0:T(8,128)(2,1)S(1)} collective-permute-done((bf16[512,128]{1,0:T(8,128)(2,1)}, bf16[512,128]{1,0:T(8,128)(2,1)S(1)}, u32[]{:S(2)}, u32[]{:S(2)}) %collective-permute-start.1) | collective-permute-done | bytes 131104 | tf_op jit(solution)/shard_map/ppermute | solution.py:260
  23.0 4.7 %collective-permute-done.row1 = bf16[512,128]{1,0:T(8,128)(2,1)S(1)} collective-permute-done((bf16[512,128]{1,0:T(8,128)(2,1)}, bf16[512,128]{1,0:T(8,128)(2,1)S(1)}, u32[]{:S(2)}, u32[]{:S(2)}) %collective-permute-start) | collective-permute-done | bytes 131104 | tf_op jit(solution)/shard_map/ppermute | solution.py:260
  27.6 0.9 %shard_map.94.far = bf16[32,64,128]{2,1,0:T(8,128)(2,1)} custom-call(bf16[4,16,128]{2,1,0:T(8,128)(2,1)S(1)} %all-to-all-done.mem, bf16[512,128]{1,0:T(8,128)(2,1)S(1)} %collective-permute-done.row1, bf16[512,128]{1,0:T(8,128)(2,1)S(1)} %collective-permute-done.1.row2, bf16[16,128,128]{2,1,0:T(8,128)(2,1)S(1)} %shard_map.91.rotq, ...), custom_call_target="tpu_custom_call" | custom-call | flops 1000 | bytes 1024 | tf_op jit(solution)/shard_map/pallas_call | solution.py:223
  28.5 0.0 copy-start
  28.5 7.0 %all-to-all-start.1 = ((bf16[32,64,128]{2,1,0:T(8,128)(2,1)}), bf16[32,64,128]{2,1,0:T(8,128)(2,1)S(1)}, u32[]{:S(2)}, u32[]{:S(2)}) async-start(bf16[32,64,128]{2,1,0:T(8,128)(2,1)} %shard_map.94.far), calls=%async_computation.1 | async-start | bytes 1048576 | tf_op jit(solution)/shard_map/all_to_all | solution.py:274
  35.5 0.0 copy-done
  35.5 0.1 shard_map.95
  35.6 4.3 %collective-permute-start.4 = (bf16[1024,128]{1,0:T(8,128)(2,1)S(1)}, bf16[1024,128]{1,0:T(8,128)(2,1)S(1)}, u32[]{:S(2)}, u32[]{:S(2)}) collective-permute-start(bf16[1024,128]{1,0:T(8,128)(2,1)S(1)} %get-tuple-element.18), channel_id=1, source_target_pairs={{0,12},{4,0},{8,4},{12,8},{16,28},{20,16},{24,20},{28,24},{32,44},... | collective-permute-start | bytes 786440 | tf_op jit(solution)/shard_map/ppermute | solution.py:280
  39.8 1.9 %collective-permute-start.2 = (bf16[1024,128]{1,0:T(8,128)(2,1)S(1)}, bf16[1024,128]{1,0:T(8,128)(2,1)S(1)}, u32[]{:S(2)}, u32[]{:S(2)}) collective-permute-start(bf16[1024,128]{1,0:T(8,128)(2,1)S(1)} %get-tuple-element.16), channel_id=1, source_target_pairs={{0,4},{4,8},{8,12},{12,0},{16,20},{20,24},{24,28},{28,16},{32,36},... | collective-permute-start | bytes 786440 | tf_op jit(solution)/shard_map/ppermute | solution.py:280
  41.8 3.6 %collective-permute-start.3 = (bf16[512,128]{1,0:T(8,128)(2,1)S(1)}, bf16[512,128]{1,0:T(8,128)(2,1)S(1)}, u32[]{:S(2)}, u32[]{:S(2)}) collective-permute-start(bf16[512,128]{1,0:T(8,128)(2,1)S(1)} %get-tuple-element.17), channel_id=1, source_target_pairs={{0,8},{4,12},{8,0},{12,4},{16,24},{20,28},{24,16},{28,20},{32,40},... | collective-permute-start | bytes 393224 | tf_op jit(solution)/shard_map/ppermute | solution.py:280
  45.4 0.0 collective-permute-done.4.r3
  45.4 3.8 %collective-permute-start.5 = (bf16[512,128]{1,0:T(8,128)(2,1)S(1)}, bf16[512,128]{1,0:T(8,128)(2,1)S(1)}, u32[]{:S(2)}, u32[]{:S(2)}) collective-permute-start(bf16[512,128]{1,0:T(8,128)(2,1)S(1)} %slice.4), channel_id=1, source_target_pairs={{0,12},{4,0},{8,4},{12,8},{16,28},{20,16},{24,20},{28,24},{32,44},... | collective-permute-start | bytes 393224 | tf_op jit(solution)/shard_map/ppermute | solution.py:285
  49.3 1.9 %collective-permute-done.3.r2 = bf16[512,128]{1,0:T(8,128)(2,1)S(1)} collective-permute-done((bf16[512,128]{1,0:T(8,128)(2,1)S(1)}, bf16[512,128]{1,0:T(8,128)(2,1)S(1)}, u32[]{:S(2)}, u32[]{:S(2)}) %collective-permute-start.3) | collective-permute-done | bytes 131104 | tf_op jit(solution)/shard_map/ppermute | solution.py:280
  51.2 0.0 collective-permute-done.2.r1
  51.2 1.3 %collective-permute-done.5.passed = bf16[512,128]{1,0:T(8,128)(2,1)S(1)} collective-permute-done((bf16[512,128]{1,0:T(8,128)(2,1)S(1)}, bf16[512,128]{1,0:T(8,128)(2,1)S(1)}, u32[]{:S(2)}, u32[]{:S(2)}) %collective-permute-start.5) | collective-permute-done | bytes 131104 | tf_op jit(solution)/shard_map/ppermute | solution.py:285
  52.5 0.0 all-to-all-done.1.mem
  52.5 2.2 %shard_map.97 = (bf16[32,2048]{1,0:T(8,128)(2,1)S(1)}, bf16[32,2048]{1,0:T(8,128)(2,1)S(1)}) custom-call(bf16[16,128,128]{2,1,0:T(8,128)(2,1)S(1)} %shard_map.91.rotq, bf16[1664,128]{1,0:T(8,128)(2,1)S(1)} %shard_map.92.bias, bf16[512,128]{1,0:T(8,128)(2,1)S(1)} %copy-done, bf16[512,128]{1,0:T(8,128)(2,1)S(1)} %collective-permute-done.row1, ...), custom_call_target="tpu_custom_call" | custom-call | flops 1000000 | bytes 1024 | tf_op jit(solution)/shard_map/pallas_call | solution.py:223
  54.7 2.3 %collective-permute-start.7 = (bf16[32,2048]{1,0:T(8,128)(2,1)S(1)}, bf16[32,2048]{1,0:T(8,128)(2,1)S(1)}, u32[]{:S(2)}, u32[]{:S(2)}) collective-permute-start(bf16[32,2048]{1,0:T(8,128)(2,1)S(1)} %get-tuple-element.21), channel_id=1, source_target_pairs={{0,2},{1,3},{2,0},{3,1},{4,6},{5,7},{6,4},{7,5},{8,10},{9,11},{10,... | collective-permute-start | bytes 393224 | tf_op jit(solution)/shard_map/ppermute | solution.py:298
  57.0 6.7 %collective-permute-start.8 = (bf16[32,2048]{1,0:T(8,128)(2,1)S(1)}, bf16[32,2048]{1,0:T(8,128)(2,1)S(1)}, u32[]{:S(2)}, u32[]{:S(2)}) collective-permute-start(bf16[32,2048]{1,0:T(8,128)(2,1)S(1)} %get-tuple-element.22), channel_id=1, source_target_pairs={{0,3},{1,2},{2,1},{3,0},{4,7},{5,6},{6,5},{7,4},{8,11},{9,10},{10,... | collective-permute-start | bytes 393224 | tf_op jit(solution)/shard_map/ppermute | solution.py:298
  63.7 2.2 %shard_map.96 = (bf16[32,2048]{1,0:T(8,128)(2,1)S(1)}, bf16[32,2048]{1,0:T(8,128)(2,1)S(1)}) custom-call(bf16[16,128,128]{2,1,0:T(8,128)(2,1)S(1)} %shard_map.91.rotq, bf16[1664,128]{1,0:T(8,128)(2,1)S(1)} %shard_map.92.bias, bf16[512,128]{1,0:T(8,128)(2,1)S(1)} %copy-done, bf16[512,128]{1,0:T(8,128)(2,1)S(1)} %collective-permute-done.row1, ...), custom_call_target="tpu_custom_call" | custom-call | flops 1000000 | bytes 1024 | tf_op jit(solution)/shard_map/pallas_call | solution.py:223
  65.9 1.9 %collective-permute-start.6 = (bf16[32,2048]{1,0:T(8,128)(2,1)S(1)}, bf16[32,2048]{1,0:T(8,128)(2,1)S(1)}, u32[]{:S(2)}, u32[]{:S(2)}) collective-permute-start(bf16[32,2048]{1,0:T(8,128)(2,1)S(1)} %get-tuple-element.20), channel_id=1, source_target_pairs={{0,1},{1,0},{2,3},{3,2},{4,5},{5,4},{6,7},{7,6},{8,9},{9,8},{10,11... | collective-permute-start | bytes 393224 | tf_op jit(solution)/shard_map/ppermute | solution.py:298
  67.8 0.0 collective-permute-done.7.c
  67.8 0.0 collective-permute-done.8.d
  67.9 1.3 %collective-permute-done.6.b = bf16[32,2048]{1,0:T(8,128)(2,1)S(1)} collective-permute-done((bf16[32,2048]{1,0:T(8,128)(2,1)S(1)}, bf16[32,2048]{1,0:T(8,128)(2,1)S(1)}, u32[]{:S(2)}, u32[]{:S(2)}) %collective-permute-start.6) | collective-permute-done | bytes 131104 | tf_op jit(solution)/shard_map/ppermute | solution.py:298
  69.2 0.8 %shard_map.98 = bf16[32,8192]{1,0:T(8,128)(2,1)} custom-call(bf16[32,2048]{1,0:T(8,128)(2,1)S(1)} %get-tuple-element.19.a, bf16[32,2048]{1,0:T(8,128)(2,1)S(1)} %collective-permute-done.6.b, bf16[32,2048]{1,0:T(8,128)(2,1)S(1)} %collective-permute-done.7.c, bf16[32,2048]{1,0:T(8,128)(2,1)S(1)} %collective-permute-done.8.d), custom_call_target="tpu_custom_call" | custom-call | flops 100000000 | bytes 1024 | tf_op jit(solution)/shard_map/pallas_call | solution.py:223
  (1 shorter events, 0.0 us)
Async XLA Ops:
  0.0 17.3 %copy-start.2 = (bf16[128,16,128]{2,1,0:T(8,128)(2,1)S(1)}, bf16[128,16,128]{2,1,0:T(8,128)(2,1)}, u32[]{:S(2)}) copy-start(bf16[128,16,128]{2,1,0:T(8,128)(2,1)} %q.1) | copy-start | bytes 1572868
  2.6 20.4 %collective-permute-start.1 = (bf16[512,128]{1,0:T(8,128)(2,1)}, bf16[512,128]{1,0:T(8,128)(2,1)S(1)}, u32[]{:S(2)}, u32[]{:S(2)}) collective-permute-start(bf16[512,128]{1,0:T(8,128)(2,1)} %get-tuple-element.14.own), channel_id=1, source_target_pairs={{480,0},{484,4},{488,8},{492,12},{496,16},{500,20},{504,24},{508,2... | collective-permute-start | bytes 393224 | tf_op jit(solution)/shard_map/ppermute | solution.py:260
  9.2 18.4 %collective-permute-start = (bf16[512,128]{1,0:T(8,128)(2,1)}, bf16[512,128]{1,0:T(8,128)(2,1)S(1)}, u32[]{:S(2)}, u32[]{:S(2)}) collective-permute-start(bf16[512,128]{1,0:T(8,128)(2,1)} %get-tuple-element.14.own), channel_id=1, source_target_pairs={{496,0},{500,4},{504,8},{508,12},{0,16},{4,20},{8,24},{12,28},{16,... | collective-permute-start | bytes 393224 | tf_op jit(solution)/shard_map/ppermute | solution.py:260
  13.2 4.1 %copy-start.1 = (s32[128]{0:T(128)S(1)}, s32[128]{0:T(128)}, u32[]{:S(2)}) copy-start(s32[128]{0:T(128)} %bs.5) | copy-start | bytes 1540
  13.3 4.0 %copy-start.3 = (f32[8,128]{1,0:T(8,128)S(1)}, f32[8,128]{1,0:T(8,128)}, u32[]{:S(2)}) copy-start(f32[8,128]{1,0:T(8,128)} %constant.2.clone.freqs) | copy-start | bytes 12292
  13.3 8.5 %all-to-all-start = ((bf16[4,16,128]{2,1,0:T(8,128)(2,1)}), bf16[4,16,128]{2,1,0:T(8,128)(2,1)S(1)}, u32[]{:S(2)}, u32[]{:S(2)}) async-start(bf16[4,16,128]{2,1,0:T(8,128)(2,1)} %get-tuple-element.15), calls=%async_computation | async-start | bytes 32768 | tf_op jit(solution)/shard_map/all_to_all | solution.py:263
  28.5 7.0 %copy-start = (bf16[512,128]{1,0:T(8,128)(2,1)S(1)}, bf16[512,128]{1,0:T(8,128)(2,1)}, u32[]{:S(2)}) copy-start(bf16[512,128]{1,0:T(8,128)(2,1)} %get-tuple-element.14.own) | copy-start | bytes 393220
  28.5 24.0 %all-to-all-start.1 = ((bf16[32,64,128]{2,1,0:T(8,128)(2,1)}), bf16[32,64,128]{2,1,0:T(8,128)(2,1)S(1)}, u32[]{:S(2)}, u32[]{:S(2)}) async-start(bf16[32,64,128]{2,1,0:T(8,128)(2,1)} %shard_map.94.far), calls=%async_computation.1 | async-start | bytes 1048576 | tf_op jit(solution)/shard_map/all_to_all | solution.py:274
  35.6 9.8 %collective-permute-start.4 = (bf16[1024,128]{1,0:T(8,128)(2,1)S(1)}, bf16[1024,128]{1,0:T(8,128)(2,1)S(1)}, u32[]{:S(2)}, u32[]{:S(2)}) collective-permute-start(bf16[1024,128]{1,0:T(8,128)(2,1)S(1)} %get-tuple-element.18), channel_id=1, source_target_pairs={{0,12},{4,0},{8,4},{12,8},{16,28},{20,16},{24,20},{28,24},{32,44},... | collective-permute-start | bytes 786440 | tf_op jit(solution)/shard_map/ppermute | solution.py:280
  39.8 11.3 %collective-permute-start.2 = (bf16[1024,128]{1,0:T(8,128)(2,1)S(1)}, bf16[1024,128]{1,0:T(8,128)(2,1)S(1)}, u32[]{:S(2)}, u32[]{:S(2)}) collective-permute-start(bf16[1024,128]{1,0:T(8,128)(2,1)S(1)} %get-tuple-element.16), channel_id=1, source_target_pairs={{0,4},{4,8},{8,12},{12,0},{16,20},{20,24},{24,28},{28,16},{32,36},... | collective-permute-start | bytes 786440 | tf_op jit(solution)/shard_map/ppermute | solution.py:280
  41.8 9.4 %collective-permute-start.3 = (bf16[512,128]{1,0:T(8,128)(2,1)S(1)}, bf16[512,128]{1,0:T(8,128)(2,1)S(1)}, u32[]{:S(2)}, u32[]{:S(2)}) collective-permute-start(bf16[512,128]{1,0:T(8,128)(2,1)S(1)} %get-tuple-element.17), channel_id=1, source_target_pairs={{0,8},{4,12},{8,0},{12,4},{16,24},{20,28},{24,16},{28,20},{32,40},... | collective-permute-start | bytes 393224 | tf_op jit(solution)/shard_map/ppermute | solution.py:280
  45.4 7.0 %collective-permute-start.5 = (bf16[512,128]{1,0:T(8,128)(2,1)S(1)}, bf16[512,128]{1,0:T(8,128)(2,1)S(1)}, u32[]{:S(2)}, u32[]{:S(2)}) collective-permute-start(bf16[512,128]{1,0:T(8,128)(2,1)S(1)} %slice.4), channel_id=1, source_target_pairs={{0,12},{4,0},{8,4},{12,8},{16,28},{20,16},{24,20},{28,24},{32,44},... | collective-permute-start | bytes 393224 | tf_op jit(solution)/shard_map/ppermute | solution.py:285
  54.7 13.1 %collective-permute-start.7 = (bf16[32,2048]{1,0:T(8,128)(2,1)S(1)}, bf16[32,2048]{1,0:T(8,128)(2,1)S(1)}, u32[]{:S(2)}, u32[]{:S(2)}) collective-permute-start(bf16[32,2048]{1,0:T(8,128)(2,1)S(1)} %get-tuple-element.21), channel_id=1, source_target_pairs={{0,2},{1,3},{2,0},{3,1},{4,6},{5,7},{6,4},{7,5},{8,10},{9,11},{10,... | collective-permute-start | bytes 393224 | tf_op jit(solution)/shard_map/ppermute | solution.py:298
  57.0 10.8 %collective-permute-start.8 = (bf16[32,2048]{1,0:T(8,128)(2,1)S(1)}, bf16[32,2048]{1,0:T(8,128)(2,1)S(1)}, u32[]{:S(2)}, u32[]{:S(2)}) collective-permute-start(bf16[32,2048]{1,0:T(8,128)(2,1)S(1)} %get-tuple-element.22), channel_id=1, source_target_pairs={{0,3},{1,2},{2,1},{3,0},{4,7},{5,6},{6,5},{7,4},{8,11},{9,10},{10,... | collective-permute-start | bytes 393224 | tf_op jit(solution)/shard_map/ppermute | solution.py:298
  65.9 3.2 %collective-permute-start.6 = (bf16[32,2048]{1,0:T(8,128)(2,1)S(1)}, bf16[32,2048]{1,0:T(8,128)(2,1)S(1)}, u32[]{:S(2)}, u32[]{:S(2)}) collective-permute-start(bf16[32,2048]{1,0:T(8,128)(2,1)S(1)} %get-tuple-element.20), channel_id=1, source_target_pairs={{0,1},{1,0},{2,3},{3,2},{4,5},{5,4},{6,7},{7,6},{8,9},{9,8},{10,11... | collective-permute-start | bytes 393224 | tf_op jit(solution)/shard_map/ppermute | solution.py:298
